TPU v7x, 32 devices: a whole 2x2x4 slice. The times are simulated.
32 devices in a mesh: exp: 8 (over z, x), sky: 4 (over y, core).
Axes of the slice: x: 2, y: 2, z: 4, core: 2. Of those that a mesh axis runs over, the one named last changes fastest.
Arguments:
- image: float32 [8, 2048, 4096], P('exp', 'sky'), may hold values from -21 to 21
- variance: float32 [8, 2048, 4096], P('exp', 'sky'), may hold values from 0.25 to 4
- mask: int32 [8, 128, 256], P('exp', 'sky'), may hold values 0 or 1
- foot_start: int32 [8], replicated, may hold values from 0 to 64
- pair_owner: int32 [8, 8], replicated, may hold values from 0 to 1, as said below
Outputs:
- coadd: float32 [2048, 4096], P('sky', 'exp')
- offsets: float32 [8, 9], replicated
Inputs may be any that keep to these rules, and one draw needn't show every extreme that they name: pair_owner is 0 or 1, zero on the diagonal, pair_owner[i, j] and pair_owner[j, i] are never both 1, and every exposure has at least one pair.
All inputs are finite; a program needn't handle non-finite values. No bound on the sum of `mask` on one device may be relied on, other than what follows from the above.
Results may differ from a plain program's by a relative error of at most 0.0003.
Values sent between devices are 32-bit elements; how exact they have to be, the bound alone decides.
No kernel may reach another device: no remote copies, remote signals or barrier semaphores. Data moves between devices by JAX's collectives and lax.ppermute only.
A program may use at most 256 MiB of HBM per device.

v0:
```python
import jax
import jax.numpy as jnp
from jax import lax
from jax.sharding import PartitionSpec as P

BIN = 16
RADIUS = 10


HIGH = lax.Precision.HIGHEST
LAMBDA_REG = 0.25
PRIOR = 1.0


def extended(shard, sides, width):
    for axis, dim in sides:
        devices, length = (lax.axis_size(axis), shard.shape[dim])
        up = [(i, (i + 1) % devices) for i in range(devices - 1)]
        down = [(j, i) for i, j in up]
        last = lax.slice_in_dim(shard, length - width, length, axis=dim)
        leading = lax.slice_in_dim(shard, 0, width, axis=dim)
        before = lax.ppermute(last, axis, up)
        after = lax.ppermute(leading, axis, down)
        shard = jnp.concatenate([before, shard, after], axis=dim)
    return shard


def chebyshev(coord):
    return jnp.stack([jnp.ones_like(coord), coord, 2.0 * coord * coord - 1.0])


def centers(count, start, total):
    return (2.0 * (jnp.arange(count) + start).astype(jnp.float32) + 1.0) / total - 1.0


def footprint(count, start, width):
    cells = jnp.arange(count)
    return ((cells >= start) & (cells < start + width)).astype(jnp.float32)


def bin_basis(rows, row_first, total_rows, cols):
    by = chebyshev(centers(rows, row_first, total_rows))
    bx = chebyshev(centers(cols, 0, cols))
    return (by[:, None, :, None] * bx[None, :, None, :]).reshape(9, rows, cols)


def pair_normals(own_image, own_weight, other_image, other_weight, basis):
    weight = own_weight * other_weight / (own_weight + other_weight + 1.0)
    diff = own_image - other_image
    weighted = weight[:, None] * basis[None]
    gram = jnp.einsum("nkpq,lpq->nkl", weighted, basis, precision=HIGH)
    rhs = jnp.einsum("nkpq,npq->nk", weighted, diff, precision=HIGH)
    return (gram, rhs)


def solve_pairs(gram, rhs, owner):
    eye = jnp.eye(9, dtype=jnp.float32)
    safe = jnp.where(owner[..., None, None] > 0, gram, eye)
    factor = jnp.linalg.cholesky(safe)
    half = jax.scipy.linalg.solve_triangular(factor, rhs[..., None], lower=True)
    fit = jax.scipy.linalg.solve_triangular(factor, half, lower=True, trans=1)[..., 0]
    return fit * owner[..., None]


def global_offsets(fits, owner):
    degree = jnp.sum(owner, 1) + jnp.sum(owner, 0) + LAMBDA_REG
    system = jnp.diag(degree) - owner - owner.T
    right = jnp.sum(fits, 1) - jnp.sum(fits, 0)
    factor = jnp.linalg.cholesky(system)
    half = jax.scipy.linalg.solve_triangular(factor, right, lower=True)
    return jax.scipy.linalg.solve_triangular(factor, half, lower=True, trans=1)


def gauss_taps():
    offs = jnp.arange(-RADIUS, RADIUS + 1).astype(jnp.float32)
    taps = jnp.exp(-offs * offs / 50.0)
    return taps / jnp.sum(taps)


def smooth_rows(padded, taps, rows):
    total = taps[0] * padded[0:rows]
    for shift in range(1, 2 * RADIUS + 1):
        total = total + taps[shift] * padded[shift : shift + rows]
    return total


def smooth_cols(field, taps):
    cols = field.shape[1]
    padded = jnp.pad(field, ((0, 0), (RADIUS, RADIUS)))
    total = taps[0] * padded[:, 0:cols]
    for shift in range(1, 2 * RADIUS + 1):
        total = total + taps[shift] * padded[:, shift : shift + cols]
    return total


def expand_blocks(blocks):
    rows_b, cols_b = blocks.shape
    return jnp.broadcast_to(blocks[:, None, :, None], (rows_b, BIN, cols_b, BIN)).reshape(
        rows_b * BIN, cols_b * BIN
    )


def per_device(image, variance, mask, foot_start, pair_owner):
    frame = image[0]
    spread = variance[0]
    blocks = mask[0].astype(jnp.float32)
    rows_dev, cols = frame.shape
    bins_row = rows_dev // BIN
    bins_col = cols // BIN
    exposures = lax.axis_size("exp")
    sky_count = lax.axis_size("sky")
    member = lax.axis_index("exp")
    band = lax.axis_index("sky")
    owner = pair_owner.astype(jnp.float32)
    start = lax.dynamic_index_in_dim(foot_start, member, 0, keepdims=False)
    bin_image = frame.reshape(bins_row, BIN, bins_col, BIN).mean(axis=(1, 3))
    inside_bins = footprint(bins_col, start, 3 * cols // 4 // BIN)
    inverse = (1.0 / spread).reshape(bins_row, BIN, bins_col, BIN).sum(axis=(1, 3))
    bin_weight = inverse * blocks * inside_bins[None, :]
    basis = bin_basis(bins_row, band * bins_row, bins_row * sky_count, bins_col)
    gram, rhs = pair_normals(
        bin_image[None],
        bin_weight[None],
        lax.all_gather(bin_image[None], "exp", axis=0, tiled=True),
        lax.all_gather(bin_weight[None], "exp", axis=0, tiled=True),
        basis,
    )
    gram_rows = lax.dynamic_update_slice_in_dim(
        jnp.zeros((exposures, exposures, 9, 9), jnp.float32), gram[None], member, 0
    )
    rhs_rows = lax.dynamic_update_slice_in_dim(
        jnp.zeros((exposures, exposures, 9), jnp.float32), rhs[None], member, 0
    )
    gram_full, rhs_full = lax.psum((gram_rows, rhs_rows), ("exp", "sky"))
    fits = solve_pairs(gram_full, rhs_full, owner)
    offsets = global_offsets(fits, owner)
    coeffs = lax.dynamic_index_in_dim(offsets, member, 0, keepdims=False).reshape(3, 3)
    ty = chebyshev(centers(rows_dev, band * rows_dev, rows_dev * sky_count))
    tx = chebyshev(centers(cols, 0, cols))
    background = jnp.dot(jnp.dot(ty.T, coeffs, precision=HIGH), tx, precision=HIGH)
    inside_pixels = footprint(cols, start * BIN, 3 * cols // 4)
    corrected = (frame - background) * inside_pixels[None, :]
    padded = extended(corrected, (("sky", 0),), RADIUS)
    taps = gauss_taps()
    smoothed = smooth_cols(smooth_rows(padded, taps, rows_dev), taps)
    weight = expand_blocks(blocks) * inside_pixels[None, :] / spread
    numer = weight * smoothed
    share = cols // exposures
    total_num, total_den = lax.psum((numer, weight), "exp")
    part_num = lax.dynamic_slice_in_dim(total_num, member * share, share, 1)
    part_den = lax.dynamic_slice_in_dim(total_den, member * share, share, 1)
    coadd = part_num / (PRIOR + part_den)
    return (coadd, offsets)


def solution(mesh):
    placed = (P("exp", "sky", None), P("exp", "sky", None), P("exp", "sky", None), P(), P())
    return jax.shard_map(
        per_device, mesh=mesh, in_specs=placed, out_specs=(P("sky", "exp"), P()), check_vma=False
    )
```

profile of v0, /device:TPU:0, one launch (start us, length us, event | category | flops | bytes accessed | tf_op | source)
XLA Modules:
  0.0 1185.4 jit_solution(12949757785812578231)
XLA Ops:
  9.5 1.2 dynamic_slice.14
  17.2 7.9 broadcast_divide_fusion
  25.1 36.0 %div.96 = f32[32,16,256,16]{3,2,1,0:T(8,128)} reshape(f32[1,512,4096]{2,1,0:T(8,128)} %broadcast_divide_fusion) | data formatting | bytes 16777216 | tf_op jit(solution)/shard_map/div | solution.py:118
  61.1 20.8 %reduce_sum.68 = f32[32,256]{1,0:T(8,128)S(1)} reduce(f32[32,16,256,16]{3,2,1,0:T(8,128)} %div.96, f32[]{:T(128)} %constant.169.clone.1), dimensions={1,3}, to_apply=%region_5.6 | reduce | flops 2088960 | bytes 8421380 | tf_op jit(solution)/shard_map/reduce_sum | solution.py:118
  81.9 32.5 %all_gather.6 = f32[8,32,256]{2,1,0:T(8,128)S(1)} all-gather(f32[1,32,256]{2,1,0:T(8,128)S(1)} %fusion.101), channel_id=1, replica_groups=mesh['exp'=8,'sky'=4] {'exp'}, dimensions={0}, use_global_device_ids=true | all-gather | bytes 294912 | tf_op jit(solution)/shard_map/all_gather | solution.py:125
  114.4 36.0 %reshape_squeeze.3 = f32[32,16,256,16]{3,2,1,0:T(8,128)} reshape(f32[1,512,4096]{2,1,0:T(8,128)} %param.5) | data formatting | bytes 16777216 | tf_op jit(solution)/shard_map/reshape;squeeze | solution.py:116
  150.5 20.8 %reduce_sum.70 = f32[32,256]{1,0:T(8,128)S(1)} reduce(f32[32,16,256,16]{3,2,1,0:T(8,128)} %reshape_squeeze.3, f32[]{:T(128)} %constant.169.clone.1), dimensions={1,3}, to_apply=%region_9.10 | reduce | flops 2088960 | bytes 8421380 | tf_op jit(solution)/shard_map/reduce_sum | solution.py:116
  171.3 30.7 %all-gather = f32[256,256]{1,0:T(8,128)S(1)} all-gather(f32[32,256]{1,0:T(8,128)S(1)} %broadcast_multiply_fusion.1), channel_id=2, replica_groups=mesh['exp'=8,'sky'=4] {'exp'}, dimensions={0}, use_global_device_ids=true | all-gather | bytes 294912 | tf_op jit(solution)/shard_map/all_gather | solution.py:124
  202.3 3.4 fusion.87
  205.7 5.2 fusion.76
  210.8 46.5 %all-reduce.1 = (f32[8,8,9]{2,1,0:T(8,128)S(1)}, f32[8,8,9,9]{3,2,1,0:T(8,128)S(1)}) all-reduce(f32[8,8,9]{2,1,0:T(8,128)S(1)} %constant_dynamic-update-slice_fusion, f32[8,8,9,9]{3,2,1,0:T(8,128)S(1)} %fusion.87), channel_id=1, replica_groups=mesh['exp'=8,'sky'=4] {'exp','sky'}, use_global_device_ids=true, to_apply=%region_10.11 | all-reduce | flops 5760 | bytes 46080 | tf_op jit(solution)/shard_map/psum | solution.py:134
  258.1 52.7 %custom-call.22 = f32[8,8,9,9]{3,2,1,0:T(8,128)S(1)} custom-call(f32[8,8,9,9]{3,2,1,0:T(8,128)S(1)} %fusion.93), custom_call_target="Cholesky" | custom-call | tf_op jit(solution)/shard_map/jit(cholesky)/cholesky | solution.py:59
  311.4 45.1 %custom-call.23 = f32[8,8,1,9,9]{3,4,2,1,0:T(8,128)S(1)} custom-call(f32[8,8,1,9,9]{4,3,2,1,0:T(8,128)S(1)} %select_bitcast_fusion), custom_call_target="InvertDiagBlocksLowerTriangular" | custom-call | tf_op jit(solution)/shard_map/jit(_solve_triangular)/vmap(vmap())/triangular_solve | solution.py:61
  357.2 0.9 fusion.90
  358.9 9.3 fusion.58
  368.3 3.2 copy-done
  371.5 1.3 collective-permute-start
  372.8 1.5 collective-permute-start.1
  376.3 21.3 %broadcast_in_dim.67 = f32[32,16,256,16]{3,2,1,0:T(8,128)} broadcast(f32[32,256]{1,0:T(8,128)S(1)} %convert_bitcast_fusion), dimensions={0,2} | broadcast | bytes 8421376 | tf_op jit(solution)/shard_map/broadcast_in_dim | solution.py:98
  397.6 54.5 %reshape.227 = f32[512,4096]{1,0:T(8,128)} reshape(f32[32,16,256,16]{3,2,1,0:T(8,128)} %broadcast_in_dim.67) | data formatting | bytes 16777216 | tf_op jit(solution)/shard_map/reshape | solution.py:98
  452.8 89.0 %fusion.3 = f32[512,4096]{1,0:T(8,128)} fusion(f32[10,4096]{1,0:T(8,128)S(1)} %collective-permute-done.1, f32[10,4096]{1,0:T(8,128)S(1)} %collective-permute-done, f32[512,4096]{1,0:T(8,128)} %copy-done, f32[]{:T(128)} %bitcast.50, f32[]{:T(128)} %bitcast.49, f32[]{:T(128)} %bitcast.48, f32[]{:T(128)} %bitcast.47, f32[]{:T(128)} %bitcast.46, f32[]{:T(128)} %bitcast.45, ...), kind=kLoop, calls=%fused_computation.21 | loop fusion | flops 127926272 | bytes 17104980 | tf_op jit(solution)/shard_map/add | solution.py:83
  541.8 121.0 %add_multiply_fusion = (f32[512,4096]{1,0:T(8,128)}, f32[512,4096]{1,0:T(8,128)}) fusion(f32[512,4096]{1,0:T(8,128)} %fusion.3, f32[]{:T(128)} %bitcast.50, f32[]{:T(128)} %bitcast.49, f32[]{:T(128)} %bitcast.48, f32[]{:T(128)} %bitcast.47, f32[]{:T(128)} %bitcast.46, f32[]{:T(128)} %bitcast.45, f32[]{:T(128)} %bitcast.44, f32[]{:T(128)} %bitcast.43, ...), kind=kLoop, calls=%fused_computation.95 | loop fusion | flops 92274688 | bytes 41959508 | tf_op jit(solution)/shard_map/mul | solution.py:147
  662.9 512.9 %all-reduce.5.cloned.1.call-done = (f32[512,4096]{1,0:T(8,128)}, f32[512,4096]{1,0:T(8,128)}) async-done(((f32[512,4096]{1,0:T(8,128)}, f32[512,4096]{1,0:T(8,128)}), (f32[512,4096]{1,0:T(8,128)}, f32[512,4096]{1,0:T(8,128)})) %all-reduce.5.cloned.1.call-update) | async-done | bytes 16777232 | tf_op jit(solution)/shard_map/psum | solution.py:149
  1175.8 2.8 add_divide_fusion
  (70 shorter events, 13.1 us)
Async XLA Ops:
  7.2 1168.6 %all-reduce.5.cloned.1.call-start = ((), (), s32[]{:S(2)}) async-start(), calls=%async_computation | async-start | bytes 33554432 | tf_op jit(solution)/shard_map/psum | solution.py:149
  61.1 20.8 %copy-start.1 = (s32[1,32,256]{2,1,0:T(8,128)S(1)}, s32[1,32,256]{2,1,0:T(8,128)}, u32[]{:S(2)}) copy-start(s32[1,32,256]{2,1,0:T(8,128)} %param.7) | copy-start | bytes 98308
  358.5 9.7 copy-start.2
  368.3 3.2 copy-start
  371.5 81.3 %collective-permute-start = (f32[10,4096]{1,0:T(8,128)S(1)}, f32[10,4096]{1,0:T(8,128)S(1)}, u32[]{:S(2)}, u32[]{:S(2)}) collective-permute-start(f32[10,4096]{1,0:T(8,128)S(1)} %get-tuple-element.12), channel_id=1, source_target_pairs={{0,1},{1,2},{2,3},{4,5},{5,6},{6,7},{8,9},{9,10},{10,11},{12,13},{... | collective-permute-start | bytes 491528 | tf_op jit(solution)/shard_map/ppermute | solution.py:22
  372.8 80.0 %collective-permute-start.1 = (f32[10,4096]{1,0:T(8,128)S(1)}, f32[10,4096]{1,0:T(8,128)S(1)}, u32[]{:S(2)}, u32[]{:S(2)}) collective-permute-start(f32[10,4096]{1,0:T(8,128)S(1)} %get-tuple-element.13), channel_id=1, source_target_pairs={{1,0},{2,1},{3,2},{5,4},{6,5},{7,6},{9,8},{10,9},{11,10},{13,12},{... | collective-permute-start | bytes 491528 | tf_op jit(solution)/shard_map/ppermute | solution.py:23
Sparse Core Ops, SparseCore 0:
  663.0 512.7 all-reduce.4
where the time goes:
time: 1190 us
  waiting for transfers between devices  513 us (43%)
  other arithmetic  369 us (31%)
  local copies, waits for them, and re-layouts  155 us (13%)
  blocking collectives  110 us (9%)
  matrix products  20 us (2%)
  between operations  15.6 us (1%)
    psum x1, waiting for transfers between devices, per_device(): total_num, total_den = lax.psum((numer, weight), 'exp')  513 us
    mul x1, other arithmetic, per_device(): numer = weight * smoothed  121 us
    add x1, other arithmetic, smooth_rows(): total = total + taps[shift] * padded[shift:shift + rows]  89 us
    reshape x1, local copies, waits for them, and re-layouts, expand_blocks(): jnp.broadcast_to(blocks[:, None, :, None], (rows_b, BIN, cols_b, BIN))  54.5 us
    another operation x4, other arithmetic, solve_pairs(): factor = jnp.linalg.cholesky(safe)  53.1 us
    psum x1, blocking collectives, per_device(): gram_full, rhs_full = lax.psum((gram_rows, rhs_rows), ('exp', 'sky'))  46.5 us
    another operation x3, other arithmetic, solve_pairs(): jax.scipy.linalg.solve_triangular(factor, half, lower=True, trans=1)[..., 0]  45.2 us
    another operation x1, local copies, waits for them, and re-layouts, per_device(): bin_image = frame.reshape(bins_row, BIN, bins_col, BIN).mean(axis=(1, 3))  36 us
  transfers between devices with their start and end apart: 3, of which 1 were waited for; matrix products, arithmetic and copies ran while one was open for 7% of the time, Pallas kernels for 0%

commit v1 on v0

v1 whole, which is shorter than its diff:
```python
import functools

import jax
import jax.numpy as jnp
import ml_dtypes
import numpy as np
from jax import lax
from jax.experimental import pallas as pl
from jax.experimental.pallas import tpu as pltpu
from jax.sharding import PartitionSpec as P

BIN = 16
RADIUS = 10
HALO = 16
SIDE = 128
TILE = 256

HIGH = lax.Precision.HIGHEST
LAMBDA_REG = 0.25
PRIOR = 1.0
VMEM = 56 * 1024 * 1024
BF16 = jnp.bfloat16
F32 = jnp.float32


def tap_values():
    offs = np.arange(-RADIUS, RADIUS + 1).astype(np.float64)
    taps = np.exp(-offs * offs / 50.0)
    return taps / taps.sum()


def band(out, width, lead):
    taps = tap_values()
    full = np.zeros((out, width), np.float64)
    for shift in range(-RADIUS, RADIUS + 1):
        rows = np.arange(out)
        full[rows, rows + lead + shift] = taps[shift + RADIUS]
    return full


def two_parts(full):
    high = full.astype(np.float32).astype(ml_dtypes.bfloat16)
    low = (full - high.astype(np.float64)).astype(np.float32).astype(ml_dtypes.bfloat16)
    return high, low


def chebyshev(coord, count=3):
    terms = [jnp.ones_like(coord), coord]
    while len(terms) < count:
        terms.append(2.0 * coord * terms[-1] - terms[-2])
    return jnp.stack(terms)


def centers(index, total):
    return (2.0 * index.astype(F32) + 1.0) / total - 1.0


def split_high_low(value):
    high = value.astype(BF16)
    return high, (value - high.astype(F32)).astype(BF16)


def mm(left, right):
    return jnp.dot(left, right, preferred_element_type=F32)


def weights_kernel(plan, width, blocks_ref, start_ref, frame_ref, spread_ref, mask_ref, *outs):
    step = pl.program_id(0)
    bins_ref, weights = outs[0], outs[1:]
    block = blocks_ref[step]
    rows, share = frame_ref.shape
    bins_row, bins_col = mask_ref.shape
    inverse = 1.0 / spread_ref[...]
    cell = (lax.broadcasted_iota(jnp.int32, (bins_col, share), 1) + block * share) // BIN
    spread_out = (lax.broadcasted_iota(jnp.int32, (bins_col, share), 0) == cell).astype(BF16)
    kept = mm(mask_ref[...].astype(F32).astype(BF16), spread_out)
    first = start_ref[0] * BIN
    col = lax.broadcasted_iota(jnp.int32, (1, share), 1) + block * share
    kept = jnp.where((col >= first) & (col < first + width), kept, 0.0)
    kept = jnp.broadcast_to(kept[:, None, :], (bins_row, BIN, share)).reshape(rows, share)
    weight = inverse * kept
    for at, (out, fresh) in enumerate(plan):
        @pl.when(step == at)
        def _(out=out, fresh=fresh):
            weights[out][...] = weight if fresh else weights[out][...] + weight

    sums = jnp.concatenate(
        [
            frame_ref[...].reshape(bins_row, BIN, share).sum(axis=1),
            inverse.reshape(bins_row, BIN, share).sum(axis=1),
        ],
        axis=0,
    )
    cell_t = (lax.broadcasted_iota(jnp.int32, (share, bins_col), 0) + block * share) // BIN
    gather = (lax.broadcasted_iota(jnp.int32, (share, bins_col), 1) == cell_t).astype(BF16)
    top, rest = split_high_low(sums)
    middle = (sums - top.astype(F32)) - rest.astype(F32)
    part = mm(top, gather) + (mm(rest, gather) + mm(middle.astype(BF16), gather))

    @pl.when(step == 0)
    def _():
        bins_ref[...] = part

    @pl.when(step > 0)
    def _():
        bins_ref[...] = bins_ref[...] + part


def pixel_weights(plan, outputs, blocks, start, frame, spread, mask, share, width):
    rows = frame.shape[0]
    bins_row, bins_col = mask.shape
    column = pl.BlockSpec((rows, share), lambda i, blocks, start: (0, blocks[i]))
    whole = lambda shape: pl.BlockSpec(shape, lambda i, blocks, start: (0, 0))
    return pl.pallas_call(
        functools.partial(weights_kernel, plan, width),
        grid_spec=pltpu.PrefetchScalarGridSpec(
            num_scalar_prefetch=2,
            grid=(len(plan),),
            in_specs=[column, column, whole((bins_row, bins_col))],
            out_specs=[whole((2 * bins_row, bins_col))] + [whole((rows, share))] * outputs,
        ),
        out_shape=[jax.ShapeDtypeStruct((2 * bins_row, bins_col), F32)]
        + [jax.ShapeDtypeStruct((rows, share), F32)] * outputs,
        compiler_params=pltpu.CompilerParams(vmem_limit_bytes=VMEM),
        cost_estimate=pl.CostEstimate(
            flops=rows * share * len(plan) * 60, bytes_accessed=rows * share * len(plan) * 12, transcendentals=0
        ),
        name="pixel_weights",
    )(blocks, start, frame, spread, mask)


def smooth_kernel(plan, width, count, blocks_ref, start_ref, *refs):
    step = pl.program_id(0)
    images, (row_hi, row_lo, col_hi, col_lo) = refs[:9], refs[9:13]
    weights, outs = refs[13 : 13 + count], refs[13 + count :]
    block = blocks_ref[step]
    rows, share = images[4].shape
    window = share + 2 * SIDE
    field = jnp.concatenate(
        [jnp.concatenate([images[3 * i + j][...] for j in range(3)], axis=1) for i in range(3)], axis=0
    )
    first = start_ref[0] * BIN
    col = lax.broadcasted_iota(jnp.int32, (1, window), 1) + (block * share - SIDE)
    field = jnp.where((col >= first) & (col < first + width), field, 0.0)
    high, low = split_high_low(field)
    band_hi = row_hi[...]
    along = mm(band_hi, high) + (mm(row_lo[...], high) + mm(band_hi, low))
    high, low = split_high_low(along)
    band_hi = col_hi[...]
    tiles = []
    for tile in range(share // TILE):
        lanes = slice(tile * TILE, (tile + 1) * TILE + 2 * SIDE)
        tiles.append(mm(high[:, lanes], band_hi) + (mm(high[:, lanes], col_lo[...]) + mm(low[:, lanes], band_hi)))
    smoothed = tiles[0] if len(tiles) == 1 else jnp.concatenate(tiles, axis=1)
    col = lax.broadcasted_iota(jnp.int32, (1, share), 1) + block * share
    smoothed = jnp.where((col >= first) & (col < first + width), smoothed, 0.0)
    for at, (out, fresh) in enumerate(plan):
        @pl.when(step == at)
        def _(out=out, fresh=fresh):
            term = weights[out][...] * smoothed
            outs[out][...] = term if fresh else outs[out][...] + term


def smoothed_terms(plan, weights, blocks, start, frame, above, below, share, width):
    rows, cols = frame.shape
    count = len(weights)
    per = share // SIDE
    last = cols // SIDE - 1
    specs = []
    for height in (HALO, rows, HALO):
        specs += [
            pl.BlockSpec((height, SIDE), lambda i, blocks, start: (0, jnp.maximum(blocks[i] * per - 1, 0))),
            pl.BlockSpec((height, share), lambda i, blocks, start: (0, blocks[i])),
            pl.BlockSpec((height, SIDE), lambda i, blocks, start: (0, jnp.minimum(blocks[i] * per + per, last))),
        ]
    whole = lambda shape: pl.BlockSpec(shape, lambda i, blocks, start: (0, 0))
    row_parts = two_parts(band(rows, rows + 2 * HALO, HALO))
    col_parts = two_parts(band(TILE, TILE + 2 * SIDE, SIDE).T)
    parts = [jnp.asarray(p) for p in row_parts + col_parts]
    flops = 6 * rows * (rows + 2 * HALO) * (share + 2 * SIDE) + 6 * rows * share * (TILE + 2 * SIDE)
    return pl.pallas_call(
        functools.partial(smooth_kernel, plan, width, count),
        grid_spec=pltpu.PrefetchScalarGridSpec(
            num_scalar_prefetch=2,
            grid=(len(plan),),
            in_specs=specs + [whole(p.shape) for p in parts] + [whole((rows, share))] * count,
            out_specs=[whole((rows, share))] * count,
        ),
        out_shape=[jax.ShapeDtypeStruct((rows, share), F32)] * count,
        compiler_params=pltpu.CompilerParams(vmem_limit_bytes=VMEM),
        cost_estimate=pl.CostEstimate(
            flops=flops * len(plan), bytes_accessed=rows * share * len(plan) * 14, transcendentals=0
        ),
        name="smoothed_terms",
    )(blocks, start, *([above] * 3 + [frame] * 3 + [below] * 3), *parts, *weights)


def contract_last(left, right):
    return lax.dot_general(left, right, (((1,), (1,)), ((), ())), precision=HIGH, preferred_element_type=F32)


def moments_kernel(image_ref, weight_ref, basis_ref, out_ref):
    image, weight = image_ref[...], weight_ref[...]
    count = image.shape[0]
    pairs, diffs = [], []
    for apart in range(1, count // 2 + 1):
        other_w = jnp.concatenate([weight[apart:], weight[:apart]], axis=0)
        other_i = jnp.concatenate([image[apart:], image[:apart]], axis=0)
        joint = weight * other_w / (weight + other_w + 1.0)
        pairs.append(joint)
        diffs.append(joint * (image - other_i))
    basis = basis_ref[...]
    out_ref[...] = jnp.concatenate(
        [
            contract_last(basis, jnp.concatenate(pairs, axis=0)),
            contract_last(basis, jnp.concatenate(diffs, axis=0)),
        ],
        axis=0,
    )


def solve_kernel(moments_ref, owner_ref, out_ref):
    owner = owner_ref[...].astype(F32)
    count = owner.shape[0]
    lanes = moments_ref.shape[1]
    exposure = lax.broadcasted_iota(jnp.int32, (count, lanes), 0)
    lane = lax.broadcasted_iota(jnp.int32, (count, lanes), 1)
    mine = lane % count
    apart = lane // count + 1
    is_i = (exposure == mine).astype(F32)
    is_j = (exposure == (mine + apart) % count).astype(F32)
    both = owner + owner.T
    listed = jnp.sum(is_i * jnp.dot(both, is_j, precision=HIGH, preferred_element_type=F32), axis=0, keepdims=True)
    lane_row = lax.broadcasted_iota(jnp.int32, (1, lanes), 1)
    once = (lane_row // count + 1 < count // 2) | (lane_row % count < count // 2)
    listed = jnp.where(once, listed, 0.0)
    held = listed > 0.0
    moment = [[moments_ref[5 * a + b : 5 * a + b + 1, :] for b in range(5)] for a in range(5)]

    def entry(k, l):
        (u, v), (s, t) = divmod(k, 3), divmod(l, 3)
        total = 0.0
        for a in (u + s, abs(u - s)):
            for b in (v + t, abs(v - t)):
                total = total + moment[a][b]
        return jnp.where(held, 0.25 * total, 1.0 if k == l else 0.0)

    factor = [[None] * 9 for _ in range(9)]
    scale = [None] * 9
    for k in range(9):
        for l in range(k, 9):
            value = entry(l, k)
            for m in range(k):
                value = value - factor[l][m] * factor[k][m]
            if l == k:
                scale[k] = 1.0 / jnp.sqrt(value)
            else:
                factor[l][k] = value * scale[k]
    half = [None] * 9
    for k in range(9):
        at = 32 + 5 * (k // 3) + k % 3
        value = moments_ref[at : at + 1, :]
        for m in range(k):
            value = value - factor[k][m] * half[m]
        half[k] = value * scale[k]
    fit = [None] * 9
    for k in reversed(range(9)):
        value = half[k]
        for m in range(k + 1, 9):
            value = value - factor[m][k] * fit[m]
        fit[k] = value * scale[k]
    fits = jnp.concatenate([jnp.where(held, f, 0.0) for f in fit] + [jnp.zeros((7, lanes), F32)], axis=0)
    right = contract_last((is_i - is_j) * listed, fits)
    row = lax.broadcasted_iota(jnp.int32, (count, count), 0)
    column = lax.broadcasted_iota(jnp.int32, (count, count), 1)
    degree = jnp.sum(both, axis=1, keepdims=True) + LAMBDA_REG
    system = jnp.where(row == column, degree, 0.0) - both
    for k in range(count):
        inverse = 1.0 / system[k : k + 1, k : k + 1]
        pivot_s, pivot_r = system[k : k + 1, :] * inverse, right[k : k + 1, :] * inverse
        lead = system[:, k : k + 1]
        chosen = row[:, :1] == k
        system = jnp.where(chosen, pivot_s, system - lead * pivot_s)
        right = jnp.where(chosen, pivot_r, right - lead * pivot_r)
    out_ref[...] = right[:, :9]


def per_device(image, variance, mask, foot_start, pair_owner):
    frame, spread, blocks = image[0], variance[0], mask[0]
    rows, cols = frame.shape
    bins_row, bins_col = blocks.shape
    exposures, sky_count = lax.axis_size("exp"), lax.axis_size("sky")
    member, strip = lax.axis_index("exp"), lax.axis_index("sky")
    share = cols // exposures
    width = 3 * cols // 4
    places = exposures // 2
    quarter = places // 4
    place, side = member // 2, member % 2
    own_start = lax.dynamic_slice_in_dim(foot_start, member, 1)
    mate_start = lax.dynamic_slice_in_dim(foot_start, member + 1 - 2 * side, 1)

    order = np.zeros((places, places), np.int32)
    for z in range(places):
        down = z < places // 2
        ends = range(quarter)
        middle = list(range(quarter, places - quarter))
        listed = []
        for q in ends:
            low = quarter - 1 - q if down else q
            listed += [low, low + places - quarter]
        order[z] = listed + (middle[::-1] if down else middle)
    middle_count = places - 2 * quarter
    my_order = lax.dynamic_index_in_dim(jnp.asarray(order), place, 0, keepdims=False)
    sent_blocks = 2 * my_order + (1 - side)
    kept_blocks = 2 * my_order + side
    folded = [(i // 2, i % 2 == 0) for i in range(2 * quarter)]
    folded += [(quarter + i, True) for i in range(middle_count)]
    plain = [(i, True) for i in range(places)]
    units = quarter + middle_count

    up = [(i, i + 1) for i in range(sky_count - 1)]
    down = [(j, i) for i, j in up]
    above = lax.ppermute(frame[rows - HALO :], "sky", up)
    below = lax.ppermute(frame[:HALO], "sky", down)

    swap = [(i, i ^ 1) for i in range(exposures)]
    bins_a, *den_sent = pixel_weights(folded, units, sent_blocks, own_start, frame, spread, blocks, share, width)
    den_got = [lax.ppermute(d, "exp", swap) for d in den_sent]
    bins_b, *den_kept = pixel_weights(plain, places, kept_blocks, own_start, frame, spread, blocks, share, width)

    bins = (bins_a + bins_b).reshape(2, bins_row, bins_col)
    cell = jnp.arange(bins_col)
    inside_bins = (cell >= own_start) & (cell < own_start + width // BIN)
    keep = jnp.where(inside_bins[None, :], blocks, 0).astype(F32)
    both = jnp.stack([bins[0] / (BIN * BIN), bins[1] * keep])
    part_rows = bins_row // exposures
    both = both.reshape(2, exposures, part_rows, bins_col).swapaxes(0, 1)
    spread_bins = lax.all_to_all(both, "exp", 0, 0)
    per_exposure = spread_bins.reshape(exposures, 2, part_rows * bins_col)
    ty = chebyshev(centers(jnp.arange(part_rows) + (strip * bins_row + member * part_rows), bins_row * sky_count), 5)
    tx = chebyshev(centers(jnp.arange(bins_col), bins_col), 5)
    basis = (ty[:, None, :, None] * tx[None, :, None, :]).reshape(25, part_rows * bins_col)
    basis = jnp.concatenate([basis, jnp.zeros((7, part_rows * bins_col), F32)])
    moments = pl.pallas_call(
        moments_kernel,
        out_shape=jax.ShapeDtypeStruct((64, exposures * exposures // 2), F32),
        cost_estimate=pl.CostEstimate(flops=10**7, bytes_accessed=3 * 10**5, transcendentals=0),
        name="pair_moments",
    )(per_exposure[:, 0], per_exposure[:, 1], basis)
    for axis, size in (("sky", sky_count), ("exp", exposures)):
        bit = 1
        while bit < size:
            moments = moments + lax.ppermute(moments, axis, [(i, i ^ bit) for i in range(size)])
            bit *= 2
    offsets = pl.pallas_call(
        solve_kernel,
        out_shape=jax.ShapeDtypeStruct((exposures, 9), F32),
        cost_estimate=pl.CostEstimate(flops=10**6, bytes_accessed=10**5, transcendentals=0),
        name="offsets",
    )(moments, pair_owner)

    taps = tap_values().astype(np.float32)
    row_at = jnp.arange(-RADIUS, rows + RADIUS) + strip * rows
    ty = chebyshev(centers(row_at, rows * sky_count))
    ty = jnp.where((row_at >= 0) & (row_at < rows * sky_count), ty, 0.0)
    rows_part = sum(float(taps[t]) * ty[:, t : t + rows] for t in range(2 * RADIUS + 1))
    col_at = jnp.arange(-RADIUS, cols + RADIUS)
    tx = chebyshev(centers(col_at, cols))

    def columns_part(start):
        masked = jnp.where((col_at >= start * BIN) & (col_at < start * BIN + width), tx, 0.0)
        return sum(float(taps[t]) * masked[:, t : t + cols] for t in range(2 * RADIUS + 1))

    def coefficients(which, start):
        coeffs = lax.dynamic_index_in_dim(offsets, which, 0, keepdims=False).reshape(3, 3)
        return jnp.sum(coeffs[:, :, None] * columns_part(start)[None], axis=1)

    own_back = coefficients(member, own_start)
    mate_back = coefficients(member + 1 - 2 * side, mate_start)

    num_sent = smoothed_terms(folded, den_sent, sent_blocks, own_start, frame, above, below, share, width)
    num_got = [lax.ppermute(d, "exp", swap) for d in num_sent]
    num_kept = smoothed_terms(plain, den_kept, kept_blocks, own_start, frame, above, below, share, width)

    def background(back, at):
        cut = lax.dynamic_slice_in_dim(back, at * share, share, 1)
        return sum(rows_part[u][:, None] * cut[u][None, :] for u in range(3))

    unit_of = [out for out, fresh in folded]
    den_sum, num_sum = [], []
    for k in range(places):
        at = kept_blocks[k]
        got_den, got_num = den_got[unit_of[k]], num_got[unit_of[k]]
        if k < 2 * quarter:
            col = jnp.arange(share) + at * share
            inside = ((col >= mate_start * BIN) & (col < mate_start * BIN + width))[None, :]
            got_den = jnp.where(inside, got_den, 0.0)
            got_num = jnp.where(inside, got_num, 0.0)
        den_sum.append(den_kept[k] + got_den)
        num_sum.append(
            (num_kept[k] - den_kept[k] * background(own_back, at)) + (got_num - got_den * background(mate_back, at))
        )

    position = np.zeros((places, places), np.int32)
    for z in range(places):
        position[z, order[z]] = np.arange(places)

    def pick(parts, wanted):
        value = None
        for at in sorted(set(wanted.values())):
            if value is None:
                value = parts[at]
                continue
            here = functools.reduce(jnp.logical_or, [place == z for z, w in wanted.items() if w == at])
            value = jnp.where(here, parts[at], value)
        return value

    def along_places(parts):
        rightward = leftward = None
        for step in range(1, places):
            senders = {z: position[z, z + places - step] for z in range(places) if z + places - step < places}
            value = pick(parts, senders)
            value = value if rightward is None else value + rightward
            rightward = lax.ppermute(
                value, "exp", [(2 * z + s, 2 * z + 2 + s) for z in senders for s in range(2)]
            )
            senders = {z: position[z, z - places + step] for z in range(places) if z - places + step >= 0}
            value = pick(parts, senders)
            value = value if leftward is None else value + leftward
            leftward = lax.ppermute(
                value, "exp", [(2 * z + s, 2 * z - 2 + s) for z in senders for s in range(2)]
            )
        return pick(parts, {z: position[z, z] for z in range(places)}) + rightward + leftward

    total_den = along_places(den_sum)
    total_num = along_places(num_sum)
    return (total_num / (PRIOR + total_den), offsets)


def solution(mesh):
    placed = (P("exp", "sky", None), P("exp", "sky", None), P("exp", "sky", None), P(), P())
    return jax.shard_map(
        per_device, mesh=mesh, in_specs=placed, out_specs=(P("sky", "exp"), P()), check_vma=False
    )
```

time: 1190 us -> 299 us (0.25)
  waiting for transfers between devices: 513 us -> 101 us
  other arithmetic: 369 us -> 39.8 us
  local copies, waits for them, and re-layouts: 155 us -> 7.6 us
  blocking collectives: 110 us -> 0 us
  Pallas kernels: 0 us -> 71.5 us
  starting transfers between devices: 2.86 us -> 67.8 us
  matrix products: 20 us -> 0 us
    psum x1 -> x0, waiting for transfers between devices: 513 us -> none  [per_device(): total_num, total_den = lax.psum((numer, weight), 'exp')]
    mul x3 -> x2, other arithmetic: 121 us -> 0.09 us  [the longest x1 0.08 us: per_device(): ty[:, None, :, None] * tx[None, :, None, :]]
    another operation x14 -> x0, other arithmetic: 101 us -> none  [the longest x4 53.1 us: solve_pairs(): factor = jnp.linalg.cholesky(safe)]
    ppermute x2 -> x25, waiting for transfers between devices: 0.01 us -> 78 us  [the longest x6 69.9 us: along_places(): lax.ppermute(value, 'exp', [(2 * z + s, 2 * z + 2 + s) for z in senders f...]
    pallas_call x0 -> x6, Pallas kernels: none -> 71.5 us  [the longest x2 47.8 us: smoothed_terms(): pl.pallas_call(functools.partial(smooth_kernel, plan, width, count), grid...]
    all_gather x2 -> x0, blocking collectives: 63.3 us -> none  [the longest x1 32.5 us: per_device(): lax.all_gather(bin_weight[None], 'exp', axis=0, tiled=True)]
    ppermute x2 -> x25, starting transfers between devices: 2.82 us -> 61.5 us  [the longest x6 30.6 us: along_places(): lax.ppermute(value, 'exp', [(2 * z + s, 2 * z + 2 + s) for z in senders f...]
    add x2 -> x18, other arithmetic: 89 us -> 32.8 us  [the longest x3 14.1 us: along_places(): value = value if rightward is None else value + rightward]
  transfers between devices with their start and end apart: 3 -> 26, of which waited for: 1 -> 12; matrix products, arithmetic and copies ran while one was open for 7% -> 13% of each run, Pallas kernels for 0% -> 24%
where the time goes in v1:
time: 299 us; the launch traced here: 294 us
  waiting for transfers between devices  101 us (34%)
  Pallas kernels  71.5 us (24%)
  starting transfers between devices  67.8 us (23%)
  other arithmetic  39.8 us (13%)
  local copies, waits for them, and re-layouts  7.6 us (3%)
  between operations  5.56 us (2%)
    ppermute x6, waiting for transfers between devices, along_places(): lax.ppermute(value, 'exp', [(2 * z + s, 2 * z + 2 + s) for z in senders f...  69.9 us
    pallas_call x2, Pallas kernels, smoothed_terms(): pl.pallas_call(functools.partial(smooth_kernel, plan, width, count), grid...  47.8 us
    ppermute x6, starting transfers between devices, along_places(): lax.ppermute(value, 'exp', [(2 * z + s, 2 * z + 2 + s) for z in senders f...  30.6 us
    all_to_all x1, waiting for transfers between devices, per_device(): spread_bins = lax.all_to_all(both, 'exp', 0, 0)  23.4 us
    pallas_call x2, Pallas kernels, pixel_weights(): pl.pallas_call(functools.partial(weights_kernel, plan, width), grid_spec=...  19.7 us
    add x3, other arithmetic, along_places(): value = value if rightward is None else value + rightward  14.1 us
    ppermute x6, starting transfers between devices, along_places(): lax.ppermute(value, 'exp', [(2 * z + s, 2 * z - 2 + s) for z in senders f...  9.14 us
    ppermute x5, starting transfers between devices, per_device(): lax.ppermute(moments, axis, [(i, i ^ bit) for i in range(size)])  8.96 us
  transfers between devices with their start and end apart: 26, of which 12 were waited for; matrix products, arithmetic and copies ran while one was open for 13% of the time, Pallas kernels for 24%

profile of v1, /device:TPU:0, one launch (start us, length us, event | category | flops | bytes accessed | tf_op | source)
XLA Modules:
  0.0 293.7 jit_solution(9240596351556460174)
XLA Ops:
  3.0 3.0 %collective-permute-start = (f32[16,4096]{1,0:T(8,128)S(1)}, f32[16,4096]{1,0:T(8,128)S(1)}, u32[]{:S(2)}, u32[]{:S(2)}) collective-permute-start(f32[16,4096]{1,0:T(8,128)S(1)} %get-tuple-element.43), channel_id=1, source_target_pairs={{0,1},{1,2},{2,3},{4,5},{5,6},{6,7},{8,9},{9,10},{10,11},{12,13},{... | collective-permute-start | bytes 786440 | tf_op jit(solution)/shard_map/ppermute | solution.py:323
  8.7 9.7 %pixel_weights.3 = (f32[64,256]{1,0:T(8,128)}, f32[512,512]{1,0:T(8,128)}, f32[512,512]{1,0:T(8,128)}, f32[512,512]{1,0:T(8,128)}) custom-call(s32[4]{0:T(128)} %get-tuple-element.83.blocks_ref, s32[1]{0:T(128)} %get-tuple-element.90.start_ref, f32[512,4096]{1,0:T(8,128)} %bitcast.64, f32[512,4096]{1,0:T(8,128)} %bitcast.72, s32[32,256]{1,0:T(8,128)} %bitcast.77), custom_call_target="tpu_custom_call" | custom-call | flops 62914560 | bytes 12582912 | tf_op jit(solution)/shard_map/pixel_weights/pallas_call | solution.py:114
  18.4 2.9 %collective-permute-start.10 = (f32[512,512]{1,0:T(8,128)}, f32[512,512]{1,0:T(8,128)S(1)}, u32[]{:S(2)}, u32[]{:S(2)}) collective-permute-start(f32[512,512]{1,0:T(8,128)} %get-tuple-element.25.refs_13_), channel_id=1, source_target_pairs={{0,4},{4,0},{8,12},{12,8},{16,20},{20,16},{24,28},{28,24},{1,5},{5... | collective-permute-start | bytes 3145736 | tf_op jit(solution)/shard_map/ppermute | solution.py:328
  22.1 10.0 %pixel_weights.2 = (f32[64,256]{1,0:T(8,128)}, f32[512,512]{1,0:T(8,128)}, f32[512,512]{1,0:T(8,128)}, f32[512,512]{1,0:T(8,128)}, f32[512,512]{1,0:T(8,128)}) custom-call(s32[4]{0:T(128)} %bitcast.94, s32[1]{0:T(128)} %get-tuple-element.90.start_ref, f32[512,4096]{1,0:T(8,128)} %bitcast.65, f32[512,4096]{1,0:T(8,128)} %bitcast.73, s32[32,256]{1,0:T(8,128)} %bitcast.78), custom_call_target="tpu_custom_call" | custom-call | flops 62914560 | bytes 12582912 | tf_op jit(solution)/shard_map/pixel_weights/pallas_call | solution.py:114
  34.4 6.3 %all-to-all-start = ((f32[8,2,4,256]{3,2,1,0:T(4,128)}), f32[8,2,4,256]{3,2,1,0:T(4,128)S(1)}, u32[]{:S(2)}, u32[]{:S(2)}) async-start(f32[8,2,4,256]{3,2,1,0:T(4,128)} %maximum_bitcast_fusion), calls=%async_computation | async-start | bytes 131072 | tf_op jit(solution)/shard_map/all_to_all | solution.py:338
  44.7 23.4 %all-to-all-done = f32[8,2,4,256]{3,2,1,0:T(4,128)S(1)} async-done(((f32[8,2,4,256]{3,2,1,0:T(4,128)}), f32[8,2,4,256]{3,2,1,0:T(4,128)S(1)}, u32[]{:S(2)}, u32[]{:S(2)}) %all-to-all-start) | async-done | bytes 65568 | tf_op jit(solution)/shard_map/all_to_all | solution.py:338
  85.2 3.0 %collective-permute-start.6 = (f32[64,32]{1,0:T(8,128)S(1)}, f32[64,32]{1,0:T(8,128)S(1)}, u32[]{:S(2)}, u32[]{:S(2)}) collective-permute-start(f32[64,32]{1,0:T(8,128)S(1)} %add.738), channel_id=1, source_target_pairs={{0,16},{4,20},{8,24},{12,28},{16,0},{20,4},{24,8},{28,12},{1,17},{... | collective-permute-start | bytes 24584 | tf_op jit(solution)/shard_map/ppermute | solution.py:353
  94.7 23.6 %smoothed_terms.3 = (f32[512,512]{1,0:T(8,128)}, f32[512,512]{1,0:T(8,128)}, f32[512,512]{1,0:T(8,128)}) custom-call(s32[4]{0:T(128)} %get-tuple-element.83.blocks_ref, s32[1]{0:T(128)} %get-tuple-element.90.start_ref, f32[16,4096]{1,0:T(8,128)} %copy-done.5, f32[16,4096]{1,0:T(8,128)} %copy-done.5, f32[16,4096]{1,0:T(8,128)} %copy-done.5, ...), custom_call_target="tpu_custom_call" | custom-call | flops 8355053568 | bytes 14680064 | tf_op jit(solution)/shard_map/smoothed_terms/pallas_call | solution.py:181
  121.0 24.2 %smoothed_terms.2 = (f32[512,512]{1,0:T(8,128)}, f32[512,512]{1,0:T(8,128)}, f32[512,512]{1,0:T(8,128)}, f32[512,512]{1,0:T(8,128)}) custom-call(s32[4]{0:T(128)} %bitcast.95, s32[1]{0:T(128)} %get-tuple-element.90.start_ref, f32[16,4096]{1,0:T(8,128)} %copy-done.5, f32[16,4096]{1,0:T(8,128)} %copy-done.5, f32[16,4096]{1,0:T(8,128)} %copy-done.5, ...), custom_call_target="tpu_custom_call" | custom-call | flops 8355053568 | bytes 14680064 | tf_op jit(solution)/shard_map/smoothed_terms/pallas_call | solution.py:181
  146.3 3.2 %subtract_add_fusion.2 = (f32[512,512]{1,0:T(8,128)}, f32[512,512]{1,0:T(8,128)S(1)}) fusion(f32[512,512]{1,0:T(8,128)} %copy-done.11, f32[512,512]{1,0:T(8,128)} %get-tuple-element.29, f32[512,512]{1,0:T(8,128)S(1)} %copy-done.9, f32[512,512]{1,0:T(8,128)S(1)} %collective-permute-done.10, f32[512]{0:T(512)S(1)} %bitcast.107, f32[512]{0:T(512)S(1)} %bitcast.105, ...), kind=kLoop, calls=%fused_computation.11 | loop fusion | flops 4718592 | bytes 6310400 | tf_op jit(solution)/shard_map/add | solution.py:401
  149.5 4.8 %collective-permute-start.13 = (f32[512,512]{1,0:T(8,128)}, f32[512,512]{1,0:T(8,128)}, u32[]{:S(2)}, u32[]{:S(2)}) collective-permute-start(f32[512,512]{1,0:T(8,128)} %get-tuple-element.46), channel_id=1, source_target_pairs={{0,8},{4,12},{1,9},{5,13},{2,10},{6,14},{3,11},{7,15}} | collective-permute-start | bytes 3145736 | tf_op jit(solution)/shard_map/ppermute | solution.py:424
  166.0 11.2 %collective-permute-done.13 = f32[512,512]{1,0:T(8,128)} collective-permute-done((f32[512,512]{1,0:T(8,128)}, f32[512,512]{1,0:T(8,128)}, u32[]{:S(2)}, u32[]{:S(2)}) %collective-permute-start.13) | collective-permute-done | bytes 1048608 | tf_op jit(solution)/shard_map/ppermute | solution.py:424
  178.7 14.9 %collective-permute-done.19 = f32[512,512]{1,0:T(8,128)} collective-permute-done((f32[512,512]{1,0:T(8,128)S(1)}, f32[512,512]{1,0:T(8,128)}, u32[]{:S(2)}, u32[]{:S(2)}) %collective-permute-start.19) | collective-permute-done | bytes 1048608 | tf_op jit(solution)/shard_map/ppermute | solution.py:424
  193.6 5.7 %select_add_fusion.6 = (f32[512,512]{1,0:T(8,128)}, f32[512,512]{1,0:T(8,128)}, f32[512,512]{1,0:T(8,128)}, f32[512,512]{1,0:T(8,128)}) fusion(f32[512,512]{1,0:T(8,128)} %collective-permute-done.13, f32[512,512]{1,0:T(8,128)} %get-tuple-element.46, pred[]{:T(512)S(6)} %eq.13, f32[512,512]{1,0:T(8,128)} %collective-permute-done.11, ...), kind=kLoop, calls=%fused_computation.7 | loop fusion | flops 5242880 | bytes 12601345 | tf_op jit(solution)/shard_map/add | solution.py:423
  199.3 6.1 %collective-permute-start.14 = (f32[512,512]{1,0:T(8,128)}, f32[512,512]{1,0:T(8,128)}, u32[]{:S(2)}, u32[]{:S(2)}) collective-permute-start(f32[512,512]{1,0:T(8,128)} %get-tuple-element.38), channel_id=1, source_target_pairs={{0,8},{4,12},{8,16},{12,20},{1,9},{5,13},{9,17},{13,21},{2,10},{6,... | collective-permute-start | bytes 3145736 | tf_op jit(solution)/shard_map/ppermute | solution.py:424
  216.1 12.2 %collective-permute-done.14 = f32[512,512]{1,0:T(8,128)} collective-permute-done((f32[512,512]{1,0:T(8,128)}, f32[512,512]{1,0:T(8,128)}, u32[]{:S(2)}, u32[]{:S(2)}) %collective-permute-start.14) | collective-permute-done | bytes 1048608 | tf_op jit(solution)/shard_map/ppermute | solution.py:424
  228.3 4.2 %select_add_fusion.7 = (f32[512,512]{1,0:T(8,128)}, f32[512,512]{1,0:T(8,128)S(1)}) fusion(f32[512,512]{1,0:T(8,128)} %collective-permute-done.14, f32[512,512]{1,0:T(8,128)} %get-tuple-element.39, f32[512,512]{1,0:T(8,128)} %get-tuple-element.46, pred[]{:T(512)S(6)} %eq.10, pred[]{:T(512)S(6)} %eq.13, f32[512,512]{1,0:T(8,128)} %collective-permute-done.7, ...), kind=kLoop, calls=%fused_computation.8 | loop fusion | flops 4718592 | bytes 9455618 | tf_op jit(solution)/shard_map/add | solution.py:423
  232.5 5.4 %collective-permute-start.15 = (f32[512,512]{1,0:T(8,128)}, f32[512,512]{1,0:T(8,128)}, u32[]{:S(2)}, u32[]{:S(2)}) collective-permute-start(f32[512,512]{1,0:T(8,128)} %get-tuple-element.36), channel_id=1, source_target_pairs={{0,8},{4,12},{8,16},{12,20},{16,24},{20,28},{1,9},{5,13},{9,17},{1... | collective-permute-start | bytes 3145736 | tf_op jit(solution)/shard_map/ppermute | solution.py:424
  241.9 8.9 %collective-permute-done.20 = f32[512,512]{1,0:T(8,128)} collective-permute-done((f32[512,512]{1,0:T(8,128)}, f32[512,512]{1,0:T(8,128)}, u32[]{:S(2)}, u32[]{:S(2)}) %collective-permute-start.20) | collective-permute-done | bytes 1048608 | tf_op jit(solution)/shard_map/ppermute | solution.py:424
  250.8 4.1 %select_add_fusion.3 = (f32[512,512]{1,0:T(8,128)}, f32[512,512]{1,0:T(8,128)}) fusion(f32[512,512]{1,0:T(8,128)} %collective-permute-done.20, f32[512,512]{1,0:T(8,128)S(1)} %copy-done.6, f32[512,512]{1,0:T(8,128)S(1)} %copy-done.2, pred[]{:T(512)S(6)} %eq.10, pred[]{:T(512)S(6)} %eq.13, f32[512,512]{1,0:T(8,128)S(1)} %copy-done, ...), kind=kLoop, calls=%fused_computation.4 | loop fusion | flops 1835008 | bytes 9437188 | tf_op jit(solution)/shard_map/add | solution.py:423
  254.9 9.9 %collective-permute-start.21 = (f32[512,512]{1,0:T(8,128)}, f32[512,512]{1,0:T(8,128)}, u32[]{:S(2)}, u32[]{:S(2)}) collective-permute-start(f32[512,512]{1,0:T(8,128)} %get-tuple-element.44), channel_id=1, source_target_pairs={{0,8},{4,12},{8,16},{12,20},{16,24},{20,28},{1,9},{5,13},{9,17},{1... | collective-permute-start | bytes 3145736 | tf_op jit(solution)/shard_map/ppermute | solution.py:424
  266.1 7.2 %collective-permute-done.15 = f32[512,512]{1,0:T(8,128)} collective-permute-done((f32[512,512]{1,0:T(8,128)}, f32[512,512]{1,0:T(8,128)}, u32[]{:S(2)}, u32[]{:S(2)}) %collective-permute-start.15) | collective-permute-done | bytes 1048608 | tf_op jit(solution)/shard_map/ppermute | solution.py:424
  273.3 15.5 %collective-permute-done.21 = f32[512,512]{1,0:T(8,128)} collective-permute-done((f32[512,512]{1,0:T(8,128)}, f32[512,512]{1,0:T(8,128)}, u32[]{:S(2)}, u32[]{:S(2)}) %collective-permute-start.21) | collective-permute-done | bytes 1048608 | tf_op jit(solution)/shard_map/ppermute | solution.py:424
  288.8 4.9 %add_divide_fusion = f32[512,512]{1,0:T(8,128)} fusion(f32[512,512]{1,0:T(8,128)} %collective-permute-done.24, f32[512,512]{1,0:T(8,128)} %collective-permute-done.21, f32[512,512]{1,0:T(8,128)} %copy-done.1, f32[512,512]{1,0:T(8,128)S(1)} %get-tuple-element.49, f32[512,512]{1,0:T(8,128)} %collective-permute-done.18, f32[512,512]{1,0:T(8,128)} %collective-permute-done.15, ...), kind=kLoop, calls=%fused_computation | loop fusion | flops 2883584 | bytes 12582914 | tf_op jit(solution)/shard_map/div | solution.py:437
  (123 shorter events, 63.7 us)
Async XLA Ops:
  1.7 92.2 %collective-permute-start.1 = (f32[16,4096]{1,0:T(8,128)S(1)}, f32[16,4096]{1,0:T(8,128)S(1)}, u32[]{:S(2)}, u32[]{:S(2)}) collective-permute-start(f32[16,4096]{1,0:T(8,128)S(1)} %get-tuple-element.42), channel_id=1, source_target_pairs={{1,0},{2,1},{3,2},{5,4},{6,5},{7,6},{9,8},{10,9},{11,10},{13,12},{... | collective-permute-start | bytes 786440 | tf_op jit(solution)/shard_map/ppermute | solution.py:324
  3.0 90.9 %collective-permute-start = (f32[16,4096]{1,0:T(8,128)S(1)}, f32[16,4096]{1,0:T(8,128)S(1)}, u32[]{:S(2)}, u32[]{:S(2)}) collective-permute-start(f32[16,4096]{1,0:T(8,128)S(1)} %get-tuple-element.43), channel_id=1, source_target_pairs={{0,1},{1,2},{2,3},{4,5},{5,6},{6,7},{8,9},{9,10},{10,11},{12,13},{... | collective-permute-start | bytes 786440 | tf_op jit(solution)/shard_map/ppermute | solution.py:323
  18.4 126.8 %collective-permute-start.10 = (f32[512,512]{1,0:T(8,128)}, f32[512,512]{1,0:T(8,128)S(1)}, u32[]{:S(2)}, u32[]{:S(2)}) collective-permute-start(f32[512,512]{1,0:T(8,128)} %get-tuple-element.25.refs_13_), channel_id=1, source_target_pairs={{0,4},{4,0},{8,12},{12,8},{16,20},{20,16},{24,28},{28,24},{1,5},{5... | collective-permute-start | bytes 3145736 | tf_op jit(solution)/shard_map/ppermute | solution.py:328
  21.4 139.5 %collective-permute-start.12 = (f32[512,512]{1,0:T(8,128)}, f32[512,512]{1,0:T(8,128)}, u32[]{:S(2)}, u32[]{:S(2)}) collective-permute-start(f32[512,512]{1,0:T(8,128)} %get-tuple-element.26.refs_14_), channel_id=1, source_target_pairs={{0,4},{4,0},{8,12},{12,8},{16,20},{20,16},{24,28},{28,24},{1,5},{5... | collective-permute-start | bytes 3145736 | tf_op jit(solution)/shard_map/ppermute | solution.py:328
  34.4 33.8 %all-to-all-start = ((f32[8,2,4,256]{3,2,1,0:T(4,128)}), f32[8,2,4,256]{3,2,1,0:T(4,128)S(1)}, u32[]{:S(2)}, u32[]{:S(2)}) async-start(f32[8,2,4,256]{3,2,1,0:T(4,128)} %maximum_bitcast_fusion), calls=%async_computation | async-start | bytes 131072 | tf_op jit(solution)/shard_map/all_to_all | solution.py:338
  76.9 4.3 %collective-permute-start.4 = (f32[64,32]{1,0:T(8,128)S(1)}, f32[64,32]{1,0:T(8,128)S(1)}, u32[]{:S(2)}, u32[]{:S(2)}) collective-permute-start(f32[64,32]{1,0:T(8,128)S(1)} %add.736), channel_id=1, source_target_pairs={{0,4},{4,0},{8,12},{12,8},{16,20},{20,16},{24,28},{28,24},{1,5},{5... | collective-permute-start | bytes 24584 | tf_op jit(solution)/shard_map/ppermute | solution.py:353
  81.2 4.0 %collective-permute-start.5 = (f32[64,32]{1,0:T(8,128)S(1)}, f32[64,32]{1,0:T(8,128)S(1)}, u32[]{:S(2)}, u32[]{:S(2)}) collective-permute-start(f32[64,32]{1,0:T(8,128)S(1)} %add.737), channel_id=1, source_target_pairs={{0,8},{4,12},{8,0},{12,4},{16,24},{20,28},{24,16},{28,20},{1,9},{5... | collective-permute-start | bytes 24584 | tf_op jit(solution)/shard_map/ppermute | solution.py:353
  85.2 4.9 %collective-permute-start.6 = (f32[64,32]{1,0:T(8,128)S(1)}, f32[64,32]{1,0:T(8,128)S(1)}, u32[]{:S(2)}, u32[]{:S(2)}) collective-permute-start(f32[64,32]{1,0:T(8,128)S(1)} %add.738), channel_id=1, source_target_pairs={{0,16},{4,20},{8,24},{12,28},{16,0},{20,4},{24,8},{28,12},{1,17},{... | collective-permute-start | bytes 24584 | tf_op jit(solution)/shard_map/ppermute | solution.py:353
  118.3 27.0 %collective-permute-start.9 = (f32[512,512]{1,0:T(8,128)}, f32[512,512]{1,0:T(8,128)S(1)}, u32[]{:S(2)}, u32[]{:S(2)}) collective-permute-start(f32[512,512]{1,0:T(8,128)} %get-tuple-element.30), channel_id=1, source_target_pairs={{0,4},{4,0},{8,12},{12,8},{16,20},{20,16},{24,28},{28,24},{1,5},{5... | collective-permute-start | bytes 3145736 | tf_op jit(solution)/shard_map/ppermute | solution.py:382
  120.7 43.4 %collective-permute-start.11 = (f32[512,512]{1,0:T(8,128)}, f32[512,512]{1,0:T(8,128)}, u32[]{:S(2)}, u32[]{:S(2)}) collective-permute-start(f32[512,512]{1,0:T(8,128)} %get-tuple-element.33), channel_id=1, source_target_pairs={{0,4},{4,0},{8,12},{12,8},{16,20},{20,16},{24,28},{28,24},{1,5},{5... | collective-permute-start | bytes 3145736 | tf_op jit(solution)/shard_map/ppermute | solution.py:382
  149.5 27.7 %collective-permute-start.13 = (f32[512,512]{1,0:T(8,128)}, f32[512,512]{1,0:T(8,128)}, u32[]{:S(2)}, u32[]{:S(2)}) collective-permute-start(f32[512,512]{1,0:T(8,128)} %get-tuple-element.46), channel_id=1, source_target_pairs={{0,8},{4,12},{1,9},{5,13},{2,10},{6,14},{3,11},{7,15}} | collective-permute-start | bytes 3145736 | tf_op jit(solution)/shard_map/ppermute | solution.py:424
  154.3 39.2 %collective-permute-start.19 = (f32[512,512]{1,0:T(8,128)S(1)}, f32[512,512]{1,0:T(8,128)}, u32[]{:S(2)}, u32[]{:S(2)}) collective-permute-start(f32[512,512]{1,0:T(8,128)S(1)} %get-tuple-element.47), channel_id=1, source_target_pairs={{0,8},{4,12},{1,9},{5,13},{2,10},{6,14},{3,11},{7,15}} | collective-permute-start | bytes 3145736 | tf_op jit(solution)/shard_map/ppermute | solution.py:424
  159.2 46.2 %collective-permute-start.16 = (f32[512,512]{1,0:T(8,128)S(1)}, f32[512,512]{1,0:T(8,128)}, u32[]{:S(2)}, u32[]{:S(2)}) collective-permute-start(f32[512,512]{1,0:T(8,128)S(1)} %get-tuple-element.48), channel_id=1, source_target_pairs={{24,16},{28,20},{25,17},{29,21},{26,18},{30,22},{27,19},{31,23}} | collective-permute-start | bytes 3145736 | tf_op jit(solution)/shard_map/ppermute | solution.py:430
  160.8 48.8 %collective-permute-start.22 = (f32[512,512]{1,0:T(8,128)S(1)}, f32[512,512]{1,0:T(8,128)}, u32[]{:S(2)}, u32[]{:S(2)}) collective-permute-start(f32[512,512]{1,0:T(8,128)S(1)} %get-tuple-element.49), channel_id=1, source_target_pairs={{24,16},{28,20},{25,17},{29,21},{26,18},{30,22},{27,19},{31,23}} | collective-permute-start | bytes 3145736 | tf_op jit(solution)/shard_map/ppermute | solution.py:430
  164.1 50.3 %collective-permute-start.8 = (f32[512,512]{1,0:T(8,128)}, f32[512,512]{1,0:T(8,128)}, u32[]{:S(2)}, u32[]{:S(2)}) collective-permute-start(f32[512,512]{1,0:T(8,128)} %get-tuple-element.27.refs_15_), channel_id=1, source_target_pairs={{0,4},{4,0},{8,12},{12,8},{16,20},{20,16},{24,28},{28,24},{1,5},{5... | collective-permute-start | bytes 3145736 | tf_op jit(solution)/shard_map/ppermute | solution.py:328
  177.2 38.9 %collective-permute-start.7 = (f32[512,512]{1,0:T(8,128)}, f32[512,512]{1,0:T(8,128)}, u32[]{:S(2)}, u32[]{:S(2)}) collective-permute-start(f32[512,512]{1,0:T(8,128)} %get-tuple-element.28), channel_id=1, source_target_pairs={{0,4},{4,0},{8,12},{12,8},{16,20},{20,16},{24,28},{28,24},{1,5},{5... | collective-permute-start | bytes 3145736 | tf_op jit(solution)/shard_map/ppermute | solution.py:382
  199.3 29.0 %collective-permute-start.14 = (f32[512,512]{1,0:T(8,128)}, f32[512,512]{1,0:T(8,128)}, u32[]{:S(2)}, u32[]{:S(2)}) collective-permute-start(f32[512,512]{1,0:T(8,128)} %get-tuple-element.38), channel_id=1, source_target_pairs={{0,8},{4,12},{8,16},{12,20},{1,9},{5,13},{9,17},{13,21},{2,10},{6,... | collective-permute-start | bytes 3145736 | tf_op jit(solution)/shard_map/ppermute | solution.py:424
  208.0 29.9 %collective-permute-start.17 = (f32[512,512]{1,0:T(8,128)}, f32[512,512]{1,0:T(8,128)}, u32[]{:S(2)}, u32[]{:S(2)}) collective-permute-start(f32[512,512]{1,0:T(8,128)} %select_add_fusion.4), channel_id=1, source_target_pairs={{16,8},{20,12},{24,16},{28,20},{17,9},{21,13},{25,17},{29,21},{18,... | collective-permute-start | bytes 3145736 | tf_op jit(solution)/shard_map/ppermute | solution.py:430
  209.6 41.2 %collective-permute-start.20 = (f32[512,512]{1,0:T(8,128)}, f32[512,512]{1,0:T(8,128)}, u32[]{:S(2)}, u32[]{:S(2)}) collective-permute-start(f32[512,512]{1,0:T(8,128)} %get-tuple-element.50), channel_id=1, source_target_pairs={{0,8},{4,12},{8,16},{12,20},{1,9},{5,13},{9,17},{13,21},{2,10},{6,... | collective-permute-start | bytes 3145736 | tf_op jit(solution)/shard_map/ppermute | solution.py:424
  214.4 36.4 %collective-permute-start.23 = (f32[512,512]{1,0:T(8,128)}, f32[512,512]{1,0:T(8,128)}, u32[]{:S(2)}, u32[]{:S(2)}) collective-permute-start(f32[512,512]{1,0:T(8,128)} %select_add_fusion), channel_id=1, source_target_pairs={{16,8},{20,12},{24,16},{28,20},{17,9},{21,13},{25,17},{29,21},{18,... | collective-permute-start | bytes 3145736 | tf_op jit(solution)/shard_map/ppermute | solution.py:430
  232.5 40.7 %collective-permute-start.15 = (f32[512,512]{1,0:T(8,128)}, f32[512,512]{1,0:T(8,128)}, u32[]{:S(2)}, u32[]{:S(2)}) collective-permute-start(f32[512,512]{1,0:T(8,128)} %get-tuple-element.36), channel_id=1, source_target_pairs={{0,8},{4,12},{8,16},{12,20},{16,24},{20,28},{1,9},{5,13},{9,17},{1... | collective-permute-start | bytes 3145736 | tf_op jit(solution)/shard_map/ppermute | solution.py:424
  240.6 32.7 %collective-permute-start.18 = (f32[512,512]{1,0:T(8,128)}, f32[512,512]{1,0:T(8,128)}, u32[]{:S(2)}, u32[]{:S(2)}) collective-permute-start(f32[512,512]{1,0:T(8,128)} %select_add_fusion.5), channel_id=1, source_target_pairs={{8,0},{12,4},{16,8},{20,12},{24,16},{28,20},{9,1},{13,5},{17,9},{2... | collective-permute-start | bytes 3145736 | tf_op jit(solution)/shard_map/ppermute | solution.py:430
  254.9 33.9 %collective-permute-start.21 = (f32[512,512]{1,0:T(8,128)}, f32[512,512]{1,0:T(8,128)}, u32[]{:S(2)}, u32[]{:S(2)}) collective-permute-start(f32[512,512]{1,0:T(8,128)} %get-tuple-element.44), channel_id=1, source_target_pairs={{0,8},{4,12},{8,16},{12,20},{16,24},{20,28},{1,9},{5,13},{9,17},{1... | collective-permute-start | bytes 3145736 | tf_op jit(solution)/shard_map/ppermute | solution.py:424
  264.8 24.0 %collective-permute-start.24 = (f32[512,512]{1,0:T(8,128)}, f32[512,512]{1,0:T(8,128)}, u32[]{:S(2)}, u32[]{:S(2)}) collective-permute-start(f32[512,512]{1,0:T(8,128)} %get-tuple-element.45), channel_id=1, source_target_pairs={{8,0},{12,4},{16,8},{20,12},{24,16},{28,20},{9,1},{13,5},{17,9},{2... | collective-permute-start | bytes 3145736 | tf_op jit(solution)/shard_map/ppermute | solution.py:430
  (17 other events, 355.3 us)

commit v2 on v1

v2 whole, which is shorter than its diff:
```python
import functools

import jax
import jax.numpy as jnp
import ml_dtypes
import numpy as np
from jax import lax
from jax.experimental import pallas as pl
from jax.experimental.pallas import tpu as pltpu
from jax.sharding import PartitionSpec as P

BIN = 16
RADIUS = 10
HALO = 16
SIDE = 128
TILE = 256

HIGH = lax.Precision.HIGHEST
LAMBDA_REG = 0.25
PRIOR = 1.0
VMEM = 56 * 1024 * 1024
BF16 = jnp.bfloat16
F32 = jnp.float32
SMALL = pl.CostEstimate(flops=1000, bytes_accessed=1000, transcendentals=0)


def tap_values():
    offs = np.arange(-RADIUS, RADIUS + 1).astype(np.float64)
    taps = np.exp(-offs * offs / 50.0)
    return taps / taps.sum()


def band(out, width, lead):
    taps = tap_values()
    full = np.zeros((out, width), np.float64)
    for shift in range(-RADIUS, RADIUS + 1):
        rows = np.arange(out)
        full[rows, rows + lead + shift] = taps[shift + RADIUS]
    return full


def two_parts(full):
    high = full.astype(np.float32).astype(ml_dtypes.bfloat16)
    low = (full - high.astype(np.float64)).astype(np.float32).astype(ml_dtypes.bfloat16)
    return high, low


def chebyshev(coord, count=3):
    terms = [jnp.ones_like(coord), coord]
    while len(terms) < count:
        terms.append(2.0 * coord * terms[-1] - terms[-2])
    return jnp.stack(terms)


def centers(index, total):
    return (2.0 * index.astype(F32) + 1.0) / total - 1.0


def split_high_low(value):
    high = value.astype(BF16)
    return high, (value - high.astype(F32)).astype(BF16)


def mm(left, right):
    return jnp.dot(left, right, preferred_element_type=F32)


def weights_kernel(plan, units, width, blocks_ref, start_ref, frame_ref, spread_ref, mask_ref, *refs):
    outs, (scatter, gather) = refs[:-2], refs[-2:]
    bins_ref, weights = outs[-1], outs[:-1]
    step = pl.program_id(1)
    block = blocks_ref[step]
    rows, share = frame_ref.shape
    bins_row, bins_col = mask_ref.shape
    per = share // BIN

    @pl.when((pl.program_id(0) == 0) & (step == 0))
    def _():
        cell = lax.broadcasted_iota(jnp.int32, (SIDE, share), 1) >> 4
        scatter[...] = (cell == lax.broadcasted_iota(jnp.int32, (SIDE, share), 0)).astype(BF16)
        cell = lax.broadcasted_iota(jnp.int32, (share, SIDE), 0) >> 4
        gather[...] = (cell == lax.broadcasted_iota(jnp.int32, (share, SIDE), 1)).astype(BF16)

    inverse = 1.0 / spread_ref[...]
    blocks_here = pltpu.roll(mask_ref[...].astype(F32), lax.rem(bins_col - block * per, bins_col), 1)[:, :SIDE]
    kept = mm(blocks_here.astype(BF16), scatter[...])
    first = start_ref[0] * BIN
    col = lax.broadcasted_iota(jnp.int32, (1, share), 1) + block * share
    kept = jnp.where((col >= first) & (col < first + width), kept, 0.0)
    weight = inverse * jnp.broadcast_to(kept[:, None, :], (bins_row, BIN, share)).reshape(rows, share)
    for at, (out, fresh) in enumerate(plan):
        @pl.when(step == at)
        def _(out=out, fresh=fresh):
            if out >= units:
                weights[-1][0] = weight
            elif fresh:
                weights[out][...] = weight
            else:
                weights[out][...] += weight

    def halved(value):
        return value.reshape(bins_row, 2, 8, share).sum(axis=1).reshape(bins_row * 8, share)

    sums = jnp.concatenate([halved(frame_ref[...]), halved(inverse)], axis=0)
    top, rest = split_high_low(sums)
    last = ((sums - top.astype(F32)) - rest.astype(F32)).astype(BF16)
    part = mm(top, gather[...]) + (mm(rest, gather[...]) + mm(last, gather[...]))
    if bins_col > SIDE:
        part = jnp.concatenate([part, jnp.zeros((part.shape[0], bins_col - SIDE), F32)], axis=1)
    part = pltpu.roll(part, block * per, 1)

    @pl.when(step == 0)
    def _():
        bins_ref[0] = part

    @pl.when(step > 0)
    def _():
        bins_ref[0] += part


ANY = pl.BlockSpec(memory_space=pl.ANY)


def rows_of_chunk(rows):
    return min(SIDE, rows)


def pixel_weights(plan, units, blocks, start, frame, spread, mask, share, width, after=()):
    rows = frame.shape[0]
    chunk = rows_of_chunk(rows)
    bins_col = mask.shape[1]
    kept = sum(out >= units for out, fresh in plan)
    lead = len(plan) - kept
    tile = pl.BlockSpec((chunk, share), lambda r, i, blocks, start: (r, blocks[i]))
    out_specs = [pl.BlockSpec((chunk, share), lambda r, i, blocks, start: (r, 0))] * units
    out_shape = [jax.ShapeDtypeStruct((rows, share), F32)] * units
    if kept:
        out_specs.append(
            pl.BlockSpec((1, chunk, share), lambda r, i, blocks, start: (jnp.maximum(i - lead, 0), r, 0))
        )
        out_shape.append(jax.ShapeDtypeStruct((kept, rows, share), F32))
    out_specs.append(pl.BlockSpec((1, chunk, bins_col), lambda r, i, blocks, start: (r, 0, 0)))
    out_shape.append(jax.ShapeDtypeStruct((rows // chunk, chunk, bins_col), F32))

    def body(blocks_ref, start_ref, frame_ref, spread_ref, mask_ref, *refs):
        weights_kernel(plan, units, width, blocks_ref, start_ref, frame_ref, spread_ref, mask_ref, *refs[len(after) :])

    return pl.pallas_call(
        body,
        grid_spec=pltpu.PrefetchScalarGridSpec(
            num_scalar_prefetch=2,
            grid=(rows // chunk, len(plan)),
            in_specs=[
                tile,
                tile,
                pl.BlockSpec((chunk // BIN, bins_col), lambda r, i, blocks, start: (r, 0)),
            ] + [ANY] * len(after),
            out_specs=out_specs,
            scratch_shapes=[pltpu.VMEM((SIDE, share), BF16), pltpu.VMEM((share, SIDE), BF16)],
        ),
        out_shape=out_shape,
        compiler_params=pltpu.CompilerParams(vmem_limit_bytes=VMEM),
        cost_estimate=SMALL,
        name="pixel_weights",
    )(blocks, start, frame, spread, mask, *after)


def smooth_kernel(plan, width, stacked, blocks_ref, start_ref, *refs):
    step = pl.program_id(0)
    images, (col_hi, col_lo, row_hi, row_lo, up_hi, up_lo, down_hi, down_lo) = refs[:9], refs[9:17]
    refs = refs[17:]
    weights, outs = refs[: len(refs) // 2], refs[len(refs) // 2 :]
    block = blocks_ref[step]
    rows, share = images[4].shape
    window = share + 2 * SIDE
    field = jnp.concatenate(
        [jnp.concatenate([images[3 * i + j][...] for j in range(3)], axis=1) for i in range(3)], axis=0
    )
    first = start_ref[0] * BIN
    col = lax.broadcasted_iota(jnp.int32, (1, window), 1) + (block * share - SIDE)
    field = jnp.where((col >= first) & (col < first + width), field, 0.0)
    high, low = split_high_low(field)

    def three(a_hi, a_lo, b_hi, b_lo):
        return mm(a_hi, b_hi) + (mm(a_lo, b_hi) + mm(a_hi, b_lo))

    tiles = []
    for tile in range(share // TILE):
        lanes = slice(tile * TILE, (tile + 1) * TILE + 2 * SIDE)
        tiles.append(three(high[:, lanes], low[:, lanes], col_hi[...], col_lo[...]))
    across = tiles[0] if len(tiles) == 1 else jnp.concatenate(tiles, axis=1)
    high, low = split_high_low(across)
    height = row_hi.shape[0]
    tiles = []
    for tile in range(rows // height):
        top = tile * height
        mid = slice(top + HALO, top + HALO + height)
        upper = slice(top, top + HALO)
        lower = slice(top + HALO + height, top + 2 * HALO + height)
        main = three(row_hi[...], row_lo[...], high[mid], low[mid])
        tiles += [
            main[:HALO] + three(up_hi[...], up_lo[...], high[upper], low[upper]),
            main[HALO : height - HALO],
            main[height - HALO :] + three(down_hi[...], down_lo[...], high[lower], low[lower]),
        ]
    smoothed = jnp.concatenate(tiles, axis=0)
    col = lax.broadcasted_iota(jnp.int32, (1, share), 1) + block * share
    smoothed = jnp.where((col >= first) & (col < first + width), smoothed, 0.0)
    if stacked:
        outs[0][0] = weights[0][0] * smoothed
        return
    for at, (out, fresh) in enumerate(plan):
        @pl.when(step == at)
        def _(out=out, fresh=fresh):
            term = weights[out][...] * smoothed
            outs[out][...] = term if fresh else outs[out][...] + term


def smoothed_terms(plan, weights, blocks, start, frame, above, below, share, width, after=()):
    rows, cols = frame.shape
    stacked = weights[0].ndim == 3
    count = len(weights)
    per = share // SIDE
    last = cols // SIDE - 1
    specs = []
    for height in (HALO, rows, HALO):
        specs += [
            pl.BlockSpec((height, SIDE), lambda i, blocks, start: (0, jnp.maximum(blocks[i] * per - 1, 0))),
            pl.BlockSpec((height, share), lambda i, blocks, start: (0, blocks[i])),
            pl.BlockSpec((height, SIDE), lambda i, blocks, start: (0, jnp.minimum(blocks[i] * per + per, last))),
        ]
    whole = lambda shape: pl.BlockSpec(shape, lambda i, blocks, start: (0, 0))
    if stacked:
        parts_spec = pl.BlockSpec((1, rows, share), lambda i, blocks, start: (i, 0, 0))
    else:
        parts_spec = whole((rows, share))
    height = min(TILE, rows)
    full = band(height, height + 2 * HALO, HALO)
    bands = [
        band(TILE, TILE + 2 * SIDE, SIDE).T,
        full[:, HALO : HALO + height],
        full[:HALO, :HALO],
        full[height - HALO :, HALO + height :],
    ]
    parts = [jnp.asarray(p) for matrix in bands for p in two_parts(matrix)]

    def body(*refs):
        lead = 2 + 9 + len(parts) + count
        smooth_kernel(plan, width, stacked, *refs[:lead], *refs[lead + len(after) :])

    return pl.pallas_call(
        body,
        grid_spec=pltpu.PrefetchScalarGridSpec(
            num_scalar_prefetch=2,
            grid=(len(plan),),
            in_specs=specs + [whole(p.shape) for p in parts] + [parts_spec] * count + [ANY] * len(after),
            out_specs=[parts_spec] * count,
        ),
        out_shape=[jax.ShapeDtypeStruct(w.shape, F32) for w in weights],
        compiler_params=pltpu.CompilerParams(vmem_limit_bytes=VMEM),
        cost_estimate=SMALL,
        name="smoothed_terms",
    )(blocks, start, *([above] * 3 + [frame] * 3 + [below] * 3), *parts, *weights, *after)


def held_until(values, after):
    def body(*refs):
        del refs

    return pl.pallas_call(
        body,
        in_specs=[ANY] * (len(values) + len(after)),
        out_specs=[ANY] * len(values),
        out_shape=[jax.ShapeDtypeStruct(v.shape, v.dtype) for v in values],
        input_output_aliases={i: i for i in range(len(values))},
        compiler_params=pltpu.CompilerParams(vmem_limit_bytes=VMEM),
        cost_estimate=SMALL,
        name="held",
    )(*values, *after)


def contract_last(left, right):
    return lax.dot_general(left, right, (((1,), (1,)), ((), ())), precision=HIGH, preferred_element_type=F32)


def contract_last_three(left, right):
    def one(a, b):
        return lax.dot_general(a, b, (((1,), (1,)), ((), ())), preferred_element_type=F32)

    (l_hi, l_lo), (r_hi, r_lo) = split_high_low(left), split_high_low(right)
    return one(l_hi, r_hi) + (one(l_lo, r_hi) + one(l_hi, r_lo))


def moments_kernel(places, strips, strip_ref, bins_ref, out_ref):
    count, _, rows, cols = bins_ref.shape
    at = [places.index(e) for e in range(count)]
    image = [bins_ref[at[e], 0] for e in range(count)]
    weight = [bins_ref[at[e], 1] for e in range(count)]
    x = centers(lax.broadcasted_iota(jnp.int32, (1, cols), 1), cols)
    tx = [jnp.ones_like(x), x]
    while len(tx) < 5:
        tx.append(2.0 * x * tx[-1] - tx[-2])
    tx = jnp.concatenate(tx + [jnp.zeros((3, cols), F32)], axis=0)
    joint, diffs = [], []
    for apart in range(1, count // 2 + 1):
        group, group_d = [], []
        for i in range(count):
            j = (i + apart) % count
            w = weight[i] * weight[j] / (weight[i] + weight[j] + 1.0)
            group.append(w)
            group_d.append(w * (image[i] - image[j]))
        joint.append(contract_last_three(tx, jnp.concatenate(group, axis=0)))
        diffs.append(contract_last_three(tx, jnp.concatenate(group_d, axis=0)))
    along = jnp.concatenate([jnp.concatenate(joint, axis=1), jnp.concatenate(diffs, axis=1)], axis=0)
    total = along.shape[1]
    row = lax.broadcasted_iota(jnp.int32, (total, SIDE), 0)
    lane = lax.broadcasted_iota(jnp.int32, (total, SIDE), 1)
    mine = row // rows == lane
    y = centers(row % rows + strip_ref[0] * rows, rows * strips)
    a_hi, a_lo = split_high_low(along)
    ty = [jnp.ones_like(y), y]
    for a in range(5):
        if a > 1:
            ty.append(2.0 * y * ty[-1] - ty[-2])
        b_hi, b_lo = split_high_low(jnp.where(mine, ty[a], 0.0))
        out_ref[:, a * SIDE : (a + 1) * SIDE] = mm(a_hi, b_hi) + (mm(a_lo, b_hi) + mm(a_hi, b_lo))


def solve_kernel(moments_ref, owner_ref, out_ref):
    owner = owner_ref[...].astype(F32)
    count = owner.shape[0]
    lanes = count * count // 2
    exposure = lax.broadcasted_iota(jnp.int32, (count, lanes), 0)
    lane = lax.broadcasted_iota(jnp.int32, (count, lanes), 1)
    mine = lane % count
    apart = lane // count + 1
    is_i = (exposure == mine).astype(F32)
    is_j = (exposure == (mine + apart) % count).astype(F32)
    both = owner + owner.T
    listed = jnp.sum(is_i * jnp.dot(both, is_j, precision=HIGH, preferred_element_type=F32), axis=0, keepdims=True)
    lane_row = lax.broadcasted_iota(jnp.int32, (1, lanes), 1)
    once = (lane_row // count + 1 < count // 2) | (lane_row % count < count // 2)
    listed = jnp.where(once, listed, 0.0)
    held = listed > 0.0
    moment = [[moments_ref[b : b + 1, a * SIDE : a * SIDE + lanes] for b in range(5)] for a in range(5)]

    def entry(k, l):
        (u, v), (s, t) = divmod(k, 3), divmod(l, 3)
        total = 0.0
        for a in (u + s, abs(u - s)):
            for b in (v + t, abs(v - t)):
                total = total + moment[a][b]
        return jnp.where(held, 0.25 * total, 1.0 if k == l else 0.0)

    factor = [[None] * 9 for _ in range(9)]
    scale = [None] * 9
    for k in range(9):
        for l in range(k, 9):
            value = entry(l, k)
            for m in range(k):
                value = value - factor[l][m] * factor[k][m]
            if l == k:
                scale[k] = 1.0 / jnp.sqrt(value)
            else:
                factor[l][k] = value * scale[k]
    half = [None] * 9
    for k in range(9):
        a, b = divmod(k, 3)
        value = moments_ref[8 + b : 9 + b, a * SIDE : a * SIDE + lanes]
        for m in range(k):
            value = value - factor[k][m] * half[m]
        half[k] = value * scale[k]
    fit = [None] * 9
    for k in reversed(range(9)):
        value = half[k]
        for m in range(k + 1, 9):
            value = value - factor[m][k] * fit[m]
        fit[k] = value * scale[k]
    fits = jnp.concatenate([jnp.where(held, f, 0.0) for f in fit] + [jnp.zeros((7, lanes), F32)], axis=0)
    right = contract_last((is_i - is_j) * listed, fits)
    row = lax.broadcasted_iota(jnp.int32, (count, count), 0)
    column = lax.broadcasted_iota(jnp.int32, (count, count), 1)
    degree = jnp.sum(both, axis=1, keepdims=True) + LAMBDA_REG
    system = jnp.where(row == column, degree, 0.0) - both
    for k in range(count):
        inverse = 1.0 / system[k : k + 1, k : k + 1]
        pivot_s, pivot_r = system[k : k + 1, :] * inverse, right[k : k + 1, :] * inverse
        lead = system[:, k : k + 1]
        chosen = row[:, :1] == k
        system = jnp.where(chosen, pivot_s, system - lead * pivot_s)
        right = jnp.where(chosen, pivot_r, right - lead * pivot_r)
    out_ref[...] = right[:, :9]


def per_device(image, variance, mask, foot_start, pair_owner):
    frame, spread, blocks = image[0], variance[0], mask[0]
    rows, cols = frame.shape
    bins_row, bins_col = blocks.shape
    exposures, sky_count = lax.axis_size("exp"), lax.axis_size("sky")
    member, strip = lax.axis_index("exp"), lax.axis_index("sky")
    share = cols // exposures
    width = 3 * cols // 4
    places = exposures // 2
    quarter = places // 4
    place, side = member // 2, member % 2
    own_start = lax.dynamic_slice_in_dim(foot_start, member, 1)
    mate_start = lax.dynamic_slice_in_dim(foot_start, member + 1 - 2 * side, 1)

    order = np.zeros((places, places), np.int32)
    for z in range(places):
        down = z < places // 2
        ends = range(quarter)
        middle = list(range(quarter, places - quarter))
        listed = []
        for q in ends:
            low = quarter - 1 - q if down else q
            listed += [low, low + places - quarter]
        order[z] = listed + (middle[::-1] if down else middle)
    middle_count = places - 2 * quarter
    my_order = lax.dynamic_index_in_dim(jnp.asarray(order), place, 0, keepdims=False)
    sent_blocks = 2 * my_order + (1 - side)
    kept_blocks = 2 * my_order + side
    ends = 2 * quarter
    folded = [(i // 2, i % 2 == 0) for i in range(ends)]
    middle = [(i, True) for i in range(middle_count)]
    plain = [(middle_count + i, True) for i in range(places)]

    up = [(i, i + 1) for i in range(sky_count - 1)]
    down = [(j, i) for i, j in up]
    above = lax.ppermute(frame[rows - HALO :], "sky", up)
    below = lax.ppermute(frame[:HALO], "sky", down)

    swap = [(i, i ^ 1) for i in range(exposures)]

    def swapped(parts):
        return [lax.ppermute(part, "exp", swap) for part in parts]

    *den_ends, bins_a = pixel_weights(
        folded, quarter, sent_blocks[:ends], own_start, frame, spread, blocks, share, width
    )
    got_ends = swapped(den_ends)
    *den_middle, den_kept, bins_b = pixel_weights(
        middle + plain,
        middle_count,
        jnp.concatenate([sent_blocks[ends:], kept_blocks]),
        own_start,
        frame,
        spread,
        blocks,
        share,
        width,
        after=(bins_a,),
    )

    bins = (bins_a + bins_b).reshape(-1, 2, bins_row * rows_of_chunk(rows) // rows, 8, bins_col).sum(axis=3)
    bins = bins.swapaxes(0, 1).reshape(2, bins_row, bins_col)
    cell = jnp.arange(bins_col)
    inside_bins = (cell >= own_start) & (cell < own_start + width // BIN)
    keep = jnp.where(inside_bins[None, :], blocks, 0).astype(F32)
    gathered = jnp.stack([bins[0] / (BIN * BIN), bins[1] * keep])[None]
    smooth = functools.partial(
        smoothed_terms, start=own_start, frame=frame, above=above, below=below, share=share, width=width
    )
    held = [0]
    bits = [1 << k for k in range(exposures.bit_length() - 1)]

    def gather_along(gathered, bit):
        other = lax.ppermute(gathered, "exp", [(i, i ^ bit) for i in range(exposures)])
        low = (member & bit) == 0
        held.extend([e | bit for e in held])
        return jnp.concatenate([jnp.where(low, gathered, other), jnp.where(low, other, gathered)])

    num_ends = smooth(folded, den_ends, sent_blocks[:ends], after=(bins_b,))
    gathered = gather_along(gathered, bits[1])
    (gathered,) = held_until([gathered], num_ends)
    for bit in bits[2:]:
        gathered = gather_along(gathered, bit)
    num_middle = smooth(middle, den_middle, sent_blocks[ends:], after=num_ends)
    gathered, *den_middle = held_until([gathered, *den_middle], num_middle)
    gathered = gather_along(gathered, bits[0])
    got_middle = swapped(den_middle)
    den_got = got_ends + got_middle
    num_got = []
    for k, part in enumerate(num_ends + num_middle):
        num_got += swapped(held_until([part], [(got_middle + num_got)[k]]))

    position = np.zeros((places, places), np.int32)
    for z in range(places):
        position[z, order[z]] = np.arange(places)

    def by_place(values):
        table = np.zeros((places,), np.int32)
        for z, value in values.items():
            table[z] = value
        return lax.dynamic_index_in_dim(jnp.asarray(table), place, 0, keepdims=False)

    def pick(parts, wanted):
        unit = {z: (at // 2 if at < ends else at - quarter) for z, at in wanted.items()}
        value = None
        for u in sorted(set(unit.values())):
            if value is None:
                value = parts[u]
                continue
            here = functools.reduce(jnp.logical_or, [place == z for z, w in unit.items() if w == u])
            value = jnp.where(here, parts[u], value)
        return value

    def own_and_mate(wanted, *arrays):
        at = by_place(wanted)
        block = kept_blocks[at]
        col = jnp.arange(share) + block * share
        inside = ((col >= mate_start * BIN) & (col < mate_start * BIN + width))[None, :]
        out = []
        for own, got in arrays:
            out.append(lax.dynamic_index_in_dim(own, at, 0, keepdims=False))
            out.append(jnp.where(inside, pick(got, wanted), 0.0))
        return block, out

    def along_places(term):
        rightward = leftward = None
        values = []

        def shift(value, rights, lefts):
            pairs = [(2 * z + s, 2 * z + 2 + s) for z in rights for s in range(2)]
            pairs += [(2 * z + s, 2 * z - 2 + s) for z in lefts for s in range(2)]
            return lax.ppermute(value, "exp", pairs)

        for step in range(1, places):
            rights = {z: position[z, z + places - step] for z in range(step)}
            lefts = {z: position[z, z - places + step] for z in range(places - step, places)}
            if step < places - 1 - step:
                value = term(rights | lefts)
                if rightward is not None:
                    value = value + jnp.where(place < places // 2, rightward, leftward)
                values.append(value)
                both = shift(value, rights, lefts)
                rightward = jnp.where(place <= step, both, 0.0)
                leftward = jnp.where(place >= places - 1 - step, both, 0.0)
                continue
            value = term(rights)
            value = value if rightward is None else value + rightward
            back = term(lefts)
            back = back if leftward is None else back + leftward
            values += [value, back]
            rightward = shift(value, rights, [])
            leftward = shift(back, [], lefts)
        return term({z: position[z, z] for z in range(places)}) + rightward + leftward, values

    def den_term(wanted):
        block, (own, mate) = own_and_mate(wanted, (den_kept, den_got))
        return own + mate

    total_den, den_values = along_places(den_term)
    (num_kept,) = smooth(
        [(i, True) for i in range(places)], [den_kept], kept_blocks, after=(den_values[0], *num_middle)
    )

    (gathered,) = held_until([gathered], [num_kept])
    moments = pl.pallas_call(
        functools.partial(moments_kernel, held, sky_count),
        in_specs=[pl.BlockSpec(memory_space=pltpu.SMEM), pl.BlockSpec(memory_space=pltpu.VMEM)],
        out_shape=jax.ShapeDtypeStruct((16, 5 * SIDE), F32),
        compiler_params=pltpu.CompilerParams(vmem_limit_bytes=VMEM),
        cost_estimate=SMALL,
        name="pair_moments",
    )(strip[None], gathered)
    bit = 1
    while bit < sky_count:
        moments = moments + lax.ppermute(moments, "sky", [(i, i ^ bit) for i in range(sky_count)])
        bit *= 2
    offsets = pl.pallas_call(
        solve_kernel,
        out_shape=jax.ShapeDtypeStruct((exposures, 9), F32),
        cost_estimate=SMALL,
        name="offsets",
    )(moments, pair_owner)

    taps = tap_values().astype(np.float32)
    row_at = jnp.arange(-RADIUS, rows + RADIUS) + strip * rows
    ty = chebyshev(centers(row_at, rows * sky_count))
    ty = jnp.where((row_at >= 0) & (row_at < rows * sky_count), ty, 0.0)
    rows_part = sum(float(taps[t]) * ty[:, t : t + rows] for t in range(2 * RADIUS + 1))
    col_at = jnp.arange(-RADIUS, cols + RADIUS)
    tx = chebyshev(centers(col_at, cols))

    def columns_part(start):
        masked = jnp.where((col_at >= start * BIN) & (col_at < start * BIN + width), tx, 0.0)
        return sum(float(taps[t]) * masked[:, t : t + cols] for t in range(2 * RADIUS + 1))

    def coefficients(which, start):
        coeffs = lax.dynamic_index_in_dim(offsets, which, 0, keepdims=False).reshape(3, 3)
        return jnp.sum(coeffs[:, :, None] * columns_part(start)[None], axis=1)

    own_back = coefficients(member, own_start)
    mate_back = coefficients(member + 1 - 2 * side, mate_start)

    def background(back, block):
        cut = lax.dynamic_slice_in_dim(back, block * share, share, 1)
        return sum(rows_part[u][:, None] * cut[u][None, :] for u in range(3))

    def num_term(wanted):
        block, (own, mate, own_den, mate_den) = own_and_mate(wanted, (num_kept, num_got), (den_kept, den_got))
        return (own - own_den * background(own_back, block)) + (mate - mate_den * background(mate_back, block))

    total_num, _ = along_places(num_term)
    return (total_num / (PRIOR + total_den), offsets)


def solution(mesh):
    placed = (P("exp", "sky", None), P("exp", "sky", None), P("exp", "sky", None), P(), P())
    return jax.shard_map(
        per_device, mesh=mesh, in_specs=placed, out_specs=(P("sky", "exp"), P()), check_vma=False
    )
```

time: 299 us -> 283 us (0.946); the launches traced: 294 us -> 281 us
  waiting for transfers between devices: 101 us -> 83.1 us
  between operations: 5.56 us -> 18.2 us
  starting transfers between devices: 67.8 us -> 56.5 us
  other arithmetic: 39.8 us -> 43.3 us
  local copies, waits for them, and re-layouts: 7.6 us -> 11.1 us
    all_to_all x1 -> x0, waiting for transfers between devices: 23.4 us -> none  [per_device(): spread_bins = lax.all_to_all(both, 'exp', 0, 0)]
    all_to_all x1 -> x0, starting transfers between devices: 6.31 us -> none  [per_device(): spread_bins = lax.all_to_all(both, 'exp', 0, 0)]
    ppermute x23 -> x21, waiting for transfers between devices: 78 us -> 83.1 us  [the longest x10 68.7 us: shift(): return lax.ppermute(value, 'exp', pairs)]
    dynamic_slice x0 -> x7, local copies, waits for them, and re-layouts: none -> 4.4 us  [the longest x6 3.71 us: by_place(): lax.dynamic_index_in_dim(jnp.asarray(table), place, 0, keepdims=False)]
    ppermute x23 -> x21, starting transfers between devices: 57.2 us -> 52.8 us  [the longest x10 35.2 us: shift(): return lax.ppermute(value, 'exp', pairs)]
    pallas_call x5 -> x12, Pallas kernels: 69.4 us -> 66.8 us  [the longest x2 34.5 us: pixel_weights(): pl.pallas_call(body, grid_spec=pltpu.PrefetchScalarGridSpec(num_scalar_pr...]
    add x12 -> x7, other arithmetic: 17.1 us -> 14.7 us  [the longest x2 6.55 us: along_places(): back = back if leftward is None else back + leftward]
    add x3 -> x4, other arithmetic: 14.1 us -> 15.9 us  [along_places(): value = value if rightward is None else value + rightward]
  transfers between devices with their start and end apart: 26 -> 23, of which waited for: 12 -> 11; matrix products, arithmetic and copies ran while one was open for 13% -> 16% of each run, Pallas kernels for 24% -> 25%
where the time goes in v2:
time: 283 us; the launch traced here: 281 us
  waiting for transfers between devices  83.1 us (29%)
  Pallas kernels  69 us (24%)
  starting transfers between devices  56.5 us (20%)
  other arithmetic  43.3 us (15%)
  between operations  18.2 us (6%)
  local copies, waits for them, and re-layouts  11.1 us (4%)
    ppermute x10, waiting for transfers between devices, shift(): return lax.ppermute(value, 'exp', pairs)  68.7 us
    ppermute x10, starting transfers between devices, shift(): return lax.ppermute(value, 'exp', pairs)  35.2 us
    pallas_call x2, Pallas kernels, pixel_weights(): pl.pallas_call(body, grid_spec=pltpu.PrefetchScalarGridSpec(num_scalar_pr...  34.5 us
    pallas_call x3, Pallas kernels, smoothed_terms(): pl.pallas_call(body, grid_spec=pltpu.PrefetchScalarGridSpec(num_scalar_pr...  28.6 us
    add x4, other arithmetic, along_places(): value = value if rightward is None else value + rightward  15.9 us
    ppermute x3, waiting for transfers between devices, gather_along(): lax.ppermute(gathered, 'exp', [(i, i ^ bit) for i in range(exposures)])  10.6 us
    ppermute x6, starting transfers between devices, swapped(): return [lax.ppermute(part, 'exp', swap) for part in parts]  7.06 us
    add x2, other arithmetic, along_places(): back = back if leftward is None else back + leftward  6.55 us
  transfers between devices with their start and end apart: 23, of which 11 were waited for; matrix products, arithmetic and copies ran while one was open for 16% of the time, Pallas kernels for 25%

profile of v2, /device:TPU:0, one launch (start us, length us, event | category | flops | bytes accessed | tf_op | source)
XLA Modules:
  0.0 281.2 jit_solution(241227224330798460)
XLA Ops:
  8.7 9.8 %pixel_weights.2 = (f32[512,512]{1,0:T(8,128)}, f32[4,128,256]{2,1,0:T(8,128)}) custom-call(s32[2]{0:T(128)} %get-tuple-element.90.blocks_ref.refs_0_, s32[1]{0:T(128)} %get-tuple-element.88.start_ref.refs_1_, f32[512,4096]{1,0:T(8,128)} %bitcast.169, f32[512,4096]{1,0:T(8,128)} %bitcast.180, s32[32,256]{1,0:T(8,128)} %bitcast.182), custom_call_target="tpu_custom_call" | custom-call | flops 1000 | bytes 1000 | tf_op jit(solution)/shard_map/pixel_weights/pallas_call | solution.py:148
  18.5 24.8 %pixel_weights.3 = (f32[512,512]{1,0:T(8,128)}, f32[512,512]{1,0:T(8,128)}, f32[4,512,512]{2,1,0:T(8,128)}, f32[4,128,256]{2,1,0:T(8,128)}) custom-call(s32[6]{0:T(128)} %pad_add_fusion.blocks_ref, s32[1]{0:T(128)} %get-tuple-element.88.start_ref.refs_1_, f32[512,4096]{1,0:T(8,128)} %bitcast.170, f32[512,4096]{1,0:T(8,128)} %bitcast.181, ...), custom_call_target="tpu_custom_call" | custom-call | flops 1000 | bytes 1000 | tf_op jit(solution)/shard_map/pixel_weights/pallas_call | solution.py:148
  53.0 8.1 %smoothed_terms.3.refs_21_.refs_1_.refs_0_ = f32[512,512]{1,0:T(8,128)} custom-call(s32[2]{0:T(128)} %get-tuple-element.90.blocks_ref.refs_0_, s32[1]{0:T(128)} %get-tuple-element.88.start_ref.refs_1_, f32[16,4096]{1,0:T(8,128)} %copy-done.7, f32[16,4096]{1,0:T(8,128)} %copy-done.7, f32[16,4096]{1,0:T(8,128)} %copy-done.7, f32[512,4096]{1,0:T(8,128)} %bitcast.171, ...), custom_call_target="tpu_custom_call" | custom-call | flops 1000 | bytes 1000 | tf_op jit(solution)/shard_map/smoothed_terms/pallas_call | solution.py:251
  64.6 8.8 %smoothed_terms.4 = (f32[512,512]{1,0:T(8,128)}, f32[512,512]{1,0:T(8,128)}) custom-call(s32[2]{0:T(128)} %copy-done.14, s32[1]{0:T(128)} %get-tuple-element.88.start_ref.refs_1_, f32[16,4096]{1,0:T(8,128)} %copy-done.7, f32[16,4096]{1,0:T(8,128)} %copy-done.7, f32[16,4096]{1,0:T(8,128)} %copy-done.7, f32[512,4096]{1,0:T(8,128)} %bitcast.174, ...), custom_call_target="tpu_custom_call" | custom-call | flops 1000 | bytes 1000 | tf_op jit(solution)/shard_map/smoothed_terms/pallas_call | solution.py:251
  95.1 10.6 %collective-permute-done.5 = f32[4,2,32,256]{3,2,1,0:T(8,128)} collective-permute-done((f32[4,2,32,256]{3,2,1,0:T(8,128)}, f32[4,2,32,256]{3,2,1,0:T(8,128)}, u32[]{:S(2)}, u32[]{:S(2)}) %collective-permute-start.5) | collective-permute-done | bytes 262176 | tf_op jit(solution)/shard_map/ppermute | solution.py:468
  110.1 11.8 %smoothed_terms.5.refs_1_ = f32[4,512,512]{2,1,0:T(8,128)} custom-call(s32[4]{0:T(128)} %bitcast.205, s32[1]{0:T(128)} %get-tuple-element.88.start_ref.refs_1_, f32[16,4096]{1,0:T(8,128)} %copy-done.7, f32[16,4096]{1,0:T(8,128)} %copy-done.7, f32[16,4096]{1,0:T(8,128)} %copy-done.7, f32[512,4096]{1,0:T(8,128)} %bitcast.177, f32[512,4096]{1,0:T(8,128)} %bitcast.178, ...), custom_call_target="tpu_custom_call" | custom-call | flops 1000 | bytes 1000 | tf_op jit(solution)/shard_map/smoothed_terms/pallas_call | solution.py:251
  130.5 4.3 %collective-permute-start.7 = (f32[16,640]{1,0:T(8,128)S(1)}, f32[16,640]{1,0:T(8,128)S(1)}, u32[]{:S(2)}, u32[]{:S(2)}) collective-permute-start(f32[16,640]{1,0:T(8,128)S(1)} %add.797), channel_id=1, source_target_pairs={{0,2},{1,3},{2,0},{3,1},{4,6},{5,7},{6,4},{7,5},{8,10},{9,11},{10,... | collective-permute-start | bytes 122888 | tf_op jit(solution)/shard_map/ppermute | solution.py:569
  138.1 4.5 %collective-permute-start.18 = (f32[512,512]{1,0:T(8,128)}, f32[512,512]{1,0:T(8,128)}, u32[]{:S(2)}, u32[]{:S(2)}) collective-permute-start(f32[512,512]{1,0:T(8,128)} %bitcast_add_fusion.5.refs_20_), channel_id=1, source_target_pairs={{0,8},{4,12},{24,16},{28,20},{1,9},{5,13},{25,17},{29,21},{2,10},{... | collective-permute-start | bytes 3145736 | tf_op jit(solution)/shard_map/ppermute | solution.py:526
  154.1 4.6 %collective-permute-start.13 = (f32[512,512]{1,0:T(8,128)}, f32[512,512]{1,0:T(8,128)}, u32[]{:S(2)}, u32[]{:S(2)}) collective-permute-start(f32[512,512]{1,0:T(8,128)} %fusion.8), channel_id=1, source_target_pairs={{0,8},{4,12},{24,16},{28,20},{1,9},{5,13},{25,17},{29,21},{2,10},{... | collective-permute-start | bytes 3145736 | tf_op jit(solution)/shard_map/ppermute | solution.py:526
  158.7 6.7 %collective-permute-done.18 = f32[512,512]{1,0:T(8,128)} collective-permute-done((f32[512,512]{1,0:T(8,128)}, f32[512,512]{1,0:T(8,128)}, u32[]{:S(2)}, u32[]{:S(2)}) %collective-permute-start.18) | collective-permute-done | bytes 1048608 | tf_op jit(solution)/shard_map/ppermute | solution.py:526
  165.4 3.8 %fusion.12 = (f32[512,512]{1,0:T(8,128)}, f32[512,512]{1,0:T(8,128)}) fusion(f32[512,512]{1,0:T(8,128)} %collective-permute-done.18, f32[4,512,512]{2,1,0:T(8,128)} %get-tuple-element.14.refs_19_, s32[]{:T(128)S(6)} %select_n.364, pred[]{:T(512)S(6)} %le.4, f32[512,512]{1,0:T(8,128)S(1)} %copy-done.3, f32[512,512]{1,0:T(8,128)S(1)} %collective-permute-done.2, ...), kind=kLoop, calls=%fused_computation.19 | loop fusion | flops 2621440 | bytes 7341068 | tf_op jit(solution)/shard_map/add | solution.py:541
  169.2 5.4 %collective-permute-start.19 = (f32[512,512]{1,0:T(8,128)}, f32[512,512]{1,0:T(8,128)}, u32[]{:S(2)}, u32[]{:S(2)}) collective-permute-start(f32[512,512]{1,0:T(8,128)} %get-tuple-element.30), channel_id=1, source_target_pairs={{0,8},{4,12},{8,16},{12,20},{1,9},{5,13},{9,17},{13,21},{2,10},{6,... | collective-permute-start | bytes 3145736 | tf_op jit(solution)/shard_map/ppermute | solution.py:526
  176.8 11.0 %collective-permute-done.13 = f32[512,512]{1,0:T(8,128)} collective-permute-done((f32[512,512]{1,0:T(8,128)}, f32[512,512]{1,0:T(8,128)}, u32[]{:S(2)}, u32[]{:S(2)}) %collective-permute-start.13) | collective-permute-done | bytes 1048608 | tf_op jit(solution)/shard_map/ppermute | solution.py:526
  196.6 4.7 %collective-permute-start.14 = (f32[512,512]{1,0:T(8,128)}, f32[512,512]{1,0:T(8,128)}, u32[]{:S(2)}, u32[]{:S(2)}) collective-permute-start(f32[512,512]{1,0:T(8,128)} %fusion.11), channel_id=1, source_target_pairs={{0,8},{4,12},{8,16},{12,20},{1,9},{5,13},{9,17},{13,21},{2,10},{6,... | collective-permute-start | bytes 3145736 | tf_op jit(solution)/shard_map/ppermute | solution.py:526
  201.4 8.9 %collective-permute-done.19 = f32[512,512]{1,0:T(8,128)} collective-permute-done((f32[512,512]{1,0:T(8,128)}, f32[512,512]{1,0:T(8,128)}, u32[]{:S(2)}, u32[]{:S(2)}) %collective-permute-start.19) | collective-permute-done | bytes 1048608 | tf_op jit(solution)/shard_map/ppermute | solution.py:526
  210.4 4.7 %fusion.16 = (f32[512,512]{1,0:T(8,128)}, f32[512,512]{1,0:T(8,128)}) fusion(f32[512,512]{1,0:T(8,128)} %collective-permute-done.19, f32[4,512,512]{2,1,0:T(8,128)} %get-tuple-element.14.refs_19_, s32[]{:T(128)S(6)} %select_n.354, f32[512,512]{1,0:T(8,128)} %collective-permute-done.11.refs_1_, f32[512,512]{1,0:T(8,128)S(1)} %copy-done.3, ...), kind=kLoop, calls=%fused_computation.25 | loop fusion | flops 2621440 | bytes 9438220 | tf_op jit(solution)/shard_map/add | solution.py:541
  216.4 6.0 %collective-permute-start.20 = (f32[512,512]{1,0:T(8,128)}, f32[512,512]{1,0:T(8,128)}, u32[]{:S(2)}, u32[]{:S(2)}) collective-permute-start(f32[512,512]{1,0:T(8,128)} %get-tuple-element.28), channel_id=1, source_target_pairs={{0,8},{4,12},{8,16},{12,20},{16,24},{20,28},{1,9},{5,13},{9,17},{1... | collective-permute-start | bytes 3145736 | tf_op jit(solution)/shard_map/ppermute | solution.py:526
  226.8 6.0 %collective-permute-done.14 = f32[512,512]{1,0:T(8,128)} collective-permute-done((f32[512,512]{1,0:T(8,128)}, f32[512,512]{1,0:T(8,128)}, u32[]{:S(2)}, u32[]{:S(2)}) %collective-permute-start.14) | collective-permute-done | bytes 1048608 | tf_op jit(solution)/shard_map/ppermute | solution.py:526
  232.8 3.8 %fusion.15 = f32[512,512]{1,0:T(8,128)} fusion(f32[512,512]{1,0:T(8,128)} %collective-permute-done.14, f32[512,512]{1,0:T(8,128)} %collective-permute-done.10, f32[512,512]{1,0:T(8,128)} %collective-permute-done.12, f32[512,512]{1,0:T(8,128)S(1)} %copy-done.5, f32[4,512,512]{2,1,0:T(8,128)S(1)} %copy-done.6, s32[]{:T(128)S(6)} %select_n.354, ...), kind=kLoop, calls=%fused_computation.24 | loop fusion | flops 5767168 | bytes 10504710 | tf_op jit(solution)/shard_map/add | solution.py:541
  236.6 4.1 %collective-permute-start.15 = (f32[512,512]{1,0:T(8,128)}, f32[512,512]{1,0:T(8,128)S(1)}, u32[]{:S(2)}, u32[]{:S(2)}) collective-permute-start(f32[512,512]{1,0:T(8,128)} %fusion.15), channel_id=1, source_target_pairs={{0,8},{4,12},{8,16},{12,20},{16,24},{20,28},{1,9},{5,13},{9,17},{1... | collective-permute-start | bytes 3145736 | tf_op jit(solution)/shard_map/ppermute | solution.py:526
  243.8 11.5 %collective-permute-done.20 = f32[512,512]{1,0:T(8,128)} collective-permute-done((f32[512,512]{1,0:T(8,128)}, f32[512,512]{1,0:T(8,128)}, u32[]{:S(2)}, u32[]{:S(2)}) %collective-permute-start.20) | collective-permute-done | bytes 1048608 | tf_op jit(solution)/shard_map/ppermute | solution.py:526
  255.3 8.2 %collective-permute-done.17 = f32[512,512]{1,0:T(8,128)} collective-permute-done((f32[512,512]{1,0:T(8,128)}, f32[512,512]{1,0:T(8,128)}, u32[]{:S(2)}, u32[]{:S(2)}) %collective-permute-start.17) | collective-permute-done | bytes 1048608 | tf_op jit(solution)/shard_map/ppermute | solution.py:526
  263.5 13.2 %collective-permute-done.15 = f32[512,512]{1,0:T(8,128)S(1)} collective-permute-done((f32[512,512]{1,0:T(8,128)}, f32[512,512]{1,0:T(8,128)S(1)}, u32[]{:S(2)}, u32[]{:S(2)}) %collective-permute-start.15) | collective-permute-done | bytes 1048608 | tf_op jit(solution)/shard_map/ppermute | solution.py:526
  276.7 4.5 %fusion.21 = f32[512,512]{1,0:T(8,128)} fusion(f32[512,512]{1,0:T(8,128)} %collective-permute-done.17, f32[512,512]{1,0:T(8,128)S(1)} %collective-permute-done.15, f32[512,512]{1,0:T(8,128)} %collective-permute-done.22, f32[512,512]{1,0:T(8,128)} %collective-permute-done.20, f32[512,512]{1,0:T(8,128)} %collective-permute-done.11.refs_1_, ...), kind=kLoop, calls=%fused_computation.32 | loop fusion | flops 6815744 | bytes 11553285 | tf_op jit(solution)/shard_map/div | solution.py:606
  (137 shorter events, 73.2 us)
Async XLA Ops:
  1.7 49.9 %collective-permute-start = (f32[16,4096]{1,0:T(8,128)S(1)}, f32[16,4096]{1,0:T(8,128)S(1)}, u32[]{:S(2)}, u32[]{:S(2)}) collective-permute-start(f32[16,4096]{1,0:T(8,128)S(1)} %get-tuple-element.27), channel_id=1, source_target_pairs={{0,1},{1,2},{2,3},{4,5},{5,6},{6,7},{8,9},{9,10},{10,11},{12,13},{... | collective-permute-start | bytes 786440 | tf_op jit(solution)/shard_map/ppermute | solution.py:430
  4.1 47.5 %collective-permute-start.1 = (f32[16,4096]{1,0:T(8,128)S(1)}, f32[16,4096]{1,0:T(8,128)S(1)}, u32[]{:S(2)}, u32[]{:S(2)}) collective-permute-start(f32[16,4096]{1,0:T(8,128)S(1)} %get-tuple-element.26), channel_id=1, source_target_pairs={{1,0},{2,1},{3,2},{5,4},{6,5},{7,6},{9,8},{10,9},{11,10},{13,12},{... | collective-permute-start | bytes 786440 | tf_op jit(solution)/shard_map/ppermute | solution.py:431
  6.1 85.5 %copy-start.13 = (s32[1,4]{1,0:T(1,128)}, s32[1,4]{1,0:T(1,128)S(1)}, u32[]{:S(2)}) copy-start(s32[1,4]{1,0:T(1,128)S(1)} %get-tuple-element.79) | copy-start | bytes 52
  45.6 5.3 %collective-permute-start.3 = (f32[1,2,32,256]{3,2,1,0:T(8,128)S(1)}, f32[1,2,32,256]{3,2,1,0:T(8,128)S(1)}, u32[]{:S(2)}, u32[]{:S(2)}) collective-permute-start(f32[1,2,32,256]{3,2,1,0:T(8,128)S(1)} %maximum_bitcast_fusion), channel_id=1, source_target_pairs={{0,8},{4,12},{8,0},{12,4},{16,24},{20,28},{24,16},{28,20},{1,9},{5... | collective-permute-start | bytes 196616 | tf_op jit(solution)/shard_map/ppermute | solution.py:468
  48.1 58.7 %collective-permute-start.2 = (f32[512,512]{1,0:T(8,128)S(1)}, f32[512,512]{1,0:T(8,128)S(1)}, u32[]{:S(2)}, u32[]{:S(2)}) collective-permute-start(f32[512,512]{1,0:T(8,128)S(1)} %copy-done.11), channel_id=1, source_target_pairs={{0,4},{4,0},{8,12},{12,8},{16,20},{20,16},{24,28},{28,24},{1,5},{5... | collective-permute-start | bytes 3145736 | tf_op jit(solution)/shard_map/ppermute | solution.py:436
  61.2 12.2 %collective-permute-start.4 = (f32[2,2,32,256]{3,2,1,0:T(8,128)}, f32[2,2,32,256]{3,2,1,0:T(8,128)S(1)}, u32[]{:S(2)}, u32[]{:S(2)}) collective-permute-start(f32[2,2,32,256]{3,2,1,0:T(8,128)} %held.6), channel_id=1, source_target_pairs={{0,16},{4,20},{8,24},{12,28},{16,0},{20,4},{24,8},{28,12},{1,17},{... | collective-permute-start | bytes 393224 | tf_op jit(solution)/shard_map/ppermute | solution.py:468
  74.3 47.7 %collective-permute-start.8 = (f32[512,512]{1,0:T(8,128)}, f32[512,512]{1,0:T(8,128)S(1)}, u32[]{:S(2)}, u32[]{:S(2)}) collective-permute-start(f32[512,512]{1,0:T(8,128)} %get-tuple-element.22), channel_id=1, source_target_pairs={{0,4},{4,0},{8,12},{12,8},{16,20},{20,16},{24,28},{28,24},{1,5},{5... | collective-permute-start | bytes 3145736 | tf_op jit(solution)/shard_map/ppermute | solution.py:436
  92.9 12.8 %collective-permute-start.5 = (f32[4,2,32,256]{3,2,1,0:T(8,128)}, f32[4,2,32,256]{3,2,1,0:T(8,128)}, u32[]{:S(2)}, u32[]{:S(2)}) collective-permute-start(f32[4,2,32,256]{3,2,1,0:T(8,128)} %get-tuple-element.21), channel_id=1, source_target_pairs={{0,4},{4,0},{8,12},{12,8},{16,20},{20,16},{24,28},{28,24},{1,5},{5... | collective-permute-start | bytes 786440 | tf_op jit(solution)/shard_map/ppermute | solution.py:468
  93.7 53.3 %collective-permute-start.11 = (f32[512,512]{1,0:T(8,128)}, f32[512,512]{1,0:T(8,128)}, u32[]{:S(2)}, u32[]{:S(2)}) collective-permute-start(f32[512,512]{1,0:T(8,128)} %get-tuple-element.23), channel_id=1, source_target_pairs={{0,4},{4,0},{8,12},{12,8},{16,20},{20,16},{24,28},{28,24},{1,5},{5... | collective-permute-start | bytes 3145736 | tf_op jit(solution)/shard_map/ppermute | solution.py:436
  122.9 27.6 %collective-permute-start.9 = (f32[512,512]{1,0:T(8,128)}, f32[512,512]{1,0:T(8,128)S(1)}, u32[]{:S(2)}, u32[]{:S(2)}) collective-permute-start(f32[512,512]{1,0:T(8,128)} %held.9), channel_id=1, source_target_pairs={{0,4},{4,0},{8,12},{12,8},{16,20},{20,16},{24,28},{28,24},{1,5},{5... | collective-permute-start | bytes 3145736 | tf_op jit(solution)/shard_map/ppermute | solution.py:436
  128.2 1.6 collective-permute-start.6
  130.5 12.0 %collective-permute-start.7 = (f32[16,640]{1,0:T(8,128)S(1)}, f32[16,640]{1,0:T(8,128)S(1)}, u32[]{:S(2)}, u32[]{:S(2)}) collective-permute-start(f32[16,640]{1,0:T(8,128)S(1)} %add.797), channel_id=1, source_target_pairs={{0,2},{1,3},{2,0},{3,1},{4,6},{5,7},{6,4},{7,5},{8,10},{9,11},{10,... | collective-permute-start | bytes 122888 | tf_op jit(solution)/shard_map/ppermute | solution.py:569
  138.1 27.3 %collective-permute-start.18 = (f32[512,512]{1,0:T(8,128)}, f32[512,512]{1,0:T(8,128)}, u32[]{:S(2)}, u32[]{:S(2)}) collective-permute-start(f32[512,512]{1,0:T(8,128)} %bitcast_add_fusion.5.refs_20_), channel_id=1, source_target_pairs={{0,8},{4,12},{24,16},{28,20},{1,9},{5,13},{25,17},{29,21},{2,10},{... | collective-permute-start | bytes 3145736 | tf_op jit(solution)/shard_map/ppermute | solution.py:526
  147.0 29.8 %collective-permute-start.12 = (f32[512,512]{1,0:T(8,128)}, f32[512,512]{1,0:T(8,128)}, u32[]{:S(2)}, u32[]{:S(2)}) collective-permute-start(f32[512,512]{1,0:T(8,128)} %held.11), channel_id=1, source_target_pairs={{0,4},{4,0},{8,12},{12,8},{16,20},{20,16},{24,28},{28,24},{1,5},{5... | collective-permute-start | bytes 3145736 | tf_op jit(solution)/shard_map/ppermute | solution.py:436
  154.1 33.8 %collective-permute-start.13 = (f32[512,512]{1,0:T(8,128)}, f32[512,512]{1,0:T(8,128)}, u32[]{:S(2)}, u32[]{:S(2)}) collective-permute-start(f32[512,512]{1,0:T(8,128)} %fusion.8), channel_id=1, source_target_pairs={{0,8},{4,12},{24,16},{28,20},{1,9},{5,13},{25,17},{29,21},{2,10},{... | collective-permute-start | bytes 3145736 | tf_op jit(solution)/shard_map/ppermute | solution.py:526
  169.2 41.1 %collective-permute-start.19 = (f32[512,512]{1,0:T(8,128)}, f32[512,512]{1,0:T(8,128)}, u32[]{:S(2)}, u32[]{:S(2)}) collective-permute-start(f32[512,512]{1,0:T(8,128)} %get-tuple-element.30), channel_id=1, source_target_pairs={{0,8},{4,12},{8,16},{12,20},{1,9},{5,13},{9,17},{13,21},{2,10},{6,... | collective-permute-start | bytes 3145736 | tf_op jit(solution)/shard_map/ppermute | solution.py:526
  174.7 35.7 %collective-permute-start.21 = (f32[512,512]{1,0:T(8,128)}, f32[512,512]{1,0:T(8,128)}, u32[]{:S(2)}, u32[]{:S(2)}) collective-permute-start(f32[512,512]{1,0:T(8,128)} %get-tuple-element.31), channel_id=1, source_target_pairs={{16,8},{20,12},{24,16},{28,20},{17,9},{21,13},{25,17},{29,21},{18,... | collective-permute-start | bytes 3145736 | tf_op jit(solution)/shard_map/ppermute | solution.py:526
  176.3 46.1 %collective-permute-start.10 = (f32[512,512]{1,0:T(8,128)}, f32[512,512]{1,0:T(8,128)}, u32[]{:S(2)}, u32[]{:S(2)}) collective-permute-start(f32[512,512]{1,0:T(8,128)} %held.10), channel_id=1, source_target_pairs={{0,4},{4,0},{8,12},{12,8},{16,20},{20,16},{24,28},{28,24},{1,5},{5... | collective-permute-start | bytes 3145736 | tf_op jit(solution)/shard_map/ppermute | solution.py:436
  191.3 31.0 %collective-permute-start.16 = (f32[512,512]{1,0:T(8,128)}, f32[512,512]{1,0:T(8,128)}, u32[]{:S(2)}, u32[]{:S(2)}) collective-permute-start(f32[512,512]{1,0:T(8,128)} %fusion.2), channel_id=1, source_target_pairs={{16,8},{20,12},{24,16},{28,20},{17,9},{21,13},{25,17},{29,21},{18,... | collective-permute-start | bytes 3145736 | tf_op jit(solution)/shard_map/ppermute | solution.py:526
  196.6 36.2 %collective-permute-start.14 = (f32[512,512]{1,0:T(8,128)}, f32[512,512]{1,0:T(8,128)}, u32[]{:S(2)}, u32[]{:S(2)}) collective-permute-start(f32[512,512]{1,0:T(8,128)} %fusion.11), channel_id=1, source_target_pairs={{0,8},{4,12},{8,16},{12,20},{1,9},{5,13},{9,17},{13,21},{2,10},{6,... | collective-permute-start | bytes 3145736 | tf_op jit(solution)/shard_map/ppermute | solution.py:526
  215.1 28.8 %collective-permute-start.22 = (f32[512,512]{1,0:T(8,128)}, f32[512,512]{1,0:T(8,128)}, u32[]{:S(2)}, u32[]{:S(2)}) collective-permute-start(f32[512,512]{1,0:T(8,128)} %get-tuple-element.29), channel_id=1, source_target_pairs={{8,0},{12,4},{16,8},{20,12},{24,16},{28,20},{9,1},{13,5},{17,9},{2... | collective-permute-start | bytes 3145736 | tf_op jit(solution)/shard_map/ppermute | solution.py:526
  216.4 38.9 %collective-permute-start.20 = (f32[512,512]{1,0:T(8,128)}, f32[512,512]{1,0:T(8,128)}, u32[]{:S(2)}, u32[]{:S(2)}) collective-permute-start(f32[512,512]{1,0:T(8,128)} %get-tuple-element.28), channel_id=1, source_target_pairs={{0,8},{4,12},{8,16},{12,20},{16,24},{20,28},{1,9},{5,13},{9,17},{1... | collective-permute-start | bytes 3145736 | tf_op jit(solution)/shard_map/ppermute | solution.py:526
  225.5 38.0 %collective-permute-start.17 = (f32[512,512]{1,0:T(8,128)}, f32[512,512]{1,0:T(8,128)}, u32[]{:S(2)}, u32[]{:S(2)}) collective-permute-start(f32[512,512]{1,0:T(8,128)} %fusion.6), channel_id=1, source_target_pairs={{8,0},{12,4},{16,8},{20,12},{24,16},{28,20},{9,1},{13,5},{17,9},{2... | collective-permute-start | bytes 3145736 | tf_op jit(solution)/shard_map/ppermute | solution.py:526
  236.6 40.1 %collective-permute-start.15 = (f32[512,512]{1,0:T(8,128)}, f32[512,512]{1,0:T(8,128)S(1)}, u32[]{:S(2)}, u32[]{:S(2)}) collective-permute-start(f32[512,512]{1,0:T(8,128)} %fusion.15), channel_id=1, source_target_pairs={{0,8},{4,12},{8,16},{12,20},{16,24},{20,28},{1,9},{5,13},{9,17},{1... | collective-permute-start | bytes 3145736 | tf_op jit(solution)/shard_map/ppermute | solution.py:526
  (20 other events, 263.7 us)

commit v3 on v2

v3 whole, which is shorter than its diff:
```python
import functools

import jax
import jax.numpy as jnp
import numpy as np
from jax import lax
from jax.experimental import pallas as pl
from jax.experimental.pallas import tpu as pltpu
from jax.sharding import PartitionSpec as P

BIN = 16
RADIUS = 10
HALO = 16
SIDE = 128
TILE = 256

HIGH = lax.Precision.HIGHEST
LAMBDA_REG = 0.25
PRIOR = 1.0
VMEM = 56 * 1024 * 1024
BF16 = jnp.bfloat16
F32 = jnp.float32
SMALL = pl.CostEstimate(flops=1000, bytes_accessed=1000, transcendentals=0)


def tap_values():
    offs = np.arange(-RADIUS, RADIUS + 1).astype(np.float64)
    taps = np.exp(-offs * offs / 50.0)
    return taps / taps.sum()


def band(out, width, lead):
    taps = tap_values()
    full = np.zeros((out, width), np.float64)
    for shift in range(-RADIUS, RADIUS + 1):
        rows = np.arange(out)
        full[rows, rows + lead + shift] = taps[shift + RADIUS]
    return full


def centers(index, total):
    return (2.0 * index.astype(F32) + 1.0) / total - 1.0


def split_high_low(value):
    high = value.astype(BF16)
    return high, (value - high.astype(F32)).astype(BF16)


def mm(left, right):
    return jnp.dot(left, right, preferred_element_type=F32)


def choose(condition, left, right):
    if isinstance(condition, (bool, np.bool_)):
        return left if condition else right
    return jnp.where(condition, left, right)


class Places:
    def __init__(self, exposures, cols):
        self.share = cols // exposures
        self.places = exposures // 2
        self.quarter = self.places // 4
        self.ends = 2 * self.quarter
        self.middle = self.places - self.ends

    def place_of(self, at, place):
        down = place < self.places // 2
        pair = at // 2
        end = choose(down, self.quarter - 1 - pair, pair) + (at % 2) * (self.places - self.quarter)
        turn = at - self.ends
        mid = choose(down, self.places - self.quarter - 1 - turn, self.quarter + turn)
        return choose(at < self.ends, end, mid)

    def position_of(self, wanted, place):
        down = place < self.places // 2
        right = wanted >= self.places - self.quarter
        low = choose(right, wanted - (self.places - self.quarter), wanted)
        pair = choose(down, self.quarter - 1 - low, low)
        turn = choose(down, self.places - self.quarter - 1 - wanted, wanted - self.quarter)
        is_end = right | (wanted < self.quarter)
        at = choose(is_end, 2 * pair + choose(right, 1, 0), self.ends + turn)
        return at, choose(is_end, pair, self.quarter + turn)

    def sent_block(self, at, meta):
        return 2 * self.place_of(at, meta[0] // 2) + 1 - meta[0] % 2

    def kept_block(self, at, meta):
        return 2 * self.place_of(at, meta[0] // 2) + meta[0] % 2


def inside(col, start, width):
    return (col >= start * BIN) & (col < start * BIN + width)


def columns(block, share, width=None, lead=0):
    return lax.broadcasted_iota(jnp.int32, (1, width or share), 1) + (block * share - lead)


def weights_kernel(block_of, plan, units, width, meta_ref, start_ref, frame_ref, spread_ref, mask_ref, *refs):
    weights, (bins_ref, total, scatter, gather) = refs[:-4], refs[-4:]
    step = pl.program_id(0)
    block = block_of(step, meta_ref)
    start = start_ref[meta_ref[0]]
    rows, share = frame_ref.shape
    bins_row, bins_col = mask_ref.shape
    per = share // BIN

    @pl.when(step == 0)
    def _():
        cell = lax.broadcasted_iota(jnp.int32, (SIDE, share), 1) >> 4
        scatter[...] = (cell == lax.broadcasted_iota(jnp.int32, (SIDE, share), 0)).astype(BF16)
        cell = lax.broadcasted_iota(jnp.int32, (share, SIDE), 0) >> 4
        gather[...] = (cell == lax.broadcasted_iota(jnp.int32, (share, SIDE), 1)).astype(BF16)
        total[...] = jnp.zeros_like(total)

    inverse = 1.0 / spread_ref[...]
    blocks_here = pltpu.roll(mask_ref[...].astype(F32), lax.rem(bins_col - block * per, bins_col), 1)[:, :SIDE]
    kept = mm(blocks_here.astype(BF16), scatter[...])
    kept = jnp.where(inside(columns(block, share), start, width), kept, 0.0)
    weight = inverse * jnp.broadcast_to(kept[:, None, :], (bins_row, BIN, share)).reshape(rows, share)
    for at, (out, fresh) in enumerate(plan):
        @pl.when(step == at)
        def _(out=out, fresh=fresh):
            if out >= units:
                weights[-1][0] = weight
            elif fresh:
                weights[out][...] = weight
            else:
                weights[out][...] += weight

    def halved(value):
        return value.reshape(bins_row, 2, 8, share).sum(axis=1).reshape(bins_row * 8, share)

    sums = jnp.concatenate([halved(frame_ref[...]), halved(inverse)], axis=0)
    top, rest = split_high_low(sums)
    last = ((sums - top.astype(F32)) - rest.astype(F32)).astype(BF16)
    part = mm(top, gather[...]) + (mm(rest, gather[...]) + mm(last, gather[...]))
    if bins_col > SIDE:
        part = jnp.concatenate([part, jnp.zeros((part.shape[0], bins_col - SIDE), F32)], axis=1)
    total[...] += pltpu.roll(part, block * per, 1)

    @pl.when(step == len(plan) - 1)
    def _():
        bins = total[...].reshape(2 * bins_row, 8, bins_col).sum(axis=1)
        cell = lax.broadcasted_iota(jnp.int32, (1, bins_col), 1) * BIN
        keep = jnp.where(inside(cell, start, width), mask_ref[...].astype(F32), 0.0)
        bins_ref[0, 0] = bins[:bins_row] / (BIN * BIN)
        bins_ref[0, 1] = bins[bins_row:] * keep


ANY = pl.BlockSpec(memory_space=pl.ANY)


def whole(shape):
    return pl.BlockSpec(shape, lambda *_: (0,) * len(shape))


def pixel_weights(block_of, plan, units, meta, starts, frame, spread, mask, share, width):
    rows = frame.shape[0]
    bins_row, bins_col = mask.shape
    kept = sum(out >= units for out, fresh in plan)
    lead = len(plan) - kept
    tile = pl.BlockSpec((rows, share), lambda i, meta, starts: (0, block_of(i, meta)))
    bins = (1, 2, bins_row, bins_col)
    return pl.pallas_call(
        functools.partial(weights_kernel, block_of, plan, units, width),
        grid_spec=pltpu.PrefetchScalarGridSpec(
            num_scalar_prefetch=2,
            grid=(len(plan),),
            in_specs=[tile, tile, whole(mask.shape)],
            out_specs=[whole((rows, share))] * units
            + [pl.BlockSpec((1, rows, share), lambda i, meta, starts: (jnp.maximum(i - lead, 0), 0, 0)), whole(bins)],
            scratch_shapes=[
                pltpu.VMEM((rows, bins_col), F32), pltpu.VMEM((SIDE, share), BF16), pltpu.VMEM((share, SIDE), BF16)
            ],
        ),
        out_shape=[pltpu.HBM((rows, share), F32)] * units
        + [pltpu.HBM((kept, rows, share), F32), jax.ShapeDtypeStruct(bins, F32)],
        compiler_params=pltpu.CompilerParams(vmem_limit_bytes=VMEM),
        cost_estimate=SMALL,
        name="pixel_weights",
    )(meta, starts, frame, spread, mask)


def smooth_kernel(block_of, plan, width, stacked, meta_ref, start_ref, *refs):
    step = pl.program_id(0)
    images, bands, scratch = refs[:9], refs[9:13], refs[-8:]
    refs = refs[13:-8]
    weights, outs = refs[: len(refs) // 2], refs[len(refs) // 2 :]

    @pl.when(step == 0)
    def _():
        for k, matrix in enumerate(bands):
            scratch[2 * k][...], scratch[2 * k + 1][...] = split_high_low(matrix[...])

    col_hi, col_lo, row_hi, row_lo, up_hi, up_lo, down_hi, down_lo = scratch
    block = block_of(step, meta_ref)
    start = start_ref[meta_ref[0]]
    rows, share = images[4].shape
    window = share + 2 * SIDE
    field = jnp.concatenate(
        [jnp.concatenate([images[3 * i + j][...] for j in range(3)], axis=1) for i in range(3)], axis=0
    )
    field = jnp.where(inside(columns(block, share, window, SIDE), start, width), field, 0.0)
    high, low = split_high_low(field)

    def three(a_hi, a_lo, b_hi, b_lo):
        return mm(a_hi, b_hi) + (mm(a_lo, b_hi) + mm(a_hi, b_lo))

    tiles = []
    for tile in range(share // TILE):
        lanes = slice(tile * TILE, (tile + 1) * TILE + 2 * SIDE)
        tiles.append(three(high[:, lanes], low[:, lanes], col_hi[...], col_lo[...]))
    across = tiles[0] if len(tiles) == 1 else jnp.concatenate(tiles, axis=1)
    high, low = split_high_low(across)
    height = row_hi.shape[0]
    tiles = []
    for tile in range(rows // height):
        top = tile * height
        mid = slice(top + HALO, top + HALO + height)
        upper = slice(top, top + HALO)
        lower = slice(top + HALO + height, top + 2 * HALO + height)
        main = three(row_hi[...], row_lo[...], high[mid], low[mid])
        tiles += [
            main[:HALO] + three(up_hi[...], up_lo[...], high[upper], low[upper]),
            main[HALO : height - HALO],
            main[height - HALO :] + three(down_hi[...], down_lo[...], high[lower], low[lower]),
        ]
    smoothed = jnp.concatenate(tiles, axis=0)
    smoothed = jnp.where(inside(columns(block, share), start, width), smoothed, 0.0)
    if stacked:
        outs[0][0] = weights[0][0] * smoothed
        return
    for at, (out, fresh) in enumerate(plan):
        @pl.when(step == at)
        def _(out=out, fresh=fresh):
            term = weights[out][...] * smoothed
            outs[out][...] = term if fresh else outs[out][...] + term


def smoothed_terms(block_of, plan, weights, meta, starts, frame, above, below, share, width, after=()):
    rows, cols = frame.shape
    stacked = weights[0].ndim == 3
    count = len(weights)
    per = share // SIDE
    last = cols // SIDE - 1
    specs = []
    for height in (HALO, rows, HALO):
        specs += [
            pl.BlockSpec((height, SIDE), lambda i, m, s: (0, jnp.maximum(block_of(i, m) * per - 1, 0))),
            pl.BlockSpec((height, share), lambda i, m, s: (0, block_of(i, m))),
            pl.BlockSpec((height, SIDE), lambda i, m, s: (0, jnp.minimum(block_of(i, m) * per + per, last))),
        ]
    if stacked:
        parts_spec = pl.BlockSpec((1, rows, share), lambda i, m, s: (i, 0, 0))
    else:
        parts_spec = whole((rows, share))
    height = min(TILE, rows)
    full = band(height, height + 2 * HALO, HALO)
    bands = [
        band(TILE, TILE + 2 * SIDE, SIDE).T,
        full[:, HALO : HALO + height],
        full[:HALO, :HALO],
        full[height - HALO :, HALO + height :],
    ]
    parts = [jnp.asarray(matrix.astype(np.float32)) for matrix in bands]

    def body(*refs):
        lead = 2 + 9 + len(parts) + count
        smooth_kernel(block_of, plan, width, stacked, *refs[:lead], *refs[lead + len(after) :])

    return pl.pallas_call(
        body,
        grid_spec=pltpu.PrefetchScalarGridSpec(
            num_scalar_prefetch=2,
            grid=(len(plan),),
            in_specs=specs + [whole(p.shape) for p in parts] + [parts_spec] * count + [ANY] * len(after),
            out_specs=[parts_spec] * count,
            scratch_shapes=[pltpu.VMEM(p.shape, BF16) for p in parts for _ in range(2)],
        ),
        out_shape=[pltpu.HBM(w.shape, F32) for w in weights],
        compiler_params=pltpu.CompilerParams(vmem_limit_bytes=VMEM),
        cost_estimate=SMALL,
        name="smoothed_terms",
    )(meta, starts, *([above] * 3 + [frame] * 3 + [below] * 3), *parts, *weights, *after)


def term_kernel(layout, width, wanted, units, received, numerator, meta_ref, start_ref, *refs):
    place = meta_ref[0] // 2
    block = 2 * wanted(place) + meta_ref[0] % 2
    _, unit = layout.position_of(wanted(place), place)
    mate_start = start_ref[meta_ref[0] + 1 - 2 * (meta_ref[0] % 2)]
    in_mate = inside(columns(block, layout.share), mate_start, width)
    *refs, out_ref = refs

    def pair():
        own = refs.pop(0)[0]
        got = refs.pop(0)[...]
        for u in units[1:]:
            got = jnp.where(unit == u, refs.pop(0)[...], got)
        return own, got

    def added(own, got, names):
        value = own + jnp.where(in_mate, got, 0.0)
        for _ in range(names):
            value = value + refs.pop(0)[...]
        return value

    if not numerator:
        out_ref[...] = added(*pair(), received)
        return
    own_den, mate_den = pair()
    own, mate = pair()
    rows_part, back = refs.pop(0)[...], refs.pop(0)[...]
    own_back = sum(rows_part[:, u : u + 1] * back[u : u + 1, :] for u in range(3))
    mate_back = sum(rows_part[:, u : u + 1] * back[3 + u : 4 + u, :] for u in range(3))
    top = added(own - own_den * own_back, mate - mate_den * mate_back, received)
    if numerator == "quotient":
        out_ref[...] = top / (PRIOR + added(own_den, mate_den, received))
    else:
        out_ref[...] = top


def block_term(layout, width, wanted, senders, meta, starts, parts, received, numerator=None, tables=(), after=()):
    kept = parts[0][0]
    rows, share = kept.shape[1:]
    chunk = min(SIDE, rows)

    def at_unit(place):
        return layout.position_of(wanted(place), place)

    units = sorted({int(at_unit(z)[1]) for z in senders})
    flat = pl.BlockSpec((chunk, share), lambda r, m, s: (r, 0))
    specs, args = [], []
    for own, got in parts:
        specs.append(pl.BlockSpec((1, chunk, share), lambda r, m, s: (at_unit(m[0] // 2)[0], r, 0)))
        args.append(own)
        for u in units:
            specs.append(
                flat
                if len(units) == 1
                else pl.BlockSpec(
                    (chunk, share), lambda r, m, s, u=u: (jnp.where(at_unit(m[0] // 2)[1] == u, r, 0), 0)
                )
            )
            args.append(got[u])
    if numerator:
        rows_part, back = tables
        strips = rows // chunk
        specs.append(pl.BlockSpec((chunk, rows_part.shape[1]), lambda r, m, s: (m[1] * strips + r, 0)))
        specs.append(
            pl.BlockSpec((back.shape[0], share), lambda r, m, s: (0, 2 * wanted(m[0] // 2) + m[0] % 2))
        )
        args += [rows_part, back]
    for sums in received:
        specs += [flat] * len(sums)
        args += list(sums)
    lead = 2 + len(args)
    body = functools.partial(term_kernel, layout, width, wanted, units, len(received[0]), numerator)
    return pl.pallas_call(
        lambda *refs: body(*refs[:lead], refs[-1]),
        grid_spec=pltpu.PrefetchScalarGridSpec(
            num_scalar_prefetch=2, grid=(rows // chunk,), in_specs=specs + [ANY] * len(after), out_specs=flat
        ),
        out_shape=jax.ShapeDtypeStruct((rows, share), F32)
        if numerator == "quotient"
        else pltpu.HBM((rows, share), F32),
        compiler_params=pltpu.CompilerParams(vmem_limit_bytes=VMEM),
        cost_estimate=SMALL,
        name="block_term",
    )(meta, starts, *args, *after)


def held_until(values, after):
    def body(*refs):
        del refs

    return pl.pallas_call(
        body,
        in_specs=[ANY] * (len(values) + len(after)),
        out_specs=[ANY] * len(values),
        out_shape=[jax.ShapeDtypeStruct(v.shape, v.dtype) for v in values],
        input_output_aliases={i: i for i in range(len(values))},
        compiler_params=pltpu.CompilerParams(vmem_limit_bytes=VMEM),
        cost_estimate=SMALL,
        name="held",
    )(*values, *after)


def contract_last(left, right):
    return lax.dot_general(left, right, (((1,), (1,)), ((), ())), precision=HIGH, preferred_element_type=F32)


def contract_last_three(left, right):
    def one(a, b):
        return lax.dot_general(a, b, (((1,), (1,)), ((), ())), preferred_element_type=F32)

    (l_hi, l_lo), (r_hi, r_lo) = split_high_low(left), split_high_low(right)
    return one(l_hi, r_hi) + (one(l_lo, r_hi) + one(l_hi, r_lo))


def moments_kernel(places, strips, meta_ref, bins_ref, out_ref):
    count, _, rows, cols = bins_ref.shape
    at = [places.index(e) for e in range(count)]
    image = [bins_ref[at[e], 0] for e in range(count)]
    weight = [bins_ref[at[e], 1] for e in range(count)]
    x = centers(lax.broadcasted_iota(jnp.int32, (1, cols), 1), cols)
    tx = [jnp.ones_like(x), x]
    while len(tx) < 5:
        tx.append(2.0 * x * tx[-1] - tx[-2])
    tx = jnp.concatenate(tx + [jnp.zeros((3, cols), F32)], axis=0)
    joint, diffs = [], []
    for apart in range(1, count // 2 + 1):
        group, group_d = [], []
        for i in range(count):
            j = (i + apart) % count
            w = weight[i] * weight[j] / (weight[i] + weight[j] + 1.0)
            group.append(w)
            group_d.append(w * (image[i] - image[j]))
        joint.append(contract_last_three(tx, jnp.concatenate(group, axis=0)))
        diffs.append(contract_last_three(tx, jnp.concatenate(group_d, axis=0)))
    along = jnp.concatenate([jnp.concatenate(joint, axis=1), jnp.concatenate(diffs, axis=1)], axis=0)
    total = along.shape[1]
    row = lax.broadcasted_iota(jnp.int32, (total, SIDE), 0)
    lane = lax.broadcasted_iota(jnp.int32, (total, SIDE), 1)
    mine = row // rows == lane
    y = centers(row % rows + meta_ref[1] * rows, rows * strips)
    a_hi, a_lo = split_high_low(along)
    ty = [jnp.ones_like(y), y]
    for a in range(5):
        if a > 1:
            ty.append(2.0 * y * ty[-1] - ty[-2])
        b_hi, b_lo = split_high_low(jnp.where(mine, ty[a], 0.0))
        out_ref[:, a * SIDE : (a + 1) * SIDE] = mm(a_hi, b_hi) + (mm(a_lo, b_hi) + mm(a_hi, b_lo))


def solve_kernel(width, meta_ref, start_ref, moments_ref, owner_ref, out_ref, back_ref):
    owner = owner_ref[...].astype(F32)
    count = owner.shape[0]
    lanes = count * count // 2
    exposure = lax.broadcasted_iota(jnp.int32, (count, lanes), 0)
    lane = lax.broadcasted_iota(jnp.int32, (count, lanes), 1)
    mine = lane % count
    apart = lane // count + 1
    is_i = (exposure == mine).astype(F32)
    is_j = (exposure == (mine + apart) % count).astype(F32)
    both = owner + owner.T
    listed = jnp.sum(is_i * jnp.dot(both, is_j, precision=HIGH, preferred_element_type=F32), axis=0, keepdims=True)
    lane_row = lax.broadcasted_iota(jnp.int32, (1, lanes), 1)
    once = (lane_row // count + 1 < count // 2) | (lane_row % count < count // 2)
    listed = jnp.where(once, listed, 0.0)
    held = listed > 0.0
    moment = [[moments_ref[b : b + 1, a * SIDE : a * SIDE + lanes] for b in range(5)] for a in range(5)]

    def entry(k, l):
        (u, v), (s, t) = divmod(k, 3), divmod(l, 3)
        total = 0.0
        for a in (u + s, abs(u - s)):
            for b in (v + t, abs(v - t)):
                total = total + moment[a][b]
        return jnp.where(held, 0.25 * total, 1.0 if k == l else 0.0)

    factor = [[None] * 9 for _ in range(9)]
    scale = [None] * 9
    for k in range(9):
        for l in range(k, 9):
            value = entry(l, k)
            for m in range(k):
                value = value - factor[l][m] * factor[k][m]
            if l == k:
                scale[k] = 1.0 / jnp.sqrt(value)
            else:
                factor[l][k] = value * scale[k]
    half = [None] * 9
    for k in range(9):
        a, b = divmod(k, 3)
        value = moments_ref[8 + b : 9 + b, a * SIDE : a * SIDE + lanes]
        for m in range(k):
            value = value - factor[k][m] * half[m]
        half[k] = value * scale[k]
    fit = [None] * 9
    for k in reversed(range(9)):
        value = half[k]
        for m in range(k + 1, 9):
            value = value - factor[m][k] * fit[m]
        fit[k] = value * scale[k]
    fits = jnp.concatenate([jnp.where(held, f, 0.0) for f in fit] + [jnp.zeros((7, lanes), F32)], axis=0)
    right = contract_last((is_i - is_j) * listed, fits)
    row = lax.broadcasted_iota(jnp.int32, (count, count), 0)
    column = lax.broadcasted_iota(jnp.int32, (count, count), 1)
    degree = jnp.sum(both, axis=1, keepdims=True) + LAMBDA_REG
    system = jnp.where(row == column, degree, 0.0) - both
    for k in range(count):
        inverse = 1.0 / system[k : k + 1, k : k + 1]
        pivot_s, pivot_r = system[k : k + 1, :] * inverse, right[k : k + 1, :] * inverse
        lead = system[:, k : k + 1]
        chosen = row[:, :1] == k
        system = jnp.where(chosen, pivot_s, system - lead * pivot_s)
        right = jnp.where(chosen, pivot_r, right - lead * pivot_r)
    out_ref[...] = right[:, :9]
    member = meta_ref[0]
    mate = member + 1 - 2 * (member % 2)
    cols = back_ref.shape[1]
    padded = cols + 2 * SIDE
    col = lax.broadcasted_iota(jnp.int32, (1, padded), 1) - SIDE
    x = centers(col, cols)
    terms = [jnp.ones_like(x), x, 2.0 * x * x - 1.0]
    fields = [jnp.where(inside(col, start_ref[e], width), t, 0.0) for e in (member, mate) for t in terms]
    fields = jnp.concatenate(fields + [jnp.zeros((2, padded), F32)], axis=0)
    taps = tap_values()
    total = float(taps[RADIUS]) * fields
    for shift in range(1, RADIUS + 1):
        both = pltpu.roll(fields, shift, 1) + pltpu.roll(fields, padded - shift, 1)
        total = total + float(taps[RADIUS + shift]) * both
    total = total[:, SIDE : SIDE + cols]
    rows = lax.broadcasted_iota(jnp.int32, (count, 16), 0)
    for k, which in enumerate((member, mate)):
        mine = jnp.sum(jnp.where(rows == which, right, 0.0), axis=0, keepdims=True)
        for u in range(3):
            back_ref[3 * k + u : 3 * k + u + 1, :] = sum(
                mine[:, 3 * u + v : 3 * u + v + 1] * total[3 * k + v : 3 * k + v + 1, :] for v in range(3)
            )
    back_ref[6:8, :] = jnp.zeros((2, cols), F32)


def filtered_rows(total_rows):
    y = (2.0 * np.arange(total_rows) + 1.0) / total_rows - 1.0
    terms = np.stack([np.ones_like(y), y, 2.0 * y * y - 1.0])
    padded = np.pad(terms, ((0, 0), (RADIUS, RADIUS)))
    taps = tap_values()
    return sum(taps[t] * padded[:, t : t + total_rows] for t in range(2 * RADIUS + 1)).T.astype(np.float32)


def per_device(image, variance, mask, foot_start, pair_owner):
    frame, spread, blocks = image[0], variance[0], mask[0]
    rows, cols = frame.shape
    exposures, sky_count = lax.axis_size("exp"), lax.axis_size("sky")
    member = lax.axis_index("exp")
    meta = jnp.stack([member, lax.axis_index("sky")])
    width = 3 * cols // 4
    layout = Places(exposures, cols)
    share, places, quarter = layout.share, layout.places, layout.quarter
    ends, middle_count = layout.ends, layout.middle
    units = quarter + middle_count
    sent = [(i // 2, i % 2 == 0) for i in range(ends)] + [(quarter + i, True) for i in range(middle_count)]
    kept = [(units + i, True) for i in range(places)]

    def sent_then_kept(i, meta):
        return jnp.where(i < places, layout.sent_block(i, meta), layout.kept_block(i - places, meta))

    swap = [(i, i ^ 1) for i in range(exposures)]

    def swapped(parts):
        return [lax.ppermute(part, "exp", swap) for part in parts]

    *den_sent, den_kept, gathered = pixel_weights(
        sent_then_kept, sent + kept, units, meta, foot_start, frame, spread, blocks, share, width
    )

    held = [0]
    bit = 1
    while bit < exposures:
        other = lax.ppermute(gathered, "exp", [(i, i ^ bit) for i in range(exposures)])
        low = (member & bit) == 0
        held = held + [e | bit for e in held]
        gathered = jnp.concatenate([jnp.where(low, gathered, other), jnp.where(low, other, gathered)])
        bit *= 2

    up = [(i, i + 1) for i in range(sky_count - 1)]
    down = [(j, i) for i, j in up]
    above = lax.ppermute(frame[rows - HALO :], "sky", up)
    below = lax.ppermute(frame[:HALO], "sky", down)
    den_got = swapped(den_sent)
    smooth = functools.partial(
        smoothed_terms, meta=meta, starts=foot_start, frame=frame, above=above, below=below, share=share, width=width
    )
    num_sent = smooth(layout.sent_block, sent, den_sent)
    num_got = swapped(num_sent)

    def to_right(step):
        return lambda z: choose(z < step, z + places - step, places - 1)

    def to_left(step):
        return lambda z: choose(z >= places - step, z - places + step, 0)

    def outward(step):
        return lambda z: choose(z < places // 2, to_right(step)(z), to_left(step)(z))

    def shift(value, rights, lefts):
        pairs = [(2 * z + s, 2 * z + 2 + s) for z in rights for s in range(2)]
        pairs += [(2 * z + s, 2 * z - 2 + s) for z in lefts for s in range(2)]
        return lax.ppermute(value, "exp", pairs)

    def along_places(step, term, sums, after):
        rights, lefts = range(step), range(places - step, places)
        if step <= places // 2:
            value = term(outward(step), [*rights, *lefts], sums, after)
            if step < places // 2:
                return (shift(value, rights, lefts),), (value,)
            return (shift(value, rights, []), shift(value, [], lefts)), (value,)
        right = term(to_right(step), rights, sums[:1], after)
        left = term(to_left(step), lefts, sums[1:], after)
        return (shift(right, rights, []), shift(left, [], lefts)), (right, left)

    def den_term(wanted, senders, sums, after):
        parts = [(den_kept, den_got)]
        return block_term(layout, width, wanted, senders, meta, foot_start, parts, [sums], after=after)

    den_sums, den_values = along_places(1, den_term, (), ())
    (num_kept,) = smooth(layout.kept_block, kept, [den_kept], after=num_sent)

    (gathered,) = held_until([gathered], [*num_sent, *den_values])
    scalars = pl.BlockSpec(memory_space=pltpu.SMEM)
    vmem = pl.BlockSpec(memory_space=pltpu.VMEM)
    moments = pl.pallas_call(
        functools.partial(moments_kernel, held, sky_count),
        in_specs=[scalars, vmem],
        out_shape=jax.ShapeDtypeStruct((16, 5 * SIDE), F32),
        compiler_params=pltpu.CompilerParams(vmem_limit_bytes=VMEM),
        cost_estimate=SMALL,
        name="pair_moments",
    )(meta, gathered)
    bit = 1
    while bit < sky_count:
        moments = moments + lax.ppermute(moments, "sky", [(i, i ^ bit) for i in range(sky_count)])
        if bit == 1:
            (moments,) = held_until([moments], [num_kept])
        bit *= 2
    offsets, back = pl.pallas_call(
        functools.partial(solve_kernel, width),
        in_specs=[scalars, scalars, vmem, vmem],
        out_shape=[jax.ShapeDtypeStruct((exposures, 9), F32), jax.ShapeDtypeStruct((8, cols), F32)],
        compiler_params=pltpu.CompilerParams(vmem_limit_bytes=VMEM),
        cost_estimate=SMALL,
        name="offsets",
    )(meta, foot_start, moments, pair_owner)

    tables = (jnp.asarray(filtered_rows(rows * sky_count)), back)
    parts = [(den_kept, den_got), (num_kept, num_got)]

    def num_term(wanted, senders, sums, after):
        return block_term(
            layout, width, wanted, senders, meta, foot_start, parts, [sums], "terms", tables, after
        )

    num_sums, num_values = along_places(1, num_term, (), den_values)
    for step in range(2, places):
        den_sums, den_values = along_places(step, den_term, den_sums, num_values)
        num_sums, num_values = along_places(step, num_term, num_sums, den_values)
    coadd = block_term(
        layout,
        width,
        lambda z: z,
        range(places),
        meta,
        foot_start,
        parts,
        [num_sums, den_sums],
        "quotient",
        tables,
    )
    return (coadd, offsets)


def solution(mesh):
    placed = (P("exp", "sky", None), P("exp", "sky", None), P("exp", "sky", None), P(), P())
    return jax.shard_map(
        per_device, mesh=mesh, in_specs=placed, out_specs=(P("sky", "exp"), P()), check_vma=False
    )
```

time: 283 us -> 230 us (0.81)
  other arithmetic: 43.3 us -> 4.41 us
  Pallas kernels: 69 us -> 93.6 us
  between operations: 18.2 us -> 0.88 us
  starting transfers between devices: 56.5 us -> 41.9 us
  waiting for transfers between devices: 83.1 us -> 78.3 us
    ppermute x10, waiting for transfers between devices: 68.7 us -> 27.7 us  [shift(): return lax.ppermute(value, 'exp', pairs)]
    ppermute x6, waiting for transfers between devices: 2.95 us -> 37.7 us  [swapped(): return [lax.ppermute(part, 'exp', swap) for part in parts]]
    add x12 -> x0, other arithmetic: 30.9 us -> none  [the longest x4 15.9 us: along_places(): value = value if rightward is None else value + rightward]
    pallas_call x3 -> x11, Pallas kernels: 36.7 us -> 65.5 us  [the longest x9 46.8 us: block_term(): pl.pallas_call(lambda *refs: body(*refs[:lead], refs[-1]), grid_spec=pltp...]
    ppermute x10, starting transfers between devices: 35.2 us -> 25 us  [shift(): return lax.ppermute(value, 'exp', pairs)]
    dynamic_slice x9 -> x0, local copies, waits for them, and re-layouts: 6.55 us -> none  [the longest x6 3.71 us: by_place(): lax.dynamic_index_in_dim(jnp.asarray(table), place, 0, keepdims=False)]
    unnamed x42 -> x38, local copies, waits for them, and re-layouts: 2.46 us -> 7.69 us
    div x2 -> x0, other arithmetic: 4.5 us -> none  [the longest x1 4.49 us: per_device(): return (total_num / (PRIOR + total_den), offsets)]
  transfers between devices with their start and end apart: 23 -> 23, of which waited for: 11 -> 11; matrix products, arithmetic and copies ran while one was open for 16% -> 2% of each run, Pallas kernels for 25% -> 31%
where the time goes in v3:
time: 230 us; the launch traced here: 228 us
  Pallas kernels  93.6 us (41%)
  waiting for transfers between devices  78.3 us (34%)
  starting transfers between devices  41.9 us (18%)
  local copies, waits for them, and re-layouts  8.75 us (4%)
  other arithmetic  4.41 us (2%)
    pallas_call x9, Pallas kernels, block_term(): pl.pallas_call(lambda *refs: body(*refs[:lead], refs[-1]), grid_spec=pltp...  46.8 us
    ppermute x6, waiting for transfers between devices, swapped(): return [lax.ppermute(part, 'exp', swap) for part in parts]  37.7 us
    ppermute x10, waiting for transfers between devices, shift(): return lax.ppermute(value, 'exp', pairs)  27.7 us
    ppermute x10, starting transfers between devices, shift(): return lax.ppermute(value, 'exp', pairs)  25 us
    pallas_call x2, Pallas kernels, smoothed_terms(): pl.pallas_call(body, grid_spec=pltpu.PrefetchScalarGridSpec(num_scalar_pr...  24.4 us
    pallas_call x1, Pallas kernels, pixel_weights(): pl.pallas_call(functools.partial(weights_kernel, block_of, plan, units, w...  16.1 us
    ppermute x3, waiting for transfers between devices, per_device(): lax.ppermute(gathered, 'exp', [(i, i ^ bit) for i in range(exposures)])  12.4 us
    unnamed x38, local copies, waits for them, and re-layouts  7.69 us
  transfers between devices with their start and end apart: 23, of which 11 were waited for; matrix products, arithmetic and copies ran while one was open for 2% of the time, Pallas kernels for 31%

profile of v3, /device:TPU:0, one launch (start us, length us, event | category | flops | bytes accessed | tf_op | source)
XLA Modules:
  0.0 227.9 jit_solution(14700192459439842424)
XLA Ops:
  1.3 16.1 %pixel_weights.1 = (f32[512,512]{1,0:T(8,128)}, f32[512,512]{1,0:T(8,128)}, f32[512,512]{1,0:T(8,128)}, f32[4,512,512]{2,1,0:T(8,128)}, f32[1,2,32,256]{3,2,1,0:T(8,128)}) custom-call(s32[2]{0:T(128)} %pad_add_fusion.meta_ref.refs_0_, s32[8]{0:T(128)} %refs_1_.21, f32[512,4096]{1,0:T(8,128)} %bitcast.9, f32[512,4096]{1,0:T(8,128)} %bitcast.16, ...), custom_call_target="tpu_custom_call" | custom-call | flops 1000 | bytes 1000 | tf_op jit(solution)/shard_map/pixel_weights/pallas_call | solution.py:167
  28.6 12.9 %smoothed_terms.2 = (f32[512,512]{1,0:T(8,128)}, f32[512,512]{1,0:T(8,128)}, f32[512,512]{1,0:T(8,128)}) custom-call(s32[2]{0:T(128)} %pad_add_fusion.meta_ref.refs_0_, s32[8]{0:T(128)} %refs_1_.21, f32[16,4096]{1,0:T(8,128)} %copy-done.4, f32[16,4096]{1,0:T(8,128)} %copy-done.4, f32[16,4096]{1,0:T(8,128)} %copy-done.4, f32[512,4096]{1,0:T(8,128)} %bitcast.10, ...), custom_call_target="tpu_custom_call" | custom-call | flops 1000 | bytes 1000 | tf_op jit(solution)/shard_map/smoothed_terms/pallas_call | solution.py:274
  45.2 12.4 %collective-permute-done.8 = f32[4,2,32,256]{3,2,1,0:T(8,128)S(1)} collective-permute-done((f32[4,2,32,256]{3,2,1,0:T(8,128)S(1)}, f32[4,2,32,256]{3,2,1,0:T(8,128)S(1)}, u32[]{:S(2)}, u32[]{:S(2)}) %collective-permute-start.8) | collective-permute-done | bytes 262176 | tf_op jit(solution)/shard_map/ppermute | solution.py:565
  59.4 4.3 %block_term.9.refs_4_.refs_8_ = f32[512,512]{1,0:T(8,128)} custom-call(s32[2]{0:T(128)} %pad_add_fusion.meta_ref.refs_0_, s32[8]{0:T(128)} %refs_1_.21, f32[4,512,512]{2,1,0:T(8,128)} %get-tuple-element.12.refs_15_.refs_2_, f32[512,512]{1,0:T(8,128)} %copy-done), custom_call_target="tpu_custom_call" | custom-call | flops 1000 | bytes 1000 | tf_op jit(solution)/shard_map/block_term/pallas_call | solution.py:362
  63.7 3.7 %pair_moments.1 = f32[16,640]{1,0:T(8,128)} custom-call(s32[2]{0:T(128)} %pad_add_fusion.meta_ref.refs_0_, f32[8,2,32,256]{3,2,1,0:T(8,128)} %held.2.bins_ref), custom_call_target="tpu_custom_call" | custom-call | flops 1000 | bytes 1000 | tf_op jit(solution)/shard_map/pair_moments/pallas_call | solution.py:617
  67.9 11.5 %smoothed_terms.3.refs_1_.refs_4_.refs_5_.refs_6_ = f32[4,512,512]{2,1,0:T(8,128)} custom-call(s32[2]{0:T(128)} %pad_add_fusion.meta_ref.refs_0_, s32[8]{0:T(128)} %refs_1_.21, f32[16,4096]{1,0:T(8,128)} %copy-done.4, f32[16,4096]{1,0:T(8,128)} %copy-done.4, f32[16,4096]{1,0:T(8,128)} %copy-done.4, f32[512,4096]{1,0:T(8,128)} %bitcast.13, ...), custom_call_target="tpu_custom_call" | custom-call | flops 1000 | bytes 1000 | tf_op jit(solution)/shard_map/smoothed_terms/pallas_call | solution.py:274
  91.2 5.2 %block_term.10.refs_6_ = f32[512,512]{1,0:T(8,128)} custom-call(s32[2]{0:T(128)} %pad_add_fusion.meta_ref.refs_0_, s32[8]{0:T(128)} %refs_1_.21, f32[4,512,512]{2,1,0:T(8,128)} %get-tuple-element.12.refs_15_.refs_2_, f32[512,512]{1,0:T(8,128)} %copy-done, f32[4,512,512]{2,1,0:T(8,128)} %smoothed_terms.3.refs_1_.refs_4_.refs_5_.refs_6_, ...), custom_call_target="tpu_custom_call" | custom-call | flops 1000 | bytes 1000 | tf_op jit(solution)/shard_map/block_term/pallas_call | solution.py:362
  98.6 9.1 %collective-permute-done.11.refs_4_ = f32[512,512]{1,0:T(8,128)S(1)} collective-permute-done((f32[512,512]{1,0:T(8,128)}, f32[512,512]{1,0:T(8,128)S(1)}, u32[]{:S(2)}, u32[]{:S(2)}) %collective-permute-start.11) | collective-permute-done | bytes 1048608 | tf_op jit(solution)/shard_map/ppermute | solution.py:556
  108.8 4.6 %block_term.11.refs_11_ = f32[512,512]{1,0:T(8,128)} custom-call(s32[2]{0:T(128)} %pad_add_fusion.meta_ref.refs_0_, s32[8]{0:T(128)} %refs_1_.21, f32[4,512,512]{2,1,0:T(8,128)} %get-tuple-element.12.refs_15_.refs_2_, f32[512,512]{1,0:T(8,128)} %copy-done, f32[512,512]{1,0:T(8,128)} %copy-done.1, f32[512,512]{1,0:T(8,128)} %collective-permute-done.14.refs_5_, ...), custom_call_target="tpu_custom_call" | custom-call | flops 1000 | bytes 1000 | tf_op jit(solution)/shard_map/block_term/pallas_call | solution.py:362
  115.1 5.1 %collective-permute-start.16 = (f32[512,512]{1,0:T(8,128)}, f32[512,512]{1,0:T(8,128)}, u32[]{:S(2)}, u32[]{:S(2)}) collective-permute-start(f32[512,512]{1,0:T(8,128)} %block_term.11.refs_11_), channel_id=1, source_target_pairs={{0,8},{4,12},{8,16},{12,20},{1,9},{5,13},{9,17},{13,21},{2,10},{6,... | collective-permute-start | bytes 3145736 | tf_op jit(solution)/shard_map/ppermute | solution.py:594
  120.2 10.0 %collective-permute-done.12.refs_7_.refs_8_ = f32[512,512]{1,0:T(8,128)S(1)} collective-permute-done((f32[512,512]{1,0:T(8,128)S(1)}, f32[512,512]{1,0:T(8,128)S(1)}, u32[]{:S(2)}, u32[]{:S(2)}) %collective-permute-start.12) | collective-permute-done | bytes 1048608 | tf_op jit(solution)/shard_map/ppermute | solution.py:556
  132.4 5.5 %block_term.12.refs_7_ = f32[512,512]{1,0:T(8,128)} custom-call(s32[2]{0:T(128)} %pad_add_fusion.meta_ref.refs_0_, s32[8]{0:T(128)} %refs_1_.21, f32[4,512,512]{2,1,0:T(8,128)} %get-tuple-element.12.refs_15_.refs_2_, f32[512,512]{1,0:T(8,128)} %copy-done, f32[512,512]{1,0:T(8,128)} %copy-done.1, ...), custom_call_target="tpu_custom_call" | custom-call | flops 1000 | bytes 1000 | tf_op jit(solution)/shard_map/block_term/pallas_call | solution.py:362
  138.6 14.1 %collective-permute-done.1.refs_5_.refs_4_ = f32[512,512]{1,0:T(8,128)S(1)} collective-permute-done((f32[512,512]{1,0:T(8,128)}, f32[512,512]{1,0:T(8,128)S(1)}, u32[]{:S(2)}, u32[]{:S(2)}) %collective-permute-start.1) | collective-permute-done | bytes 1048608 | tf_op jit(solution)/shard_map/ppermute | solution.py:556
  154.4 4.7 %block_term.14.refs_14_ = f32[512,512]{1,0:T(8,128)} custom-call(s32[2]{0:T(128)} %pad_add_fusion.meta_ref.refs_0_, s32[8]{0:T(128)} %refs_1_.21, f32[4,512,512]{2,1,0:T(8,128)} %get-tuple-element.12.refs_15_.refs_2_, f32[512,512]{1,0:T(8,128)} %copy-done, f32[512,512]{1,0:T(8,128)} %copy-done.1, f32[512,512]{1,0:T(8,128)} %copy-done.3, ...), custom_call_target="tpu_custom_call" | custom-call | flops 1000 | bytes 1000 | tf_op jit(solution)/shard_map/block_term/pallas_call | solution.py:362
  160.5 4.7 %block_term.13.refs_13_ = f32[512,512]{1,0:T(8,128)} custom-call(s32[2]{0:T(128)} %pad_add_fusion.meta_ref.refs_0_, s32[8]{0:T(128)} %refs_1_.21, f32[4,512,512]{2,1,0:T(8,128)} %get-tuple-element.12.refs_15_.refs_2_, f32[512,512]{1,0:T(8,128)} %copy-done, f32[512,512]{1,0:T(8,128)} %copy-done.1, f32[512,512]{1,0:T(8,128)} %copy-done.3, ...), custom_call_target="tpu_custom_call" | custom-call | flops 1000 | bytes 1000 | tf_op jit(solution)/shard_map/block_term/pallas_call | solution.py:362
  165.2 4.6 %collective-permute-start.21 = (f32[512,512]{1,0:T(8,128)}, f32[512,512]{1,0:T(8,128)S(1)}, u32[]{:S(2)}, u32[]{:S(2)}) collective-permute-start(f32[512,512]{1,0:T(8,128)} %block_term.13.refs_13_), channel_id=1, source_target_pairs={{0,8},{4,12},{8,16},{12,20},{16,24},{20,28},{1,9},{5,13},{9,17},{1... | collective-permute-start | bytes 3145736 | tf_op jit(solution)/shard_map/ppermute | solution.py:594
  169.8 4.5 %collective-permute-done.5.refs_9_.refs_7_ = f32[512,512]{1,0:T(8,128)S(1)} collective-permute-done((f32[512,512]{1,0:T(8,128)S(1)}, f32[512,512]{1,0:T(8,128)S(1)}, u32[]{:S(2)}, u32[]{:S(2)}) %collective-permute-start.5) | collective-permute-done | bytes 1048608 | tf_op jit(solution)/shard_map/ppermute | solution.py:556
  176.3 5.7 %block_term.16 = f32[512,512]{1,0:T(8,128)} custom-call(s32[2]{0:T(128)} %pad_add_fusion.meta_ref.refs_0_, s32[8]{0:T(128)} %refs_1_.21, f32[4,512,512]{2,1,0:T(8,128)} %get-tuple-element.12.refs_15_.refs_2_, f32[512,512]{1,0:T(8,128)} %copy-done, f32[512,512]{1,0:T(8,128)} %copy-done.1, f32[512,512]{1,0:T(8,128)} %copy-done.3, ...), custom_call_target="tpu_custom_call" | custom-call | flops 1000 | bytes 1000 | tf_op jit(solution)/shard_map/block_term/pallas_call | solution.py:362
  184.3 5.7 %block_term.15 = f32[512,512]{1,0:T(8,128)} custom-call(s32[2]{0:T(128)} %pad_add_fusion.meta_ref.refs_0_, s32[8]{0:T(128)} %refs_1_.21, f32[4,512,512]{2,1,0:T(8,128)} %get-tuple-element.12.refs_15_.refs_2_, f32[512,512]{1,0:T(8,128)} %copy-done, f32[512,512]{1,0:T(8,128)} %copy-done.1, f32[512,512]{1,0:T(8,128)} %copy-done.3, ...), custom_call_target="tpu_custom_call" | custom-call | flops 1000 | bytes 1000 | tf_op jit(solution)/shard_map/block_term/pallas_call | solution.py:362
  190.0 4.6 %collective-permute-start.18 = (f32[512,512]{1,0:T(8,128)}, f32[512,512]{1,0:T(8,128)S(1)}, u32[]{:S(2)}, u32[]{:S(2)}) collective-permute-start(f32[512,512]{1,0:T(8,128)} %block_term.15), channel_id=1, source_target_pairs={{0,8},{4,12},{8,16},{12,20},{16,24},{20,28},{1,9},{5,13},{9,17},{1... | collective-permute-start | bytes 3145736 | tf_op jit(solution)/shard_map/ppermute | solution.py:594
  194.6 6.1 %collective-permute-done.21.refs_12_ = f32[512,512]{1,0:T(8,128)S(1)} collective-permute-done((f32[512,512]{1,0:T(8,128)}, f32[512,512]{1,0:T(8,128)S(1)}, u32[]{:S(2)}, u32[]{:S(2)}) %collective-permute-start.21) | collective-permute-done | bytes 1048608 | tf_op jit(solution)/shard_map/ppermute | solution.py:594
  200.7 7.6 %collective-permute-done.20.refs_11_ = f32[512,512]{1,0:T(8,128)S(1)} collective-permute-done((f32[512,512]{1,0:T(8,128)}, f32[512,512]{1,0:T(8,128)S(1)}, u32[]{:S(2)}, u32[]{:S(2)}) %collective-permute-start.20) | collective-permute-done | bytes 1048608 | tf_op jit(solution)/shard_map/ppermute | solution.py:594
  208.4 12.3 %collective-permute-done.18.refs_10_ = f32[512,512]{1,0:T(8,128)S(1)} collective-permute-done((f32[512,512]{1,0:T(8,128)}, f32[512,512]{1,0:T(8,128)S(1)}, u32[]{:S(2)}, u32[]{:S(2)}) %collective-permute-start.18) | collective-permute-done | bytes 1048608 | tf_op jit(solution)/shard_map/ppermute | solution.py:594
  221.6 6.3 %block_term.17 = f32[512,512]{1,0:T(8,128)} custom-call(s32[2]{0:T(128)} %pad_add_fusion.meta_ref.refs_0_, s32[8]{0:T(128)} %refs_1_.21, f32[4,512,512]{2,1,0:T(8,128)} %get-tuple-element.12.refs_15_.refs_2_, f32[512,512]{1,0:T(8,128)} %copy-done, f32[512,512]{1,0:T(8,128)} %copy-done.3, f32[4,512,512]{2,1,0:T(8,128)} %smoothed_terms.3.refs_1_.refs_4_.refs_5_.refs_6_, ...), custom_call_target="tpu_custom_call" | custom-call | flops 1000 | bytes 1000 | tf_op jit(solution)/shard_map/block_term/pallas_call | solution.py:362
  (86 shorter events, 45.7 us)
Async XLA Ops:
  17.4 6.8 %collective-permute-start.6 = (f32[1,2,32,256]{3,2,1,0:T(8,128)}, f32[1,2,32,256]{3,2,1,0:T(8,128)S(1)}, u32[]{:S(2)}, u32[]{:S(2)}) collective-permute-start(f32[1,2,32,256]{3,2,1,0:T(8,128)} %get-tuple-element.19), channel_id=1, source_target_pairs={{0,4},{4,0},{8,12},{12,8},{16,20},{20,16},{24,28},{28,24},{1,5},{5... | collective-permute-start | bytes 196616 | tf_op jit(solution)/shard_map/ppermute | solution.py:565
  21.4 5.9 %collective-permute-start.2 = (f32[16,4096]{1,0:T(8,128)S(1)}, f32[16,4096]{1,0:T(8,128)S(1)}, u32[]{:S(2)}, u32[]{:S(2)}) collective-permute-start(f32[16,4096]{1,0:T(8,128)S(1)} %get-tuple-element.23), channel_id=1, source_target_pairs={{0,1},{1,2},{2,3},{4,5},{5,6},{6,7},{8,9},{9,10},{10,11},{12,13},{... | collective-permute-start | bytes 786440 | tf_op jit(solution)/shard_map/ppermute | solution.py:573
  22.9 5.0 %collective-permute-start.3 = (f32[16,4096]{1,0:T(8,128)S(1)}, f32[16,4096]{1,0:T(8,128)S(1)}, u32[]{:S(2)}, u32[]{:S(2)}) collective-permute-start(f32[16,4096]{1,0:T(8,128)S(1)} %get-tuple-element.22), channel_id=1, source_target_pairs={{1,0},{2,1},{3,2},{5,4},{6,5},{7,6},{9,8},{10,9},{11,10},{13,12},{... | collective-permute-start | bytes 786440 | tf_op jit(solution)/shard_map/ppermute | solution.py:574
  25.0 17.5 %collective-permute-start.7 = (f32[2,2,32,256]{3,2,1,0:T(8,128)S(1)}, f32[2,2,32,256]{3,2,1,0:T(8,128)S(1)}, u32[]{:S(2)}, u32[]{:S(2)}) collective-permute-start(f32[2,2,32,256]{3,2,1,0:T(8,128)S(1)} %pad_maximum_fusion.2), channel_id=1, source_target_pairs={{0,8},{4,12},{8,0},{12,4},{16,24},{20,28},{24,16},{28,20},{1,9},{5... | collective-permute-start | bytes 393224 | tf_op jit(solution)/shard_map/ppermute | solution.py:565
  26.7 31.8 %collective-permute-start = (f32[512,512]{1,0:T(8,128)}, f32[512,512]{1,0:T(8,128)S(1)}, u32[]{:S(2)}, u32[]{:S(2)}) collective-permute-start(f32[512,512]{1,0:T(8,128)} %get-tuple-element.13.refs_15_), channel_id=1, source_target_pairs={{0,4},{4,0},{8,12},{12,8},{16,20},{20,16},{24,28},{28,24},{1,5},{5... | collective-permute-start | bytes 3145736 | tf_op jit(solution)/shard_map/ppermute | solution.py:556
  41.5 48.7 %collective-permute-start.4 = (f32[512,512]{1,0:T(8,128)}, f32[512,512]{1,0:T(8,128)S(1)}, u32[]{:S(2)}, u32[]{:S(2)}) collective-permute-start(f32[512,512]{1,0:T(8,128)} %get-tuple-element.16.refs_16_.refs_1_), channel_id=1, source_target_pairs={{0,4},{4,0},{8,12},{12,8},{16,20},{20,16},{24,28},{28,24},{1,5},{5... | collective-permute-start | bytes 3145736 | tf_op jit(solution)/shard_map/ppermute | solution.py:556
  42.6 15.0 %collective-permute-start.8 = (f32[4,2,32,256]{3,2,1,0:T(8,128)S(1)}, f32[4,2,32,256]{3,2,1,0:T(8,128)S(1)}, u32[]{:S(2)}, u32[]{:S(2)}) collective-permute-start(f32[4,2,32,256]{3,2,1,0:T(8,128)S(1)} %pad_maximum_fusion.1), channel_id=1, source_target_pairs={{0,16},{4,20},{8,24},{12,28},{16,0},{20,4},{24,8},{28,12},{1,17},{... | collective-permute-start | bytes 786440 | tf_op jit(solution)/shard_map/ppermute | solution.py:565
  67.4 12.1 %collective-permute-start.9 = (f32[16,640]{1,0:T(8,128)}, f32[16,640]{1,0:T(8,128)S(1)}, u32[]{:S(2)}, u32[]{:S(2)}) collective-permute-start(f32[16,640]{1,0:T(8,128)} %pair_moments.1), channel_id=1, source_target_pairs={{0,1},{1,0},{2,3},{3,2},{4,5},{5,4},{6,7},{7,6},{8,9},{9,8},{10,11... | collective-permute-start | bytes 122888 | tf_op jit(solution)/shard_map/ppermute | solution.py:627
  80.1 6.1 %collective-permute-start.10 = (f32[16,640]{1,0:T(8,128)}, f32[16,640]{1,0:T(8,128)S(1)}, u32[]{:S(2)}, u32[]{:S(2)}) collective-permute-start(f32[16,640]{1,0:T(8,128)} %held.3), channel_id=1, source_target_pairs={{0,2},{1,3},{2,0},{3,1},{4,6},{5,7},{6,4},{7,5},{8,10},{9,11},{10,... | collective-permute-start | bytes 122888 | tf_op jit(solution)/shard_map/ppermute | solution.py:627
  81.5 26.2 %collective-permute-start.11 = (f32[512,512]{1,0:T(8,128)}, f32[512,512]{1,0:T(8,128)S(1)}, u32[]{:S(2)}, u32[]{:S(2)}) collective-permute-start(f32[512,512]{1,0:T(8,128)} %get-tuple-element.15.refs_16_), channel_id=1, source_target_pairs={{0,4},{4,0},{8,12},{12,8},{16,20},{20,16},{24,28},{28,24},{1,5},{5... | collective-permute-start | bytes 3145736 | tf_op jit(solution)/shard_map/ppermute | solution.py:556
  82.0 48.2 %collective-permute-start.12 = (f32[512,512]{1,0:T(8,128)S(1)}, f32[512,512]{1,0:T(8,128)S(1)}, u32[]{:S(2)}, u32[]{:S(2)}) collective-permute-start(f32[512,512]{1,0:T(8,128)S(1)} %copy-done.10), channel_id=1, source_target_pairs={{0,4},{4,0},{8,12},{12,8},{16,20},{20,16},{24,28},{28,24},{1,5},{5... | collective-permute-start | bytes 3145736 | tf_op jit(solution)/shard_map/ppermute | solution.py:556
  83.5 25.3 %collective-permute-start.14 = (f32[512,512]{1,0:T(8,128)S(1)}, f32[512,512]{1,0:T(8,128)}, u32[]{:S(2)}, u32[]{:S(2)}) collective-permute-start(f32[512,512]{1,0:T(8,128)S(1)} %copy-done.8), channel_id=1, source_target_pairs={{0,8},{4,12},{24,16},{28,20},{1,9},{5,13},{25,17},{29,21},{2,10},{... | collective-permute-start | bytes 3145736 | tf_op jit(solution)/shard_map/ppermute | solution.py:594
  91.2 39.0 %copy-start.9 = (f32[512,512]{1,0:T(8,128)S(1)}, f32[512,512]{1,0:T(8,128)}, u32[]{:S(2)}) copy-start(f32[512,512]{1,0:T(8,128)} %get-tuple-element.18.refs_18_.refs_3_) | copy-start | bytes 3145732
  96.4 35.0 %collective-permute-start.13 = (f32[512,512]{1,0:T(8,128)}, f32[512,512]{1,0:T(8,128)S(1)}, u32[]{:S(2)}, u32[]{:S(2)}) collective-permute-start(f32[512,512]{1,0:T(8,128)} %block_term.10.refs_6_), channel_id=1, source_target_pairs={{0,8},{4,12},{24,16},{28,20},{1,9},{5,13},{25,17},{29,21},{2,10},{... | collective-permute-start | bytes 3145736 | tf_op jit(solution)/shard_map/ppermute | solution.py:594
  97.8 54.9 %collective-permute-start.1 = (f32[512,512]{1,0:T(8,128)}, f32[512,512]{1,0:T(8,128)S(1)}, u32[]{:S(2)}, u32[]{:S(2)}) collective-permute-start(f32[512,512]{1,0:T(8,128)} %get-tuple-element.14.refs_17_), channel_id=1, source_target_pairs={{0,4},{4,0},{8,12},{12,8},{16,20},{20,16},{24,28},{28,24},{1,5},{5... | collective-permute-start | bytes 3145736 | tf_op jit(solution)/shard_map/ppermute | solution.py:556
  113.4 41.0 %collective-permute-start.17 = (f32[512,512]{1,0:T(8,128)}, f32[512,512]{1,0:T(8,128)}, u32[]{:S(2)}, u32[]{:S(2)}) collective-permute-start(f32[512,512]{1,0:T(8,128)} %block_term.11.refs_11_), channel_id=1, source_target_pairs={{16,8},{20,12},{24,16},{28,20},{17,9},{21,13},{25,17},{29,21},{18,... | collective-permute-start | bytes 3145736 | tf_op jit(solution)/shard_map/ppermute | solution.py:594
  115.1 45.4 %collective-permute-start.16 = (f32[512,512]{1,0:T(8,128)}, f32[512,512]{1,0:T(8,128)}, u32[]{:S(2)}, u32[]{:S(2)}) collective-permute-start(f32[512,512]{1,0:T(8,128)} %block_term.11.refs_11_), channel_id=1, source_target_pairs={{0,8},{4,12},{8,16},{12,20},{1,9},{5,13},{9,17},{13,21},{2,10},{6,... | collective-permute-start | bytes 3145736 | tf_op jit(solution)/shard_map/ppermute | solution.py:594
  130.2 44.0 %collective-permute-start.5 = (f32[512,512]{1,0:T(8,128)S(1)}, f32[512,512]{1,0:T(8,128)S(1)}, u32[]{:S(2)}, u32[]{:S(2)}) collective-permute-start(f32[512,512]{1,0:T(8,128)S(1)} %copy-done.9), channel_id=1, source_target_pairs={{0,4},{4,0},{8,12},{12,8},{16,20},{20,16},{24,28},{28,24},{1,5},{5... | collective-permute-start | bytes 3145736 | tf_op jit(solution)/shard_map/ppermute | solution.py:556
  137.9 36.4 %collective-permute-start.19 = (f32[512,512]{1,0:T(8,128)}, f32[512,512]{1,0:T(8,128)S(1)}, u32[]{:S(2)}, u32[]{:S(2)}) collective-permute-start(f32[512,512]{1,0:T(8,128)} %block_term.12.refs_7_), channel_id=1, source_target_pairs={{16,8},{20,12},{24,16},{28,20},{17,9},{21,13},{25,17},{29,21},{18,... | collective-permute-start | bytes 3145736 | tf_op jit(solution)/shard_map/ppermute | solution.py:594
  152.7 30.6 %collective-permute-start.15 = (f32[512,512]{1,0:T(8,128)}, f32[512,512]{1,0:T(8,128)S(1)}, u32[]{:S(2)}, u32[]{:S(2)}) collective-permute-start(f32[512,512]{1,0:T(8,128)} %block_term.12.refs_7_), channel_id=1, source_target_pairs={{0,8},{4,12},{8,16},{12,20},{1,9},{5,13},{9,17},{13,21},{2,10},{6,... | collective-permute-start | bytes 3145736 | tf_op jit(solution)/shard_map/ppermute | solution.py:594
  159.2 35.5 %collective-permute-start.22 = (f32[512,512]{1,0:T(8,128)}, f32[512,512]{1,0:T(8,128)S(1)}, u32[]{:S(2)}, u32[]{:S(2)}) collective-permute-start(f32[512,512]{1,0:T(8,128)} %block_term.14.refs_14_), channel_id=1, source_target_pairs={{8,0},{12,4},{16,8},{20,12},{24,16},{28,20},{9,1},{13,5},{17,9},{2... | collective-permute-start | bytes 3145736 | tf_op jit(solution)/shard_map/ppermute | solution.py:594
  165.2 35.6 %collective-permute-start.21 = (f32[512,512]{1,0:T(8,128)}, f32[512,512]{1,0:T(8,128)S(1)}, u32[]{:S(2)}, u32[]{:S(2)}) collective-permute-start(f32[512,512]{1,0:T(8,128)} %block_term.13.refs_13_), channel_id=1, source_target_pairs={{0,8},{4,12},{8,16},{12,20},{16,24},{20,28},{1,9},{5,13},{9,17},{1... | collective-permute-start | bytes 3145736 | tf_op jit(solution)/shard_map/ppermute | solution.py:594
  182.0 26.4 %collective-permute-start.20 = (f32[512,512]{1,0:T(8,128)}, f32[512,512]{1,0:T(8,128)S(1)}, u32[]{:S(2)}, u32[]{:S(2)}) collective-permute-start(f32[512,512]{1,0:T(8,128)} %block_term.16), channel_id=1, source_target_pairs={{8,0},{12,4},{16,8},{20,12},{24,16},{28,20},{9,1},{13,5},{17,9},{2... | collective-permute-start | bytes 3145736 | tf_op jit(solution)/shard_map/ppermute | solution.py:594
  190.0 30.6 %collective-permute-start.18 = (f32[512,512]{1,0:T(8,128)}, f32[512,512]{1,0:T(8,128)S(1)}, u32[]{:S(2)}, u32[]{:S(2)}) collective-permute-start(f32[512,512]{1,0:T(8,128)} %block_term.15), channel_id=1, source_target_pairs={{0,8},{4,12},{8,16},{12,20},{16,24},{20,28},{1,9},{5,13},{9,17},{1... | collective-permute-start | bytes 3145736 | tf_op jit(solution)/shard_map/ppermute | solution.py:594
  (18 other events, 113.5 us)

commit v4 on v3

--- a/solution.py
+++ b/solution.py
@@ -12,12 +12,14 @@
 RADIUS = 10
 HALO = 16
 SIDE = 128
+TOKEN = (8, 128)
 TILE = 256
 
 HIGH = lax.Precision.HIGHEST
 LAMBDA_REG = 0.25
 PRIOR = 1.0
-VMEM = 56 * 1024 * 1024
+VMEM = 127 * 512 * 1024
+SOME = 24 * 1024 * 1024
 BF16 = jnp.bfloat16
 F32 = jnp.float32
 SMALL = pl.CostEstimate(flops=1000, bytes_accessed=1000, transcendentals=0)
@@ -98,12 +100,16 @@
     return lax.broadcasted_iota(jnp.int32, (1, width or share), 1) + (block * share - lead)
 
 
-def weights_kernel(block_of, plan, units, width, meta_ref, start_ref, frame_ref, spread_ref, mask_ref, *refs):
-    weights, (bins_ref, total, scatter, gather) = refs[:-4], refs[-4:]
+def weights_kernel(block_of, plan, units, width, meta_ref, start_ref, *refs):
+    binned = len(refs) > 4 + units
+    frame_ref, refs = (refs[0], refs[1:]) if binned else (None, refs)
+    spread_ref, mask_ref, *refs = refs
+    weights, scratch = (refs[:-4], refs[-4:]) if binned else (refs[:-1], refs[-1:])
+    scatter = scratch[-1]
     step = pl.program_id(0)
     block = block_of(step, meta_ref)
     start = start_ref[meta_ref[0]]
-    rows, share = frame_ref.shape
+    rows, share = spread_ref.shape
     bins_row, bins_col = mask_ref.shape
     per = share // BIN
 
@@ -111,18 +117,18 @@
     def _():
         cell = lax.broadcasted_iota(jnp.int32, (SIDE, share), 1) >> 4
         scatter[...] = (cell == lax.broadcasted_iota(jnp.int32, (SIDE, share), 0)).astype(BF16)
-        cell = lax.broadcasted_iota(jnp.int32, (share, SIDE), 0) >> 4
-        gather[...] = (cell == lax.broadcasted_iota(jnp.int32, (share, SIDE), 1)).astype(BF16)
-        total[...] = jnp.zeros_like(total)
 
     inverse = 1.0 / spread_ref[...]
     blocks_here = pltpu.roll(mask_ref[...].astype(F32), lax.rem(bins_col - block * per, bins_col), 1)[:, :SIDE]
     kept = mm(blocks_here.astype(BF16), scatter[...])
     kept = jnp.where(inside(columns(block, share), start, width), kept, 0.0)
     weight = inverse * jnp.broadcast_to(kept[:, None, :], (bins_row, BIN, share)).reshape(rows, share)
-    for at, (out, fresh) in enumerate(plan):
+    for at, part in enumerate(plan):
+        if part is None:
+            continue
+
         @pl.when(step == at)
-        def _(out=out, fresh=fresh):
+        def _(out=part[0], fresh=part[1]):
             if out >= units:
                 weights[-1][0] = weight
             elif fresh:
@@ -130,16 +136,33 @@
             else:
                 weights[out][...] += weight
 
+    if not binned:
+        return
+    bins_ref, total, gather, _ = scratch
+
+    @pl.when(step == 0)
+    def _():
+        cell = lax.broadcasted_iota(jnp.int32, (share, SIDE), 0) >> 4
+        gather[...] = (cell == lax.broadcasted_iota(jnp.int32, (share, SIDE), 1)).astype(BF16)
+        total[...] = jnp.zeros_like(total)
+
     def halved(value):
         return value.reshape(bins_row, 2, 8, share).sum(axis=1).reshape(bins_row * 8, share)
 
-    sums = jnp.concatenate([halved(frame_ref[...]), halved(inverse)], axis=0)
-    top, rest = split_high_low(sums)
-    last = ((sums - top.astype(F32)) - rest.astype(F32)).astype(BF16)
-    part = mm(top, gather[...]) + (mm(rest, gather[...]) + mm(last, gather[...]))
-    if bins_col > SIDE:
-        part = jnp.concatenate([part, jnp.zeros((part.shape[0], bins_col - SIDE), F32)], axis=1)
-    total[...] += pltpu.roll(part, block * per, 1)
+    def gathered(value, parts):
+        result = None
+        for _ in range(parts):
+            rounded = value.astype(BF16)
+            value = value - rounded.astype(F32)
+            product = mm(rounded, gather[...])
+            result = product if result is None else result + product
+        if bins_col > SIDE:
+            result = jnp.concatenate([result, jnp.zeros((result.shape[0], bins_col - SIDE), F32)], axis=1)
+        return pltpu.roll(result, block * per, 1)
+
+    half = bins_row * 8
+    total[:half] += gathered(halved(frame_ref[...]), 3)
+    total[half:] += gathered(halved(inverse), 2)
 
     @pl.when(step == len(plan) - 1)
     def _():
@@ -157,31 +180,40 @@
     return pl.BlockSpec(shape, lambda *_: (0,) * len(shape))
 
 
-def pixel_weights(block_of, plan, units, meta, starts, frame, spread, mask, share, width):
-    rows = frame.shape[0]
+def pixel_weights(block_of, plan, units, meta, starts, frame, spread, mask, share, width, after=()):
+    rows = spread.shape[0]
     bins_row, bins_col = mask.shape
-    kept = sum(out >= units for out, fresh in plan)
+    kept = sum(part is not None and part[0] >= units for part in plan)
     lead = len(plan) - kept
     tile = pl.BlockSpec((rows, share), lambda i, meta, starts: (0, block_of(i, meta)))
-    bins = (1, 2, bins_row, bins_col)
+    out_specs = [whole((rows, share))] * units
+    out_shape = [pltpu.HBM((rows, share), F32)] * units
+    scratch = [pltpu.VMEM((SIDE, share), BF16)]
+    images = []
+    if frame is not None:
+        images = [frame]
+        bins = (1, 2, bins_row, bins_col)
+        out_specs += [
+            pl.BlockSpec((1, rows, share), lambda i, meta, starts: (jnp.maximum(i - lead, 0), 0, 0)), whole(bins)
+        ]
+        out_shape += [pltpu.HBM((kept, rows, share), F32), jax.ShapeDtypeStruct(bins, F32)]
+        scratch = [pltpu.VMEM((rows, bins_col), F32), pltpu.VMEM((share, SIDE), BF16)] + scratch
+    given = 2 + len(images) + 2
+    kernel = functools.partial(weights_kernel, block_of, plan, units, width)
     return pl.pallas_call(
-        functools.partial(weights_kernel, block_of, plan, units, width),
+        lambda *refs: kernel(*refs[:given], *refs[given + len(after) :]),
         grid_spec=pltpu.PrefetchScalarGridSpec(
             num_scalar_prefetch=2,
             grid=(len(plan),),
-            in_specs=[tile, tile, whole(mask.shape)],
-            out_specs=[whole((rows, share))] * units
-            + [pl.BlockSpec((1, rows, share), lambda i, meta, starts: (jnp.maximum(i - lead, 0), 0, 0)), whole(bins)],
-            scratch_shapes=[
-                pltpu.VMEM((rows, bins_col), F32), pltpu.VMEM((SIDE, share), BF16), pltpu.VMEM((share, SIDE), BF16)
-            ],
+            in_specs=[tile] * len(images) + [tile, whole(mask.shape)] + [ANY] * len(after),
+            out_specs=out_specs,
+            scratch_shapes=scratch,
         ),
-        out_shape=[pltpu.HBM((rows, share), F32)] * units
-        + [pltpu.HBM((kept, rows, share), F32), jax.ShapeDtypeStruct(bins, F32)],
+        out_shape=out_shape,
         compiler_params=pltpu.CompilerParams(vmem_limit_bytes=VMEM),
         cost_estimate=SMALL,
         name="pixel_weights",
-    )(meta, starts, frame, spread, mask)
+    )(meta, starts, *images, spread, mask, *after)
 
 
 def smooth_kernel(block_of, plan, width, stacked, meta_ref, start_ref, *refs):
@@ -293,7 +325,8 @@
     _, unit = layout.position_of(wanted(place), place)
     mate_start = start_ref[meta_ref[0] + 1 - 2 * (meta_ref[0] % 2)]
     in_mate = inside(columns(block, layout.share), mate_start, width)
-    *refs, out_ref = refs
+    *refs, out_ref, token_ref = refs
+    token_ref[...] = jnp.zeros_like(token_ref)
 
     def pair():
         own = refs.pop(0)[0]
@@ -326,7 +359,7 @@
 def block_term(layout, width, wanted, senders, meta, starts, parts, received, numerator=None, tables=(), after=()):
     kept = parts[0][0]
     rows, share = kept.shape[1:]
-    chunk = min(SIDE, rows)
+    chunk = min(TILE, rows)
 
     def at_unit(place):
         return layout.position_of(wanted(place), place)
@@ -360,14 +393,12 @@
     lead = 2 + len(args)
     body = functools.partial(term_kernel, layout, width, wanted, units, len(received[0]), numerator)
     return pl.pallas_call(
-        lambda *refs: body(*refs[:lead], refs[-1]),
+        lambda *refs: body(*refs[:lead], *refs[-2:]),
         grid_spec=pltpu.PrefetchScalarGridSpec(
-            num_scalar_prefetch=2, grid=(rows // chunk,), in_specs=specs + [ANY] * len(after), out_specs=flat
+            num_scalar_prefetch=2, grid=(rows // chunk,), in_specs=specs + [ANY] * len(after), out_specs=[flat, whole(TOKEN)]
         ),
-        out_shape=jax.ShapeDtypeStruct((rows, share), F32)
-        if numerator == "quotient"
-        else pltpu.HBM((rows, share), F32),
-        compiler_params=pltpu.CompilerParams(vmem_limit_bytes=VMEM),
+        out_shape=[jax.ShapeDtypeStruct((rows, share), F32), jax.ShapeDtypeStruct(TOKEN, F32)],
+        compiler_params=pltpu.CompilerParams(vmem_limit_bytes=SOME),
         cost_estimate=SMALL,
         name="block_term",
     )(meta, starts, *args, *after)
@@ -387,6 +418,20 @@
         cost_estimate=SMALL,
         name="held",
     )(*values, *after)
+
+
+def arrived(values):
+    def body(*refs):
+        refs[-1][...] = jnp.zeros_like(refs[-1])
+
+    return pl.pallas_call(
+        body,
+        in_specs=[ANY] * len(values),
+        out_shape=jax.ShapeDtypeStruct(TOKEN, F32),
+        compiler_params=pltpu.CompilerParams(vmem_limit_bytes=SOME),
+        cost_estimate=pl.CostEstimate(flops=1000, bytes_accessed=8 * 10**6, transcendentals=0),
+        name="arrived",
+    )(*values)
 
 
 def contract_last(left, right):
@@ -544,8 +589,9 @@
     share, places, quarter = layout.share, layout.places, layout.quarter
     ends, middle_count = layout.ends, layout.middle
     units = quarter + middle_count
-    sent = [(i // 2, i % 2 == 0) for i in range(ends)] + [(quarter + i, True) for i in range(middle_count)]
-    kept = [(units + i, True) for i in range(places)]
+    folded = [(i // 2, i % 2 == 0) for i in range(ends)]
+    sent = folded + [(quarter + i, True) for i in range(middle_count)]
+    rest = [None] * ends + [(i, True) for i in range(middle_count + places)]
 
     def sent_then_kept(i, meta):
         return jnp.where(i < places, layout.sent_block(i, meta), layout.kept_block(i - places, meta))
@@ -555,30 +601,30 @@
     def swapped(parts):
         return [lax.ppermute(part, "exp", swap) for part in parts]
 
-    *den_sent, den_kept, gathered = pixel_weights(
-        sent_then_kept, sent + kept, units, meta, foot_start, frame, spread, blocks, share, width
+    den_ends = pixel_weights(
+        layout.sent_block, folded, quarter, meta, foot_start, None, spread, blocks, share, width
     )
+    *den_middle, den_kept, gathered = pixel_weights(
+        sent_then_kept, rest, middle_count, meta, foot_start, frame, spread, blocks, share, width, after=den_ends
+    )
+    got_ends = swapped(den_ends)
 
     held = [0]
-    bit = 1
-    while bit < exposures:
+    bits = [1 << k for k in range(exposures.bit_length() - 1)]
+    for bit in bits[1:] + bits[:1]:
+        if bit == 1:
+            (gathered,) = held_until([gathered], got_ends)
         other = lax.ppermute(gathered, "exp", [(i, i ^ bit) for i in range(exposures)])
         low = (member & bit) == 0
         held = held + [e | bit for e in held]
         gathered = jnp.concatenate([jnp.where(low, gathered, other), jnp.where(low, other, gathered)])
-        bit *= 2
-
     up = [(i, i + 1) for i in range(sky_count - 1)]
     down = [(j, i) for i, j in up]
     above = lax.ppermute(frame[rows - HALO :], "sky", up)
     below = lax.ppermute(frame[:HALO], "sky", down)
-    den_got = swapped(den_sent)
     smooth = functools.partial(
         smoothed_terms, meta=meta, starts=foot_start, frame=frame, above=above, below=below, share=share, width=width
     )
-    num_sent = smooth(layout.sent_block, sent, den_sent)
-    num_got = swapped(num_sent)
-
     def to_right(step):
         return lambda z: choose(z < step, z + places - step, places - 1)
 
@@ -593,46 +639,49 @@
         pairs += [(2 * z + s, 2 * z - 2 + s) for z in lefts for s in range(2)]
         return lax.ppermute(value, "exp", pairs)
 
-    def along_places(step, term, sums, after):
+    def along_places(step, term, sums, after, after_left=()):
         rights, lefts = range(step), range(places - step, places)
         if step <= places // 2:
-            value = term(outward(step), [*rights, *lefts], sums, after)
+            value, token = term(outward(step), [*rights, *lefts], sums, after)
             if step < places // 2:
-                return (shift(value, rights, lefts),), (value,)
-            return (shift(value, rights, []), shift(value, [], lefts)), (value,)
-        right = term(to_right(step), rights, sums[:1], after)
-        left = term(to_left(step), lefts, sums[1:], after)
-        return (shift(right, rights, []), shift(left, [], lefts)), (right, left)
+                return (shift(value, rights, lefts),), (token,)
+            return (shift(value, rights, []), shift(value, [], lefts)), (token,)
+        right, token = term(to_right(step), rights, sums[:1], (*after, sums[1]))
+        left, token_left = term(to_left(step), lefts, sums[1:], after_left or after)
+        return (shift(right, rights, []), shift(left, [], lefts)), (token, token_left)
 
     def den_term(wanted, senders, sums, after):
-        parts = [(den_kept, den_got)]
+        parts = [(den_kept, got_ends + got_middle)]
         return block_term(layout, width, wanted, senders, meta, foot_start, parts, [sums], after=after)
 
+    got_middle = []
     den_sums, den_values = along_places(1, den_term, (), ())
-    (num_kept,) = smooth(layout.kept_block, kept, [den_kept], after=num_sent)
-
-    (gathered,) = held_until([gathered], [*num_sent, *den_values])
+    den_middle = held_until(den_middle, den_values)
+    got_middle = swapped(den_middle)
+    den_got = got_ends + got_middle
+    num_sent = smooth(layout.sent_block, sent, [*den_ends, *den_middle], after=[gathered])
+    num_got = swapped(num_sent)
+    (num_kept,) = smooth(layout.kept_block, [(i, True) for i in range(places)], [den_kept], after=num_sent)
+
     scalars = pl.BlockSpec(memory_space=pltpu.SMEM)
     vmem = pl.BlockSpec(memory_space=pltpu.VMEM)
     moments = pl.pallas_call(
         functools.partial(moments_kernel, held, sky_count),
         in_specs=[scalars, vmem],
         out_shape=jax.ShapeDtypeStruct((16, 5 * SIDE), F32),
-        compiler_params=pltpu.CompilerParams(vmem_limit_bytes=VMEM),
+        compiler_params=pltpu.CompilerParams(vmem_limit_bytes=SOME),
         cost_estimate=SMALL,
         name="pair_moments",
     )(meta, gathered)
     bit = 1
     while bit < sky_count:
         moments = moments + lax.ppermute(moments, "sky", [(i, i ^ bit) for i in range(sky_count)])
-        if bit == 1:
-            (moments,) = held_until([moments], [num_kept])
         bit *= 2
     offsets, back = pl.pallas_call(
         functools.partial(solve_kernel, width),
         in_specs=[scalars, scalars, vmem, vmem],
         out_shape=[jax.ShapeDtypeStruct((exposures, 9), F32), jax.ShapeDtypeStruct((8, cols), F32)],
-        compiler_params=pltpu.CompilerParams(vmem_limit_bytes=VMEM),
+        compiler_params=pltpu.CompilerParams(vmem_limit_bytes=SOME),
         cost_estimate=SMALL,
         name="offsets",
     )(meta, foot_start, moments, pair_owner)
@@ -645,11 +694,13 @@
             layout, width, wanted, senders, meta, foot_start, parts, [sums], "terms", tables, after
         )
 
+    den_sums, den_values = along_places(2, den_term, den_sums, ())
     num_sums, num_values = along_places(1, num_term, (), den_values)
-    for step in range(2, places):
+    num_sums, num_values = along_places(2, num_term, num_sums, [arrived(den_sums)])
+    for step in range(3, places):
         den_sums, den_values = along_places(step, den_term, den_sums, num_values)
-        num_sums, num_values = along_places(step, num_term, num_sums, den_values)
-    coadd = block_term(
+        num_sums, num_values = along_places(step, num_term, num_sums, den_values, [arrived(den_sums)])
+    coadd, _ = block_term(
         layout,
         width,
         lambda z: z,

time: 230 us -> 246 us (1.070)
  waiting for transfers between devices: 78.3 us -> 104 us
  Pallas kernels: 93.6 us -> 74 us
  starting transfers between devices: 41.9 us -> 50.7 us
    ppermute x10, waiting for transfers between devices: 27.7 us -> 94.7 us  [shift(): return lax.ppermute(value, 'exp', pairs)]
    ppermute x6, waiting for transfers between devices: 37.7 us -> 0.02 us  [swapped(): return [lax.ppermute(part, 'exp', swap) for part in parts]]
    pallas_call x10 -> x13, Pallas kernels: 62.9 us -> 44.9 us  [the longest x9 26.3 us: block_term(): pl.pallas_call(lambda *refs: body(*refs[:lead], *refs[-2:]), grid_spec=pl...]
    ppermute x10, starting transfers between devices: 25 us -> 30.7 us  [shift(): return lax.ppermute(value, 'exp', pairs)]
    ppermute x3, waiting for transfers between devices: 12.4 us -> 8.22 us  [per_device(): lax.ppermute(gathered, 'exp', [(i, i ^ bit) for i in range(exposures)])]
    ppermute x2, starting transfers between devices: 1.94 us -> 4.9 us  [per_device(): lax.ppermute(moments, 'sky', [(i, i ^ bit) for i in range(sky_count)])]
    ppermute x6, starting transfers between devices: 5 us -> 7.77 us  [swapped(): return [lax.ppermute(part, 'exp', swap) for part in parts]]
    ppermute x3, starting transfers between devices: 7.23 us -> 4.73 us  [per_device(): lax.ppermute(gathered, 'exp', [(i, i ^ bit) for i in range(exposures)])]
  transfers between devices with their start and end apart: 23 -> 23, of which waited for: 11 -> 10; matrix products, arithmetic and copies ran while one was open for 2% -> 2% of each run, Pallas kernels for 31% -> 25%
where the time goes in v4:
time: 246 us; the launch traced here: 244 us
  waiting for transfers between devices  104 us (42%)
  Pallas kernels  74 us (30%)
  starting transfers between devices  50.7 us (21%)
  local copies, waits for them, and re-layouts  10.8 us (4%)
  other arithmetic  4.17 us (2%)
    ppermute x10, waiting for transfers between devices, shift(): return lax.ppermute(value, 'exp', pairs)  94.7 us
    ppermute x10, starting transfers between devices, shift(): return lax.ppermute(value, 'exp', pairs)  30.7 us
    pallas_call x9, Pallas kernels, block_term(): pl.pallas_call(lambda *refs: body(*refs[:lead], *refs[-2:]), grid_spec=pl...  26.3 us
    pallas_call x2, Pallas kernels, smoothed_terms(): pl.pallas_call(body, grid_spec=pltpu.PrefetchScalarGridSpec(num_scalar_pr...  24.6 us
    pallas_call x2, Pallas kernels, pixel_weights(): pl.pallas_call(lambda *refs: kernel(*refs[:given], *refs[given + len(afte...  18.7 us
    unnamed x36, local copies, waits for them, and re-layouts  8.91 us
    ppermute x3, waiting for transfers between devices, per_device(): lax.ppermute(gathered, 'exp', [(i, i ^ bit) for i in range(exposures)])  8.22 us
    ppermute x6, starting transfers between devices, swapped(): return [lax.ppermute(part, 'exp', swap) for part in parts]  7.77 us
  transfers between devices with their start and end apart: 23, of which 10 were waited for; matrix products, arithmetic and copies ran while one was open for 2% of the time, Pallas kernels for 25%

profile of v4, /device:TPU:0, one launch (start us, length us, event | category | flops | bytes accessed | tf_op | source)
XLA Modules:
  0.0 244.5 jit_solution(7111687703493348389)
XLA Ops:
  1.3 3.8 %pixel_weights.2.refs_5_.refs_15_ = f32[512,512]{1,0:T(8,128)} custom-call(s32[2]{0:T(128)} %pad_add_fusion.refs_0_.meta_ref, s32[8]{0:T(128)} %refs_1_.25, f32[512,4096]{1,0:T(8,128)} %bitcast.16, s32[32,256]{1,0:T(8,128)} %bitcast.18), custom_call_target="tpu_custom_call" | custom-call | flops 1000 | bytes 1000 | tf_op jit(solution)/shard_map/pixel_weights/pallas_call | solution.py:203
  5.0 2.9 %collective-permute-start = (f32[512,512]{1,0:T(8,128)}, f32[512,512]{1,0:T(8,128)}, u32[]{:S(2)}, u32[]{:S(2)}) collective-permute-start(f32[512,512]{1,0:T(8,128)} %pixel_weights.2.refs_5_.refs_15_), channel_id=1, source_target_pairs={{0,4},{4,0},{8,12},{12,8},{16,20},{20,16},{24,28},{28,24},{1,5},{5... | collective-permute-start | bytes 3145736 | tf_op jit(solution)/shard_map/ppermute | solution.py:602
  8.0 14.9 %pixel_weights.3 = (f32[512,512]{1,0:T(8,128)}, f32[512,512]{1,0:T(8,128)}, f32[4,512,512]{2,1,0:T(8,128)}, f32[1,2,32,256]{3,2,1,0:T(8,128)}) custom-call(s32[2]{0:T(128)} %pad_add_fusion.refs_0_.meta_ref, s32[8]{0:T(128)} %refs_1_.25, f32[512,4096]{1,0:T(8,128)} %bitcast.9, f32[512,4096]{1,0:T(8,128)} %bitcast.17, s32[32,256]{1,0:T(8,128)} %bitcast.19, ...), custom_call_target="tpu_custom_call" | custom-call | flops 1000 | bytes 1000 | tf_op jit(solution)/shard_map/pixel_weights/pallas_call | solution.py:203
  24.5 2.9 %collective-permute-done.4 = f32[1,2,32,256]{3,2,1,0:T(8,128)S(1)} collective-permute-done((f32[1,2,32,256]{3,2,1,0:T(8,128)}, f32[1,2,32,256]{3,2,1,0:T(8,128)S(1)}, u32[]{:S(2)}, u32[]{:S(2)}) %collective-permute-start.4) | collective-permute-done | bytes 65568 | tf_op jit(solution)/shard_map/ppermute | solution.py:617
  30.9 5.3 %collective-permute-done.5 = f32[2,2,32,256]{3,2,1,0:T(8,128)S(1)} collective-permute-done((f32[2,2,32,256]{3,2,1,0:T(8,128)S(1)}, f32[2,2,32,256]{3,2,1,0:T(8,128)S(1)}, u32[]{:S(2)}, u32[]{:S(2)}) %collective-permute-start.5) | collective-permute-done | bytes 131104 | tf_op jit(solution)/shard_map/ppermute | solution.py:617
  49.1 3.5 %collective-permute-start.13 = (f32[512,512]{1,0:T(8,128)}, f32[512,512]{1,0:T(8,128)}, u32[]{:S(2)}, u32[]{:S(2)}) collective-permute-start(f32[512,512]{1,0:T(8,128)} %copy-done.14), channel_id=1, source_target_pairs={{0,8},{4,12},{24,16},{28,20},{1,9},{5,13},{25,17},{29,21},{2,10},{... | collective-permute-start | bytes 3145736 | tf_op jit(solution)/shard_map/ppermute | solution.py:640
  55.2 13.0 %smoothed_terms.2 = (f32[512,512]{1,0:T(8,128)}, f32[512,512]{1,0:T(8,128)}, f32[512,512]{1,0:T(8,128)}) custom-call(s32[2]{0:T(128)} %pad_add_fusion.refs_0_.meta_ref, s32[8]{0:T(128)} %refs_1_.25, f32[16,4096]{1,0:T(8,128)} %copy-done.15, f32[16,4096]{1,0:T(8,128)} %copy-done.15, f32[16,4096]{1,0:T(8,128)} %copy-done.15, f32[512,4096]{1,0:T(8,128)} %bitcast.10, ...), custom_call_target="tpu_custom_call" | custom-call | flops 1000 | bytes 1000 | tf_op jit(solution)/shard_map/smoothed_terms/pallas_call | solution.py:306
  75.4 2.8 %collective-permute-start.10 = (f32[16,640]{1,0:T(8,128)S(1)}, f32[16,640]{1,0:T(8,128)S(1)}, u32[]{:S(2)}, u32[]{:S(2)}) collective-permute-start(f32[16,640]{1,0:T(8,128)S(1)} %add.6), channel_id=1, source_target_pairs={{0,2},{1,3},{2,0},{3,1},{4,6},{5,7},{6,4},{7,5},{8,10},{9,11},{10,... | collective-permute-start | bytes 122888 | tf_op jit(solution)/shard_map/ppermute | solution.py:678
  79.7 11.5 %smoothed_terms.3.refs_4_.refs_5_.refs_6_ = f32[4,512,512]{2,1,0:T(8,128)} custom-call(s32[2]{0:T(128)} %pad_add_fusion.refs_0_.meta_ref, s32[8]{0:T(128)} %refs_1_.25, f32[16,4096]{1,0:T(8,128)} %copy-done.15, f32[16,4096]{1,0:T(8,128)} %copy-done.15, f32[16,4096]{1,0:T(8,128)} %copy-done.15, f32[512,4096]{1,0:T(8,128)} %bitcast.13, f32[512,4096]{1,0:T(8,128)} %bitcast.14, ...), custom_call_target="tpu_custom_call" | custom-call | flops 1000 | bytes 1000 | tf_op jit(solution)/shard_map/smoothed_terms/pallas_call | solution.py:306
  101.8 3.1 %block_term.11 = (f32[512,512]{1,0:T(8,128)S(1)}, f32[8,128]{1,0:T(8,128)}) custom-call(s32[2]{0:T(128)S(1)} %copy-done.9, s32[8]{0:T(128)S(1)} %copy-done.11, f32[4,512,512]{2,1,0:T(8,128)S(1)} %copy-done.1, f32[512,512]{1,0:T(8,128)} %collective-permute-done.refs_3_.refs_1_, f32[4,512,512]{2,1,0:T(8,128)S(1)} %copy-done.3, ...), custom_call_target="tpu_custom_call" | custom-call | flops 1000 | bytes 1000 | tf_op jit(solution)/shard_map/block_term/pallas_call | solution.py:395
  107.8 15.5 %collective-permute-done.15.refs_0_.refs_6_ = f32[512,512]{1,0:T(8,128)S(1)} collective-permute-done((f32[512,512]{1,0:T(8,128)S(1)}, f32[512,512]{1,0:T(8,128)S(1)}, u32[]{:S(2)}, u32[]{:S(2)}) %collective-permute-start.15) | collective-permute-done | bytes 1048608 | tf_op jit(solution)/shard_map/ppermute | solution.py:640
  123.3 21.4 %collective-permute-done.14.refs_10_ = f32[512,512]{1,0:T(8,128)S(1)} collective-permute-done((f32[512,512]{1,0:T(8,128)S(1)}, f32[512,512]{1,0:T(8,128)S(1)}, u32[]{:S(2)}, u32[]{:S(2)}) %collective-permute-start.14) | collective-permute-done | bytes 1048608 | tf_op jit(solution)/shard_map/ppermute | solution.py:640
  144.7 3.1 %block_term.12 = (f32[512,512]{1,0:T(8,128)S(1)}, f32[8,128]{1,0:T(8,128)S(1)}) custom-call(s32[2]{0:T(128)S(1)} %copy-done.9, s32[8]{0:T(128)S(1)} %copy-done.11, f32[4,512,512]{2,1,0:T(8,128)S(1)} %copy-done.2, f32[512,512]{1,0:T(8,128)} %collective-permute-done.refs_3_.refs_1_, f32[512,512]{1,0:T(8,128)} %collective-permute-done.11.refs_4_, ...), custom_call_target="tpu_custom_call" | custom-call | flops 1000 | bytes 1000 | tf_op jit(solution)/shard_map/block_term/pallas_call | solution.py:395
  150.0 4.5 %collective-permute-start.20 = (f32[512,512]{1,0:T(8,128)S(1)}, f32[512,512]{1,0:T(8,128)S(1)}, u32[]{:S(2)}, u32[]{:S(2)}) collective-permute-start(f32[512,512]{1,0:T(8,128)S(1)} %get-tuple-element.47), channel_id=1, source_target_pairs={{0,8},{4,12},{8,16},{12,20},{16,24},{20,28},{1,9},{5,13},{9,17},{1... | collective-permute-start | bytes 3145736 | tf_op jit(solution)/shard_map/ppermute | solution.py:640
  158.4 4.6 %collective-permute-start.17 = (f32[512,512]{1,0:T(8,128)S(1)}, f32[512,512]{1,0:T(8,128)S(1)}, u32[]{:S(2)}, u32[]{:S(2)}) collective-permute-start(f32[512,512]{1,0:T(8,128)S(1)} %get-tuple-element.42), channel_id=1, source_target_pairs={{0,8},{4,12},{8,16},{12,20},{1,9},{5,13},{9,17},{13,21},{2,10},{6,... | collective-permute-start | bytes 3145736 | tf_op jit(solution)/shard_map/ppermute | solution.py:640
  163.8 14.2 %collective-permute-done.20.refs_0_.refs_12_ = f32[512,512]{1,0:T(8,128)S(1)} collective-permute-done((f32[512,512]{1,0:T(8,128)S(1)}, f32[512,512]{1,0:T(8,128)S(1)}, u32[]{:S(2)}, u32[]{:S(2)}) %collective-permute-start.20) | collective-permute-done | bytes 1048608 | tf_op jit(solution)/shard_map/ppermute | solution.py:640
  178.0 4.5 %collective-permute-done.21.refs_1_.refs_13_ = f32[512,512]{1,0:T(8,128)S(1)} collective-permute-done((f32[512,512]{1,0:T(8,128)S(1)}, f32[512,512]{1,0:T(8,128)S(1)}, u32[]{:S(2)}, u32[]{:S(2)}) %collective-permute-start.21) | collective-permute-done | bytes 1048608 | tf_op jit(solution)/shard_map/ppermute | solution.py:640
  182.5 15.9 %collective-permute-done.17.refs_12_ = f32[512,512]{1,0:T(8,128)S(1)} collective-permute-done((f32[512,512]{1,0:T(8,128)S(1)}, f32[512,512]{1,0:T(8,128)S(1)}, u32[]{:S(2)}, u32[]{:S(2)}) %collective-permute-start.17) | collective-permute-done | bytes 1048608 | tf_op jit(solution)/shard_map/ppermute | solution.py:640
  198.4 3.8 %block_term.15 = (f32[512,512]{1,0:T(8,128)S(1)}, f32[8,128]{1,0:T(8,128)}) custom-call(s32[2]{0:T(128)S(1)} %copy-done.9, s32[8]{0:T(128)S(1)} %copy-done.11, f32[4,512,512]{2,1,0:T(8,128)S(1)} %copy-done.2, f32[512,512]{1,0:T(8,128)} %collective-permute-done.refs_3_.refs_1_, f32[512,512]{1,0:T(8,128)} %collective-permute-done.11.refs_4_, ...), custom_call_target="tpu_custom_call" | custom-call | flops 1000 | bytes 1000 | tf_op jit(solution)/shard_map/block_term/pallas_call | solution.py:395
  202.2 10.2 %collective-permute-start.19 = (f32[512,512]{1,0:T(8,128)S(1)}, f32[512,512]{1,0:T(8,128)S(1)}, u32[]{:S(2)}, u32[]{:S(2)}) collective-permute-start(f32[512,512]{1,0:T(8,128)S(1)} %get-tuple-element.46), channel_id=1, source_target_pairs={{0,8},{4,12},{8,16},{12,20},{16,24},{20,28},{1,9},{5,13},{9,17},{1... | collective-permute-start | bytes 3145736 | tf_op jit(solution)/shard_map/ppermute | solution.py:640
  212.4 3.8 %block_term.16 = (f32[512,512]{1,0:T(8,128)S(1)}, f32[8,128]{1,0:T(8,128)}) custom-call(s32[2]{0:T(128)S(1)} %copy-done.9, s32[8]{0:T(128)S(1)} %copy-done.11, f32[4,512,512]{2,1,0:T(8,128)S(1)} %copy-done.2, f32[512,512]{1,0:T(8,128)} %collective-permute-done.refs_3_.refs_1_, f32[512,512]{1,0:T(8,128)} %collective-permute-done.11.refs_4_, ...), custom_call_target="tpu_custom_call" | custom-call | flops 1000 | bytes 1000 | tf_op jit(solution)/shard_map/block_term/pallas_call | solution.py:395
  217.5 15.3 %collective-permute-done.19.refs_10_ = f32[512,512]{1,0:T(8,128)S(1)} collective-permute-done((f32[512,512]{1,0:T(8,128)S(1)}, f32[512,512]{1,0:T(8,128)S(1)}, u32[]{:S(2)}, u32[]{:S(2)}) %collective-permute-start.19) | collective-permute-done | bytes 1048608 | tf_op jit(solution)/shard_map/ppermute | solution.py:640
  232.7 7.9 %collective-permute-done.22.refs_11_ = f32[512,512]{1,0:T(8,128)S(1)} collective-permute-done((f32[512,512]{1,0:T(8,128)S(1)}, f32[512,512]{1,0:T(8,128)S(1)}, u32[]{:S(2)}, u32[]{:S(2)}) %collective-permute-start.22) | collective-permute-done | bytes 1048608 | tf_op jit(solution)/shard_map/ppermute | solution.py:640
  240.7 3.8 %block_term.17 = (f32[512,512]{1,0:T(8,128)}, f32[8,128]{1,0:T(8,128)}) custom-call(s32[2]{0:T(128)S(1)} %copy-done.9, s32[8]{0:T(128)S(1)} %copy-done.11, f32[4,512,512]{2,1,0:T(8,128)S(1)} %copy-done.2, f32[512,512]{1,0:T(8,128)} %collective-permute-done.refs_3_.refs_1_, f32[512,512]{1,0:T(8,128)S(1)} %collective-permute-done.1.refs_5_.refs_4_, ...), custom_call_target="tpu_custom_call" | custom-call | flops 1000 | bytes 1000 | tf_op jit(solution)/shard_map/block_term/pallas_call | solution.py:395
  (87 shorter events, 51.2 us)
Async XLA Ops:
  5.0 32.0 %collective-permute-start = (f32[512,512]{1,0:T(8,128)}, f32[512,512]{1,0:T(8,128)}, u32[]{:S(2)}, u32[]{:S(2)}) collective-permute-start(f32[512,512]{1,0:T(8,128)} %pixel_weights.2.refs_5_.refs_15_), channel_id=1, source_target_pairs={{0,4},{4,0},{8,12},{12,8},{16,20},{20,16},{24,28},{28,24},{1,5},{5... | collective-permute-start | bytes 3145736 | tf_op jit(solution)/shard_map/ppermute | solution.py:602
  22.9 4.5 %collective-permute-start.4 = (f32[1,2,32,256]{3,2,1,0:T(8,128)}, f32[1,2,32,256]{3,2,1,0:T(8,128)S(1)}, u32[]{:S(2)}, u32[]{:S(2)}) collective-permute-start(f32[1,2,32,256]{3,2,1,0:T(8,128)} %get-tuple-element.33), channel_id=1, source_target_pairs={{0,8},{4,12},{8,0},{12,4},{16,24},{20,28},{24,16},{28,20},{1,9},{5... | collective-permute-start | bytes 196616 | tf_op jit(solution)/shard_map/ppermute | solution.py:617
  28.2 8.0 %collective-permute-start.5 = (f32[2,2,32,256]{3,2,1,0:T(8,128)S(1)}, f32[2,2,32,256]{3,2,1,0:T(8,128)S(1)}, u32[]{:S(2)}, u32[]{:S(2)}) collective-permute-start(f32[2,2,32,256]{3,2,1,0:T(8,128)S(1)} %pad_maximum_fusion.2), channel_id=1, source_target_pairs={{0,16},{4,20},{8,24},{12,28},{16,0},{20,4},{24,8},{28,12},{1,17},{... | collective-permute-start | bytes 393224 | tf_op jit(solution)/shard_map/ppermute | solution.py:617
  37.0 15.7 %collective-permute-start.6 = (f32[4,2,32,256]{3,2,1,0:T(8,128)}, f32[4,2,32,256]{3,2,1,0:T(8,128)}, u32[]{:S(2)}, u32[]{:S(2)}) collective-permute-start(f32[4,2,32,256]{3,2,1,0:T(8,128)} %held.3), channel_id=1, source_target_pairs={{0,4},{4,0},{8,12},{12,8},{16,20},{20,16},{24,28},{28,24},{1,5},{5... | collective-permute-start | bytes 786440 | tf_op jit(solution)/shard_map/ppermute | solution.py:617
  39.3 15.2 %collective-permute-start.2 = (f32[16,4096]{1,0:T(8,128)}, f32[16,4096]{1,0:T(8,128)S(1)}, u32[]{:S(2)}, u32[]{:S(2)}) collective-permute-start(f32[16,4096]{1,0:T(8,128)} %get-tuple-element.53), channel_id=1, source_target_pairs={{0,1},{1,2},{2,3},{4,5},{5,6},{6,7},{8,9},{9,10},{10,11},{12,13},{... | collective-permute-start | bytes 786440 | tf_op jit(solution)/shard_map/ppermute | solution.py:623
  40.6 13.9 %collective-permute-start.3 = (f32[16,4096]{1,0:T(8,128)}, f32[16,4096]{1,0:T(8,128)}, u32[]{:S(2)}, u32[]{:S(2)}) collective-permute-start(f32[16,4096]{1,0:T(8,128)} %get-tuple-element.52), channel_id=1, source_target_pairs={{1,0},{2,1},{3,2},{5,4},{6,5},{7,6},{9,8},{10,9},{11,10},{13,12},{... | collective-permute-start | bytes 786440 | tf_op jit(solution)/shard_map/ppermute | solution.py:624
  47.6 45.8 %collective-permute-start.11 = (f32[512,512]{1,0:T(8,128)}, f32[512,512]{1,0:T(8,128)}, u32[]{:S(2)}, u32[]{:S(2)}) collective-permute-start(f32[512,512]{1,0:T(8,128)} %get-tuple-element.32.refs_16_), channel_id=1, source_target_pairs={{0,4},{4,0},{8,12},{12,8},{16,20},{20,16},{24,28},{28,24},{1,5},{5... | collective-permute-start | bytes 3145736 | tf_op jit(solution)/shard_map/ppermute | solution.py:602
  49.1 44.2 %collective-permute-start.13 = (f32[512,512]{1,0:T(8,128)}, f32[512,512]{1,0:T(8,128)}, u32[]{:S(2)}, u32[]{:S(2)}) collective-permute-start(f32[512,512]{1,0:T(8,128)} %copy-done.14), channel_id=1, source_target_pairs={{0,8},{4,12},{24,16},{28,20},{1,9},{5,13},{25,17},{29,21},{2,10},{... | collective-permute-start | bytes 3145736 | tf_op jit(solution)/shard_map/ppermute | solution.py:640
  68.3 32.3 %collective-permute-start.7 = (f32[512,512]{1,0:T(8,128)}, f32[512,512]{1,0:T(8,128)}, u32[]{:S(2)}, u32[]{:S(2)}) collective-permute-start(f32[512,512]{1,0:T(8,128)} %get-tuple-element.34.refs_16_), channel_id=1, source_target_pairs={{0,4},{4,0},{8,12},{12,8},{16,20},{20,16},{24,28},{28,24},{1,5},{5... | collective-permute-start | bytes 3145736 | tf_op jit(solution)/shard_map/ppermute | solution.py:602
  72.5 3.0 %collective-permute-start.9 = (f32[16,640]{1,0:T(8,128)S(1)}, f32[16,640]{1,0:T(8,128)S(1)}, u32[]{:S(2)}, u32[]{:S(2)}) collective-permute-start(f32[16,640]{1,0:T(8,128)S(1)} %pair_moments.1), channel_id=1, source_target_pairs={{0,1},{1,0},{2,3},{3,2},{4,5},{5,4},{6,7},{7,6},{8,9},{9,8},{10,11... | collective-permute-start | bytes 122888 | tf_op jit(solution)/shard_map/ppermute | solution.py:678
  75.4 15.9 %collective-permute-start.10 = (f32[16,640]{1,0:T(8,128)S(1)}, f32[16,640]{1,0:T(8,128)S(1)}, u32[]{:S(2)}, u32[]{:S(2)}) collective-permute-start(f32[16,640]{1,0:T(8,128)S(1)} %add.6), channel_id=1, source_target_pairs={{0,2},{1,3},{2,0},{3,1},{4,6},{5,7},{6,4},{7,5},{8,10},{9,11},{10,... | collective-permute-start | bytes 122888 | tf_op jit(solution)/shard_map/ppermute | solution.py:678
  78.2 45.1 %collective-permute-start.12 = (f32[512,512]{1,0:T(8,128)}, f32[512,512]{1,0:T(8,128)}, u32[]{:S(2)}, u32[]{:S(2)}) collective-permute-start(f32[512,512]{1,0:T(8,128)} %get-tuple-element.35.refs_17_), channel_id=1, source_target_pairs={{0,4},{4,0},{8,12},{12,8},{16,20},{20,16},{24,28},{28,24},{1,5},{5... | collective-permute-start | bytes 3145736 | tf_op jit(solution)/shard_map/ppermute | solution.py:602
  95.5 49.2 %copy-start.5 = (f32[2048,3]{1,0:T(8,128)S(1)}, f32[2048,3]{1,0:T(8,128)}, u32[]{:S(2)}) copy-start(f32[2048,3]{1,0:T(8,128)} %constant.31.clone.refs_6_.refs_8_.refs_10_) | copy-start | bytes 73732
  98.2 25.1 %collective-permute-start.15 = (f32[512,512]{1,0:T(8,128)S(1)}, f32[512,512]{1,0:T(8,128)S(1)}, u32[]{:S(2)}, u32[]{:S(2)}) collective-permute-start(f32[512,512]{1,0:T(8,128)S(1)} %get-tuple-element.41), channel_id=1, source_target_pairs={{0,8},{4,12},{8,16},{12,20},{1,9},{5,13},{9,17},{13,21},{2,10},{6,... | collective-permute-start | bytes 3145736 | tf_op jit(solution)/shard_map/ppermute | solution.py:640
  99.8 23.5 %collective-permute-start.16 = (f32[512,512]{1,0:T(8,128)S(1)}, f32[512,512]{1,0:T(8,128)S(1)}, u32[]{:S(2)}, u32[]{:S(2)}) collective-permute-start(f32[512,512]{1,0:T(8,128)S(1)} %get-tuple-element.41), channel_id=1, source_target_pairs={{16,8},{20,12},{24,16},{28,20},{17,9},{21,13},{25,17},{29,21},{18,... | collective-permute-start | bytes 3145736 | tf_op jit(solution)/shard_map/ppermute | solution.py:640
  105.0 39.7 %collective-permute-start.14 = (f32[512,512]{1,0:T(8,128)S(1)}, f32[512,512]{1,0:T(8,128)S(1)}, u32[]{:S(2)}, u32[]{:S(2)}) collective-permute-start(f32[512,512]{1,0:T(8,128)S(1)} %get-tuple-element.40), channel_id=1, source_target_pairs={{0,8},{4,12},{24,16},{28,20},{1,9},{5,13},{25,17},{29,21},{2,10},{... | collective-permute-start | bytes 3145736 | tf_op jit(solution)/shard_map/ppermute | solution.py:640
  107.2 40.6 %collective-permute-start.1 = (f32[512,512]{1,0:T(8,128)S(1)}, f32[512,512]{1,0:T(8,128)S(1)}, u32[]{:S(2)}, u32[]{:S(2)}) collective-permute-start(f32[512,512]{1,0:T(8,128)S(1)} %copy-done.16), channel_id=1, source_target_pairs={{0,4},{4,0},{8,12},{12,8},{16,20},{20,16},{24,28},{28,24},{1,5},{5... | collective-permute-start | bytes 3145736 | tf_op jit(solution)/shard_map/ppermute | solution.py:602
  150.0 28.0 %collective-permute-start.20 = (f32[512,512]{1,0:T(8,128)S(1)}, f32[512,512]{1,0:T(8,128)S(1)}, u32[]{:S(2)}, u32[]{:S(2)}) collective-permute-start(f32[512,512]{1,0:T(8,128)S(1)} %get-tuple-element.47), channel_id=1, source_target_pairs={{0,8},{4,12},{8,16},{12,20},{16,24},{20,28},{1,9},{5,13},{9,17},{1... | collective-permute-start | bytes 3145736 | tf_op jit(solution)/shard_map/ppermute | solution.py:640
  156.5 25.9 %collective-permute-start.21 = (f32[512,512]{1,0:T(8,128)S(1)}, f32[512,512]{1,0:T(8,128)S(1)}, u32[]{:S(2)}, u32[]{:S(2)}) collective-permute-start(f32[512,512]{1,0:T(8,128)S(1)} %get-tuple-element.48), channel_id=1, source_target_pairs={{8,0},{12,4},{16,8},{20,12},{24,16},{28,20},{9,1},{13,5},{17,9},{2... | collective-permute-start | bytes 3145736 | tf_op jit(solution)/shard_map/ppermute | solution.py:640
  157.8 24.6 %collective-permute-start.8 = (f32[512,512]{1,0:T(8,128)S(1)}, f32[512,512]{1,0:T(8,128)S(1)}, u32[]{:S(2)}, u32[]{:S(2)}) collective-permute-start(f32[512,512]{1,0:T(8,128)S(1)} %copy-done.17), channel_id=1, source_target_pairs={{0,4},{4,0},{8,12},{12,8},{16,20},{20,16},{24,28},{28,24},{1,5},{5... | collective-permute-start | bytes 3145736 | tf_op jit(solution)/shard_map/ppermute | solution.py:602
  158.4 40.0 %collective-permute-start.17 = (f32[512,512]{1,0:T(8,128)S(1)}, f32[512,512]{1,0:T(8,128)S(1)}, u32[]{:S(2)}, u32[]{:S(2)}) collective-permute-start(f32[512,512]{1,0:T(8,128)S(1)} %get-tuple-element.42), channel_id=1, source_target_pairs={{0,8},{4,12},{8,16},{12,20},{1,9},{5,13},{9,17},{13,21},{2,10},{6,... | collective-permute-start | bytes 3145736 | tf_op jit(solution)/shard_map/ppermute | solution.py:640
  163.0 35.4 %collective-permute-start.18 = (f32[512,512]{1,0:T(8,128)S(1)}, f32[512,512]{1,0:T(8,128)S(1)}, u32[]{:S(2)}, u32[]{:S(2)}) collective-permute-start(f32[512,512]{1,0:T(8,128)S(1)} %get-tuple-element.42), channel_id=1, source_target_pairs={{16,8},{20,12},{24,16},{28,20},{17,9},{21,13},{25,17},{29,21},{18,... | collective-permute-start | bytes 3145736 | tf_op jit(solution)/shard_map/ppermute | solution.py:640
  202.2 30.5 %collective-permute-start.19 = (f32[512,512]{1,0:T(8,128)S(1)}, f32[512,512]{1,0:T(8,128)S(1)}, u32[]{:S(2)}, u32[]{:S(2)}) collective-permute-start(f32[512,512]{1,0:T(8,128)S(1)} %get-tuple-element.46), channel_id=1, source_target_pairs={{0,8},{4,12},{8,16},{12,20},{16,24},{20,28},{1,9},{5,13},{9,17},{1... | collective-permute-start | bytes 3145736 | tf_op jit(solution)/shard_map/ppermute | solution.py:640
  216.2 24.5 %collective-permute-start.22 = (f32[512,512]{1,0:T(8,128)S(1)}, f32[512,512]{1,0:T(8,128)S(1)}, u32[]{:S(2)}, u32[]{:S(2)}) collective-permute-start(f32[512,512]{1,0:T(8,128)S(1)} %get-tuple-element.49), channel_id=1, source_target_pairs={{8,0},{12,4},{16,8},{20,12},{24,16},{28,20},{9,1},{13,5},{17,9},{2... | collective-permute-start | bytes 3145736 | tf_op jit(solution)/shard_map/ppermute | solution.py:640
  (17 other events, 198.4 us)

commit v5 on v4

--- a/solution.py
+++ b/solution.py
@@ -14,6 +14,7 @@
 SIDE = 128
 TOKEN = (8, 128)
 TILE = 256
+CHUNK = 64
 
 HIGH = lax.Precision.HIGHEST
 LAMBDA_REG = 0.25
@@ -100,12 +101,21 @@
     return lax.broadcasted_iota(jnp.int32, (1, width or share), 1) + (block * share - lead)
 
 
+def reciprocal(value):
+    rough = pl.reciprocal(value, approx=True)
+    rough = rough * (2.0 - value * rough)
+    return rough * (2.0 - value * rough)
+
+
 def weights_kernel(block_of, plan, units, width, meta_ref, start_ref, *refs):
-    binned = len(refs) > 4 + units
+    binned = len(refs) > 5 + units
     frame_ref, refs = (refs[0], refs[1:]) if binned else (None, refs)
     spread_ref, mask_ref, *refs = refs
-    weights, scratch = (refs[:-4], refs[-4:]) if binned else (refs[:-1], refs[-1:])
-    scatter = scratch[-1]
+    weights, scratch = (refs[:-10], refs[-10:]) if binned else (refs[:-2], refs[-2:])
+    *scratch, scatter, weight = scratch
+    if binned:
+        bins_ref, total, gather, *splits = scratch
+        image_parts, weight_parts = splits[:3], splits[3:]
     step = pl.program_id(0)
     block = block_of(step, meta_ref)
     start = start_ref[meta_ref[0]]
@@ -118,11 +128,22 @@
         cell = lax.broadcasted_iota(jnp.int32, (SIDE, share), 1) >> 4
         scatter[...] = (cell == lax.broadcasted_iota(jnp.int32, (SIDE, share), 0)).astype(BF16)
 
-    inverse = 1.0 / spread_ref[...]
     blocks_here = pltpu.roll(mask_ref[...].astype(F32), lax.rem(bins_col - block * per, bins_col), 1)[:, :SIDE]
     kept = mm(blocks_here.astype(BF16), scatter[...])
     kept = jnp.where(inside(columns(block, share), start, width), kept, 0.0)
-    weight = inverse * jnp.broadcast_to(kept[:, None, :], (bins_row, BIN, share)).reshape(rows, share)
+    for top in range(0, rows, CHUNK):
+        here = slice(top, top + CHUNK)
+        inverse = reciprocal(spread_ref[here])
+        bins_here = slice(top // BIN, (top + CHUNK) // BIN)
+        factor = jnp.broadcast_to(kept[bins_here][:, None, :], (CHUNK // BIN, BIN, share)).reshape(CHUNK, share)
+        weight[here] = inverse * factor
+        if binned:
+            for value, splits in ((frame_ref[here], image_parts), (inverse, weight_parts)):
+                value = value.reshape(CHUNK // BIN, 2, 8, share).sum(axis=1).reshape(CHUNK // 2, share)
+                for split in splits:
+                    rounded = value.astype(BF16)
+                    split[top // 2 : (top + CHUNK) // 2] = rounded
+                    value = value - rounded.astype(F32)
     for at, part in enumerate(plan):
         if part is None:
             continue
@@ -130,15 +151,14 @@
         @pl.when(step == at)
         def _(out=part[0], fresh=part[1]):
             if out >= units:
-                weights[-1][0] = weight
+                weights[-1][0] = weight[...]
             elif fresh:
-                weights[out][...] = weight
+                weights[out][...] = weight[...]
             else:
-                weights[out][...] += weight
+                weights[out][...] += weight[...]
 
     if not binned:
         return
-    bins_ref, total, gather, _ = scratch
 
     @pl.when(step == 0)
     def _():
@@ -146,23 +166,18 @@
         gather[...] = (cell == lax.broadcasted_iota(jnp.int32, (share, SIDE), 1)).astype(BF16)
         total[...] = jnp.zeros_like(total)
 
-    def halved(value):
-        return value.reshape(bins_row, 2, 8, share).sum(axis=1).reshape(bins_row * 8, share)
-
-    def gathered(value, parts):
+    def gathered(splits):
         result = None
-        for _ in range(parts):
-            rounded = value.astype(BF16)
-            value = value - rounded.astype(F32)
-            product = mm(rounded, gather[...])
+        for split in splits:
+            product = mm(split[...], gather[...])
             result = product if result is None else result + product
         if bins_col > SIDE:
             result = jnp.concatenate([result, jnp.zeros((result.shape[0], bins_col - SIDE), F32)], axis=1)
         return pltpu.roll(result, block * per, 1)
 
     half = bins_row * 8
-    total[:half] += gathered(halved(frame_ref[...]), 3)
-    total[half:] += gathered(halved(inverse), 2)
+    total[:half] += gathered(image_parts)
+    total[half:] += gathered(weight_parts)
 
     @pl.when(step == len(plan) - 1)
     def _():
@@ -188,7 +203,7 @@
     tile = pl.BlockSpec((rows, share), lambda i, meta, starts: (0, block_of(i, meta)))
     out_specs = [whole((rows, share))] * units
     out_shape = [pltpu.HBM((rows, share), F32)] * units
-    scratch = [pltpu.VMEM((SIDE, share), BF16)]
+    scratch = [pltpu.VMEM((SIDE, share), BF16), pltpu.VMEM((rows, share), F32)]
     images = []
     if frame is not None:
         images = [frame]
@@ -197,7 +212,8 @@
             pl.BlockSpec((1, rows, share), lambda i, meta, starts: (jnp.maximum(i - lead, 0), 0, 0)), whole(bins)
         ]
         out_shape += [pltpu.HBM((kept, rows, share), F32), jax.ShapeDtypeStruct(bins, F32)]
-        scratch = [pltpu.VMEM((rows, bins_col), F32), pltpu.VMEM((share, SIDE), BF16)] + scratch
+        splits = [pltpu.VMEM((rows // 2, share), BF16)] * 5
+        scratch = [pltpu.VMEM((rows, bins_col), F32), pltpu.VMEM((share, SIDE), BF16), *splits, *scratch]
     given = 2 + len(images) + 2
     kernel = functools.partial(weights_kernel, block_of, plan, units, width)
     return pl.pallas_call(
@@ -220,6 +236,8 @@
     step = pl.program_id(0)
     images, bands, scratch = refs[:9], refs[9:13], refs[-8:]
     refs = refs[13:-8]
+    *refs, token_ref = refs
+    token_ref[...] = jnp.zeros_like(token_ref)
     weights, outs = refs[: len(refs) // 2], refs[len(refs) // 2 :]
 
     @pl.when(step == 0)
@@ -309,10 +327,10 @@
             num_scalar_prefetch=2,
             grid=(len(plan),),
             in_specs=specs + [whole(p.shape) for p in parts] + [parts_spec] * count + [ANY] * len(after),
-            out_specs=[parts_spec] * count,
+            out_specs=[parts_spec] * count + [whole(TOKEN)],
             scratch_shapes=[pltpu.VMEM(p.shape, BF16) for p in parts for _ in range(2)],
         ),
-        out_shape=[pltpu.HBM(w.shape, F32) for w in weights],
+        out_shape=[pltpu.HBM(w.shape, F32) for w in weights] + [jax.ShapeDtypeStruct(TOKEN, F32)],
         compiler_params=pltpu.CompilerParams(vmem_limit_bytes=VMEM),
         cost_estimate=SMALL,
         name="smoothed_terms",
@@ -369,7 +387,7 @@
     specs, args = [], []
     for own, got in parts:
         specs.append(pl.BlockSpec((1, chunk, share), lambda r, m, s: (at_unit(m[0] // 2)[0], r, 0)))
-        args.append(own)
+        args.append(pltpu.with_memory_space_constraint(own, pltpu.HBM))
         for u in units:
             specs.append(
                 flat
@@ -608,16 +626,9 @@
         sent_then_kept, rest, middle_count, meta, foot_start, frame, spread, blocks, share, width, after=den_ends
     )
     got_ends = swapped(den_ends)
-
-    held = [0]
-    bits = [1 << k for k in range(exposures.bit_length() - 1)]
-    for bit in bits[1:] + bits[:1]:
-        if bit == 1:
-            (gathered,) = held_until([gathered], got_ends)
-        other = lax.ppermute(gathered, "exp", [(i, i ^ bit) for i in range(exposures)])
-        low = (member & bit) == 0
-        held = held + [e | bit for e in held]
-        gathered = jnp.concatenate([jnp.where(low, gathered, other), jnp.where(low, other, gathered)])
+    got_middle = swapped(den_middle)
+    den_got = got_ends + got_middle
+
     up = [(i, i + 1) for i in range(sky_count - 1)]
     down = [(j, i) for i, j in up]
     above = lax.ppermute(frame[rows - HALO :], "sky", up)
@@ -625,6 +636,21 @@
     smooth = functools.partial(
         smoothed_terms, meta=meta, starts=foot_start, frame=frame, above=above, below=below, share=share, width=width
     )
+
+    held = [0]
+    bits = [1 << k for k in range(exposures.bit_length() - 1)]
+
+    def gather_along(gathered, bit):
+        other = lax.ppermute(gathered, "exp", [(i, i ^ bit) for i in range(exposures)])
+        low = (member & bit) == 0
+        held.extend([e | bit for e in held])
+        return jnp.concatenate([jnp.where(low, gathered, other), jnp.where(low, other, gathered)])
+
+    gathered = gather_along(gathered, bits[1])
+    (gathered,) = held_until([gathered], [above, below])
+    for bit in bits[2:]:
+        gathered = gather_along(gathered, bit)
+
     def to_right(step):
         return lambda z: choose(z < step, z + places - step, places - 1)
 
@@ -651,18 +677,18 @@
         return (shift(right, rights, []), shift(left, [], lefts)), (token, token_left)
 
     def den_term(wanted, senders, sums, after):
-        parts = [(den_kept, got_ends + got_middle)]
+        parts = [(den_kept, den_got)]
         return block_term(layout, width, wanted, senders, meta, foot_start, parts, [sums], after=after)
 
-    got_middle = []
     den_sums, den_values = along_places(1, den_term, (), ())
-    den_middle = held_until(den_middle, den_values)
-    got_middle = swapped(den_middle)
-    den_got = got_ends + got_middle
-    num_sent = smooth(layout.sent_block, sent, [*den_ends, *den_middle], after=[gathered])
+    *num_sent, token = smooth(layout.sent_block, sent, [*den_ends, *den_middle], after=den_values)
     num_got = swapped(num_sent)
-    (num_kept,) = smooth(layout.kept_block, [(i, True) for i in range(places)], [den_kept], after=num_sent)
-
+    (gathered,) = held_until([gathered], [token])
+    gathered = gather_along(gathered, bits[0])
+    num_kept, token = smooth(layout.kept_block, [(i, True) for i in range(places)], [den_kept], after=[token])
+    den_sums, den_values = along_places(2, den_term, den_sums, [token])
+
+    (gathered,) = held_until([gathered], den_values)
     scalars = pl.BlockSpec(memory_space=pltpu.SMEM)
     vmem = pl.BlockSpec(memory_space=pltpu.VMEM)
     moments = pl.pallas_call(
@@ -694,12 +720,11 @@
             layout, width, wanted, senders, meta, foot_start, parts, [sums], "terms", tables, after
         )
 
-    den_sums, den_values = along_places(2, den_term, den_sums, ())
     num_sums, num_values = along_places(1, num_term, (), den_values)
-    num_sums, num_values = along_places(2, num_term, num_sums, [arrived(den_sums)])
     for step in range(3, places):
         den_sums, den_values = along_places(step, den_term, den_sums, num_values)
-        num_sums, num_values = along_places(step, num_term, num_sums, den_values, [arrived(den_sums)])
+        num_sums, num_values = along_places(step - 1, num_term, num_sums, den_values)
+    num_sums, num_values = along_places(places - 1, num_term, num_sums, num_values, [arrived(den_sums)])
     coadd, _ = block_term(
         layout,
         width,

time: 246 us -> 240 us (0.976)
  starting transfers between devices: 50.7 us -> 44.9 us
  Pallas kernels: 74 us -> 78.6 us
  local copies, waits for them, and re-layouts: 10.8 us -> 6.84 us
    ppermute x10, waiting for transfers between devices: 94.7 us -> 61.8 us  [shift(): return lax.ppermute(value, 'exp', pairs)]
    ppermute x6, waiting for transfers between devices: 0.02 us -> 20.4 us  [swapped(): return [lax.ppermute(part, 'exp', swap) for part in parts]]
    ppermute x3, waiting for transfers between devices: 8.22 us -> 17.7 us  [gather_along(): lax.ppermute(gathered, 'exp', [(i, i ^ bit) for i in range(exposures)])]
    ppermute x10, starting transfers between devices: 30.7 us -> 26.8 us  [shift(): return lax.ppermute(value, 'exp', pairs)]
    unnamed x36 -> x34, local copies, waits for them, and re-layouts: 8.91 us -> 5.78 us
    pallas_call x9, Pallas kernels: 26.3 us -> 29 us  [block_term(): pl.pallas_call(lambda *refs: body(*refs[:lead], *refs[-2:]), grid_spec=pl...]
  transfers between devices with their start and end apart: 23 -> 23, of which waited for: 10 -> 11; matrix products, arithmetic and copies ran while one was open for 2% -> 2% of each run, Pallas kernels for 25% -> 28%
where the time goes in v5:
time: 240 us; the launch traced here: 239 us
  waiting for transfers between devices  103 us (43%)
  Pallas kernels  78.6 us (33%)
  starting transfers between devices  44.9 us (19%)
  local copies, waits for them, and re-layouts  6.84 us (3%)
  other arithmetic  4.69 us (2%)
    ppermute x10, waiting for transfers between devices, shift(): return lax.ppermute(value, 'exp', pairs)  61.8 us
    pallas_call x9, Pallas kernels, block_term(): pl.pallas_call(lambda *refs: body(*refs[:lead], *refs[-2:]), grid_spec=pl...  29 us
    ppermute x10, starting transfers between devices, shift(): return lax.ppermute(value, 'exp', pairs)  26.8 us
    pallas_call x2, Pallas kernels, smoothed_terms(): pl.pallas_call(body, grid_spec=pltpu.PrefetchScalarGridSpec(num_scalar_pr...  24.6 us
    pallas_call x2, Pallas kernels, pixel_weights(): pl.pallas_call(lambda *refs: kernel(*refs[:given], *refs[given + len(afte...  20.4 us
    ppermute x6, waiting for transfers between devices, swapped(): return [lax.ppermute(part, 'exp', swap) for part in parts]  20.4 us
    ppermute x3, waiting for transfers between devices, gather_along(): lax.ppermute(gathered, 'exp', [(i, i ^ bit) for i in range(exposures)])  17.7 us
    ppermute x6, starting transfers between devices, swapped(): return [lax.ppermute(part, 'exp', swap) for part in parts]  7.59 us
  transfers between devices with their start and end apart: 23, of which 11 were waited for; matrix products, arithmetic and copies ran while one was open for 2% of the time, Pallas kernels for 28%

profile of v5, /device:TPU:0, one launch (start us, length us, event | category | flops | bytes accessed | tf_op | source)
XLA Modules:
  0.0 239.1 jit_solution(1551868195950272199)
XLA Ops:
  1.2 4.1 %pixel_weights.2.refs_5_.refs_15_ = f32[512,512]{1,0:T(8,128)} custom-call(s32[2]{0:T(128)} %pad_add_fusion.refs_0_.meta_ref, s32[8]{0:T(128)} %refs_1_.25, f32[512,4096]{1,0:T(8,128)} %bitcast.16, s32[32,256]{1,0:T(8,128)} %bitcast.18), custom_call_target="tpu_custom_call" | custom-call | flops 1000 | bytes 1000 | tf_op jit(solution)/shard_map/pixel_weights/pallas_call | solution.py:219
  5.3 2.9 %collective-permute-start = (f32[512,512]{1,0:T(8,128)}, f32[512,512]{1,0:T(8,128)}, u32[]{:S(2)}, u32[]{:S(2)}) collective-permute-start(f32[512,512]{1,0:T(8,128)} %pixel_weights.2.refs_5_.refs_15_), channel_id=1, source_target_pairs={{0,4},{4,0},{8,12},{12,8},{16,20},{20,16},{24,28},{28,24},{1,5},{5... | collective-permute-start | bytes 3145736 | tf_op jit(solution)/shard_map/ppermute | solution.py:620
  8.2 16.4 %pixel_weights.3 = (f32[512,512]{1,0:T(8,128)}, f32[512,512]{1,0:T(8,128)}, f32[4,512,512]{2,1,0:T(8,128)}, f32[1,2,32,256]{3,2,1,0:T(8,128)}) custom-call(s32[2]{0:T(128)} %pad_add_fusion.refs_0_.meta_ref, s32[8]{0:T(128)} %refs_1_.25, f32[512,4096]{1,0:T(8,128)} %bitcast.9, f32[512,4096]{1,0:T(8,128)} %bitcast.17, s32[32,256]{1,0:T(8,128)} %bitcast.19, ...), custom_call_target="tpu_custom_call" | custom-call | flops 1000 | bytes 1000 | tf_op jit(solution)/shard_map/pixel_weights/pallas_call | solution.py:219
  37.0 2.9 %block_term.9 = (f32[512,512]{1,0:T(8,128)}, f32[8,128]{1,0:T(8,128)S(1)}) custom-call(s32[2]{0:T(128)S(1)} %copy-done.3, s32[8]{0:T(128)S(1)} %copy-done.5, f32[4,512,512]{2,1,0:T(8,128)} %get-tuple-element.29.refs_2_.refs_15_, f32[512,512]{1,0:T(8,128)} %collective-permute-done.refs_3_), custom_call_target="tpu_custom_call" | custom-call | flops 1000 | bytes 1000 | tf_op jit(solution)/shard_map/block_term/pallas_call | solution.py:413
  40.6 3.3 %collective-permute-start.10 = (f32[512,512]{1,0:T(8,128)}, f32[512,512]{1,0:T(8,128)}, u32[]{:S(2)}, u32[]{:S(2)}) collective-permute-start(f32[512,512]{1,0:T(8,128)} %get-tuple-element.38), channel_id=1, source_target_pairs={{0,8},{4,12},{24,16},{28,20},{1,9},{5,13},{25,17},{29,21},{2,10},{... | collective-permute-start | bytes 3145736 | tf_op jit(solution)/shard_map/ppermute | solution.py:666
  43.9 13.0 %smoothed_terms.2 = (f32[512,512]{1,0:T(8,128)}, f32[512,512]{1,0:T(8,128)}, f32[512,512]{1,0:T(8,128)}, f32[8,128]{1,0:T(8,128)}) custom-call(s32[2]{0:T(128)} %pad_add_fusion.refs_0_.meta_ref, s32[8]{0:T(128)} %refs_1_.25, f32[16,4096]{1,0:T(8,128)} %copy-done.13, f32[16,4096]{1,0:T(8,128)} %copy-done.13, f32[16,4096]{1,0:T(8,128)} %copy-done.13, ...), custom_call_target="tpu_custom_call" | custom-call | flops 1000 | bytes 1000 | tf_op jit(solution)/shard_map/smoothed_terms/pallas_call | solution.py:324
  59.8 11.5 %smoothed_terms.3 = (f32[4,512,512]{2,1,0:T(8,128)}, f32[8,128]{1,0:T(8,128)}) custom-call(s32[2]{0:T(128)} %pad_add_fusion.refs_0_.meta_ref, s32[8]{0:T(128)} %refs_1_.25, f32[16,4096]{1,0:T(8,128)} %copy-done.13, f32[16,4096]{1,0:T(8,128)} %copy-done.13, f32[16,4096]{1,0:T(8,128)} %copy-done.13, f32[512,4096]{1,0:T(8,128)} %bitcast.13, ...), custom_call_target="tpu_custom_call" | custom-call | flops 1000 | bytes 1000 | tf_op jit(solution)/shard_map/smoothed_terms/pallas_call | solution.py:324
  71.3 17.7 %collective-permute-done.8 = f32[4,2,32,256]{3,2,1,0:T(8,128)} collective-permute-done((f32[4,2,32,256]{3,2,1,0:T(8,128)}, f32[4,2,32,256]{3,2,1,0:T(8,128)}, u32[]{:S(2)}, u32[]{:S(2)}) %collective-permute-start.8) | collective-permute-done | bytes 262176 | tf_op jit(solution)/shard_map/ppermute | solution.py:644
  91.6 2.7 %block_term.10 = (f32[512,512]{1,0:T(8,128)S(1)}, f32[8,128]{1,0:T(8,128)S(1)}) custom-call(s32[2]{0:T(128)S(1)} %copy-done.4, s32[8]{0:T(128)S(1)} %copy-done.6, f32[4,512,512]{2,1,0:T(8,128)} %get-tuple-element.29.refs_2_.refs_15_, f32[512,512]{1,0:T(8,128)} %collective-permute-done.refs_3_, f32[512,512]{1,0:T(8,128)} %collective-permute-done.9.refs_4_, ...), custom_call_target="tpu_custom_call" | custom-call | flops 1000 | bytes 1000 | tf_op jit(solution)/shard_map/block_term/pallas_call | solution.py:413
  112.7 3.2 %block_term.11 = (f32[512,512]{1,0:T(8,128)S(1)}, f32[8,128]{1,0:T(8,128)S(1)}) custom-call(s32[2]{0:T(128)S(1)} %copy-done.4, s32[8]{0:T(128)S(1)} %copy-done.6, f32[4,512,512]{2,1,0:T(8,128)} %get-tuple-element.29.refs_2_.refs_15_, f32[512,512]{1,0:T(8,128)} %collective-permute-done.refs_3_, f32[4,512,512]{2,1,0:T(8,128)} %get-tuple-element.34.refs_4_.refs_5_.refs_6_, ...), custom_call_target="tpu_custom_call" | custom-call | flops 1000 | bytes 1000 | tf_op jit(solution)/shard_map/block_term/pallas_call | solution.py:413
  115.9 3.1 %collective-permute-start.14 = (f32[512,512]{1,0:T(8,128)S(1)}, f32[512,512]{1,0:T(8,128)S(1)}, u32[]{:S(2)}, u32[]{:S(2)}) collective-permute-start(f32[512,512]{1,0:T(8,128)S(1)} %get-tuple-element.43), channel_id=1, source_target_pairs={{0,8},{4,12},{24,16},{28,20},{1,9},{5,13},{25,17},{29,21},{2,10},{... | collective-permute-start | bytes 3145736 | tf_op jit(solution)/shard_map/ppermute | solution.py:666
  119.0 10.9 %collective-permute-done.1.refs_5_.refs_4_ = f32[512,512]{1,0:T(8,128)S(1)} collective-permute-done((f32[512,512]{1,0:T(8,128)}, f32[512,512]{1,0:T(8,128)S(1)}, u32[]{:S(2)}, u32[]{:S(2)}) %collective-permute-start.1) | collective-permute-done | bytes 1048608 | tf_op jit(solution)/shard_map/ppermute | solution.py:620
  134.2 4.9 %collective-permute-start.20 = (f32[512,512]{1,0:T(8,128)S(1)}, f32[512,512]{1,0:T(8,128)S(1)}, u32[]{:S(2)}, u32[]{:S(2)}) collective-permute-start(f32[512,512]{1,0:T(8,128)S(1)} %get-tuple-element.51), channel_id=1, source_target_pairs={{0,8},{4,12},{8,16},{12,20},{16,24},{20,28},{1,9},{5,13},{9,17},{1... | collective-permute-start | bytes 3145736 | tf_op jit(solution)/shard_map/ppermute | solution.py:666
  142.8 9.5 %collective-permute-done.13.refs_7_.refs_8_ = f32[512,512]{1,0:T(8,128)S(1)} collective-permute-done((f32[512,512]{1,0:T(8,128)}, f32[512,512]{1,0:T(8,128)S(1)}, u32[]{:S(2)}, u32[]{:S(2)}) %collective-permute-start.13) | collective-permute-done | bytes 1048608 | tf_op jit(solution)/shard_map/ppermute | solution.py:620
  154.2 3.3 %block_term.14 = (f32[512,512]{1,0:T(8,128)S(1)}, f32[8,128]{1,0:T(8,128)S(1)}) custom-call(s32[2]{0:T(128)S(1)} %copy-done.4, s32[8]{0:T(128)S(1)} %copy-done.6, f32[4,512,512]{2,1,0:T(8,128)} %get-tuple-element.29.refs_2_.refs_15_, f32[512,512]{1,0:T(8,128)} %collective-permute-done.refs_3_, f32[512,512]{1,0:T(8,128)} %collective-permute-done.9.refs_4_, ...), custom_call_target="tpu_custom_call" | custom-call | flops 1000 | bytes 1000 | tf_op jit(solution)/shard_map/block_term/pallas_call | solution.py:413
  157.6 4.6 %collective-permute-start.17 = (f32[512,512]{1,0:T(8,128)S(1)}, f32[512,512]{1,0:T(8,128)S(1)}, u32[]{:S(2)}, u32[]{:S(2)}) collective-permute-start(f32[512,512]{1,0:T(8,128)S(1)} %get-tuple-element.48), channel_id=1, source_target_pairs={{0,8},{4,12},{8,16},{12,20},{1,9},{5,13},{9,17},{13,21},{2,10},{6,... | collective-permute-start | bytes 3145736 | tf_op jit(solution)/shard_map/ppermute | solution.py:666
  162.9 13.8 %collective-permute-done.20.refs_0_.refs_12_ = f32[512,512]{1,0:T(8,128)S(1)} collective-permute-done((f32[512,512]{1,0:T(8,128)S(1)}, f32[512,512]{1,0:T(8,128)S(1)}, u32[]{:S(2)}, u32[]{:S(2)}) %collective-permute-start.20) | collective-permute-done | bytes 1048608 | tf_op jit(solution)/shard_map/ppermute | solution.py:666
  176.7 20.8 %collective-permute-done.17.refs_12_ = f32[512,512]{1,0:T(8,128)S(1)} collective-permute-done((f32[512,512]{1,0:T(8,128)S(1)}, f32[512,512]{1,0:T(8,128)S(1)}, u32[]{:S(2)}, u32[]{:S(2)}) %collective-permute-start.17) | collective-permute-done | bytes 1048608 | tf_op jit(solution)/shard_map/ppermute | solution.py:666
  197.5 3.9 %block_term.15 = (f32[512,512]{1,0:T(8,128)S(1)}, f32[8,128]{1,0:T(8,128)}) custom-call(s32[2]{0:T(128)S(1)} %copy-done.4, s32[8]{0:T(128)S(1)} %copy-done.6, f32[4,512,512]{2,1,0:T(8,128)} %get-tuple-element.29.refs_2_.refs_15_, f32[512,512]{1,0:T(8,128)} %collective-permute-done.refs_3_, f32[512,512]{1,0:T(8,128)} %collective-permute-done.9.refs_4_, ...), custom_call_target="tpu_custom_call" | custom-call | flops 1000 | bytes 1000 | tf_op jit(solution)/shard_map/block_term/pallas_call | solution.py:413
  201.4 4.4 %collective-permute-start.19 = (f32[512,512]{1,0:T(8,128)S(1)}, f32[512,512]{1,0:T(8,128)S(1)}, u32[]{:S(2)}, u32[]{:S(2)}) collective-permute-start(f32[512,512]{1,0:T(8,128)S(1)} %get-tuple-element.50), channel_id=1, source_target_pairs={{0,8},{4,12},{8,16},{12,20},{16,24},{20,28},{1,9},{5,13},{9,17},{1... | collective-permute-start | bytes 3145736 | tf_op jit(solution)/shard_map/ppermute | solution.py:666
  205.8 4.0 %block_term.16 = (f32[512,512]{1,0:T(8,128)S(1)}, f32[8,128]{1,0:T(8,128)}) custom-call(s32[2]{0:T(128)S(1)} %copy-done.4, s32[8]{0:T(128)S(1)} %copy-done.6, f32[4,512,512]{2,1,0:T(8,128)} %get-tuple-element.29.refs_2_.refs_15_, f32[512,512]{1,0:T(8,128)} %collective-permute-done.refs_3_, f32[512,512]{1,0:T(8,128)} %collective-permute-done.9.refs_4_, ...), custom_call_target="tpu_custom_call" | custom-call | flops 1000 | bytes 1000 | tf_op jit(solution)/shard_map/block_term/pallas_call | solution.py:413
  211.1 15.6 %collective-permute-done.19.refs_10_ = f32[512,512]{1,0:T(8,128)S(1)} collective-permute-done((f32[512,512]{1,0:T(8,128)S(1)}, f32[512,512]{1,0:T(8,128)S(1)}, u32[]{:S(2)}, u32[]{:S(2)}) %collective-permute-start.19) | collective-permute-done | bytes 1048608 | tf_op jit(solution)/shard_map/ppermute | solution.py:666
  226.7 8.2 %collective-permute-done.22.refs_11_ = f32[512,512]{1,0:T(8,128)S(1)} collective-permute-done((f32[512,512]{1,0:T(8,128)S(1)}, f32[512,512]{1,0:T(8,128)S(1)}, u32[]{:S(2)}, u32[]{:S(2)}) %collective-permute-start.22) | collective-permute-done | bytes 1048608 | tf_op jit(solution)/shard_map/ppermute | solution.py:666
  235.0 4.2 %block_term.17 = (f32[512,512]{1,0:T(8,128)}, f32[8,128]{1,0:T(8,128)}) custom-call(s32[2]{0:T(128)S(1)} %copy-done.4, s32[8]{0:T(128)S(1)} %copy-done.6, f32[4,512,512]{2,1,0:T(8,128)} %get-tuple-element.29.refs_2_.refs_15_, f32[512,512]{1,0:T(8,128)} %collective-permute-done.refs_3_, f32[512,512]{1,0:T(8,128)S(1)} %collective-permute-done.1.refs_5_.refs_4_, ...), custom_call_target="tpu_custom_call" | custom-call | flops 1000 | bytes 1000 | tf_op jit(solution)/shard_map/block_term/pallas_call | solution.py:413
  (85 shorter events, 49.2 us)
Async XLA Ops:
  5.3 31.7 %collective-permute-start = (f32[512,512]{1,0:T(8,128)}, f32[512,512]{1,0:T(8,128)}, u32[]{:S(2)}, u32[]{:S(2)}) collective-permute-start(f32[512,512]{1,0:T(8,128)} %pixel_weights.2.refs_5_.refs_15_), channel_id=1, source_target_pairs={{0,4},{4,0},{8,12},{12,8},{16,20},{20,16},{24,28},{28,24},{1,5},{5... | collective-permute-start | bytes 3145736 | tf_op jit(solution)/shard_map/ppermute | solution.py:620
  24.6 5.3 %collective-permute-start.6 = (f32[1,2,32,256]{3,2,1,0:T(8,128)}, f32[1,2,32,256]{3,2,1,0:T(8,128)S(1)}, u32[]{:S(2)}, u32[]{:S(2)}) collective-permute-start(f32[1,2,32,256]{3,2,1,0:T(8,128)} %get-tuple-element.37), channel_id=1, source_target_pairs={{0,8},{4,12},{8,0},{12,4},{16,24},{20,28},{24,16},{28,20},{1,9},{5... | collective-permute-start | bytes 196616 | tf_op jit(solution)/shard_map/ppermute | solution.py:644
  27.3 4.2 %collective-permute-start.2 = (f32[16,4096]{1,0:T(8,128)S(1)}, f32[16,4096]{1,0:T(8,128)S(1)}, u32[]{:S(2)}, u32[]{:S(2)}) collective-permute-start(f32[16,4096]{1,0:T(8,128)S(1)} %get-tuple-element.57), channel_id=1, source_target_pairs={{0,1},{1,2},{2,3},{4,5},{5,6},{6,7},{8,9},{9,10},{10,11},{12,13},{... | collective-permute-start | bytes 786440 | tf_op jit(solution)/shard_map/ppermute | solution.py:634
  28.6 5.3 %collective-permute-start.3 = (f32[16,4096]{1,0:T(8,128)S(1)}, f32[16,4096]{1,0:T(8,128)}, u32[]{:S(2)}, u32[]{:S(2)}) collective-permute-start(f32[16,4096]{1,0:T(8,128)S(1)} %get-tuple-element.56), channel_id=1, source_target_pairs={{1,0},{2,1},{3,2},{5,4},{6,5},{7,6},{9,8},{10,9},{11,10},{13,12},{... | collective-permute-start | bytes 786440 | tf_op jit(solution)/shard_map/ppermute | solution.py:635
  33.9 24.6 %collective-permute-start.7 = (f32[2,2,32,256]{3,2,1,0:T(8,128)}, f32[2,2,32,256]{3,2,1,0:T(8,128)S(1)}, u32[]{:S(2)}, u32[]{:S(2)}) collective-permute-start(f32[2,2,32,256]{3,2,1,0:T(8,128)} %held.3), channel_id=1, source_target_pairs={{0,16},{4,20},{8,24},{12,28},{16,0},{20,4},{24,8},{28,12},{1,17},{... | collective-permute-start | bytes 393224 | tf_op jit(solution)/shard_map/ppermute | solution.py:644
  36.5 54.4 %collective-permute-start.9 = (f32[512,512]{1,0:T(8,128)}, f32[512,512]{1,0:T(8,128)}, u32[]{:S(2)}, u32[]{:S(2)}) collective-permute-start(f32[512,512]{1,0:T(8,128)} %get-tuple-element.31.refs_16_), channel_id=1, source_target_pairs={{0,4},{4,0},{8,12},{12,8},{16,20},{20,16},{24,28},{28,24},{1,5},{5... | collective-permute-start | bytes 3145736 | tf_op jit(solution)/shard_map/ppermute | solution.py:620
  40.6 50.3 %collective-permute-start.10 = (f32[512,512]{1,0:T(8,128)}, f32[512,512]{1,0:T(8,128)}, u32[]{:S(2)}, u32[]{:S(2)}) collective-permute-start(f32[512,512]{1,0:T(8,128)} %get-tuple-element.38), channel_id=1, source_target_pairs={{0,8},{4,12},{24,16},{28,20},{1,9},{5,13},{25,17},{29,21},{2,10},{... | collective-permute-start | bytes 3145736 | tf_op jit(solution)/shard_map/ppermute | solution.py:666
  57.0 53.8 %collective-permute-start.4 = (f32[512,512]{1,0:T(8,128)}, f32[512,512]{1,0:T(8,128)}, u32[]{:S(2)}, u32[]{:S(2)}) collective-permute-start(f32[512,512]{1,0:T(8,128)} %get-tuple-element.35), channel_id=1, source_target_pairs={{0,4},{4,0},{8,12},{12,8},{16,20},{20,16},{24,28},{28,24},{1,5},{5... | collective-permute-start | bytes 3145736 | tf_op jit(solution)/shard_map/ppermute | solution.py:620
  59.3 29.8 %collective-permute-start.8 = (f32[4,2,32,256]{3,2,1,0:T(8,128)}, f32[4,2,32,256]{3,2,1,0:T(8,128)}, u32[]{:S(2)}, u32[]{:S(2)}) collective-permute-start(f32[4,2,32,256]{3,2,1,0:T(8,128)} %held.4), channel_id=1, source_target_pairs={{0,4},{4,0},{8,12},{12,8},{16,20},{20,16},{24,28},{28,24},{1,5},{5... | collective-permute-start | bytes 786440 | tf_op jit(solution)/shard_map/ppermute | solution.py:644
  71.3 37.4 %copy-start.11 = (s32[8,8]{1,0:T(8,128)S(1)}, s32[8,8]{1,0:T(8,128)}, u32[]{:S(2)}) copy-start(s32[8,8]{1,0:T(8,128)} %owner_ref.1) | copy-start | bytes 772
  99.5 2.6 %collective-permute-start.11 = (f32[16,640]{1,0:T(8,128)S(1)}, f32[16,640]{1,0:T(8,128)S(1)}, u32[]{:S(2)}, u32[]{:S(2)}) collective-permute-start(f32[16,640]{1,0:T(8,128)S(1)} %pair_moments.1), channel_id=1, source_target_pairs={{0,1},{1,0},{2,3},{3,2},{4,5},{5,4},{6,7},{7,6},{8,9},{9,8},{10,11... | collective-permute-start | bytes 122888 | tf_op jit(solution)/shard_map/ppermute | solution.py:704
  102.1 5.9 %collective-permute-start.12 = (f32[16,640]{1,0:T(8,128)S(1)}, f32[16,640]{1,0:T(8,128)S(1)}, u32[]{:S(2)}, u32[]{:S(2)}) collective-permute-start(f32[16,640]{1,0:T(8,128)S(1)} %add.6), channel_id=1, source_target_pairs={{0,2},{1,3},{2,0},{3,1},{4,6},{5,7},{6,4},{7,5},{8,10},{9,11},{10,... | collective-permute-start | bytes 122888 | tf_op jit(solution)/shard_map/ppermute | solution.py:704
  103.6 26.3 %collective-permute-start.1 = (f32[512,512]{1,0:T(8,128)}, f32[512,512]{1,0:T(8,128)S(1)}, u32[]{:S(2)}, u32[]{:S(2)}) collective-permute-start(f32[512,512]{1,0:T(8,128)} %get-tuple-element.30.refs_17_), channel_id=1, source_target_pairs={{0,4},{4,0},{8,12},{12,8},{16,20},{20,16},{24,28},{28,24},{1,5},{5... | collective-permute-start | bytes 3145736 | tf_op jit(solution)/shard_map/ppermute | solution.py:620
  104.1 48.2 %collective-permute-start.13 = (f32[512,512]{1,0:T(8,128)}, f32[512,512]{1,0:T(8,128)S(1)}, u32[]{:S(2)}, u32[]{:S(2)}) collective-permute-start(f32[512,512]{1,0:T(8,128)} %get-tuple-element.42), channel_id=1, source_target_pairs={{0,4},{4,0},{8,12},{12,8},{16,20},{20,16},{24,28},{28,24},{1,5},{5... | collective-permute-start | bytes 3145736 | tf_op jit(solution)/shard_map/ppermute | solution.py:620
  105.6 26.3 %collective-permute-start.15 = (f32[512,512]{1,0:T(8,128)}, f32[512,512]{1,0:T(8,128)S(1)}, u32[]{:S(2)}, u32[]{:S(2)}) collective-permute-start(f32[512,512]{1,0:T(8,128)} %copy-done.12), channel_id=1, source_target_pairs={{0,8},{4,12},{8,16},{12,20},{1,9},{5,13},{9,17},{13,21},{2,10},{6,... | collective-permute-start | bytes 3145736 | tf_op jit(solution)/shard_map/ppermute | solution.py:666
  108.0 23.8 %collective-permute-start.16 = (f32[512,512]{1,0:T(8,128)}, f32[512,512]{1,0:T(8,128)S(1)}, u32[]{:S(2)}, u32[]{:S(2)}) collective-permute-start(f32[512,512]{1,0:T(8,128)} %copy-done.12), channel_id=1, source_target_pairs={{16,8},{20,12},{24,16},{28,20},{17,9},{21,13},{25,17},{29,21},{18,... | collective-permute-start | bytes 3145736 | tf_op jit(solution)/shard_map/ppermute | solution.py:666
  115.9 38.4 %collective-permute-start.14 = (f32[512,512]{1,0:T(8,128)S(1)}, f32[512,512]{1,0:T(8,128)S(1)}, u32[]{:S(2)}, u32[]{:S(2)}) collective-permute-start(f32[512,512]{1,0:T(8,128)S(1)} %get-tuple-element.43), channel_id=1, source_target_pairs={{0,8},{4,12},{24,16},{28,20},{1,9},{5,13},{25,17},{29,21},{2,10},{... | collective-permute-start | bytes 3145736 | tf_op jit(solution)/shard_map/ppermute | solution.py:666
  129.8 46.9 %collective-permute-start.5 = (f32[512,512]{1,0:T(8,128)S(1)}, f32[512,512]{1,0:T(8,128)S(1)}, u32[]{:S(2)}, u32[]{:S(2)}) collective-permute-start(f32[512,512]{1,0:T(8,128)S(1)} %copy-done.16), channel_id=1, source_target_pairs={{0,4},{4,0},{8,12},{12,8},{16,20},{20,16},{24,28},{28,24},{1,5},{5... | collective-permute-start | bytes 3145736 | tf_op jit(solution)/shard_map/ppermute | solution.py:620
  134.2 42.5 %collective-permute-start.20 = (f32[512,512]{1,0:T(8,128)S(1)}, f32[512,512]{1,0:T(8,128)S(1)}, u32[]{:S(2)}, u32[]{:S(2)}) collective-permute-start(f32[512,512]{1,0:T(8,128)S(1)} %get-tuple-element.51), channel_id=1, source_target_pairs={{0,8},{4,12},{8,16},{12,20},{16,24},{20,28},{1,9},{5,13},{9,17},{1... | collective-permute-start | bytes 3145736 | tf_op jit(solution)/shard_map/ppermute | solution.py:666
  141.5 35.2 %collective-permute-start.21 = (f32[512,512]{1,0:T(8,128)S(1)}, f32[512,512]{1,0:T(8,128)S(1)}, u32[]{:S(2)}, u32[]{:S(2)}) collective-permute-start(f32[512,512]{1,0:T(8,128)S(1)} %get-tuple-element.52), channel_id=1, source_target_pairs={{8,0},{12,4},{16,8},{20,12},{24,16},{28,20},{9,1},{13,5},{17,9},{2... | collective-permute-start | bytes 3145736 | tf_op jit(solution)/shard_map/ppermute | solution.py:666
  157.6 39.9 %collective-permute-start.17 = (f32[512,512]{1,0:T(8,128)S(1)}, f32[512,512]{1,0:T(8,128)S(1)}, u32[]{:S(2)}, u32[]{:S(2)}) collective-permute-start(f32[512,512]{1,0:T(8,128)S(1)} %get-tuple-element.48), channel_id=1, source_target_pairs={{0,8},{4,12},{8,16},{12,20},{1,9},{5,13},{9,17},{13,21},{2,10},{6,... | collective-permute-start | bytes 3145736 | tf_op jit(solution)/shard_map/ppermute | solution.py:666
  162.1 35.3 %collective-permute-start.18 = (f32[512,512]{1,0:T(8,128)S(1)}, f32[512,512]{1,0:T(8,128)S(1)}, u32[]{:S(2)}, u32[]{:S(2)}) collective-permute-start(f32[512,512]{1,0:T(8,128)S(1)} %get-tuple-element.48), channel_id=1, source_target_pairs={{16,8},{20,12},{24,16},{28,20},{17,9},{21,13},{25,17},{29,21},{18,... | collective-permute-start | bytes 3145736 | tf_op jit(solution)/shard_map/ppermute | solution.py:666
  201.4 25.3 %collective-permute-start.19 = (f32[512,512]{1,0:T(8,128)S(1)}, f32[512,512]{1,0:T(8,128)S(1)}, u32[]{:S(2)}, u32[]{:S(2)}) collective-permute-start(f32[512,512]{1,0:T(8,128)S(1)} %get-tuple-element.50), channel_id=1, source_target_pairs={{0,8},{4,12},{8,16},{12,20},{16,24},{20,28},{1,9},{5,13},{9,17},{1... | collective-permute-start | bytes 3145736 | tf_op jit(solution)/shard_map/ppermute | solution.py:666
  209.9 25.1 %collective-permute-start.22 = (f32[512,512]{1,0:T(8,128)S(1)}, f32[512,512]{1,0:T(8,128)S(1)}, u32[]{:S(2)}, u32[]{:S(2)}) collective-permute-start(f32[512,512]{1,0:T(8,128)S(1)} %get-tuple-element.53), channel_id=1, source_target_pairs={{8,0},{12,4},{16,8},{20,12},{24,16},{28,20},{9,1},{13,5},{17,9},{2... | collective-permute-start | bytes 3145736 | tf_op jit(solution)/shard_map/ppermute | solution.py:666
  (16 other events, 211.3 us)

commit v6 on v5

--- a/solution.py
+++ b/solution.py
@@ -368,13 +368,10 @@
     own_back = sum(rows_part[:, u : u + 1] * back[u : u + 1, :] for u in range(3))
     mate_back = sum(rows_part[:, u : u + 1] * back[3 + u : 4 + u, :] for u in range(3))
     top = added(own - own_den * own_back, mate - mate_den * mate_back, received)
-    if numerator == "quotient":
-        out_ref[...] = top / (PRIOR + added(own_den, mate_den, received))
-    else:
-        out_ref[...] = top
-
-
-def block_term(layout, width, wanted, senders, meta, starts, parts, received, numerator=None, tables=(), after=()):
+    out_ref[...] = top
+
+
+def block_term(layout, width, wanted, senders, meta, starts, parts, received, tables=(), after=()):
     kept = parts[0][0]
     rows, share = kept.shape[1:]
     chunk = min(TILE, rows)
@@ -397,7 +394,7 @@
                 )
             )
             args.append(got[u])
-    if numerator:
+    if tables:
         rows_part, back = tables
         strips = rows // chunk
         specs.append(pl.BlockSpec((chunk, rows_part.shape[1]), lambda r, m, s: (m[1] * strips + r, 0)))
@@ -405,11 +402,10 @@
             pl.BlockSpec((back.shape[0], share), lambda r, m, s: (0, 2 * wanted(m[0] // 2) + m[0] % 2))
         )
         args += [rows_part, back]
-    for sums in received:
-        specs += [flat] * len(sums)
-        args += list(sums)
+    specs += [flat] * len(received)
+    args += list(received)
     lead = 2 + len(args)
-    body = functools.partial(term_kernel, layout, width, wanted, units, len(received[0]), numerator)
+    body = functools.partial(term_kernel, layout, width, wanted, units, len(received), bool(tables))
     return pl.pallas_call(
         lambda *refs: body(*refs[:lead], *refs[-2:]),
         grid_spec=pltpu.PrefetchScalarGridSpec(
@@ -640,16 +636,18 @@
     held = [0]
     bits = [1 << k for k in range(exposures.bit_length() - 1)]
 
-    def gather_along(gathered, bit):
-        other = lax.ppermute(gathered, "exp", [(i, i ^ bit) for i in range(exposures)])
+    def asked(gathered, bit):
+        return lax.ppermute(gathered, "exp", [(i, i ^ bit) for i in range(exposures)])
+
+    def joined(gathered, other, bit):
         low = (member & bit) == 0
         held.extend([e | bit for e in held])
         return jnp.concatenate([jnp.where(low, gathered, other), jnp.where(low, other, gathered)])
 
-    gathered = gather_along(gathered, bits[1])
-    (gathered,) = held_until([gathered], [above, below])
-    for bit in bits[2:]:
-        gathered = gather_along(gathered, bit)
+    for bit in bits[1:]:
+        if bit > 2:
+            (gathered,) = held_until([gathered], got_ends)
+        gathered = joined(gathered, asked(gathered, bit), bit)
 
     def to_right(step):
         return lambda z: choose(z < step, z + places - step, places - 1)
@@ -665,30 +663,30 @@
         pairs += [(2 * z + s, 2 * z - 2 + s) for z in lefts for s in range(2)]
         return lax.ppermute(value, "exp", pairs)
 
-    def along_places(step, term, sums, after, after_left=()):
+    def along_places(step, term, sums, after):
         rights, lefts = range(step), range(places - step, places)
         if step <= places // 2:
             value, token = term(outward(step), [*rights, *lefts], sums, after)
             if step < places // 2:
                 return (shift(value, rights, lefts),), (token,)
             return (shift(value, rights, []), shift(value, [], lefts)), (token,)
-        right, token = term(to_right(step), rights, sums[:1], (*after, sums[1]))
-        left, token_left = term(to_left(step), lefts, sums[1:], after_left or after)
+        right, token = term(to_right(step), rights, sums[:1], after)
+        left, token_left = term(to_left(step), lefts, sums[1:], after)
         return (shift(right, rights, []), shift(left, [], lefts)), (token, token_left)
 
     def den_term(wanted, senders, sums, after):
         parts = [(den_kept, den_got)]
-        return block_term(layout, width, wanted, senders, meta, foot_start, parts, [sums], after=after)
-
-    den_sums, den_values = along_places(1, den_term, (), ())
+        return block_term(layout, width, wanted, senders, meta, foot_start, parts, sums, after=after)
+
+    den_sums, den_values = along_places(1, den_term, (), [gathered])
     *num_sent, token = smooth(layout.sent_block, sent, [*den_ends, *den_middle], after=den_values)
+    other = asked(gathered, bits[0])
+    num_kept, token = smooth(layout.kept_block, [(i, True) for i in range(places)], [den_kept], after=[token])
+    num_sent = held_until(num_sent, [token, other])
     num_got = swapped(num_sent)
-    (gathered,) = held_until([gathered], [token])
-    gathered = gather_along(gathered, bits[0])
-    num_kept, token = smooth(layout.kept_block, [(i, True) for i in range(places)], [den_kept], after=[token])
     den_sums, den_values = along_places(2, den_term, den_sums, [token])
 
-    (gathered,) = held_until([gathered], den_values)
+    (gathered,) = held_until([joined(gathered, other, bits[0])], den_values)
     scalars = pl.BlockSpec(memory_space=pltpu.SMEM)
     vmem = pl.BlockSpec(memory_space=pltpu.VMEM)
     moments = pl.pallas_call(
@@ -717,26 +715,25 @@
 
     def num_term(wanted, senders, sums, after):
         return block_term(
-            layout, width, wanted, senders, meta, foot_start, parts, [sums], "terms", tables, after
+            layout, width, wanted, senders, meta, foot_start, parts, sums, tables, after
         )
 
     num_sums, num_values = along_places(1, num_term, (), den_values)
     for step in range(3, places):
         den_sums, den_values = along_places(step, den_term, den_sums, num_values)
         num_sums, num_values = along_places(step - 1, num_term, num_sums, den_values)
-    num_sums, num_values = along_places(places - 1, num_term, num_sums, num_values, [arrived(den_sums)])
-    coadd, _ = block_term(
-        layout,
-        width,
-        lambda z: z,
-        range(places),
-        meta,
-        foot_start,
-        parts,
-        [num_sums, den_sums],
-        "quotient",
-        tables,
-    )
+
+    ahead = [*num_values, arrived(den_sums)]
+    terms = []
+    for wanted, senders in ((to_right(places - 1), range(places - 1)), (to_left(places - 1), range(1, places))):
+        value, token = num_term(wanted, senders, (), ahead)
+        terms.append(value)
+        ahead = [token]
+    rightward = shift(terms[0] + num_sums[0], range(places - 1), [])
+    leftward = shift(terms[1] + num_sums[1], [], range(1, places))
+    own_den, token = den_term(lambda z: z, range(places), den_sums, ahead)
+    own_num, _ = num_term(lambda z: z, range(places), (), [token])
+    coadd = (own_num + rightward + leftward) / (PRIOR + own_den)
     return (coadd, offsets)
 
 

time: 240 us -> 213 us (0.89)
  waiting for transfers between devices: 103 us -> 78.3 us
  starting transfers between devices: 44.9 us -> 39.7 us
    ppermute x10, waiting for transfers between devices: 61.8 us -> 33.7 us  [shift(): return lax.ppermute(value, 'exp', pairs)]
    ppermute x6, waiting for transfers between devices: 20.4 us -> 40.5 us  [swapped(): return [lax.ppermute(part, 'exp', swap) for part in parts]]
    ppermute x3, waiting for transfers between devices: 17.7 us -> 2.9 us  [asked(): lax.ppermute(gathered, 'exp', [(i, i ^ bit) for i in range(exposures)])]
    ppermute x10, starting transfers between devices: 26.8 us -> 18.5 us  [shift(): return lax.ppermute(value, 'exp', pairs)]
    ppermute x1, waiting for transfers between devices: 2.46 us -> 0.01 us  [per_device(): below = lax.ppermute(frame[:HALO], 'sky', down)]
    ppermute x1, starting transfers between devices: 1.31 us -> 3.74 us  [per_device(): above = lax.ppermute(frame[rows - HALO:], 'sky', up)]
    pallas_call x9 -> x10, Pallas kernels: 29 us -> 30.2 us  [block_term(): pl.pallas_call(lambda *refs: body(*refs[:lead], *refs[-2:]), grid_spec=pl...]
    unnamed x34 -> x30, local copies, waits for them, and re-layouts: 5.78 us -> 5.8 us
  transfers between devices with their start and end apart: 23 -> 23, of which waited for: 11 -> 11; matrix products, arithmetic and copies ran while one was open for 2% -> 3% of each run, Pallas kernels for 28% -> 36%
where the time goes in v6:
time: 213 us; the launch traced here: 212 us
  Pallas kernels  79.5 us (37%)
  waiting for transfers between devices  78.3 us (37%)
  starting transfers between devices  39.7 us (19%)
  local copies, waits for them, and re-layouts  6.86 us (3%)
  other arithmetic  6.8 us (3%)
    ppermute x6, waiting for transfers between devices, swapped(): return [lax.ppermute(part, 'exp', swap) for part in parts]  40.5 us
    ppermute x10, waiting for transfers between devices, shift(): return lax.ppermute(value, 'exp', pairs)  33.7 us
    pallas_call x10, Pallas kernels, block_term(): pl.pallas_call(lambda *refs: body(*refs[:lead], *refs[-2:]), grid_spec=pl...  30.2 us
    pallas_call x2, Pallas kernels, smoothed_terms(): pl.pallas_call(body, grid_spec=pltpu.PrefetchScalarGridSpec(num_scalar_pr...  24.4 us
    pallas_call x2, Pallas kernels, pixel_weights(): pl.pallas_call(lambda *refs: kernel(*refs[:given], *refs[given + len(afte...  20.4 us
    ppermute x10, starting transfers between devices, shift(): return lax.ppermute(value, 'exp', pairs)  18.5 us
    ppermute x6, starting transfers between devices, swapped(): return [lax.ppermute(part, 'exp', swap) for part in parts]  8.52 us
    ppermute x3, starting transfers between devices, asked(): lax.ppermute(gathered, 'exp', [(i, i ^ bit) for i in range(exposures)])  5.98 us
  transfers between devices with their start and end apart: 23, of which 11 were waited for; matrix products, arithmetic and copies ran while one was open for 3% of the time, Pallas kernels for 36%

profile of v6, /device:TPU:0, one launch (start us, length us, event | category | flops | bytes accessed | tf_op | source)
XLA Modules:
  0.0 212.2 jit_solution(10182844596738173538)
XLA Ops:
  1.2 4.1 %pixel_weights.2.refs_5_.refs_15_ = f32[512,512]{1,0:T(8,128)} custom-call(s32[2]{0:T(128)} %pad_add_fusion.refs_0_.meta_ref, s32[8]{0:T(128)} %refs_1_.27, f32[512,4096]{1,0:T(8,128)} %bitcast.16, s32[32,256]{1,0:T(8,128)} %bitcast.18), custom_call_target="tpu_custom_call" | custom-call | flops 1000 | bytes 1000 | tf_op jit(solution)/shard_map/pixel_weights/pallas_call | solution.py:219
  5.3 2.9 %collective-permute-start = (f32[512,512]{1,0:T(8,128)}, f32[512,512]{1,0:T(8,128)}, u32[]{:S(2)}, u32[]{:S(2)}) collective-permute-start(f32[512,512]{1,0:T(8,128)} %pixel_weights.2.refs_5_.refs_15_), channel_id=1, source_target_pairs={{0,4},{4,0},{8,12},{12,8},{16,20},{20,16},{24,28},{28,24},{1,5},{5... | collective-permute-start | bytes 3145736 | tf_op jit(solution)/shard_map/ppermute | solution.py:616
  8.2 16.3 %pixel_weights.3 = (f32[512,512]{1,0:T(8,128)}, f32[512,512]{1,0:T(8,128)}, f32[4,512,512]{2,1,0:T(8,128)}, f32[1,2,32,256]{3,2,1,0:T(8,128)}) custom-call(s32[2]{0:T(128)} %pad_add_fusion.refs_0_.meta_ref, s32[8]{0:T(128)} %refs_1_.27, f32[512,4096]{1,0:T(8,128)} %bitcast.9, f32[512,4096]{1,0:T(8,128)} %bitcast.17, s32[32,256]{1,0:T(8,128)} %bitcast.19, ...), custom_call_target="tpu_custom_call" | custom-call | flops 1000 | bytes 1000 | tf_op jit(solution)/shard_map/pixel_weights/pallas_call | solution.py:219
  26.1 2.9 %collective-permute-done.4 = f32[1,2,32,256]{3,2,1,0:T(8,128)S(1)} collective-permute-done((f32[1,2,32,256]{3,2,1,0:T(8,128)}, f32[1,2,32,256]{3,2,1,0:T(8,128)S(1)}, u32[]{:S(2)}, u32[]{:S(2)}) %collective-permute-start.4) | collective-permute-done | bytes 65568 | tf_op jit(solution)/shard_map/ppermute | solution.py:640
  31.7 2.8 %collective-permute-start.5 = (f32[2,2,32,256]{3,2,1,0:T(8,128)}, f32[2,2,32,256]{3,2,1,0:T(8,128)S(1)}, u32[]{:S(2)}, u32[]{:S(2)}) collective-permute-start(f32[2,2,32,256]{3,2,1,0:T(8,128)} %held.3), channel_id=1, source_target_pairs={{0,16},{4,20},{8,24},{12,28},{16,0},{20,4},{24,8},{28,12},{1,17},{... | collective-permute-start | bytes 393224 | tf_op jit(solution)/shard_map/ppermute | solution.py:640
  36.9 3.7 %collective-permute-start.2 = (f32[16,4096]{1,0:T(8,128)S(1)}, f32[16,4096]{1,0:T(8,128)}, u32[]{:S(2)}, u32[]{:S(2)}) collective-permute-start(f32[16,4096]{1,0:T(8,128)S(1)} %get-tuple-element.71), channel_id=1, source_target_pairs={{0,1},{1,2},{2,3},{4,5},{5,6},{6,7},{8,9},{9,10},{10,11},{12,13},{... | collective-permute-start | bytes 786440 | tf_op jit(solution)/shard_map/ppermute | solution.py:630
  43.7 2.9 %block_term.10 = (f32[512,512]{1,0:T(8,128)}, f32[8,128]{1,0:T(8,128)S(1)}) custom-call(s32[2]{0:T(128)S(1)} %copy-done.3, s32[8]{0:T(128)S(1)} %copy-done.5, f32[4,512,512]{2,1,0:T(8,128)} %get-tuple-element.36.refs_2_.refs_15_, f32[512,512]{1,0:T(8,128)} %collective-permute-done.refs_1_.refs_3_, f32[4,2,32,256]{3,2,1,0:T(8,128)S(1)} %pad_maximum_fusion.1.refs_4_), custom_call_target="tpu_custom_call" | custom-call | flops 1000 | bytes 1000 | tf_op jit(solution)/shard_map/block_term/pallas_call | solution.py:409
  47.3 4.5 %collective-permute-start.10 = (f32[512,512]{1,0:T(8,128)}, f32[512,512]{1,0:T(8,128)}, u32[]{:S(2)}, u32[]{:S(2)}) collective-permute-start(f32[512,512]{1,0:T(8,128)} %get-tuple-element.49), channel_id=1, source_target_pairs={{0,8},{4,12},{24,16},{28,20},{1,9},{5,13},{25,17},{29,21},{2,10},{... | collective-permute-start | bytes 3145736 | tf_op jit(solution)/shard_map/ppermute | solution.py:664
  51.7 12.9 %smoothed_terms.2 = (f32[512,512]{1,0:T(8,128)}, f32[512,512]{1,0:T(8,128)}, f32[512,512]{1,0:T(8,128)}, f32[8,128]{1,0:T(8,128)}) custom-call(s32[2]{0:T(128)} %pad_add_fusion.refs_0_.meta_ref, s32[8]{0:T(128)} %refs_1_.27, f32[16,4096]{1,0:T(8,128)} %collective-permute-done.2.refs_2_.refs_3_.refs_4_, ...), custom_call_target="tpu_custom_call" | custom-call | flops 1000 | bytes 1000 | tf_op jit(solution)/shard_map/smoothed_terms/pallas_call | solution.py:324
  64.7 11.5 %smoothed_terms.3 = (f32[4,512,512]{2,1,0:T(8,128)}, f32[8,128]{1,0:T(8,128)}) custom-call(s32[2]{0:T(128)} %pad_add_fusion.refs_0_.meta_ref, s32[8]{0:T(128)} %refs_1_.27, f32[16,4096]{1,0:T(8,128)} %collective-permute-done.2.refs_2_.refs_3_.refs_4_, f32[16,4096]{1,0:T(8,128)} %collective-permute-done.2.refs_2_.refs_3_.refs_4_, ...), custom_call_target="tpu_custom_call" | custom-call | flops 1000 | bytes 1000 | tf_op jit(solution)/shard_map/smoothed_terms/pallas_call | solution.py:324
  97.2 5.5 %collective-permute-done.7.refs_5_.refs_6_.refs_7_ = f32[512,512]{1,0:T(8,128)} collective-permute-done((f32[512,512]{1,0:T(8,128)}, f32[512,512]{1,0:T(8,128)}, u32[]{:S(2)}, u32[]{:S(2)}) %collective-permute-start.7) | collective-permute-done | bytes 1048608 | tf_op jit(solution)/shard_map/ppermute | solution.py:616
  104.6 3.2 %block_term.12 = (f32[512,512]{1,0:T(8,128)S(1)}, f32[8,128]{1,0:T(8,128)S(1)}) custom-call(s32[2]{0:T(128)S(1)} %copy-done.4, s32[8]{0:T(128)S(1)} %copy-done.6, f32[4,512,512]{2,1,0:T(8,128)} %get-tuple-element.36.refs_2_.refs_15_, f32[512,512]{1,0:T(8,128)} %collective-permute-done.refs_1_.refs_3_, ...), custom_call_target="tpu_custom_call" | custom-call | flops 1000 | bytes 1000 | tf_op jit(solution)/shard_map/block_term/pallas_call | solution.py:409
  109.3 15.7 %collective-permute-done.1.refs_5_.refs_4_ = f32[512,512]{1,0:T(8,128)S(1)} collective-permute-done((f32[512,512]{1,0:T(8,128)}, f32[512,512]{1,0:T(8,128)S(1)}, u32[]{:S(2)}, u32[]{:S(2)}) %collective-permute-start.1) | collective-permute-done | bytes 1048608 | tf_op jit(solution)/shard_map/ppermute | solution.py:616
  134.1 13.4 %collective-permute-done.17.refs_7_.refs_8_ = f32[512,512]{1,0:T(8,128)S(1)} collective-permute-done((f32[512,512]{1,0:T(8,128)}, f32[512,512]{1,0:T(8,128)S(1)}, u32[]{:S(2)}, u32[]{:S(2)}) %collective-permute-start.17) | collective-permute-done | bytes 1048608 | tf_op jit(solution)/shard_map/ppermute | solution.py:616
  147.5 3.4 %block_term.15 = (f32[512,512]{1,0:T(8,128)S(1)}, f32[8,128]{1,0:T(8,128)S(1)}) custom-call(s32[2]{0:T(128)S(1)} %copy-done.4, s32[8]{0:T(128)S(1)} %copy-done.6, f32[4,512,512]{2,1,0:T(8,128)} %get-tuple-element.36.refs_2_.refs_15_, f32[512,512]{1,0:T(8,128)} %collective-permute-done.refs_1_.refs_3_, f32[512,512]{1,0:T(8,128)} %collective-permute-done.9.refs_4_, ...), custom_call_target="tpu_custom_call" | custom-call | flops 1000 | bytes 1000 | tf_op jit(solution)/shard_map/block_term/pallas_call | solution.py:409
  153.0 10.8 %collective-permute-done.14.refs_0_.refs_5_ = f32[512,512]{1,0:T(8,128)S(1)} collective-permute-done((f32[512,512]{1,0:T(8,128)S(1)}, f32[512,512]{1,0:T(8,128)S(1)}, u32[]{:S(2)}, u32[]{:S(2)}) %collective-permute-start.14) | collective-permute-done | bytes 1048608 | tf_op jit(solution)/shard_map/ppermute | solution.py:664
  163.8 4.7 %collective-permute-done.8.refs_9_.refs_7_ = f32[512,512]{1,0:T(8,128)S(1)} collective-permute-done((f32[512,512]{1,0:T(8,128)S(1)}, f32[512,512]{1,0:T(8,128)S(1)}, u32[]{:S(2)}, u32[]{:S(2)}) %collective-permute-start.8) | collective-permute-done | bytes 1048608 | tf_op jit(solution)/shard_map/ppermute | solution.py:616
  168.5 3.4 %block_term.16 = (f32[512,512]{1,0:T(8,128)S(1)}, f32[8,128]{1,0:T(8,128)S(1)}) custom-call(s32[2]{0:T(128)S(1)} %copy-done.4, s32[8]{0:T(128)S(1)} %copy-done.6, f32[4,512,512]{2,1,0:T(8,128)} %get-tuple-element.36.refs_2_.refs_15_, f32[512,512]{1,0:T(8,128)} %collective-permute-done.refs_1_.refs_3_, f32[512,512]{1,0:T(8,128)} %collective-permute-done.9.refs_4_, ...), custom_call_target="tpu_custom_call" | custom-call | flops 1000 | bytes 1000 | tf_op jit(solution)/shard_map/block_term/pallas_call | solution.py:409
  172.0 3.5 %block_term.17 = (f32[512,512]{1,0:T(8,128)S(1)}, f32[8,128]{1,0:T(8,128)S(1)}) custom-call(s32[2]{0:T(128)S(1)} %copy-done.4, s32[8]{0:T(128)S(1)} %copy-done.6, f32[4,512,512]{2,1,0:T(8,128)} %get-tuple-element.36.refs_2_.refs_15_, f32[512,512]{1,0:T(8,128)} %collective-permute-done.refs_1_.refs_3_, f32[512,512]{1,0:T(8,128)} %collective-permute-done.9.refs_4_, ...), custom_call_target="tpu_custom_call" | custom-call | flops 1000 | bytes 1000 | tf_op jit(solution)/shard_map/block_term/pallas_call | solution.py:409
  177.0 7.8 %collective-permute-done.19 = f32[512,512]{1,0:T(8,128)S(1)} collective-permute-done((f32[512,512]{1,0:T(8,128)S(1)}, f32[512,512]{1,0:T(8,128)S(1)}, u32[]{:S(2)}, u32[]{:S(2)}) %collective-permute-start.19) | collective-permute-done | bytes 1048608 | tf_op jit(solution)/shard_map/ppermute | solution.py:664
  185.1 4.5 %collective-permute-start.20 = (f32[512,512]{1,0:T(8,128)S(1)}, f32[512,512]{1,0:T(8,128)S(1)}, u32[]{:S(2)}, u32[]{:S(2)}) collective-permute-start(f32[512,512]{1,0:T(8,128)S(1)} %add.26), channel_id=1, source_target_pairs={{0,8},{4,12},{8,16},{12,20},{16,24},{20,28},{1,9},{5,13},{9,17},{1... | collective-permute-start | bytes 3145736 | tf_op jit(solution)/shard_map/ppermute | solution.py:664
  191.8 3.8 %block_term.19 = (f32[512,512]{1,0:T(8,128)S(1)}, f32[8,128]{1,0:T(8,128)}) custom-call(s32[2]{0:T(128)S(1)} %copy-done.4, s32[8]{0:T(128)S(1)} %copy-done.6, f32[4,512,512]{2,1,0:T(8,128)} %get-tuple-element.36.refs_2_.refs_15_, f32[512,512]{1,0:T(8,128)} %collective-permute-done.refs_1_.refs_3_, f32[512,512]{1,0:T(8,128)S(1)} %collective-permute-done.1.refs_5_.refs_4_, ...), custom_call_target="tpu_custom_call" | custom-call | flops 1000 | bytes 1000 | tf_op jit(solution)/shard_map/block_term/pallas_call | solution.py:409
  195.7 5.7 %collective-permute-done.22 = f32[512,512]{1,0:T(8,128)S(1)} collective-permute-done((f32[512,512]{1,0:T(8,128)S(1)}, f32[512,512]{1,0:T(8,128)S(1)}, u32[]{:S(2)}, u32[]{:S(2)}) %collective-permute-start.22) | collective-permute-done | bytes 1048608 | tf_op jit(solution)/shard_map/ppermute | solution.py:664
  201.4 9.4 %collective-permute-done.20 = f32[512,512]{1,0:T(8,128)S(1)} collective-permute-done((f32[512,512]{1,0:T(8,128)S(1)}, f32[512,512]{1,0:T(8,128)S(1)}, u32[]{:S(2)}, u32[]{:S(2)}) %collective-permute-start.20) | collective-permute-done | bytes 1048608 | tf_op jit(solution)/shard_map/ppermute | solution.py:664
  (85 shorter events, 51.8 us)
Async XLA Ops:
  5.3 26.4 %collective-permute-start = (f32[512,512]{1,0:T(8,128)}, f32[512,512]{1,0:T(8,128)}, u32[]{:S(2)}, u32[]{:S(2)}) collective-permute-start(f32[512,512]{1,0:T(8,128)} %pixel_weights.2.refs_5_.refs_15_), channel_id=1, source_target_pairs={{0,4},{4,0},{8,12},{12,8},{16,20},{20,16},{24,28},{28,24},{1,5},{5... | collective-permute-start | bytes 3145736 | tf_op jit(solution)/shard_map/ppermute | solution.py:616
  8.2 35.5 %copy-start.5 = (s32[8]{0:T(128)S(1)}, s32[8]{0:T(128)}, u32[]{:S(2)}) copy-start(s32[8]{0:T(128)} %refs_1_.27) | copy-start | bytes 100
  24.5 4.5 %collective-permute-start.4 = (f32[1,2,32,256]{3,2,1,0:T(8,128)}, f32[1,2,32,256]{3,2,1,0:T(8,128)S(1)}, u32[]{:S(2)}, u32[]{:S(2)}) collective-permute-start(f32[1,2,32,256]{3,2,1,0:T(8,128)} %get-tuple-element.39), channel_id=1, source_target_pairs={{0,8},{4,12},{8,0},{12,4},{16,24},{20,28},{24,16},{28,20},{1,9},{5... | collective-permute-start | bytes 196616 | tf_op jit(solution)/shard_map/ppermute | solution.py:640
  31.7 9.0 %collective-permute-start.5 = (f32[2,2,32,256]{3,2,1,0:T(8,128)}, f32[2,2,32,256]{3,2,1,0:T(8,128)S(1)}, u32[]{:S(2)}, u32[]{:S(2)}) collective-permute-start(f32[2,2,32,256]{3,2,1,0:T(8,128)} %held.3), channel_id=1, source_target_pairs={{0,16},{4,20},{8,24},{12,28},{16,0},{20,4},{24,8},{28,12},{1,17},{... | collective-permute-start | bytes 393224 | tf_op jit(solution)/shard_map/ppermute | solution.py:640
  35.6 16.1 %collective-permute-start.3 = (f32[16,4096]{1,0:T(8,128)S(1)}, f32[16,4096]{1,0:T(8,128)}, u32[]{:S(2)}, u32[]{:S(2)}) collective-permute-start(f32[16,4096]{1,0:T(8,128)S(1)} %get-tuple-element.70), channel_id=1, source_target_pairs={{1,0},{2,1},{3,2},{5,4},{6,5},{7,6},{9,8},{10,9},{11,10},{13,12},{... | collective-permute-start | bytes 786440 | tf_op jit(solution)/shard_map/ppermute | solution.py:631
  36.9 14.8 %collective-permute-start.2 = (f32[16,4096]{1,0:T(8,128)S(1)}, f32[16,4096]{1,0:T(8,128)}, u32[]{:S(2)}, u32[]{:S(2)}) collective-permute-start(f32[16,4096]{1,0:T(8,128)S(1)} %get-tuple-element.71), channel_id=1, source_target_pairs={{0,1},{1,2},{2,3},{4,5},{5,6},{6,7},{8,9},{9,10},{10,11},{12,13},{... | collective-permute-start | bytes 786440 | tf_op jit(solution)/shard_map/ppermute | solution.py:630
  41.6 34.5 %collective-permute-start.6 = (f32[4,2,32,256]{3,2,1,0:T(8,128)S(1)}, f32[4,2,32,256]{3,2,1,0:T(8,128)}, u32[]{:S(2)}, u32[]{:S(2)}) collective-permute-start(f32[4,2,32,256]{3,2,1,0:T(8,128)S(1)} %pad_maximum_fusion.1.refs_4_), channel_id=1, source_target_pairs={{0,4},{4,0},{8,12},{12,8},{16,20},{20,16},{24,28},{28,24},{1,5},{5... | collective-permute-start | bytes 786440 | tf_op jit(solution)/shard_map/ppermute | solution.py:640
  43.2 36.4 %collective-permute-start.9 = (f32[512,512]{1,0:T(8,128)}, f32[512,512]{1,0:T(8,128)}, u32[]{:S(2)}, u32[]{:S(2)}) collective-permute-start(f32[512,512]{1,0:T(8,128)} %get-tuple-element.38.refs_16_), channel_id=1, source_target_pairs={{0,4},{4,0},{8,12},{12,8},{16,20},{20,16},{24,28},{28,24},{1,5},{5... | collective-permute-start | bytes 3145736 | tf_op jit(solution)/shard_map/ppermute | solution.py:616
  47.3 32.3 %collective-permute-start.10 = (f32[512,512]{1,0:T(8,128)}, f32[512,512]{1,0:T(8,128)}, u32[]{:S(2)}, u32[]{:S(2)}) collective-permute-start(f32[512,512]{1,0:T(8,128)} %get-tuple-element.49), channel_id=1, source_target_pairs={{0,8},{4,12},{24,16},{28,20},{1,9},{5,13},{25,17},{29,21},{2,10},{... | collective-permute-start | bytes 3145736 | tf_op jit(solution)/shard_map/ppermute | solution.py:664
  76.2 26.5 %collective-permute-start.7 = (f32[512,512]{1,0:T(8,128)}, f32[512,512]{1,0:T(8,128)}, u32[]{:S(2)}, u32[]{:S(2)}) collective-permute-start(f32[512,512]{1,0:T(8,128)} %get-tuple-element.47), channel_id=1, source_target_pairs={{0,4},{4,0},{8,12},{12,8},{16,20},{20,16},{24,28},{28,24},{1,5},{5... | collective-permute-start | bytes 3145736 | tf_op jit(solution)/shard_map/ppermute | solution.py:616
  88.2 1.3 collective-permute-start.11
  89.5 4.3 %collective-permute-start.12 = (f32[16,640]{1,0:T(8,128)S(1)}, f32[16,640]{1,0:T(8,128)S(1)}, u32[]{:S(2)}, u32[]{:S(2)}) collective-permute-start(f32[16,640]{1,0:T(8,128)S(1)} %add.24), channel_id=1, source_target_pairs={{0,2},{1,3},{2,0},{3,1},{4,6},{5,7},{6,4},{7,5},{8,10},{9,11},{10,... | collective-permute-start | bytes 122888 | tf_op jit(solution)/shard_map/ppermute | solution.py:702
  91.0 34.0 %collective-permute-start.1 = (f32[512,512]{1,0:T(8,128)}, f32[512,512]{1,0:T(8,128)S(1)}, u32[]{:S(2)}, u32[]{:S(2)}) collective-permute-start(f32[512,512]{1,0:T(8,128)} %get-tuple-element.37.refs_17_), channel_id=1, source_target_pairs={{0,4},{4,0},{8,12},{12,8},{16,20},{20,16},{24,28},{28,24},{1,5},{5... | collective-permute-start | bytes 3145736 | tf_op jit(solution)/shard_map/ppermute | solution.py:616
  91.5 55.9 %collective-permute-start.17 = (f32[512,512]{1,0:T(8,128)}, f32[512,512]{1,0:T(8,128)S(1)}, u32[]{:S(2)}, u32[]{:S(2)}) collective-permute-start(f32[512,512]{1,0:T(8,128)} %get-tuple-element.56), channel_id=1, source_target_pairs={{0,4},{4,0},{8,12},{12,8},{16,20},{20,16},{24,28},{28,24},{1,5},{5... | collective-permute-start | bytes 3145736 | tf_op jit(solution)/shard_map/ppermute | solution.py:616
  93.0 37.3 %collective-permute-start.15 = (f32[512,512]{1,0:T(8,128)}, f32[512,512]{1,0:T(8,128)S(1)}, u32[]{:S(2)}, u32[]{:S(2)}) collective-permute-start(f32[512,512]{1,0:T(8,128)} %copy-done.12), channel_id=1, source_target_pairs={{16,8},{20,12},{24,16},{28,20},{17,9},{21,13},{25,17},{29,21},{18,... | collective-permute-start | bytes 3145736 | tf_op jit(solution)/shard_map/ppermute | solution.py:664
  93.8 32.7 %collective-permute-start.13 = (f32[512,512]{1,0:T(8,128)}, f32[512,512]{1,0:T(8,128)S(1)}, u32[]{:S(2)}, u32[]{:S(2)}) collective-permute-start(f32[512,512]{1,0:T(8,128)} %copy-done.12), channel_id=1, source_target_pairs={{0,8},{4,12},{8,16},{12,20},{1,9},{5,13},{9,17},{13,21},{2,10},{6,... | collective-permute-start | bytes 3145736 | tf_op jit(solution)/shard_map/ppermute | solution.py:664
  107.7 39.8 %collective-permute-start.18 = (f32[512,512]{1,0:T(8,128)S(1)}, f32[512,512]{1,0:T(8,128)S(1)}, u32[]{:S(2)}, u32[]{:S(2)}) collective-permute-start(f32[512,512]{1,0:T(8,128)S(1)} %get-tuple-element.57), channel_id=1, source_target_pairs={{0,8},{4,12},{24,16},{28,20},{1,9},{5,13},{25,17},{29,21},{2,10},{... | collective-permute-start | bytes 3145736 | tf_op jit(solution)/shard_map/ppermute | solution.py:664
  125.0 43.5 %collective-permute-start.8 = (f32[512,512]{1,0:T(8,128)S(1)}, f32[512,512]{1,0:T(8,128)S(1)}, u32[]{:S(2)}, u32[]{:S(2)}) collective-permute-start(f32[512,512]{1,0:T(8,128)S(1)} %copy-done.14), channel_id=1, source_target_pairs={{0,4},{4,0},{8,12},{12,8},{16,20},{20,16},{24,28},{28,24},{1,5},{5... | collective-permute-start | bytes 3145736 | tf_op jit(solution)/shard_map/ppermute | solution.py:616
  128.9 34.9 %collective-permute-start.14 = (f32[512,512]{1,0:T(8,128)S(1)}, f32[512,512]{1,0:T(8,128)S(1)}, u32[]{:S(2)}, u32[]{:S(2)}) collective-permute-start(f32[512,512]{1,0:T(8,128)S(1)} %get-tuple-element.54), channel_id=1, source_target_pairs={{0,8},{4,12},{8,16},{12,20},{16,24},{20,28},{1,9},{5,13},{9,17},{1... | collective-permute-start | bytes 3145736 | tf_op jit(solution)/shard_map/ppermute | solution.py:664
  132.8 31.0 %collective-permute-start.16 = (f32[512,512]{1,0:T(8,128)S(1)}, f32[512,512]{1,0:T(8,128)S(1)}, u32[]{:S(2)}, u32[]{:S(2)}) collective-permute-start(f32[512,512]{1,0:T(8,128)S(1)} %get-tuple-element.55), channel_id=1, source_target_pairs={{8,0},{12,4},{16,8},{20,12},{24,16},{28,20},{9,1},{13,5},{17,9},{2... | collective-permute-start | bytes 3145736 | tf_op jit(solution)/shard_map/ppermute | solution.py:664
  150.9 24.6 %collective-permute-start.21 = (f32[512,512]{1,0:T(8,128)S(1)}, f32[512,512]{1,0:T(8,128)S(1)}, u32[]{:S(2)}, u32[]{:S(2)}) collective-permute-start(f32[512,512]{1,0:T(8,128)S(1)} %get-tuple-element.66), channel_id=1, source_target_pairs={{16,8},{20,12},{24,16},{28,20},{17,9},{21,13},{25,17},{29,21},{18,... | collective-permute-start | bytes 3145736 | tf_op jit(solution)/shard_map/ppermute | solution.py:664
  151.6 33.2 %collective-permute-start.19 = (f32[512,512]{1,0:T(8,128)S(1)}, f32[512,512]{1,0:T(8,128)S(1)}, u32[]{:S(2)}, u32[]{:S(2)}) collective-permute-start(f32[512,512]{1,0:T(8,128)S(1)} %get-tuple-element.66), channel_id=1, source_target_pairs={{0,8},{4,12},{8,16},{12,20},{1,9},{5,13},{9,17},{13,21},{2,10},{6,... | collective-permute-start | bytes 3145736 | tf_op jit(solution)/shard_map/ppermute | solution.py:664
  175.7 25.7 %collective-permute-start.22 = (f32[512,512]{1,0:T(8,128)S(1)}, f32[512,512]{1,0:T(8,128)S(1)}, u32[]{:S(2)}, u32[]{:S(2)}) collective-permute-start(f32[512,512]{1,0:T(8,128)S(1)} %add.28), channel_id=1, source_target_pairs={{8,0},{12,4},{16,8},{20,12},{24,16},{28,20},{9,1},{13,5},{17,9},{2... | collective-permute-start | bytes 3145736 | tf_op jit(solution)/shard_map/ppermute | solution.py:664
  185.1 25.7 %collective-permute-start.20 = (f32[512,512]{1,0:T(8,128)S(1)}, f32[512,512]{1,0:T(8,128)S(1)}, u32[]{:S(2)}, u32[]{:S(2)}) collective-permute-start(f32[512,512]{1,0:T(8,128)S(1)} %add.26), channel_id=1, source_target_pairs={{0,8},{4,12},{8,16},{12,20},{16,24},{20,28},{1,9},{5,13},{9,17},{1... | collective-permute-start | bytes 3145736 | tf_op jit(solution)/shard_map/ppermute | solution.py:664
  (14 other events, 133.8 us)

commit v7 on v6

--- a/solution.py
+++ b/solution.py
@@ -107,20 +107,15 @@
     return rough * (2.0 - value * rough)
 
 
-def weights_kernel(block_of, plan, units, width, meta_ref, start_ref, *refs):
-    binned = len(refs) > 5 + units
-    frame_ref, refs = (refs[0], refs[1:]) if binned else (None, refs)
-    spread_ref, mask_ref, *refs = refs
-    weights, scratch = (refs[:-10], refs[-10:]) if binned else (refs[:-2], refs[-2:])
-    *scratch, scatter, weight = scratch
-    if binned:
-        bins_ref, total, gather, *splits = scratch
-        image_parts, weight_parts = splits[:3], splits[3:]
+def expanded(kept, rows):
+    return jnp.broadcast_to(kept[:, None, :], (kept.shape[0], BIN, kept.shape[1])).reshape(rows, kept.shape[1])
+
+
+def folded_kernel(layout, width, meta_ref, start_ref, spread_ref, mask_ref, out_ref, scatter):
     step = pl.program_id(0)
-    block = block_of(step, meta_ref)
-    start = start_ref[meta_ref[0]]
+    block = layout.sent_block(step, meta_ref)
     rows, share = spread_ref.shape
-    bins_row, bins_col = mask_ref.shape
+    bins_col = mask_ref.shape[1]
     per = share // BIN
 
     @pl.when(step == 0)
@@ -130,62 +125,76 @@
 
     blocks_here = pltpu.roll(mask_ref[...].astype(F32), lax.rem(bins_col - block * per, bins_col), 1)[:, :SIDE]
     kept = mm(blocks_here.astype(BF16), scatter[...])
-    kept = jnp.where(inside(columns(block, share), start, width), kept, 0.0)
+    kept = jnp.where(inside(columns(block, share), start_ref[meta_ref[0]], width), kept, 0.0)
     for top in range(0, rows, CHUNK):
         here = slice(top, top + CHUNK)
-        inverse = reciprocal(spread_ref[here])
-        bins_here = slice(top // BIN, (top + CHUNK) // BIN)
-        factor = jnp.broadcast_to(kept[bins_here][:, None, :], (CHUNK // BIN, BIN, share)).reshape(CHUNK, share)
-        weight[here] = inverse * factor
-        if binned:
-            for value, splits in ((frame_ref[here], image_parts), (inverse, weight_parts)):
-                value = value.reshape(CHUNK // BIN, 2, 8, share).sum(axis=1).reshape(CHUNK // 2, share)
-                for split in splits:
-                    rounded = value.astype(BF16)
-                    split[top // 2 : (top + CHUNK) // 2] = rounded
-                    value = value - rounded.astype(F32)
-    for at, part in enumerate(plan):
-        if part is None:
-            continue
-
-        @pl.when(step == at)
-        def _(out=part[0], fresh=part[1]):
-            if out >= units:
-                weights[-1][0] = weight[...]
-            elif fresh:
-                weights[out][...] = weight[...]
-            else:
-                weights[out][...] += weight[...]
-
-    if not binned:
-        return
-
-    @pl.when(step == 0)
+        weight = reciprocal(spread_ref[here]) * expanded(kept[top // BIN : (top + CHUNK) // BIN], CHUNK)
+        out_ref[0, here] = jnp.where(step % 2 == 0, weight, out_ref[0, here] + weight)
+
+
+def weights_kernel(layout, width, meta_ref, start_ref, frame_ref, spread_ref, mask_ref, *refs):
+    *outs, kept_ref, bins_ref, scatter, gather, kept_mask, inverse_ref = refs[:-5]
+    splits = refs[-5:]
+    share = layout.share
+    blocks = 2 * layout.places
+    rows, cols = spread_ref.shape
+    bins_row, bins_col = mask_ref.shape
+    per = share // BIN
+    start = start_ref[meta_ref[0]]
+    half = SIDE * BIN
+
+    @pl.when(pl.program_id(0) == 0)
     def _():
+        cell = lax.broadcasted_iota(jnp.int32, (SIDE, half), 1) >> 4
+        scatter[...] = (cell == lax.broadcasted_iota(jnp.int32, (SIDE, half), 0)).astype(BF16)
         cell = lax.broadcasted_iota(jnp.int32, (share, SIDE), 0) >> 4
         gather[...] = (cell == lax.broadcasted_iota(jnp.int32, (share, SIDE), 1)).astype(BF16)
-        total[...] = jnp.zeros_like(total)
-
-    def gathered(splits):
-        result = None
-        for split in splits:
-            product = mm(split[...], gather[...])
-            result = product if result is None else result + product
-        if bins_col > SIDE:
-            result = jnp.concatenate([result, jnp.zeros((result.shape[0], bins_col - SIDE), F32)], axis=1)
-        return pltpu.roll(result, block * per, 1)
-
-    half = bins_row * 8
-    total[:half] += gathered(image_parts)
-    total[half:] += gathered(weight_parts)
-
-    @pl.when(step == len(plan) - 1)
-    def _():
-        bins = total[...].reshape(2 * bins_row, 8, bins_col).sum(axis=1)
-        cell = lax.broadcasted_iota(jnp.int32, (1, bins_col), 1) * BIN
-        keep = jnp.where(inside(cell, start, width), mask_ref[...].astype(F32), 0.0)
-        bins_ref[0, 0] = bins[:bins_row] / (BIN * BIN)
-        bins_ref[0, 1] = bins[bins_row:] * keep
+
+    mask = mask_ref[...].astype(F32)
+    for part in range(bins_col // SIDE):
+        here = slice(part * half, (part + 1) * half)
+        kept = mm(mask[:, part * SIDE : (part + 1) * SIDE].astype(BF16), scatter[...])
+        kept_mask[:, here] = jnp.where(inside(columns(part, half), start, width), kept, 0.0)
+    tall = rows // 2
+    for block in range(blocks):
+        here = slice(block * share, (block + 1) * share)
+        inverse = reciprocal(spread_ref[:, here])
+        inverse_ref[:, here] = inverse
+        for value, parts in ((frame_ref[:, here], splits[:3]), (inverse, splits[3:])):
+            value = value.reshape(bins_row, 2, 8, share).sum(axis=1).reshape(tall, share)
+            for split in parts:
+                rounded = value.astype(BF16)
+                split[block * tall : (block + 1) * tall] = rounded
+                value = value - rounded.astype(F32)
+
+    def block_weights(block):
+        here = pl.ds(pl.multiple_of(block * share, share), share)
+        return inverse_ref[:, here] * expanded(kept_mask[:, here], rows)
+
+    for at, out in enumerate(outs):
+        out[...] = block_weights(layout.sent_block(at + layout.ends, meta_ref))
+    for at in range(layout.places):
+        kept_ref[at] = block_weights(layout.kept_block(at, meta_ref))
+
+    def binned(parts):
+        sums = mm(parts[0][...], gather[...])
+        for split in parts[1:]:
+            sums = sums + mm(split[...], gather[...])
+        sums = sums.reshape(blocks * bins_row, 8, SIDE).sum(axis=1)
+        halves = []
+        for part in range(bins_col // SIDE):
+            group = SIDE // per
+            halves.append(
+                sum(
+                    pltpu.roll(sums[block * bins_row : (block + 1) * bins_row], (block % group) * per, 1)
+                    for block in range(part * group, (part + 1) * group)
+                )
+            )
+        return jnp.concatenate(halves, axis=1)
+
+    cell = lax.broadcasted_iota(jnp.int32, (1, bins_col), 1) * BIN
+    bins_ref[0, 0] = binned(splits[:3]) / (BIN * BIN)
+    bins_ref[0, 1] = binned(splits[3:]) * jnp.where(inside(cell, start, width), mask, 0.0)
 
 
 ANY = pl.BlockSpec(memory_space=pl.ANY)
@@ -195,41 +204,61 @@
     return pl.BlockSpec(shape, lambda *_: (0,) * len(shape))
 
 
-def pixel_weights(block_of, plan, units, meta, starts, frame, spread, mask, share, width, after=()):
-    rows = spread.shape[0]
-    bins_row, bins_col = mask.shape
-    kept = sum(part is not None and part[0] >= units for part in plan)
-    lead = len(plan) - kept
-    tile = pl.BlockSpec((rows, share), lambda i, meta, starts: (0, block_of(i, meta)))
-    out_specs = [whole((rows, share))] * units
-    out_shape = [pltpu.HBM((rows, share), F32)] * units
-    scratch = [pltpu.VMEM((SIDE, share), BF16), pltpu.VMEM((rows, share), F32)]
-    images = []
-    if frame is not None:
-        images = [frame]
-        bins = (1, 2, bins_row, bins_col)
-        out_specs += [
-            pl.BlockSpec((1, rows, share), lambda i, meta, starts: (jnp.maximum(i - lead, 0), 0, 0)), whole(bins)
-        ]
-        out_shape += [pltpu.HBM((kept, rows, share), F32), jax.ShapeDtypeStruct(bins, F32)]
-        splits = [pltpu.VMEM((rows // 2, share), BF16)] * 5
-        scratch = [pltpu.VMEM((rows, bins_col), F32), pltpu.VMEM((share, SIDE), BF16), *splits, *scratch]
-    given = 2 + len(images) + 2
-    kernel = functools.partial(weights_kernel, block_of, plan, units, width)
-    return pl.pallas_call(
-        lambda *refs: kernel(*refs[:given], *refs[given + len(after) :]),
+def folded_weights(layout, width, meta, starts, spread, mask):
+    rows, share = spread.shape[0], layout.share
+    out = pl.pallas_call(
+        functools.partial(folded_kernel, layout, width),
         grid_spec=pltpu.PrefetchScalarGridSpec(
             num_scalar_prefetch=2,
-            grid=(len(plan),),
-            in_specs=[tile] * len(images) + [tile, whole(mask.shape)] + [ANY] * len(after),
-            out_specs=out_specs,
-            scratch_shapes=scratch,
+            grid=(layout.ends,),
+            in_specs=[
+                pl.BlockSpec((rows, share), lambda i, meta, starts: (0, layout.sent_block(i, meta))),
+                whole(mask.shape),
+            ],
+            out_specs=pl.BlockSpec((1, rows, share), lambda i, meta, starts: (i // 2, 0, 0)),
+            scratch_shapes=[pltpu.VMEM((SIDE, share), BF16)],
         ),
-        out_shape=out_shape,
+        out_shape=pltpu.HBM((layout.quarter, rows, share), F32),
+        compiler_params=pltpu.CompilerParams(vmem_limit_bytes=VMEM),
+        cost_estimate=SMALL,
+        name="folded_weights",
+    )(meta, starts, spread, mask)
+    return [out.reshape(rows, share)] if layout.quarter == 1 else [out[k] for k in range(layout.quarter)]
+
+
+def pixel_weights(layout, width, meta, starts, frame, spread, mask, after):
+    rows, cols = spread.shape
+    bins_row, bins_col = mask.shape
+    share, places = layout.share, layout.places
+    tall = min(SIDE, rows)
+    tile = pl.BlockSpec((tall, cols), lambda i, meta, starts: (i, 0))
+    kernel = functools.partial(weights_kernel, layout, width)
+    return pl.pallas_call(
+        lambda *refs: kernel(*refs[:5], *refs[5 + len(after) :]),
+        grid_spec=pltpu.PrefetchScalarGridSpec(
+            num_scalar_prefetch=2,
+            grid=(rows // tall,),
+            in_specs=[tile, tile, pl.BlockSpec((tall // BIN, bins_col), lambda i, meta, starts: (i, 0))]
+            + [ANY] * len(after),
+            out_specs=[pl.BlockSpec((tall, share), lambda i, meta, starts: (i, 0))] * layout.middle
+            + [
+                pl.BlockSpec((places, tall, share), lambda i, meta, starts: (0, i, 0)),
+                pl.BlockSpec((1, 2, tall // BIN, bins_col), lambda i, meta, starts: (0, 0, i, 0)),
+            ],
+            scratch_shapes=[
+                pltpu.VMEM((SIDE, SIDE * BIN), BF16),
+                pltpu.VMEM((share, SIDE), BF16),
+                pltpu.VMEM((tall // BIN, cols), F32),
+                pltpu.VMEM((tall, cols), F32),
+            ]
+            + [pltpu.VMEM((2 * places * tall // 2, share), BF16)] * 5,
+        ),
+        out_shape=[pltpu.HBM((rows, share), F32)] * layout.middle
+        + [pltpu.HBM((places, rows, share), F32), jax.ShapeDtypeStruct((1, 2, bins_row, bins_col), F32)],
         compiler_params=pltpu.CompilerParams(vmem_limit_bytes=VMEM),
         cost_estimate=SMALL,
         name="pixel_weights",
-    )(meta, starts, *images, spread, mask, *after)
+    )(meta, starts, frame, spread, mask, *after)
 
 
 def smooth_kernel(block_of, plan, width, stacked, meta_ref, start_ref, *refs):
@@ -602,24 +631,15 @@
     layout = Places(exposures, cols)
     share, places, quarter = layout.share, layout.places, layout.quarter
     ends, middle_count = layout.ends, layout.middle
-    units = quarter + middle_count
-    folded = [(i // 2, i % 2 == 0) for i in range(ends)]
-    sent = folded + [(quarter + i, True) for i in range(middle_count)]
-    rest = [None] * ends + [(i, True) for i in range(middle_count + places)]
-
-    def sent_then_kept(i, meta):
-        return jnp.where(i < places, layout.sent_block(i, meta), layout.kept_block(i - places, meta))
-
+    sent = [(i // 2, i % 2 == 0) for i in range(ends)] + [(quarter + i, True) for i in range(middle_count)]
     swap = [(i, i ^ 1) for i in range(exposures)]
 
     def swapped(parts):
         return [lax.ppermute(part, "exp", swap) for part in parts]
 
-    den_ends = pixel_weights(
-        layout.sent_block, folded, quarter, meta, foot_start, None, spread, blocks, share, width
-    )
+    den_ends = folded_weights(layout, width, meta, foot_start, spread, blocks)
     *den_middle, den_kept, gathered = pixel_weights(
-        sent_then_kept, rest, middle_count, meta, foot_start, frame, spread, blocks, share, width, after=den_ends
+        layout, width, meta, foot_start, frame, spread, blocks, den_ends
     )
     got_ends = swapped(den_ends)
     got_middle = swapped(den_middle)
@@ -678,15 +698,13 @@
         parts = [(den_kept, den_got)]
         return block_term(layout, width, wanted, senders, meta, foot_start, parts, sums, after=after)
 
-    den_sums, den_values = along_places(1, den_term, (), [gathered])
+    den_sums, den_values = along_places(1, den_term, (), ())
     *num_sent, token = smooth(layout.sent_block, sent, [*den_ends, *den_middle], after=den_values)
     other = asked(gathered, bits[0])
-    num_kept, token = smooth(layout.kept_block, [(i, True) for i in range(places)], [den_kept], after=[token])
-    num_sent = held_until(num_sent, [token, other])
-    num_got = swapped(num_sent)
-    den_sums, den_values = along_places(2, den_term, den_sums, [token])
-
-    (gathered,) = held_until([joined(gathered, other, bits[0])], den_values)
+    num_sent = held_until(num_sent, [other, got_middle[0]])
+    num_got = swapped(num_sent[:quarter])
+    num_got += swapped(held_until(num_sent[quarter:], num_got))
+    gathered = joined(gathered, other, bits[0])
     scalars = pl.BlockSpec(memory_space=pltpu.SMEM)
     vmem = pl.BlockSpec(memory_space=pltpu.VMEM)
     moments = pl.pallas_call(
@@ -697,9 +715,12 @@
         cost_estimate=SMALL,
         name="pair_moments",
     )(meta, gathered)
+    den_sums, den_values = along_places(2, den_term, den_sums, [token, moments])
+    num_kept, token = smooth(layout.kept_block, [(i, True) for i in range(places)], [den_kept], after=den_values)
     bit = 1
     while bit < sky_count:
         moments = moments + lax.ppermute(moments, "sky", [(i, i ^ bit) for i in range(sky_count)])
+        (moments,) = held_until([moments], den_values if bit == 1 else [token])
         bit *= 2
     offsets, back = pl.pallas_call(
         functools.partial(solve_kernel, width),

time: 213 us -> 206 us (0.967)
  waiting for transfers between devices: 78.3 us -> 67 us
  starting transfers between devices: 39.7 us -> 44.9 us
  Pallas kernels: 79.5 us -> 77.2 us
    ppermute x6, waiting for transfers between devices: 40.5 us -> 23.9 us  [swapped(): return [lax.ppermute(part, 'exp', swap) for part in parts]]
    ppermute x10, starting transfers between devices: 18.5 us -> 27.3 us  [shift(): return lax.ppermute(value, 'exp', pairs)]
    ppermute x10, waiting for transfers between devices: 33.7 us -> 39.8 us  [shift(): return lax.ppermute(value, 'exp', pairs)]
    pallas_call x2, Pallas kernels: 20.4 us -> 16.4 us  [the longest x1 12.4 us: pixel_weights(): pl.pallas_call(lambda *refs: kernel(*refs[:5], *refs[5 + len(after):]), g...]
    unnamed x30 -> x40, local copies, waits for them, and re-layouts: 5.8 us -> 5.66 us
where the time goes in v7:
time: 206 us; the launch traced here: 205 us
  Pallas kernels  77.2 us (37%)
  waiting for transfers between devices  67 us (33%)
  starting transfers between devices  44.9 us (22%)
  other arithmetic  8.06 us (4%)
  local copies, waits for them, and re-layouts  6.72 us (3%)
    ppermute x10, waiting for transfers between devices, shift(): return lax.ppermute(value, 'exp', pairs)  39.8 us
    pallas_call x10, Pallas kernels, block_term(): pl.pallas_call(lambda *refs: body(*refs[:lead], *refs[-2:]), grid_spec=pl...  31.7 us
    ppermute x10, starting transfers between devices, shift(): return lax.ppermute(value, 'exp', pairs)  27.3 us
    pallas_call x2, Pallas kernels, smoothed_terms(): pl.pallas_call(body, grid_spec=pltpu.PrefetchScalarGridSpec(num_scalar_pr...  24.5 us
    ppermute x6, waiting for transfers between devices, swapped(): return [lax.ppermute(part, 'exp', swap) for part in parts]  23.9 us
    pallas_call x1, Pallas kernels, pixel_weights(): pl.pallas_call(lambda *refs: kernel(*refs[:5], *refs[5 + len(after):]), g...  12.4 us
    ppermute x6, starting transfers between devices, swapped(): return [lax.ppermute(part, 'exp', swap) for part in parts]  6.67 us
    ppermute x3, starting transfers between devices, asked(): lax.ppermute(gathered, 'exp', [(i, i ^ bit) for i in range(exposures)])  6.23 us
  transfers between devices with their start and end apart: 23, of which 11 were waited for; matrix products, arithmetic and copies ran while one was open for 3% of the time, Pallas kernels for 36%

profile of v7, /device:TPU:0, one launch (start us, length us, event | category | flops | bytes accessed | tf_op | source)
XLA Modules:
  0.0 204.8 jit_solution(7305424753177719963)
XLA Ops:
  1.3 4.1 %folded_weights.1 = f32[1,512,512]{2,1,0:T(8,128)} custom-call(s32[2]{0:T(128)} %pad_add_fusion.meta_ref.refs_0_, s32[8]{0:T(128)} %refs_1_.25, f32[512,4096]{1,0:T(8,128)} %bitcast.17, s32[32,256]{1,0:T(8,128)} %bitcast.22), custom_call_target="tpu_custom_call" | custom-call | flops 1000 | bytes 1000 | tf_op jit(solution)/shard_map/folded_weights/pallas_call | solution.py:209
  8.3 12.4 %pixel_weights.1 = (f32[512,512]{1,0:T(8,128)}, f32[512,512]{1,0:T(8,128)}, f32[4,512,512]{2,1,0:T(8,128)}, f32[1,2,32,256]{3,2,1,0:T(8,128)}) custom-call(s32[2]{0:T(128)} %pad_add_fusion.meta_ref.refs_0_, s32[8]{0:T(128)} %refs_1_.25, f32[512,4096]{1,0:T(8,128)} %bitcast.10, f32[512,4096]{1,0:T(8,128)} %bitcast.18, s32[32,256]{1,0:T(8,128)} %bitcast.23, ...), custom_call_target="tpu_custom_call" | custom-call | flops 1000 | bytes 1000 | tf_op jit(solution)/shard_map/pixel_weights/pallas_call | solution.py:236
  26.7 5.9 %collective-permute-done.refs_3_.refs_1_ = f32[512,512]{1,0:T(8,128)} collective-permute-done((f32[512,512]{1,0:T(8,128)}, f32[512,512]{1,0:T(8,128)}, u32[]{:S(2)}, u32[]{:S(2)}) %collective-permute-start) | collective-permute-done | bytes 1048608 | tf_op jit(solution)/shard_map/ppermute | solution.py:638
  32.6 3.2 %collective-permute-start.7 = (f32[2,2,32,256]{3,2,1,0:T(8,128)}, f32[2,2,32,256]{3,2,1,0:T(8,128)S(1)}, u32[]{:S(2)}, u32[]{:S(2)}) collective-permute-start(f32[2,2,32,256]{3,2,1,0:T(8,128)} %held.5), channel_id=1, source_target_pairs={{0,16},{4,20},{8,24},{12,28},{16,0},{20,4},{24,8},{28,12},{1,17},{... | collective-permute-start | bytes 393224 | tf_op jit(solution)/shard_map/ppermute | solution.py:660
  38.1 3.0 %collective-permute-start.2 = (f32[16,4096]{1,0:T(8,128)S(1)}, f32[16,4096]{1,0:T(8,128)S(1)}, u32[]{:S(2)}, u32[]{:S(2)}) collective-permute-start(f32[16,4096]{1,0:T(8,128)S(1)} %get-tuple-element.75), channel_id=1, source_target_pairs={{0,1},{1,2},{2,3},{4,5},{5,6},{6,7},{8,9},{9,10},{10,11},{12,13},{... | collective-permute-start | bytes 786440 | tf_op jit(solution)/shard_map/ppermute | solution.py:650
  44.4 3.0 %block_term.10 = (f32[512,512]{1,0:T(8,128)}, f32[8,128]{1,0:T(8,128)S(1)}) custom-call(s32[2]{0:T(128)S(1)} %copy-done.3, s32[8]{0:T(128)S(1)} %copy-done.6, f32[4,512,512]{2,1,0:T(8,128)} %get-tuple-element.38.refs_2_.refs_15_, f32[512,512]{1,0:T(8,128)} %collective-permute-done.refs_3_.refs_1_), custom_call_target="tpu_custom_call" | custom-call | flops 1000 | bytes 1000 | tf_op jit(solution)/shard_map/block_term/pallas_call | solution.py:438
  47.9 4.5 %collective-permute-start.5 = (f32[512,512]{1,0:T(8,128)}, f32[512,512]{1,0:T(8,128)}, u32[]{:S(2)}, u32[]{:S(2)}) collective-permute-start(f32[512,512]{1,0:T(8,128)} %get-tuple-element.41), channel_id=1, source_target_pairs={{0,8},{4,12},{24,16},{28,20},{1,9},{5,13},{25,17},{29,21},{2,10},{... | collective-permute-start | bytes 3145736 | tf_op jit(solution)/shard_map/ppermute | solution.py:684
  53.2 13.1 %smoothed_terms.2 = (f32[512,512]{1,0:T(8,128)}, f32[512,512]{1,0:T(8,128)}, f32[512,512]{1,0:T(8,128)}, f32[8,128]{1,0:T(8,128)}) custom-call(s32[2]{0:T(128)} %pad_add_fusion.meta_ref.refs_0_, s32[8]{0:T(128)} %refs_1_.25, f32[16,4096]{1,0:T(8,128)} %copy-done.16, f32[16,4096]{1,0:T(8,128)} %copy-done.16, f32[16,4096]{1,0:T(8,128)} %copy-done.16, ...), custom_call_target="tpu_custom_call" | custom-call | flops 1000 | bytes 1000 | tf_op jit(solution)/shard_map/smoothed_terms/pallas_call | solution.py:353
  82.5 5.0 %collective-permute-start.13 = (f32[512,512]{1,0:T(8,128)}, f32[512,512]{1,0:T(8,128)}, u32[]{:S(2)}, u32[]{:S(2)}) collective-permute-start(f32[512,512]{1,0:T(8,128)} %copy-done.14), channel_id=1, source_target_pairs={{0,8},{4,12},{8,16},{12,20},{1,9},{5,13},{9,17},{13,21},{2,10},{6,... | collective-permute-start | bytes 3145736 | tf_op jit(solution)/shard_map/ppermute | solution.py:684
  87.5 11.4 %smoothed_terms.3 = (f32[4,512,512]{2,1,0:T(8,128)}, f32[8,128]{1,0:T(8,128)}) custom-call(s32[2]{0:T(128)} %pad_add_fusion.meta_ref.refs_0_, s32[8]{0:T(128)} %refs_1_.25, f32[16,4096]{1,0:T(8,128)} %copy-done.16, f32[16,4096]{1,0:T(8,128)} %copy-done.16, f32[16,4096]{1,0:T(8,128)} %copy-done.16, f32[512,4096]{1,0:T(8,128)} %bitcast.14, ...), custom_call_target="tpu_custom_call" | custom-call | flops 1000 | bytes 1000 | tf_op jit(solution)/shard_map/smoothed_terms/pallas_call | solution.py:353
  105.1 3.2 %block_term.12 = (f32[512,512]{1,0:T(8,128)S(1)}, f32[8,128]{1,0:T(8,128)S(1)}) custom-call(s32[2]{0:T(128)S(1)} %copy-done.5, s32[8]{0:T(128)S(1)} %copy-done.8, f32[4,512,512]{2,1,0:T(8,128)} %get-tuple-element.38.refs_2_.refs_15_, f32[512,512]{1,0:T(8,128)} %collective-permute-done.refs_3_.refs_1_, ...), custom_call_target="tpu_custom_call" | custom-call | flops 1000 | bytes 1000 | tf_op jit(solution)/shard_map/block_term/pallas_call | solution.py:438
  108.3 3.8 %collective-permute-start.18 = (f32[512,512]{1,0:T(8,128)S(1)}, f32[512,512]{1,0:T(8,128)S(1)}, u32[]{:S(2)}, u32[]{:S(2)}) collective-permute-start(f32[512,512]{1,0:T(8,128)S(1)} %get-tuple-element.61), channel_id=1, source_target_pairs={{0,8},{4,12},{24,16},{28,20},{1,9},{5,13},{25,17},{29,21},{2,10},{... | collective-permute-start | bytes 3145736 | tf_op jit(solution)/shard_map/ppermute | solution.py:684
  112.1 3.0 %collective-permute-done.1.refs_5_.refs_4_ = f32[512,512]{1,0:T(8,128)} collective-permute-done((f32[512,512]{1,0:T(8,128)}, f32[512,512]{1,0:T(8,128)}, u32[]{:S(2)}, u32[]{:S(2)}) %collective-permute-start.1) | collective-permute-done | bytes 1048608 | tf_op jit(solution)/shard_map/ppermute | solution.py:638
  124.3 13.2 %collective-permute-done.17.refs_7_.refs_8_ = f32[512,512]{1,0:T(8,128)S(1)} collective-permute-done((f32[512,512]{1,0:T(8,128)}, f32[512,512]{1,0:T(8,128)S(1)}, u32[]{:S(2)}, u32[]{:S(2)}) %collective-permute-start.17) | collective-permute-done | bytes 1048608 | tf_op jit(solution)/shard_map/ppermute | solution.py:638
  137.5 3.3 %block_term.15 = (f32[512,512]{1,0:T(8,128)S(1)}, f32[8,128]{1,0:T(8,128)S(1)}) custom-call(s32[2]{0:T(128)S(1)} %copy-done.5, s32[8]{0:T(128)S(1)} %copy-done.8, f32[4,512,512]{2,1,0:T(8,128)} %get-tuple-element.38.refs_2_.refs_15_, f32[512,512]{1,0:T(8,128)} %collective-permute-done.refs_3_.refs_1_, f32[512,512]{1,0:T(8,128)} %collective-permute-done.4.refs_4_, ...), custom_call_target="tpu_custom_call" | custom-call | flops 1000 | bytes 1000 | tf_op jit(solution)/shard_map/block_term/pallas_call | solution.py:438
  141.6 3.1 %collective-permute-start.19 = (f32[512,512]{1,0:T(8,128)S(1)}, f32[512,512]{1,0:T(8,128)S(1)}, u32[]{:S(2)}, u32[]{:S(2)}) collective-permute-start(f32[512,512]{1,0:T(8,128)S(1)} %get-tuple-element.70), channel_id=1, source_target_pairs={{0,8},{4,12},{8,16},{12,20},{1,9},{5,13},{9,17},{13,21},{2,10},{6,... | collective-permute-start | bytes 3145736 | tf_op jit(solution)/shard_map/ppermute | solution.py:684
  144.7 13.3 %collective-permute-done.14.refs_0_.refs_5_ = f32[512,512]{1,0:T(8,128)S(1)} collective-permute-done((f32[512,512]{1,0:T(8,128)S(1)}, f32[512,512]{1,0:T(8,128)S(1)}, u32[]{:S(2)}, u32[]{:S(2)}) %collective-permute-start.14) | collective-permute-done | bytes 1048608 | tf_op jit(solution)/shard_map/ppermute | solution.py:684
  159.7 3.5 %block_term.16 = (f32[512,512]{1,0:T(8,128)S(1)}, f32[8,128]{1,0:T(8,128)S(1)}) custom-call(s32[2]{0:T(128)S(1)} %copy-done.5, s32[8]{0:T(128)S(1)} %copy-done.8, f32[4,512,512]{2,1,0:T(8,128)} %get-tuple-element.38.refs_2_.refs_15_, f32[512,512]{1,0:T(8,128)} %collective-permute-done.refs_3_.refs_1_, f32[512,512]{1,0:T(8,128)} %collective-permute-done.4.refs_4_, ...), custom_call_target="tpu_custom_call" | custom-call | flops 1000 | bytes 1000 | tf_op jit(solution)/shard_map/block_term/pallas_call | solution.py:438
  163.2 3.6 %block_term.17 = (f32[512,512]{1,0:T(8,128)S(1)}, f32[8,128]{1,0:T(8,128)S(1)}) custom-call(s32[2]{0:T(128)S(1)} %copy-done.5, s32[8]{0:T(128)S(1)} %copy-done.8, f32[4,512,512]{2,1,0:T(8,128)} %get-tuple-element.38.refs_2_.refs_15_, f32[512,512]{1,0:T(8,128)} %collective-permute-done.refs_3_.refs_1_, f32[512,512]{1,0:T(8,128)} %collective-permute-done.4.refs_4_, ...), custom_call_target="tpu_custom_call" | custom-call | flops 1000 | bytes 1000 | tf_op jit(solution)/shard_map/block_term/pallas_call | solution.py:438
  168.4 9.9 %collective-permute-done.19 = f32[512,512]{1,0:T(8,128)S(1)} collective-permute-done((f32[512,512]{1,0:T(8,128)S(1)}, f32[512,512]{1,0:T(8,128)S(1)}, u32[]{:S(2)}, u32[]{:S(2)}) %collective-permute-start.19) | collective-permute-done | bytes 1048608 | tf_op jit(solution)/shard_map/ppermute | solution.py:684
  178.5 4.5 %collective-permute-start.20 = (f32[512,512]{1,0:T(8,128)S(1)}, f32[512,512]{1,0:T(8,128)S(1)}, u32[]{:S(2)}, u32[]{:S(2)}) collective-permute-start(f32[512,512]{1,0:T(8,128)S(1)} %add.26), channel_id=1, source_target_pairs={{0,8},{4,12},{8,16},{12,20},{16,24},{20,28},{1,9},{5,13},{9,17},{1... | collective-permute-start | bytes 3145736 | tf_op jit(solution)/shard_map/ppermute | solution.py:684
  185.4 4.0 %block_term.19 = (f32[512,512]{1,0:T(8,128)S(1)}, f32[8,128]{1,0:T(8,128)}) custom-call(s32[2]{0:T(128)S(1)} %copy-done.5, s32[8]{0:T(128)S(1)} %copy-done.8, f32[4,512,512]{2,1,0:T(8,128)} %get-tuple-element.38.refs_2_.refs_15_, f32[512,512]{1,0:T(8,128)} %collective-permute-done.refs_3_.refs_1_, f32[512,512]{1,0:T(8,128)} %collective-permute-done.1.refs_5_.refs_4_, ...), custom_call_target="tpu_custom_call" | custom-call | flops 1000 | bytes 1000 | tf_op jit(solution)/shard_map/block_term/pallas_call | solution.py:438
  189.3 4.5 %collective-permute-done.22 = f32[512,512]{1,0:T(8,128)S(1)} collective-permute-done((f32[512,512]{1,0:T(8,128)S(1)}, f32[512,512]{1,0:T(8,128)S(1)}, u32[]{:S(2)}, u32[]{:S(2)}) %collective-permute-start.22) | collective-permute-done | bytes 1048608 | tf_op jit(solution)/shard_map/ppermute | solution.py:684
  193.8 9.5 %collective-permute-done.20 = f32[512,512]{1,0:T(8,128)S(1)} collective-permute-done((f32[512,512]{1,0:T(8,128)S(1)}, f32[512,512]{1,0:T(8,128)S(1)}, u32[]{:S(2)}, u32[]{:S(2)}) %collective-permute-start.20) | collective-permute-done | bytes 1048608 | tf_op jit(solution)/shard_map/ppermute | solution.py:684
  (97 shorter events, 55.9 us)
Async XLA Ops:
  5.4 27.2 %collective-permute-start = (f32[512,512]{1,0:T(8,128)}, f32[512,512]{1,0:T(8,128)}, u32[]{:S(2)}, u32[]{:S(2)}) collective-permute-start(f32[512,512]{1,0:T(8,128)} %bitcast.19), channel_id=1, source_target_pairs={{0,4},{4,0},{8,12},{12,8},{16,20},{20,16},{24,28},{28,24},{1,5},{5... | collective-permute-start | bytes 3145736 | tf_op jit(solution)/shard_map/ppermute | solution.py:638
  8.3 36.1 %copy-start.6 = (s32[8]{0:T(128)S(1)}, s32[8]{0:T(128)}, u32[]{:S(2)}) copy-start(s32[8]{0:T(128)} %refs_1_.25) | copy-start | bytes 100
  20.7 4.5 %collective-permute-start.6 = (f32[1,2,32,256]{3,2,1,0:T(8,128)}, f32[1,2,32,256]{3,2,1,0:T(8,128)S(1)}, u32[]{:S(2)}, u32[]{:S(2)}) collective-permute-start(f32[1,2,32,256]{3,2,1,0:T(8,128)} %get-tuple-element.44), channel_id=1, source_target_pairs={{0,8},{4,12},{8,0},{12,4},{16,24},{20,28},{24,16},{28,20},{1,9},{5... | collective-permute-start | bytes 196616 | tf_op jit(solution)/shard_map/ppermute | solution.py:660
  22.2 44.1 %collective-permute-start.4 = (f32[512,512]{1,0:T(8,128)}, f32[512,512]{1,0:T(8,128)}, u32[]{:S(2)}, u32[]{:S(2)}) collective-permute-start(f32[512,512]{1,0:T(8,128)} %get-tuple-element.40.refs_16_), channel_id=1, source_target_pairs={{0,4},{4,0},{8,12},{12,8},{16,20},{20,16},{24,28},{28,24},{1,5},{5... | collective-permute-start | bytes 3145736 | tf_op jit(solution)/shard_map/ppermute | solution.py:638
  32.6 8.6 %collective-permute-start.7 = (f32[2,2,32,256]{3,2,1,0:T(8,128)}, f32[2,2,32,256]{3,2,1,0:T(8,128)S(1)}, u32[]{:S(2)}, u32[]{:S(2)}) collective-permute-start(f32[2,2,32,256]{3,2,1,0:T(8,128)} %held.5), channel_id=1, source_target_pairs={{0,16},{4,20},{8,24},{12,28},{16,0},{20,4},{24,8},{28,12},{1,17},{... | collective-permute-start | bytes 393224 | tf_op jit(solution)/shard_map/ppermute | solution.py:660
  36.8 15.6 %collective-permute-start.3 = (f32[16,4096]{1,0:T(8,128)S(1)}, f32[16,4096]{1,0:T(8,128)S(1)}, u32[]{:S(2)}, u32[]{:S(2)}) collective-permute-start(f32[16,4096]{1,0:T(8,128)S(1)} %get-tuple-element.74), channel_id=1, source_target_pairs={{1,0},{2,1},{3,2},{5,4},{6,5},{7,6},{9,8},{10,9},{11,10},{13,12},{... | collective-permute-start | bytes 786440 | tf_op jit(solution)/shard_map/ppermute | solution.py:651
  38.1 14.3 %collective-permute-start.2 = (f32[16,4096]{1,0:T(8,128)S(1)}, f32[16,4096]{1,0:T(8,128)S(1)}, u32[]{:S(2)}, u32[]{:S(2)}) collective-permute-start(f32[16,4096]{1,0:T(8,128)S(1)} %get-tuple-element.75), channel_id=1, source_target_pairs={{0,1},{1,2},{2,3},{4,5},{5,6},{6,7},{8,9},{9,10},{10,11},{12,13},{... | collective-permute-start | bytes 786440 | tf_op jit(solution)/shard_map/ppermute | solution.py:650
  42.9 23.4 %collective-permute-start.8 = (f32[4,2,32,256]{3,2,1,0:T(8,128)}, f32[4,2,32,256]{3,2,1,0:T(8,128)}, u32[]{:S(2)}, u32[]{:S(2)}) collective-permute-start(f32[4,2,32,256]{3,2,1,0:T(8,128)} %pad_maximum_fusion.1), channel_id=1, source_target_pairs={{0,4},{4,0},{8,12},{12,8},{16,20},{20,16},{24,28},{28,24},{1,5},{5... | collective-permute-start | bytes 786440 | tf_op jit(solution)/shard_map/ppermute | solution.py:660
  47.9 27.2 %collective-permute-start.5 = (f32[512,512]{1,0:T(8,128)}, f32[512,512]{1,0:T(8,128)}, u32[]{:S(2)}, u32[]{:S(2)}) collective-permute-start(f32[512,512]{1,0:T(8,128)} %get-tuple-element.41), channel_id=1, source_target_pairs={{0,8},{4,12},{24,16},{28,20},{1,9},{5,13},{25,17},{29,21},{2,10},{... | collective-permute-start | bytes 3145736 | tf_op jit(solution)/shard_map/ppermute | solution.py:684
  66.3 36.0 %collective-permute-start.9 = (f32[512,512]{1,0:T(8,128)}, f32[512,512]{1,0:T(8,128)}, u32[]{:S(2)}, u32[]{:S(2)}) collective-permute-start(f32[512,512]{1,0:T(8,128)} %get-tuple-element.50), channel_id=1, source_target_pairs={{0,4},{4,0},{8,12},{12,8},{16,20},{20,16},{24,28},{28,24},{1,5},{5... | collective-permute-start | bytes 3145736 | tf_op jit(solution)/shard_map/ppermute | solution.py:638
  70.6 1.3 collective-permute-start.11
  80.1 18.8 %collective-permute-start.12 = (f32[16,640]{1,0:T(8,128)}, f32[16,640]{1,0:T(8,128)S(1)}, u32[]{:S(2)}, u32[]{:S(2)}) collective-permute-start(f32[16,640]{1,0:T(8,128)} %held.8), channel_id=1, source_target_pairs={{0,2},{1,3},{2,0},{3,1},{4,6},{5,7},{6,4},{7,5},{8,10},{9,11},{10,... | collective-permute-start | bytes 122888 | tf_op jit(solution)/shard_map/ppermute | solution.py:722
  80.1 35.0 %collective-permute-start.1 = (f32[512,512]{1,0:T(8,128)}, f32[512,512]{1,0:T(8,128)}, u32[]{:S(2)}, u32[]{:S(2)}) collective-permute-start(f32[512,512]{1,0:T(8,128)} %get-tuple-element.39.refs_17_), channel_id=1, source_target_pairs={{0,4},{4,0},{8,12},{12,8},{16,20},{20,16},{24,28},{28,24},{1,5},{5... | collective-permute-start | bytes 3145736 | tf_op jit(solution)/shard_map/ppermute | solution.py:638
  80.7 39.3 %collective-permute-start.15 = (f32[512,512]{1,0:T(8,128)}, f32[512,512]{1,0:T(8,128)}, u32[]{:S(2)}, u32[]{:S(2)}) collective-permute-start(f32[512,512]{1,0:T(8,128)} %copy-done.14), channel_id=1, source_target_pairs={{16,8},{20,12},{24,16},{28,20},{17,9},{21,13},{25,17},{29,21},{18,... | collective-permute-start | bytes 3145736 | tf_op jit(solution)/shard_map/ppermute | solution.py:684
  82.5 33.2 %collective-permute-start.13 = (f32[512,512]{1,0:T(8,128)}, f32[512,512]{1,0:T(8,128)}, u32[]{:S(2)}, u32[]{:S(2)}) collective-permute-start(f32[512,512]{1,0:T(8,128)} %copy-done.14), channel_id=1, source_target_pairs={{0,8},{4,12},{8,16},{12,20},{1,9},{5,13},{9,17},{13,21},{2,10},{6,... | collective-permute-start | bytes 3145736 | tf_op jit(solution)/shard_map/ppermute | solution.py:684
  102.4 35.1 %collective-permute-start.17 = (f32[512,512]{1,0:T(8,128)}, f32[512,512]{1,0:T(8,128)S(1)}, u32[]{:S(2)}, u32[]{:S(2)}) collective-permute-start(f32[512,512]{1,0:T(8,128)} %get-tuple-element.60), channel_id=1, source_target_pairs={{0,4},{4,0},{8,12},{12,8},{16,20},{20,16},{24,28},{28,24},{1,5},{5... | collective-permute-start | bytes 3145736 | tf_op jit(solution)/shard_map/ppermute | solution.py:638
  108.3 29.2 %collective-permute-start.18 = (f32[512,512]{1,0:T(8,128)S(1)}, f32[512,512]{1,0:T(8,128)S(1)}, u32[]{:S(2)}, u32[]{:S(2)}) collective-permute-start(f32[512,512]{1,0:T(8,128)S(1)} %get-tuple-element.61), channel_id=1, source_target_pairs={{0,8},{4,12},{24,16},{28,20},{1,9},{5,13},{25,17},{29,21},{2,10},{... | collective-permute-start | bytes 3145736 | tf_op jit(solution)/shard_map/ppermute | solution.py:684
  115.2 44.5 %collective-permute-start.10 = (f32[512,512]{1,0:T(8,128)S(1)}, f32[512,512]{1,0:T(8,128)S(1)}, u32[]{:S(2)}, u32[]{:S(2)}) collective-permute-start(f32[512,512]{1,0:T(8,128)S(1)} %copy-done.17), channel_id=1, source_target_pairs={{0,4},{4,0},{8,12},{12,8},{16,20},{20,16},{24,28},{28,24},{1,5},{5... | collective-permute-start | bytes 3145736 | tf_op jit(solution)/shard_map/ppermute | solution.py:638
  118.7 39.3 %collective-permute-start.14 = (f32[512,512]{1,0:T(8,128)S(1)}, f32[512,512]{1,0:T(8,128)S(1)}, u32[]{:S(2)}, u32[]{:S(2)}) collective-permute-start(f32[512,512]{1,0:T(8,128)S(1)} %get-tuple-element.58), channel_id=1, source_target_pairs={{0,8},{4,12},{8,16},{12,20},{16,24},{20,28},{1,9},{5,13},{9,17},{1... | collective-permute-start | bytes 3145736 | tf_op jit(solution)/shard_map/ppermute | solution.py:684
  123.0 35.0 %collective-permute-start.16 = (f32[512,512]{1,0:T(8,128)S(1)}, f32[512,512]{1,0:T(8,128)S(1)}, u32[]{:S(2)}, u32[]{:S(2)}) collective-permute-start(f32[512,512]{1,0:T(8,128)S(1)} %get-tuple-element.59), channel_id=1, source_target_pairs={{8,0},{12,4},{16,8},{20,12},{24,16},{28,20},{9,1},{13,5},{17,9},{2... | collective-permute-start | bytes 3145736 | tf_op jit(solution)/shard_map/ppermute | solution.py:684
  140.9 26.0 %collective-permute-start.21 = (f32[512,512]{1,0:T(8,128)S(1)}, f32[512,512]{1,0:T(8,128)S(1)}, u32[]{:S(2)}, u32[]{:S(2)}) collective-permute-start(f32[512,512]{1,0:T(8,128)S(1)} %get-tuple-element.70), channel_id=1, source_target_pairs={{16,8},{20,12},{24,16},{28,20},{17,9},{21,13},{25,17},{29,21},{18,... | collective-permute-start | bytes 3145736 | tf_op jit(solution)/shard_map/ppermute | solution.py:684
  141.6 36.6 %collective-permute-start.19 = (f32[512,512]{1,0:T(8,128)S(1)}, f32[512,512]{1,0:T(8,128)S(1)}, u32[]{:S(2)}, u32[]{:S(2)}) collective-permute-start(f32[512,512]{1,0:T(8,128)S(1)} %get-tuple-element.70), channel_id=1, source_target_pairs={{0,8},{4,12},{8,16},{12,20},{1,9},{5,13},{9,17},{13,21},{2,10},{6,... | collective-permute-start | bytes 3145736 | tf_op jit(solution)/shard_map/ppermute | solution.py:684
  167.1 26.7 %collective-permute-start.22 = (f32[512,512]{1,0:T(8,128)S(1)}, f32[512,512]{1,0:T(8,128)S(1)}, u32[]{:S(2)}, u32[]{:S(2)}) collective-permute-start(f32[512,512]{1,0:T(8,128)S(1)} %add.28), channel_id=1, source_target_pairs={{8,0},{12,4},{16,8},{20,12},{24,16},{28,20},{9,1},{13,5},{17,9},{2... | collective-permute-start | bytes 3145736 | tf_op jit(solution)/shard_map/ppermute | solution.py:684
  178.5 24.9 %collective-permute-start.20 = (f32[512,512]{1,0:T(8,128)S(1)}, f32[512,512]{1,0:T(8,128)S(1)}, u32[]{:S(2)}, u32[]{:S(2)}) collective-permute-start(f32[512,512]{1,0:T(8,128)S(1)} %add.26), channel_id=1, source_target_pairs={{0,8},{4,12},{8,16},{12,20},{16,24},{20,28},{1,9},{5,13},{9,17},{1... | collective-permute-start | bytes 3145736 | tf_op jit(solution)/shard_map/ppermute | solution.py:684
  (19 other events, 211.6 us)

commit v8 on v7

--- a/solution.py
+++ b/solution.py
@@ -664,11 +664,6 @@
         held.extend([e | bit for e in held])
         return jnp.concatenate([jnp.where(low, gathered, other), jnp.where(low, other, gathered)])
 
-    for bit in bits[1:]:
-        if bit > 2:
-            (gathered,) = held_until([gathered], got_ends)
-        gathered = joined(gathered, asked(gathered, bit), bit)
-
     def to_right(step):
         return lambda z: choose(z < step, z + places - step, places - 1)
 
@@ -698,13 +693,21 @@
         parts = [(den_kept, den_got)]
         return block_term(layout, width, wanted, senders, meta, foot_start, parts, sums, after=after)
 
+    gathered = joined(gathered, asked(gathered, bits[1]), bits[1])
     den_sums, den_values = along_places(1, den_term, (), ())
+    (gathered,) = held_until([gathered], [*den_values, above, below])
+    for bit in bits[2:-1]:
+        gathered = joined(gathered, asked(gathered, bit), bit)
+    other = asked(gathered, bits[-1])
     *num_sent, token = smooth(layout.sent_block, sent, [*den_ends, *den_middle], after=den_values)
+    (other,) = held_until([other], [token])
+    gathered = joined(gathered, other, bits[-1])
     other = asked(gathered, bits[0])
-    num_sent = held_until(num_sent, [other, got_middle[0]])
+    den_sums, den_values = along_places(2, den_term, den_sums, [token])
+    num_sent = held_until(num_sent, [other, *den_values])
     num_got = swapped(num_sent[:quarter])
     num_got += swapped(held_until(num_sent[quarter:], num_got))
-    gathered = joined(gathered, other, bits[0])
+    (gathered,) = held_until([joined(gathered, other, bits[0])], den_values)
     scalars = pl.BlockSpec(memory_space=pltpu.SMEM)
     vmem = pl.BlockSpec(memory_space=pltpu.VMEM)
     moments = pl.pallas_call(
@@ -715,7 +718,6 @@
         cost_estimate=SMALL,
         name="pair_moments",
     )(meta, gathered)
-    den_sums, den_values = along_places(2, den_term, den_sums, [token, moments])
     num_kept, token = smooth(layout.kept_block, [(i, True) for i in range(places)], [den_kept], after=den_values)
     bit = 1
     while bit < sky_count:
@@ -739,7 +741,7 @@
             layout, width, wanted, senders, meta, foot_start, parts, sums, tables, after
         )
 
-    num_sums, num_values = along_places(1, num_term, (), den_values)
+    num_sums, num_values = along_places(1, num_term, (), [arrived(den_sums)])
     for step in range(3, places):
         den_sums, den_values = along_places(step, den_term, den_sums, num_values)
         num_sums, num_values = along_places(step - 1, num_term, num_sums, den_values)

time: 206 us -> 211 us (1.024)
  starting transfers between devices: 44.9 us -> 56.2 us
  waiting for transfers between devices: 67 us -> 59.4 us
    ppermute x6, waiting for transfers between devices: 23.9 us -> 13.1 us  [swapped(): return [lax.ppermute(part, 'exp', swap) for part in parts]]
    ppermute x10, starting transfers between devices: 27.3 us -> 37.4 us  [shift(): return lax.ppermute(value, 'exp', pairs)]
    ppermute x3, waiting for transfers between devices: 2.35 us -> 7.5 us  [asked(): lax.ppermute(gathered, 'exp', [(i, i ^ bit) for i in range(exposures)])]
    ppermute x3, starting transfers between devices: 6.23 us -> 3.14 us  [asked(): lax.ppermute(gathered, 'exp', [(i, i ^ bit) for i in range(exposures)])]
    ppermute x2, starting transfers between devices: 0.35 us -> 2.6 us  [per_device(): lax.ppermute(moments, 'sky', [(i, i ^ bit) for i in range(sky_count)])]
    ppermute x10, waiting for transfers between devices: 39.8 us -> 37.6 us  [shift(): return lax.ppermute(value, 'exp', pairs)]
  transfers between devices with their start and end apart: 23 -> 23, of which waited for: 11 -> 10; matrix products, arithmetic and copies ran while one was open for 3% -> 3% of each run, Pallas kernels for 36% -> 35%
where the time goes in v8:
time: 211 us; the launch traced here: 210 us
  Pallas kernels  77.2 us (37%)
  waiting for transfers between devices  59.4 us (28%)
  starting transfers between devices  56.2 us (27%)
  local copies, waits for them, and re-layouts  8.31 us (4%)
  other arithmetic  8.09 us (4%)
    ppermute x10, waiting for transfers between devices, shift(): return lax.ppermute(value, 'exp', pairs)  37.6 us
    ppermute x10, starting transfers between devices, shift(): return lax.ppermute(value, 'exp', pairs)  37.4 us
    pallas_call x10, Pallas kernels, block_term(): pl.pallas_call(lambda *refs: body(*refs[:lead], *refs[-2:]), grid_spec=pl...  31.7 us
    pallas_call x2, Pallas kernels, smoothed_terms(): pl.pallas_call(body, grid_spec=pltpu.PrefetchScalarGridSpec(num_scalar_pr...  24.5 us
    ppermute x6, waiting for transfers between devices, swapped(): return [lax.ppermute(part, 'exp', swap) for part in parts]  13.1 us
    pallas_call x1, Pallas kernels, pixel_weights(): pl.pallas_call(lambda *refs: kernel(*refs[:5], *refs[5 + len(after):]), g...  12.4 us
    ppermute x6, starting transfers between devices, swapped(): return [lax.ppermute(part, 'exp', swap) for part in parts]  8.08 us
    ppermute x3, waiting for transfers between devices, asked(): lax.ppermute(gathered, 'exp', [(i, i ^ bit) for i in range(exposures)])  7.5 us
  transfers between devices with their start and end apart: 23, of which 10 were waited for; matrix products, arithmetic and copies ran while one was open for 3% of the time, Pallas kernels for 35%

profile of v8, /device:TPU:0, one launch (start us, length us, event | category | flops | bytes accessed | tf_op | source)
XLA Modules:
  0.0 210.2 jit_solution(18388020478688821950)
XLA Ops:
  1.3 4.1 %folded_weights.1 = f32[1,512,512]{2,1,0:T(8,128)} custom-call(s32[2]{0:T(128)} %pad_add_fusion.meta_ref.refs_0_, s32[8]{0:T(128)} %refs_1_.25, f32[512,4096]{1,0:T(8,128)} %bitcast.17, s32[32,256]{1,0:T(8,128)} %bitcast.22), custom_call_target="tpu_custom_call" | custom-call | flops 1000 | bytes 1000 | tf_op jit(solution)/shard_map/folded_weights/pallas_call | solution.py:209
  8.3 12.4 %pixel_weights.1 = (f32[512,512]{1,0:T(8,128)}, f32[512,512]{1,0:T(8,128)}, f32[4,512,512]{2,1,0:T(8,128)}, f32[1,2,32,256]{3,2,1,0:T(8,128)}) custom-call(s32[2]{0:T(128)} %pad_add_fusion.meta_ref.refs_0_, s32[8]{0:T(128)} %refs_1_.25, f32[512,4096]{1,0:T(8,128)} %bitcast.10, f32[512,4096]{1,0:T(8,128)} %bitcast.18, s32[32,256]{1,0:T(8,128)} %bitcast.23, ...), custom_call_target="tpu_custom_call" | custom-call | flops 1000 | bytes 1000 | tf_op jit(solution)/shard_map/pixel_weights/pallas_call | solution.py:236
  24.6 3.8 %collective-permute-start.2 = (f32[16,4096]{1,0:T(8,128)S(1)}, f32[16,4096]{1,0:T(8,128)}, u32[]{:S(2)}, u32[]{:S(2)}) collective-permute-start(f32[16,4096]{1,0:T(8,128)S(1)} %get-tuple-element.75), channel_id=1, source_target_pairs={{0,1},{1,2},{2,3},{4,5},{5,6},{6,7},{8,9},{9,10},{10,11},{12,13},{... | collective-permute-start | bytes 786440 | tf_op jit(solution)/shard_map/ppermute | solution.py:650
  28.9 3.3 %collective-permute-done.refs_3_ = f32[512,512]{1,0:T(8,128)} collective-permute-done((f32[512,512]{1,0:T(8,128)}, f32[512,512]{1,0:T(8,128)}, u32[]{:S(2)}, u32[]{:S(2)}) %collective-permute-start) | collective-permute-done | bytes 1048608 | tf_op jit(solution)/shard_map/ppermute | solution.py:638
  32.2 3.0 %block_term.10 = (f32[512,512]{1,0:T(8,128)}, f32[8,128]{1,0:T(8,128)S(1)}) custom-call(s32[2]{0:T(128)S(1)} %copy-done.4, s32[8]{0:T(128)S(1)} %copy-done.7, f32[4,512,512]{2,1,0:T(8,128)} %get-tuple-element.38.refs_2_.refs_15_, f32[512,512]{1,0:T(8,128)} %collective-permute-done.refs_3_), custom_call_target="tpu_custom_call" | custom-call | flops 1000 | bytes 1000 | tf_op jit(solution)/shard_map/block_term/pallas_call | solution.py:438
  35.7 5.5 %collective-permute-start.5 = (f32[512,512]{1,0:T(8,128)}, f32[512,512]{1,0:T(8,128)}, u32[]{:S(2)}, u32[]{:S(2)}) collective-permute-start(f32[512,512]{1,0:T(8,128)} %get-tuple-element.41), channel_id=1, source_target_pairs={{0,8},{4,12},{24,16},{28,20},{1,9},{5,13},{25,17},{29,21},{2,10},{... | collective-permute-start | bytes 3145736 | tf_op jit(solution)/shard_map/ppermute | solution.py:679
  43.5 13.1 %smoothed_terms.2 = (f32[512,512]{1,0:T(8,128)}, f32[512,512]{1,0:T(8,128)}, f32[512,512]{1,0:T(8,128)}, f32[8,128]{1,0:T(8,128)}) custom-call(s32[2]{0:T(128)} %pad_add_fusion.meta_ref.refs_0_, s32[8]{0:T(128)} %refs_1_.25, f32[16,4096]{1,0:T(8,128)} %collective-permute-done.2.refs_2_.refs_3_.refs_4_, ...), custom_call_target="tpu_custom_call" | custom-call | flops 1000 | bytes 1000 | tf_op jit(solution)/shard_map/smoothed_terms/pallas_call | solution.py:353
  56.6 7.2 %collective-permute-done.7.refs_0_ = f32[2,2,32,256]{3,2,1,0:T(8,128)S(1)} collective-permute-done((f32[2,2,32,256]{3,2,1,0:T(8,128)}, f32[2,2,32,256]{3,2,1,0:T(8,128)S(1)}, u32[]{:S(2)}, u32[]{:S(2)}) %collective-permute-start.7) | collective-permute-done | bytes 131104 | tf_op jit(solution)/shard_map/ppermute | solution.py:660
  76.3 5.3 %collective-permute-start.13 = (f32[512,512]{1,0:T(8,128)}, f32[512,512]{1,0:T(8,128)}, u32[]{:S(2)}, u32[]{:S(2)}) collective-permute-start(f32[512,512]{1,0:T(8,128)} %copy-done.14), channel_id=1, source_target_pairs={{0,8},{4,12},{8,16},{12,20},{1,9},{5,13},{9,17},{13,21},{2,10},{6,... | collective-permute-start | bytes 3145736 | tf_op jit(solution)/shard_map/ppermute | solution.py:679
  91.5 11.4 %smoothed_terms.3 = (f32[4,512,512]{2,1,0:T(8,128)}, f32[8,128]{1,0:T(8,128)}) custom-call(s32[2]{0:T(128)} %pad_add_fusion.meta_ref.refs_0_, s32[8]{0:T(128)} %refs_1_.25, f32[16,4096]{1,0:T(8,128)} %collective-permute-done.2.refs_2_.refs_3_.refs_4_, f32[16,4096]{1,0:T(8,128)} %collective-permute-done.2.refs_2_.refs_3_.refs_4_, ...), custom_call_target="tpu_custom_call" | custom-call | flops 1000 | bytes 1000 | tf_op jit(solution)/shard_map/smoothed_terms/pallas_call | solution.py:353
  109.6 3.2 %block_term.12 = (f32[512,512]{1,0:T(8,128)S(1)}, f32[8,128]{1,0:T(8,128)S(1)}) custom-call(s32[2]{0:T(128)S(1)} %copy-done.6, s32[8]{0:T(128)S(1)} %copy-done.9, f32[4,512,512]{2,1,0:T(8,128)} %get-tuple-element.38.refs_2_.refs_15_, f32[512,512]{1,0:T(8,128)} %collective-permute-done.refs_3_, f32[4,512,512]{2,1,0:T(8,128)} %get-tuple-element.45.refs_4_.refs_5_.refs_6_, ...), custom_call_target="tpu_custom_call" | custom-call | flops 1000 | bytes 1000 | tf_op jit(solution)/shard_map/block_term/pallas_call | solution.py:438
  112.8 3.8 %collective-permute-start.18 = (f32[512,512]{1,0:T(8,128)S(1)}, f32[512,512]{1,0:T(8,128)S(1)}, u32[]{:S(2)}, u32[]{:S(2)}) collective-permute-start(f32[512,512]{1,0:T(8,128)S(1)} %get-tuple-element.61), channel_id=1, source_target_pairs={{0,8},{4,12},{24,16},{28,20},{1,9},{5,13},{25,17},{29,21},{2,10},{... | collective-permute-start | bytes 3145736 | tf_op jit(solution)/shard_map/ppermute | solution.py:679
  120.8 6.3 %collective-permute-start.15 = (f32[512,512]{1,0:T(8,128)S(1)}, f32[512,512]{1,0:T(8,128)S(1)}, u32[]{:S(2)}, u32[]{:S(2)}) collective-permute-start(f32[512,512]{1,0:T(8,128)S(1)} %get-tuple-element.58), channel_id=1, source_target_pairs={{0,8},{4,12},{8,16},{12,20},{16,24},{20,28},{1,9},{5,13},{9,17},{1... | collective-permute-start | bytes 3145736 | tf_op jit(solution)/shard_map/ppermute | solution.py:679
  127.1 3.0 %block_term.14 = (f32[512,512]{1,0:T(8,128)S(1)}, f32[8,128]{1,0:T(8,128)S(1)}) custom-call(s32[2]{0:T(128)S(1)} %copy-done.6, s32[8]{0:T(128)S(1)} %copy-done.9, f32[4,512,512]{2,1,0:T(8,128)} %get-tuple-element.38.refs_2_.refs_15_, f32[512,512]{1,0:T(8,128)} %collective-permute-done.refs_3_, f32[512,512]{1,0:T(8,128)} %collective-permute-done.4.refs_4_, ...), custom_call_target="tpu_custom_call" | custom-call | flops 1000 | bytes 1000 | tf_op jit(solution)/shard_map/block_term/pallas_call | solution.py:438
  131.4 8.8 %collective-permute-done.17.refs_7_.refs_8_ = f32[512,512]{1,0:T(8,128)S(1)} collective-permute-done((f32[512,512]{1,0:T(8,128)}, f32[512,512]{1,0:T(8,128)S(1)}, u32[]{:S(2)}, u32[]{:S(2)}) %collective-permute-start.17) | collective-permute-done | bytes 1048608 | tf_op jit(solution)/shard_map/ppermute | solution.py:638
  140.2 3.3 %block_term.15 = (f32[512,512]{1,0:T(8,128)S(1)}, f32[8,128]{1,0:T(8,128)S(1)}) custom-call(s32[2]{0:T(128)S(1)} %copy-done.6, s32[8]{0:T(128)S(1)} %copy-done.9, f32[4,512,512]{2,1,0:T(8,128)} %get-tuple-element.38.refs_2_.refs_15_, f32[512,512]{1,0:T(8,128)} %collective-permute-done.refs_3_, f32[512,512]{1,0:T(8,128)} %collective-permute-done.4.refs_4_, ...), custom_call_target="tpu_custom_call" | custom-call | flops 1000 | bytes 1000 | tf_op jit(solution)/shard_map/block_term/pallas_call | solution.py:438
  144.3 7.1 %collective-permute-start.19 = (f32[512,512]{1,0:T(8,128)S(1)}, f32[512,512]{1,0:T(8,128)S(1)}, u32[]{:S(2)}, u32[]{:S(2)}) collective-permute-start(f32[512,512]{1,0:T(8,128)S(1)} %get-tuple-element.70), channel_id=1, source_target_pairs={{0,8},{4,12},{8,16},{12,20},{1,9},{5,13},{9,17},{13,21},{2,10},{6,... | collective-permute-start | bytes 3145736 | tf_op jit(solution)/shard_map/ppermute | solution.py:679
  151.4 11.1 %collective-permute-done.15.refs_0_.refs_5_ = f32[512,512]{1,0:T(8,128)S(1)} collective-permute-done((f32[512,512]{1,0:T(8,128)S(1)}, f32[512,512]{1,0:T(8,128)S(1)}, u32[]{:S(2)}, u32[]{:S(2)}) %collective-permute-start.15) | collective-permute-done | bytes 1048608 | tf_op jit(solution)/shard_map/ppermute | solution.py:679
  162.4 3.6 %block_term.16 = (f32[512,512]{1,0:T(8,128)S(1)}, f32[8,128]{1,0:T(8,128)S(1)}) custom-call(s32[2]{0:T(128)S(1)} %copy-done.6, s32[8]{0:T(128)S(1)} %copy-done.9, f32[4,512,512]{2,1,0:T(8,128)} %get-tuple-element.38.refs_2_.refs_15_, f32[512,512]{1,0:T(8,128)} %collective-permute-done.refs_3_, f32[512,512]{1,0:T(8,128)} %collective-permute-done.4.refs_4_, ...), custom_call_target="tpu_custom_call" | custom-call | flops 1000 | bytes 1000 | tf_op jit(solution)/shard_map/block_term/pallas_call | solution.py:438
  166.0 3.6 %block_term.17 = (f32[512,512]{1,0:T(8,128)S(1)}, f32[8,128]{1,0:T(8,128)S(1)}) custom-call(s32[2]{0:T(128)S(1)} %copy-done.6, s32[8]{0:T(128)S(1)} %copy-done.9, f32[4,512,512]{2,1,0:T(8,128)} %get-tuple-element.38.refs_2_.refs_15_, f32[512,512]{1,0:T(8,128)} %collective-permute-done.refs_3_, f32[512,512]{1,0:T(8,128)} %collective-permute-done.4.refs_4_, ...), custom_call_target="tpu_custom_call" | custom-call | flops 1000 | bytes 1000 | tf_op jit(solution)/shard_map/block_term/pallas_call | solution.py:438
  171.2 12.0 %collective-permute-done.19 = f32[512,512]{1,0:T(8,128)S(1)} collective-permute-done((f32[512,512]{1,0:T(8,128)S(1)}, f32[512,512]{1,0:T(8,128)S(1)}, u32[]{:S(2)}, u32[]{:S(2)}) %collective-permute-start.19) | collective-permute-done | bytes 1048608 | tf_op jit(solution)/shard_map/ppermute | solution.py:679
  183.4 4.5 %collective-permute-start.20 = (f32[512,512]{1,0:T(8,128)S(1)}, f32[512,512]{1,0:T(8,128)S(1)}, u32[]{:S(2)}, u32[]{:S(2)}) collective-permute-start(f32[512,512]{1,0:T(8,128)S(1)} %add.26), channel_id=1, source_target_pairs={{0,8},{4,12},{8,16},{12,20},{16,24},{20,28},{1,9},{5,13},{9,17},{1... | collective-permute-start | bytes 3145736 | tf_op jit(solution)/shard_map/ppermute | solution.py:679
  190.3 4.0 %block_term.19 = (f32[512,512]{1,0:T(8,128)S(1)}, f32[8,128]{1,0:T(8,128)}) custom-call(s32[2]{0:T(128)S(1)} %copy-done.6, s32[8]{0:T(128)S(1)} %copy-done.9, f32[4,512,512]{2,1,0:T(8,128)} %get-tuple-element.38.refs_2_.refs_15_, f32[512,512]{1,0:T(8,128)} %collective-permute-done.refs_3_, f32[512,512]{1,0:T(8,128)} %collective-permute-done.1.refs_5_.refs_4_, ...), custom_call_target="tpu_custom_call" | custom-call | flops 1000 | bytes 1000 | tf_op jit(solution)/shard_map/block_term/pallas_call | solution.py:438
  197.0 11.8 %collective-permute-done.20 = f32[512,512]{1,0:T(8,128)S(1)} collective-permute-done((f32[512,512]{1,0:T(8,128)S(1)}, f32[512,512]{1,0:T(8,128)S(1)}, u32[]{:S(2)}, u32[]{:S(2)}) %collective-permute-start.20) | collective-permute-done | bytes 1048608 | tf_op jit(solution)/shard_map/ppermute | solution.py:679
  (100 shorter events, 54.4 us)
Async XLA Ops:
  5.4 26.8 %collective-permute-start = (f32[512,512]{1,0:T(8,128)}, f32[512,512]{1,0:T(8,128)}, u32[]{:S(2)}, u32[]{:S(2)}) collective-permute-start(f32[512,512]{1,0:T(8,128)} %bitcast.19), channel_id=1, source_target_pairs={{0,4},{4,0},{8,12},{12,8},{16,20},{20,16},{24,28},{28,24},{1,5},{5... | collective-permute-start | bytes 3145736 | tf_op jit(solution)/shard_map/ppermute | solution.py:638
  8.3 23.9 %copy-start.7 = (s32[8]{0:T(128)S(1)}, s32[8]{0:T(128)}, u32[]{:S(2)}) copy-start(s32[8]{0:T(128)} %refs_1_.25) | copy-start | bytes 100
  20.7 20.5 %collective-permute-start.6 = (f32[1,2,32,256]{3,2,1,0:T(8,128)}, f32[1,2,32,256]{3,2,1,0:T(8,128)S(1)}, u32[]{:S(2)}, u32[]{:S(2)}) collective-permute-start(f32[1,2,32,256]{3,2,1,0:T(8,128)} %get-tuple-element.49), channel_id=1, source_target_pairs={{0,8},{4,12},{8,0},{12,4},{16,24},{20,28},{24,16},{28,20},{1,9},{5... | collective-permute-start | bytes 196616 | tf_op jit(solution)/shard_map/ppermute | solution.py:660
  23.3 19.4 %collective-permute-start.3 = (f32[16,4096]{1,0:T(8,128)S(1)}, f32[16,4096]{1,0:T(8,128)S(1)}, u32[]{:S(2)}, u32[]{:S(2)}) collective-permute-start(f32[16,4096]{1,0:T(8,128)S(1)} %get-tuple-element.74), channel_id=1, source_target_pairs={{1,0},{2,1},{3,2},{5,4},{6,5},{7,6},{9,8},{10,9},{11,10},{13,12},{... | collective-permute-start | bytes 786440 | tf_op jit(solution)/shard_map/ppermute | solution.py:651
  24.6 18.1 %collective-permute-start.2 = (f32[16,4096]{1,0:T(8,128)S(1)}, f32[16,4096]{1,0:T(8,128)}, u32[]{:S(2)}, u32[]{:S(2)}) collective-permute-start(f32[16,4096]{1,0:T(8,128)S(1)} %get-tuple-element.75), channel_id=1, source_target_pairs={{0,1},{1,2},{2,3},{4,5},{5,6},{6,7},{8,9},{9,10},{10,11},{12,13},{... | collective-permute-start | bytes 786440 | tf_op jit(solution)/shard_map/ppermute | solution.py:650
  28.4 38.5 %collective-permute-start.4 = (f32[512,512]{1,0:T(8,128)}, f32[512,512]{1,0:T(8,128)}, u32[]{:S(2)}, u32[]{:S(2)}) collective-permute-start(f32[512,512]{1,0:T(8,128)} %get-tuple-element.40.refs_16_), channel_id=1, source_target_pairs={{0,4},{4,0},{8,12},{12,8},{16,20},{20,16},{24,28},{28,24},{1,5},{5... | collective-permute-start | bytes 3145736 | tf_op jit(solution)/shard_map/ppermute | solution.py:638
  35.7 31.2 %collective-permute-start.5 = (f32[512,512]{1,0:T(8,128)}, f32[512,512]{1,0:T(8,128)}, u32[]{:S(2)}, u32[]{:S(2)}) collective-permute-start(f32[512,512]{1,0:T(8,128)} %get-tuple-element.41), channel_id=1, source_target_pairs={{0,8},{4,12},{24,16},{28,20},{1,9},{5,13},{25,17},{29,21},{2,10},{... | collective-permute-start | bytes 3145736 | tf_op jit(solution)/shard_map/ppermute | solution.py:679
  43.4 20.3 %collective-permute-start.7 = (f32[2,2,32,256]{3,2,1,0:T(8,128)}, f32[2,2,32,256]{3,2,1,0:T(8,128)S(1)}, u32[]{:S(2)}, u32[]{:S(2)}) collective-permute-start(f32[2,2,32,256]{3,2,1,0:T(8,128)} %held.7), channel_id=1, source_target_pairs={{0,16},{4,20},{8,24},{12,28},{16,0},{20,4},{24,8},{28,12},{1,17},{... | collective-permute-start | bytes 393224 | tf_op jit(solution)/shard_map/ppermute | solution.py:660
  65.3 6.9 %collective-permute-start.8 = (f32[4,2,32,256]{3,2,1,0:T(8,128)S(1)}, f32[4,2,32,256]{3,2,1,0:T(8,128)}, u32[]{:S(2)}, u32[]{:S(2)}) collective-permute-start(f32[4,2,32,256]{3,2,1,0:T(8,128)S(1)} %pad_maximum_fusion.1), channel_id=1, source_target_pairs={{0,4},{4,0},{8,12},{12,8},{16,20},{20,16},{24,28},{28,24},{1,5},{5... | collective-permute-start | bytes 786440 | tf_op jit(solution)/shard_map/ppermute | solution.py:660
  72.2 34.1 %collective-permute-start.9 = (f32[512,512]{1,0:T(8,128)}, f32[512,512]{1,0:T(8,128)}, u32[]{:S(2)}, u32[]{:S(2)}) collective-permute-start(f32[512,512]{1,0:T(8,128)} %get-tuple-element.50), channel_id=1, source_target_pairs={{0,4},{4,0},{8,12},{12,8},{16,20},{20,16},{24,28},{28,24},{1,5},{5... | collective-permute-start | bytes 3145736 | tf_op jit(solution)/shard_map/ppermute | solution.py:638
  74.6 33.7 %collective-permute-start.14 = (f32[512,512]{1,0:T(8,128)}, f32[512,512]{1,0:T(8,128)}, u32[]{:S(2)}, u32[]{:S(2)}) collective-permute-start(f32[512,512]{1,0:T(8,128)} %copy-done.14), channel_id=1, source_target_pairs={{16,8},{20,12},{24,16},{28,20},{17,9},{21,13},{25,17},{29,21},{18,... | collective-permute-start | bytes 3145736 | tf_op jit(solution)/shard_map/ppermute | solution.py:679
  76.3 32.1 %collective-permute-start.13 = (f32[512,512]{1,0:T(8,128)}, f32[512,512]{1,0:T(8,128)}, u32[]{:S(2)}, u32[]{:S(2)}) collective-permute-start(f32[512,512]{1,0:T(8,128)} %copy-done.14), channel_id=1, source_target_pairs={{0,8},{4,12},{8,16},{12,20},{1,9},{5,13},{9,17},{13,21},{2,10},{6,... | collective-permute-start | bytes 3145736 | tf_op jit(solution)/shard_map/ppermute | solution.py:679
  87.0 1.3 collective-permute-start.11
  88.9 14.0 %collective-permute-start.12 = (f32[16,640]{1,0:T(8,128)}, f32[16,640]{1,0:T(8,128)S(1)}, u32[]{:S(2)}, u32[]{:S(2)}) collective-permute-start(f32[16,640]{1,0:T(8,128)} %held.12), channel_id=1, source_target_pairs={{0,2},{1,3},{2,0},{3,1},{4,6},{5,7},{6,4},{7,5},{8,10},{9,11},{10,... | collective-permute-start | bytes 122888 | tf_op jit(solution)/shard_map/ppermute | solution.py:724
  91.5 26.4 %collective-permute-start.1 = (f32[512,512]{1,0:T(8,128)}, f32[512,512]{1,0:T(8,128)}, u32[]{:S(2)}, u32[]{:S(2)}) collective-permute-start(f32[512,512]{1,0:T(8,128)} %get-tuple-element.39.refs_17_), channel_id=1, source_target_pairs={{0,4},{4,0},{8,12},{12,8},{16,20},{20,16},{24,28},{28,24},{1,5},{5... | collective-permute-start | bytes 3145736 | tf_op jit(solution)/shard_map/ppermute | solution.py:638
  106.3 33.8 %collective-permute-start.17 = (f32[512,512]{1,0:T(8,128)}, f32[512,512]{1,0:T(8,128)S(1)}, u32[]{:S(2)}, u32[]{:S(2)}) collective-permute-start(f32[512,512]{1,0:T(8,128)} %get-tuple-element.60), channel_id=1, source_target_pairs={{0,4},{4,0},{8,12},{12,8},{16,20},{20,16},{24,28},{28,24},{1,5},{5... | collective-permute-start | bytes 3145736 | tf_op jit(solution)/shard_map/ppermute | solution.py:638
  112.8 27.4 %collective-permute-start.18 = (f32[512,512]{1,0:T(8,128)S(1)}, f32[512,512]{1,0:T(8,128)S(1)}, u32[]{:S(2)}, u32[]{:S(2)}) collective-permute-start(f32[512,512]{1,0:T(8,128)S(1)} %get-tuple-element.61), channel_id=1, source_target_pairs={{0,8},{4,12},{24,16},{28,20},{1,9},{5,13},{25,17},{29,21},{2,10},{... | collective-permute-start | bytes 3145736 | tf_op jit(solution)/shard_map/ppermute | solution.py:679
  116.6 45.8 %collective-permute-start.10 = (f32[512,512]{1,0:T(8,128)S(1)}, f32[512,512]{1,0:T(8,128)S(1)}, u32[]{:S(2)}, u32[]{:S(2)}) collective-permute-start(f32[512,512]{1,0:T(8,128)S(1)} %copy-done.16), channel_id=1, source_target_pairs={{0,4},{4,0},{8,12},{12,8},{16,20},{20,16},{24,28},{28,24},{1,5},{5... | collective-permute-start | bytes 3145736 | tf_op jit(solution)/shard_map/ppermute | solution.py:638
  120.8 41.7 %collective-permute-start.15 = (f32[512,512]{1,0:T(8,128)S(1)}, f32[512,512]{1,0:T(8,128)S(1)}, u32[]{:S(2)}, u32[]{:S(2)}) collective-permute-start(f32[512,512]{1,0:T(8,128)S(1)} %get-tuple-element.58), channel_id=1, source_target_pairs={{0,8},{4,12},{8,16},{12,20},{16,24},{20,28},{1,9},{5,13},{9,17},{1... | collective-permute-start | bytes 3145736 | tf_op jit(solution)/shard_map/ppermute | solution.py:679
  130.1 32.4 %collective-permute-start.16 = (f32[512,512]{1,0:T(8,128)S(1)}, f32[512,512]{1,0:T(8,128)S(1)}, u32[]{:S(2)}, u32[]{:S(2)}) collective-permute-start(f32[512,512]{1,0:T(8,128)S(1)} %get-tuple-element.59), channel_id=1, source_target_pairs={{8,0},{12,4},{16,8},{20,12},{24,16},{28,20},{9,1},{13,5},{17,9},{2... | collective-permute-start | bytes 3145736 | tf_op jit(solution)/shard_map/ppermute | solution.py:679
  143.5 26.1 %collective-permute-start.21 = (f32[512,512]{1,0:T(8,128)S(1)}, f32[512,512]{1,0:T(8,128)S(1)}, u32[]{:S(2)}, u32[]{:S(2)}) collective-permute-start(f32[512,512]{1,0:T(8,128)S(1)} %get-tuple-element.70), channel_id=1, source_target_pairs={{16,8},{20,12},{24,16},{28,20},{17,9},{21,13},{25,17},{29,21},{18,... | collective-permute-start | bytes 3145736 | tf_op jit(solution)/shard_map/ppermute | solution.py:679
  144.3 38.9 %collective-permute-start.19 = (f32[512,512]{1,0:T(8,128)S(1)}, f32[512,512]{1,0:T(8,128)S(1)}, u32[]{:S(2)}, u32[]{:S(2)}) collective-permute-start(f32[512,512]{1,0:T(8,128)S(1)} %get-tuple-element.70), channel_id=1, source_target_pairs={{0,8},{4,12},{8,16},{12,20},{1,9},{5,13},{9,17},{13,21},{2,10},{6,... | collective-permute-start | bytes 3145736 | tf_op jit(solution)/shard_map/ppermute | solution.py:679
  169.9 27.1 %collective-permute-start.22 = (f32[512,512]{1,0:T(8,128)S(1)}, f32[512,512]{1,0:T(8,128)S(1)}, u32[]{:S(2)}, u32[]{:S(2)}) collective-permute-start(f32[512,512]{1,0:T(8,128)S(1)} %add.28), channel_id=1, source_target_pairs={{8,0},{12,4},{16,8},{20,12},{24,16},{28,20},{9,1},{13,5},{17,9},{2... | collective-permute-start | bytes 3145736 | tf_op jit(solution)/shard_map/ppermute | solution.py:679
  183.4 25.4 %collective-permute-start.20 = (f32[512,512]{1,0:T(8,128)S(1)}, f32[512,512]{1,0:T(8,128)S(1)}, u32[]{:S(2)}, u32[]{:S(2)}) collective-permute-start(f32[512,512]{1,0:T(8,128)S(1)} %add.26), channel_id=1, source_target_pairs={{0,8},{4,12},{8,16},{12,20},{16,24},{20,28},{1,9},{5,13},{9,17},{1... | collective-permute-start | bytes 3145736 | tf_op jit(solution)/shard_map/ppermute | solution.py:679
  (19 other events, 189.5 us)

commit v9 on v8

--- a/solution.py
+++ b/solution.py
@@ -700,6 +700,7 @@
         gathered = joined(gathered, asked(gathered, bit), bit)
     other = asked(gathered, bits[-1])
     *num_sent, token = smooth(layout.sent_block, sent, [*den_ends, *den_middle], after=den_values)
+    num_kept, token = smooth(layout.kept_block, [(i, True) for i in range(places)], [den_kept], after=[token])
     (other,) = held_until([other], [token])
     gathered = joined(gathered, other, bits[-1])
     other = asked(gathered, bits[0])
@@ -718,11 +719,9 @@
         cost_estimate=SMALL,
         name="pair_moments",
     )(meta, gathered)
-    num_kept, token = smooth(layout.kept_block, [(i, True) for i in range(places)], [den_kept], after=den_values)
     bit = 1
     while bit < sky_count:
         moments = moments + lax.ppermute(moments, "sky", [(i, i ^ bit) for i in range(sky_count)])
-        (moments,) = held_until([moments], den_values if bit == 1 else [token])
         bit *= 2
     offsets, back = pl.pallas_call(
         functools.partial(solve_kernel, width),

time: 211 us -> 203 us (0.962)
  waiting for transfers between devices: 59.4 us -> 48.4 us
  starting transfers between devices: 56.2 us -> 61.3 us
    ppermute x10, waiting for transfers between devices: 37.6 us -> 11.7 us  [shift(): return lax.ppermute(value, 'exp', pairs)]
    ppermute x6, waiting for transfers between devices: 13.1 us -> 33 us  [swapped(): return [lax.ppermute(part, 'exp', swap) for part in parts]]
    ppermute x3, waiting for transfers between devices: 7.5 us -> 0.01 us  [asked(): lax.ppermute(gathered, 'exp', [(i, i ^ bit) for i in range(exposures)])]
    ppermute x10, starting transfers between devices: 37.4 us -> 43.4 us  [shift(): return lax.ppermute(value, 'exp', pairs)]
    ppermute x2, waiting for transfers between devices: 1.21 us -> 3.67 us  [per_device(): lax.ppermute(moments, 'sky', [(i, i ^ bit) for i in range(sky_count)])]
    unnamed x40 -> x32, local copies, waits for them, and re-layouts: 7.24 us -> 6.47 us
  transfers between devices with their start and end apart: 23 -> 23, of which waited for: 10 -> 9; matrix products, arithmetic and copies ran while one was open for 3% -> 3% of each run, Pallas kernels for 35% -> 36%
where the time goes in v9:
time: 203 us; the launch traced here: 202 us
  Pallas kernels  77.3 us (38%)
  starting transfers between devices  61.3 us (30%)
  waiting for transfers between devices  48.4 us (24%)
  local copies, waits for them, and re-layouts  7.53 us (4%)
  other arithmetic  6.89 us (3%)
    ppermute x10, starting transfers between devices, shift(): return lax.ppermute(value, 'exp', pairs)  43.4 us
    ppermute x6, waiting for transfers between devices, swapped(): return [lax.ppermute(part, 'exp', swap) for part in parts]  33 us
    pallas_call x10, Pallas kernels, block_term(): pl.pallas_call(lambda *refs: body(*refs[:lead], *refs[-2:]), grid_spec=pl...  31.9 us
    pallas_call x2, Pallas kernels, smoothed_terms(): pl.pallas_call(body, grid_spec=pltpu.PrefetchScalarGridSpec(num_scalar_pr...  24.5 us
    pallas_call x1, Pallas kernels, pixel_weights(): pl.pallas_call(lambda *refs: kernel(*refs[:5], *refs[5 + len(after):]), g...  12.4 us
    ppermute x10, waiting for transfers between devices, shift(): return lax.ppermute(value, 'exp', pairs)  11.7 us
    ppermute x6, starting transfers between devices, swapped(): return [lax.ppermute(part, 'exp', swap) for part in parts]  8.08 us
    unnamed x32, local copies, waits for them, and re-layouts  6.47 us
  transfers between devices with their start and end apart: 23, of which 9 were waited for; matrix products, arithmetic and copies ran while one was open for 3% of the time, Pallas kernels for 36%

profile of v9, /device:TPU:0, one launch (start us, length us, event | category | flops | bytes accessed | tf_op | source)
XLA Modules:
  0.0 202.4 jit_solution(12302458217283893326)
XLA Ops:
  1.3 4.1 %folded_weights.1 = f32[1,512,512]{2,1,0:T(8,128)} custom-call(s32[2]{0:T(128)} %pad_add_fusion.meta_ref.refs_0_, s32[8]{0:T(128)} %refs_1_.25, f32[512,4096]{1,0:T(8,128)} %bitcast.17, s32[32,256]{1,0:T(8,128)} %bitcast.22), custom_call_target="tpu_custom_call" | custom-call | flops 1000 | bytes 1000 | tf_op jit(solution)/shard_map/folded_weights/pallas_call | solution.py:209
  8.3 12.4 %pixel_weights.1 = (f32[512,512]{1,0:T(8,128)}, f32[512,512]{1,0:T(8,128)}, f32[4,512,512]{2,1,0:T(8,128)}, f32[1,2,32,256]{3,2,1,0:T(8,128)}) custom-call(s32[2]{0:T(128)} %pad_add_fusion.meta_ref.refs_0_, s32[8]{0:T(128)} %refs_1_.25, f32[512,4096]{1,0:T(8,128)} %bitcast.10, f32[512,4096]{1,0:T(8,128)} %bitcast.18, s32[32,256]{1,0:T(8,128)} %bitcast.23, ...), custom_call_target="tpu_custom_call" | custom-call | flops 1000 | bytes 1000 | tf_op jit(solution)/shard_map/pixel_weights/pallas_call | solution.py:236
  24.6 3.7 %collective-permute-start.2 = (f32[16,4096]{1,0:T(8,128)S(1)}, f32[16,4096]{1,0:T(8,128)}, u32[]{:S(2)}, u32[]{:S(2)}) collective-permute-start(f32[16,4096]{1,0:T(8,128)S(1)} %get-tuple-element.75), channel_id=1, source_target_pairs={{0,1},{1,2},{2,3},{4,5},{5,6},{6,7},{8,9},{9,10},{10,11},{12,13},{... | collective-permute-start | bytes 786440 | tf_op jit(solution)/shard_map/ppermute | solution.py:650
  28.9 3.2 %collective-permute-done.refs_3_ = f32[512,512]{1,0:T(8,128)} collective-permute-done((f32[512,512]{1,0:T(8,128)}, f32[512,512]{1,0:T(8,128)}, u32[]{:S(2)}, u32[]{:S(2)}) %collective-permute-start) | collective-permute-done | bytes 1048608 | tf_op jit(solution)/shard_map/ppermute | solution.py:638
  32.2 2.9 %block_term.10 = (f32[512,512]{1,0:T(8,128)}, f32[8,128]{1,0:T(8,128)S(1)}) custom-call(s32[2]{0:T(128)S(1)} %copy-done.3, s32[8]{0:T(128)S(1)} %copy-done.5, f32[4,512,512]{2,1,0:T(8,128)} %get-tuple-element.38.refs_2_.refs_15_, f32[512,512]{1,0:T(8,128)} %collective-permute-done.refs_3_), custom_call_target="tpu_custom_call" | custom-call | flops 1000 | bytes 1000 | tf_op jit(solution)/shard_map/block_term/pallas_call | solution.py:438
  35.7 5.4 %collective-permute-start.8 = (f32[512,512]{1,0:T(8,128)}, f32[512,512]{1,0:T(8,128)}, u32[]{:S(2)}, u32[]{:S(2)}) collective-permute-start(f32[512,512]{1,0:T(8,128)} %get-tuple-element.49), channel_id=1, source_target_pairs={{0,8},{4,12},{24,16},{28,20},{1,9},{5,13},{25,17},{29,21},{2,10},{... | collective-permute-start | bytes 3145736 | tf_op jit(solution)/shard_map/ppermute | solution.py:679
  43.4 12.9 %smoothed_terms.2 = (f32[512,512]{1,0:T(8,128)}, f32[512,512]{1,0:T(8,128)}, f32[512,512]{1,0:T(8,128)}, f32[8,128]{1,0:T(8,128)}) custom-call(s32[2]{0:T(128)} %pad_add_fusion.meta_ref.refs_0_, s32[8]{0:T(128)} %refs_1_.25, f32[16,4096]{1,0:T(8,128)} %collective-permute-done.2.refs_2_.refs_3_.refs_4_, ...), custom_call_target="tpu_custom_call" | custom-call | flops 1000 | bytes 1000 | tf_op jit(solution)/shard_map/smoothed_terms/pallas_call | solution.py:353
  56.4 11.5 %smoothed_terms.3 = (f32[4,512,512]{2,1,0:T(8,128)}, f32[8,128]{1,0:T(8,128)}) custom-call(s32[2]{0:T(128)} %pad_add_fusion.meta_ref.refs_0_, s32[8]{0:T(128)} %refs_1_.25, f32[16,4096]{1,0:T(8,128)} %collective-permute-done.2.refs_2_.refs_3_.refs_4_, f32[16,4096]{1,0:T(8,128)} %collective-permute-done.2.refs_2_.refs_3_.refs_4_, ...), custom_call_target="tpu_custom_call" | custom-call | flops 1000 | bytes 1000 | tf_op jit(solution)/shard_map/smoothed_terms/pallas_call | solution.py:353
  79.9 5.9 %collective-permute-start.13 = (f32[512,512]{1,0:T(8,128)}, f32[512,512]{1,0:T(8,128)}, u32[]{:S(2)}, u32[]{:S(2)}) collective-permute-start(f32[512,512]{1,0:T(8,128)} %copy-done.11), channel_id=1, source_target_pairs={{0,8},{4,12},{8,16},{12,20},{1,9},{5,13},{9,17},{13,21},{2,10},{6,... | collective-permute-start | bytes 3145736 | tf_op jit(solution)/shard_map/ppermute | solution.py:679
  104.3 3.2 %block_term.12 = (f32[512,512]{1,0:T(8,128)S(1)}, f32[8,128]{1,0:T(8,128)S(1)}) custom-call(s32[2]{0:T(128)S(1)} %copy-done.4, s32[8]{0:T(128)S(1)} %copy-done.6, f32[4,512,512]{2,1,0:T(8,128)} %get-tuple-element.38.refs_2_.refs_15_, f32[512,512]{1,0:T(8,128)} %collective-permute-done.refs_3_, f32[4,512,512]{2,1,0:T(8,128)} %get-tuple-element.43.refs_4_.refs_5_.refs_6_, ...), custom_call_target="tpu_custom_call" | custom-call | flops 1000 | bytes 1000 | tf_op jit(solution)/shard_map/block_term/pallas_call | solution.py:438
  107.5 6.5 %collective-permute-start.18 = (f32[512,512]{1,0:T(8,128)S(1)}, f32[512,512]{1,0:T(8,128)S(1)}, u32[]{:S(2)}, u32[]{:S(2)}) collective-permute-start(f32[512,512]{1,0:T(8,128)S(1)} %get-tuple-element.61), channel_id=1, source_target_pairs={{0,8},{4,12},{24,16},{28,20},{1,9},{5,13},{25,17},{29,21},{2,10},{... | collective-permute-start | bytes 3145736 | tf_op jit(solution)/shard_map/ppermute | solution.py:679
  114.2 9.1 %collective-permute-done.1.refs_5_.refs_4_ = f32[512,512]{1,0:T(8,128)} collective-permute-done((f32[512,512]{1,0:T(8,128)}, f32[512,512]{1,0:T(8,128)}, u32[]{:S(2)}, u32[]{:S(2)}) %collective-permute-start.1) | collective-permute-done | bytes 1048608 | tf_op jit(solution)/shard_map/ppermute | solution.py:638
  123.2 2.9 %block_term.13 = (f32[512,512]{1,0:T(8,128)S(1)}, f32[8,128]{1,0:T(8,128)S(1)}) custom-call(s32[2]{0:T(128)S(1)} %copy-done.4, s32[8]{0:T(128)S(1)} %copy-done.6, f32[4,512,512]{2,1,0:T(8,128)} %get-tuple-element.38.refs_2_.refs_15_, f32[512,512]{1,0:T(8,128)} %collective-permute-done.refs_3_, f32[512,512]{1,0:T(8,128)} %collective-permute-done.7.refs_4_, ...), custom_call_target="tpu_custom_call" | custom-call | flops 1000 | bytes 1000 | tf_op jit(solution)/shard_map/block_term/pallas_call | solution.py:438
  126.2 6.2 %collective-permute-start.15 = (f32[512,512]{1,0:T(8,128)S(1)}, f32[512,512]{1,0:T(8,128)S(1)}, u32[]{:S(2)}, u32[]{:S(2)}) collective-permute-start(f32[512,512]{1,0:T(8,128)S(1)} %get-tuple-element.58), channel_id=1, source_target_pairs={{0,8},{4,12},{8,16},{12,20},{16,24},{20,28},{1,9},{5,13},{9,17},{1... | collective-permute-start | bytes 3145736 | tf_op jit(solution)/shard_map/ppermute | solution.py:679
  132.3 3.0 %block_term.14 = (f32[512,512]{1,0:T(8,128)S(1)}, f32[8,128]{1,0:T(8,128)S(1)}) custom-call(s32[2]{0:T(128)S(1)} %copy-done.4, s32[8]{0:T(128)S(1)} %copy-done.6, f32[4,512,512]{2,1,0:T(8,128)} %get-tuple-element.38.refs_2_.refs_15_, f32[512,512]{1,0:T(8,128)} %collective-permute-done.refs_3_, f32[512,512]{1,0:T(8,128)} %collective-permute-done.7.refs_4_, ...), custom_call_target="tpu_custom_call" | custom-call | flops 1000 | bytes 1000 | tf_op jit(solution)/shard_map/block_term/pallas_call | solution.py:438
  136.6 9.0 %collective-permute-done.17.refs_7_.refs_8_ = f32[512,512]{1,0:T(8,128)S(1)} collective-permute-done((f32[512,512]{1,0:T(8,128)}, f32[512,512]{1,0:T(8,128)S(1)}, u32[]{:S(2)}, u32[]{:S(2)}) %collective-permute-start.17) | collective-permute-done | bytes 1048608 | tf_op jit(solution)/shard_map/ppermute | solution.py:638
  145.6 3.4 %block_term.15 = (f32[512,512]{1,0:T(8,128)S(1)}, f32[8,128]{1,0:T(8,128)S(1)}) custom-call(s32[2]{0:T(128)S(1)} %copy-done.4, s32[8]{0:T(128)S(1)} %copy-done.6, f32[4,512,512]{2,1,0:T(8,128)} %get-tuple-element.38.refs_2_.refs_15_, f32[512,512]{1,0:T(8,128)} %collective-permute-done.refs_3_, f32[512,512]{1,0:T(8,128)} %collective-permute-done.7.refs_4_, ...), custom_call_target="tpu_custom_call" | custom-call | flops 1000 | bytes 1000 | tf_op jit(solution)/shard_map/block_term/pallas_call | solution.py:438
  149.7 6.9 %collective-permute-start.19 = (f32[512,512]{1,0:T(8,128)S(1)}, f32[512,512]{1,0:T(8,128)S(1)}, u32[]{:S(2)}, u32[]{:S(2)}) collective-permute-start(f32[512,512]{1,0:T(8,128)S(1)} %get-tuple-element.70), channel_id=1, source_target_pairs={{0,8},{4,12},{8,16},{12,20},{1,9},{5,13},{9,17},{13,21},{2,10},{6,... | collective-permute-start | bytes 3145736 | tf_op jit(solution)/shard_map/ppermute | solution.py:679
  156.7 9.4 %collective-permute-done.10.refs_9_.refs_7_ = f32[512,512]{1,0:T(8,128)S(1)} collective-permute-done((f32[512,512]{1,0:T(8,128)S(1)}, f32[512,512]{1,0:T(8,128)S(1)}, u32[]{:S(2)}, u32[]{:S(2)}) %collective-permute-start.10) | collective-permute-done | bytes 1048608 | tf_op jit(solution)/shard_map/ppermute | solution.py:638
  166.1 3.6 %block_term.16 = (f32[512,512]{1,0:T(8,128)S(1)}, f32[8,128]{1,0:T(8,128)S(1)}) custom-call(s32[2]{0:T(128)S(1)} %copy-done.4, s32[8]{0:T(128)S(1)} %copy-done.6, f32[4,512,512]{2,1,0:T(8,128)} %get-tuple-element.38.refs_2_.refs_15_, f32[512,512]{1,0:T(8,128)} %collective-permute-done.refs_3_, f32[512,512]{1,0:T(8,128)} %collective-permute-done.7.refs_4_, ...), custom_call_target="tpu_custom_call" | custom-call | flops 1000 | bytes 1000 | tf_op jit(solution)/shard_map/block_term/pallas_call | solution.py:438
  169.7 3.6 %block_term.17 = (f32[512,512]{1,0:T(8,128)S(1)}, f32[8,128]{1,0:T(8,128)S(1)}) custom-call(s32[2]{0:T(128)S(1)} %copy-done.4, s32[8]{0:T(128)S(1)} %copy-done.6, f32[4,512,512]{2,1,0:T(8,128)} %get-tuple-element.38.refs_2_.refs_15_, f32[512,512]{1,0:T(8,128)} %collective-permute-done.refs_3_, f32[512,512]{1,0:T(8,128)} %collective-permute-done.7.refs_4_, ...), custom_call_target="tpu_custom_call" | custom-call | flops 1000 | bytes 1000 | tf_op jit(solution)/shard_map/block_term/pallas_call | solution.py:438
  175.1 7.6 %collective-permute-start.20 = (f32[512,512]{1,0:T(8,128)S(1)}, f32[512,512]{1,0:T(8,128)S(1)}, u32[]{:S(2)}, u32[]{:S(2)}) collective-permute-start(f32[512,512]{1,0:T(8,128)S(1)} %add.26), channel_id=1, source_target_pairs={{0,8},{4,12},{8,16},{12,20},{16,24},{20,28},{1,9},{5,13},{9,17},{1... | collective-permute-start | bytes 3145736 | tf_op jit(solution)/shard_map/ppermute | solution.py:679
  185.2 4.0 %block_term.19 = (f32[512,512]{1,0:T(8,128)S(1)}, f32[8,128]{1,0:T(8,128)}) custom-call(s32[2]{0:T(128)S(1)} %copy-done.4, s32[8]{0:T(128)S(1)} %copy-done.6, f32[4,512,512]{2,1,0:T(8,128)} %get-tuple-element.38.refs_2_.refs_15_, f32[512,512]{1,0:T(8,128)} %collective-permute-done.refs_3_, f32[512,512]{1,0:T(8,128)} %collective-permute-done.1.refs_5_.refs_4_, ...), custom_call_target="tpu_custom_call" | custom-call | flops 1000 | bytes 1000 | tf_op jit(solution)/shard_map/block_term/pallas_call | solution.py:438
  189.2 10.3 %collective-permute-done.22 = f32[512,512]{1,0:T(8,128)S(1)} collective-permute-done((f32[512,512]{1,0:T(8,128)S(1)}, f32[512,512]{1,0:T(8,128)S(1)}, u32[]{:S(2)}, u32[]{:S(2)}) %collective-permute-start.22) | collective-permute-done | bytes 1048608 | tf_op jit(solution)/shard_map/ppermute | solution.py:679
  (90 shorter events, 50.7 us)
Async XLA Ops:
  5.4 26.8 %collective-permute-start = (f32[512,512]{1,0:T(8,128)}, f32[512,512]{1,0:T(8,128)}, u32[]{:S(2)}, u32[]{:S(2)}) collective-permute-start(f32[512,512]{1,0:T(8,128)} %bitcast.19), channel_id=1, source_target_pairs={{0,4},{4,0},{8,12},{12,8},{16,20},{20,16},{24,28},{28,24},{1,5},{5... | collective-permute-start | bytes 3145736 | tf_op jit(solution)/shard_map/ppermute | solution.py:638
  20.7 20.5 %collective-permute-start.4 = (f32[1,2,32,256]{3,2,1,0:T(8,128)}, f32[1,2,32,256]{3,2,1,0:T(8,128)S(1)}, u32[]{:S(2)}, u32[]{:S(2)}) collective-permute-start(f32[1,2,32,256]{3,2,1,0:T(8,128)} %get-tuple-element.47), channel_id=1, source_target_pairs={{0,8},{4,12},{8,0},{12,4},{16,24},{20,28},{24,16},{28,20},{1,9},{5... | collective-permute-start | bytes 196616 | tf_op jit(solution)/shard_map/ppermute | solution.py:660
  23.3 19.4 %collective-permute-start.3 = (f32[16,4096]{1,0:T(8,128)S(1)}, f32[16,4096]{1,0:T(8,128)S(1)}, u32[]{:S(2)}, u32[]{:S(2)}) collective-permute-start(f32[16,4096]{1,0:T(8,128)S(1)} %get-tuple-element.74), channel_id=1, source_target_pairs={{1,0},{2,1},{3,2},{5,4},{6,5},{7,6},{9,8},{10,9},{11,10},{13,12},{... | collective-permute-start | bytes 786440 | tf_op jit(solution)/shard_map/ppermute | solution.py:651
  24.6 18.1 %collective-permute-start.2 = (f32[16,4096]{1,0:T(8,128)S(1)}, f32[16,4096]{1,0:T(8,128)}, u32[]{:S(2)}, u32[]{:S(2)}) collective-permute-start(f32[16,4096]{1,0:T(8,128)S(1)} %get-tuple-element.75), channel_id=1, source_target_pairs={{0,1},{1,2},{2,3},{4,5},{5,6},{6,7},{8,9},{9,10},{10,11},{12,13},{... | collective-permute-start | bytes 786440 | tf_op jit(solution)/shard_map/ppermute | solution.py:650
  28.4 42.8 %collective-permute-start.7 = (f32[512,512]{1,0:T(8,128)}, f32[512,512]{1,0:T(8,128)}, u32[]{:S(2)}, u32[]{:S(2)}) collective-permute-start(f32[512,512]{1,0:T(8,128)} %get-tuple-element.40.refs_16_), channel_id=1, source_target_pairs={{0,4},{4,0},{8,12},{12,8},{16,20},{20,16},{24,28},{28,24},{1,5},{5... | collective-permute-start | bytes 3145736 | tf_op jit(solution)/shard_map/ppermute | solution.py:638
  35.7 35.4 %collective-permute-start.8 = (f32[512,512]{1,0:T(8,128)}, f32[512,512]{1,0:T(8,128)}, u32[]{:S(2)}, u32[]{:S(2)}) collective-permute-start(f32[512,512]{1,0:T(8,128)} %get-tuple-element.49), channel_id=1, source_target_pairs={{0,8},{4,12},{24,16},{28,20},{1,9},{5,13},{25,17},{29,21},{2,10},{... | collective-permute-start | bytes 3145736 | tf_op jit(solution)/shard_map/ppermute | solution.py:679
  43.4 24.5 %collective-permute-start.5 = (f32[2,2,32,256]{3,2,1,0:T(8,128)}, f32[2,2,32,256]{3,2,1,0:T(8,128)S(1)}, u32[]{:S(2)}, u32[]{:S(2)}) collective-permute-start(f32[2,2,32,256]{3,2,1,0:T(8,128)} %held.5), channel_id=1, source_target_pairs={{0,16},{4,20},{8,24},{12,28},{16,0},{20,4},{24,8},{28,12},{1,17},{... | collective-permute-start | bytes 393224 | tf_op jit(solution)/shard_map/ppermute | solution.py:660
  67.9 28.5 %copy-start.10 = (s32[8,8]{1,0:T(8,128)S(1)}, s32[8,8]{1,0:T(8,128)}, u32[]{:S(2)}) copy-start(s32[8,8]{1,0:T(8,128)} %owner_ref.1) | copy-start | bytes 772
  69.6 6.6 %collective-permute-start.6 = (f32[4,2,32,256]{3,2,1,0:T(8,128)S(1)}, f32[4,2,32,256]{3,2,1,0:T(8,128)}, u32[]{:S(2)}, u32[]{:S(2)}) collective-permute-start(f32[4,2,32,256]{3,2,1,0:T(8,128)S(1)} %pad_maximum_fusion.1), channel_id=1, source_target_pairs={{0,4},{4,0},{8,12},{12,8},{16,20},{20,16},{24,28},{28,24},{1,5},{5... | collective-permute-start | bytes 786440 | tf_op jit(solution)/shard_map/ppermute | solution.py:660
  76.2 24.6 %collective-permute-start.9 = (f32[512,512]{1,0:T(8,128)}, f32[512,512]{1,0:T(8,128)}, u32[]{:S(2)}, u32[]{:S(2)}) collective-permute-start(f32[512,512]{1,0:T(8,128)} %get-tuple-element.51), channel_id=1, source_target_pairs={{0,4},{4,0},{8,12},{12,8},{16,20},{20,16},{24,28},{28,24},{1,5},{5... | collective-permute-start | bytes 3145736 | tf_op jit(solution)/shard_map/ppermute | solution.py:638
  78.3 24.8 %collective-permute-start.14 = (f32[512,512]{1,0:T(8,128)}, f32[512,512]{1,0:T(8,128)}, u32[]{:S(2)}, u32[]{:S(2)}) collective-permute-start(f32[512,512]{1,0:T(8,128)} %copy-done.11), channel_id=1, source_target_pairs={{16,8},{20,12},{24,16},{28,20},{17,9},{21,13},{25,17},{29,21},{18,... | collective-permute-start | bytes 3145736 | tf_op jit(solution)/shard_map/ppermute | solution.py:679
  79.9 23.2 %collective-permute-start.13 = (f32[512,512]{1,0:T(8,128)}, f32[512,512]{1,0:T(8,128)}, u32[]{:S(2)}, u32[]{:S(2)}) collective-permute-start(f32[512,512]{1,0:T(8,128)} %copy-done.11), channel_id=1, source_target_pairs={{0,8},{4,12},{8,16},{12,20},{1,9},{5,13},{9,17},{13,21},{2,10},{6,... | collective-permute-start | bytes 3145736 | tf_op jit(solution)/shard_map/ppermute | solution.py:679
  91.1 1.3 collective-permute-start.11
  92.4 4.0 %collective-permute-start.12 = (f32[16,640]{1,0:T(8,128)S(1)}, f32[16,640]{1,0:T(8,128)S(1)}, u32[]{:S(2)}, u32[]{:S(2)}) collective-permute-start(f32[16,640]{1,0:T(8,128)S(1)} %add.24), channel_id=1, source_target_pairs={{0,2},{1,3},{2,0},{3,1},{4,6},{5,7},{6,4},{7,5},{8,10},{9,11},{10,... | collective-permute-start | bytes 122888 | tf_op jit(solution)/shard_map/ppermute | solution.py:724
  94.0 29.2 %collective-permute-start.1 = (f32[512,512]{1,0:T(8,128)}, f32[512,512]{1,0:T(8,128)}, u32[]{:S(2)}, u32[]{:S(2)}) collective-permute-start(f32[512,512]{1,0:T(8,128)} %get-tuple-element.39.refs_17_), channel_id=1, source_target_pairs={{0,4},{4,0},{8,12},{12,8},{16,20},{20,16},{24,28},{28,24},{1,5},{5... | collective-permute-start | bytes 3145736 | tf_op jit(solution)/shard_map/ppermute | solution.py:638
  100.8 44.8 %collective-permute-start.17 = (f32[512,512]{1,0:T(8,128)}, f32[512,512]{1,0:T(8,128)S(1)}, u32[]{:S(2)}, u32[]{:S(2)}) collective-permute-start(f32[512,512]{1,0:T(8,128)} %get-tuple-element.60), channel_id=1, source_target_pairs={{0,4},{4,0},{8,12},{12,8},{16,20},{20,16},{24,28},{28,24},{1,5},{5... | collective-permute-start | bytes 3145736 | tf_op jit(solution)/shard_map/ppermute | solution.py:638
  107.5 38.1 %collective-permute-start.18 = (f32[512,512]{1,0:T(8,128)S(1)}, f32[512,512]{1,0:T(8,128)S(1)}, u32[]{:S(2)}, u32[]{:S(2)}) collective-permute-start(f32[512,512]{1,0:T(8,128)S(1)} %get-tuple-element.61), channel_id=1, source_target_pairs={{0,8},{4,12},{24,16},{28,20},{1,9},{5,13},{25,17},{29,21},{2,10},{... | collective-permute-start | bytes 3145736 | tf_op jit(solution)/shard_map/ppermute | solution.py:679
  114.0 52.1 %collective-permute-start.10 = (f32[512,512]{1,0:T(8,128)S(1)}, f32[512,512]{1,0:T(8,128)S(1)}, u32[]{:S(2)}, u32[]{:S(2)}) collective-permute-start(f32[512,512]{1,0:T(8,128)S(1)} %copy-done.13), channel_id=1, source_target_pairs={{0,4},{4,0},{8,12},{12,8},{16,20},{20,16},{24,28},{28,24},{1,5},{5... | collective-permute-start | bytes 3145736 | tf_op jit(solution)/shard_map/ppermute | solution.py:638
  126.2 30.5 %collective-permute-start.15 = (f32[512,512]{1,0:T(8,128)S(1)}, f32[512,512]{1,0:T(8,128)S(1)}, u32[]{:S(2)}, u32[]{:S(2)}) collective-permute-start(f32[512,512]{1,0:T(8,128)S(1)} %get-tuple-element.58), channel_id=1, source_target_pairs={{0,8},{4,12},{8,16},{12,20},{16,24},{20,28},{1,9},{5,13},{9,17},{1... | collective-permute-start | bytes 3145736 | tf_op jit(solution)/shard_map/ppermute | solution.py:679
  135.3 21.3 %collective-permute-start.16 = (f32[512,512]{1,0:T(8,128)S(1)}, f32[512,512]{1,0:T(8,128)S(1)}, u32[]{:S(2)}, u32[]{:S(2)}) collective-permute-start(f32[512,512]{1,0:T(8,128)S(1)} %get-tuple-element.59), channel_id=1, source_target_pairs={{8,0},{12,4},{16,8},{20,12},{24,16},{28,20},{9,1},{13,5},{17,9},{2... | collective-permute-start | bytes 3145736 | tf_op jit(solution)/shard_map/ppermute | solution.py:679
  149.0 24.3 %collective-permute-start.21 = (f32[512,512]{1,0:T(8,128)S(1)}, f32[512,512]{1,0:T(8,128)S(1)}, u32[]{:S(2)}, u32[]{:S(2)}) collective-permute-start(f32[512,512]{1,0:T(8,128)S(1)} %get-tuple-element.70), channel_id=1, source_target_pairs={{16,8},{20,12},{24,16},{28,20},{17,9},{21,13},{25,17},{29,21},{18,... | collective-permute-start | bytes 3145736 | tf_op jit(solution)/shard_map/ppermute | solution.py:679
  149.7 25.1 %collective-permute-start.19 = (f32[512,512]{1,0:T(8,128)S(1)}, f32[512,512]{1,0:T(8,128)S(1)}, u32[]{:S(2)}, u32[]{:S(2)}) collective-permute-start(f32[512,512]{1,0:T(8,128)S(1)} %get-tuple-element.70), channel_id=1, source_target_pairs={{0,8},{4,12},{8,16},{12,20},{1,9},{5,13},{9,17},{13,21},{2,10},{6,... | collective-permute-start | bytes 3145736 | tf_op jit(solution)/shard_map/ppermute | solution.py:679
  173.6 26.0 %collective-permute-start.22 = (f32[512,512]{1,0:T(8,128)S(1)}, f32[512,512]{1,0:T(8,128)S(1)}, u32[]{:S(2)}, u32[]{:S(2)}) collective-permute-start(f32[512,512]{1,0:T(8,128)S(1)} %add.28), channel_id=1, source_target_pairs={{8,0},{12,4},{16,8},{20,12},{24,16},{28,20},{9,1},{13,5},{17,9},{2... | collective-permute-start | bytes 3145736 | tf_op jit(solution)/shard_map/ppermute | solution.py:679
  175.1 25.8 %collective-permute-start.20 = (f32[512,512]{1,0:T(8,128)S(1)}, f32[512,512]{1,0:T(8,128)S(1)}, u32[]{:S(2)}, u32[]{:S(2)}) collective-permute-start(f32[512,512]{1,0:T(8,128)S(1)} %add.26), channel_id=1, source_target_pairs={{0,8},{4,12},{8,16},{12,20},{16,24},{20,28},{1,9},{5,13},{9,17},{1... | collective-permute-start | bytes 3145736 | tf_op jit(solution)/shard_map/ppermute | solution.py:679
  (15 other events, 131.7 us)
